TPU v7x, 32 devices: a whole 2x2x4 slice. The times are simulated.
32 devices in a mesh: dp: 2 (over x), ctx: 4 (over y, core), seq: 4 (over z).
Axes of the slice: x: 2, y: 2, z: 4, core: 2. Of those that a mesh axis runs over, the one named last changes fastest.
Arguments:
- inputs: bfloat16 [4, 1024, 2304], P('dp', ('ctx', 'seq')), may hold values from -6 to 6
- positions: int32 [4, 1024], P('dp', 'ctx'), may hold values from 0 to 1023, as said below
- query_weight: bfloat16 [2304, 2048], P(('dp', 'ctx'), 'seq'), may hold values from -0.25 to 0.25
- key_weight: bfloat16 [2304, 1024], P(('dp', 'ctx', 'seq')), may hold values from -0.25 to 0.25
- value_weight: bfloat16 [2304, 1024], P(('dp', 'ctx', 'seq')), may hold values from -0.125 to 0.125
- output_weight: bfloat16 [2048, 2304], P('seq', ('dp', 'ctx')), may hold values from -0.125 to 0.125
- gate_weight: bfloat16 [2304, 9216], P(('dp', 'ctx'), 'seq'), may hold values from -0.125 to 0.125
- up_weight: bfloat16 [2304, 9216], P(('dp', 'ctx'), 'seq'), may hold values from -0.125 to 0.125
- down_weight: bfloat16 [9216, 2304], P('seq', ('dp', 'ctx')), may hold values from -0.0625 to 0.0625
- pre_attn_gain: bfloat16 [2304], P(('dp', 'ctx')), may hold values from 0.099609375 to 1.8984375
- post_attn_gain: bfloat16 [2304], P(('dp', 'ctx')), may hold values from 0.099609375 to 1.8984375
- pre_ffn_gain: bfloat16 [2304], P(('dp', 'ctx')), may hold values from 0.099609375 to 1.8984375
- post_ffn_gain: bfloat16 [2304], P(('dp', 'ctx')), may hold values from 0.099609375 to 1.8984375
- cotangent: bfloat16 [4, 1024, 2304], P('dp', ('ctx', 'seq')), may hold values from -6 to 6
Outputs:
- layer_output: bfloat16 [4, 1024, 2304], P('dp', ('ctx', 'seq'))
- input_grad: bfloat16 [4, 1024, 2304], P('dp', ('ctx', 'seq'))
- grad_query: float32 [2304, 2048], P(('dp', 'ctx'), 'seq')
- grad_key: float32 [2304, 1024], P(('dp', 'ctx', 'seq'))
- grad_value: float32 [2304, 1024], P(('dp', 'ctx', 'seq'))
- grad_output: float32 [2048, 2304], P('seq', ('dp', 'ctx'))
- grad_gate: float32 [2304, 9216], P(('dp', 'ctx'), 'seq')
- grad_up: float32 [2304, 9216], P(('dp', 'ctx'), 'seq')
- grad_down: float32 [9216, 2304], P('seq', ('dp', 'ctx'))
- grad_pre_attn: float32 [2304], P(('dp', 'ctx', 'seq'))
- grad_post_attn: float32 [2304], P(('dp', 'ctx', 'seq'))
- grad_pre_ffn: float32 [2304], P(('dp', 'ctx', 'seq'))
- grad_post_ffn: float32 [2304], P(('dp', 'ctx', 'seq'))
Inputs may be any that keep to these rules, and one draw needn't show every extreme that they name: Within each sequence positions count 0, 1, 2, ... and restart at 0 where a new document begins; a sequence holds 1 to 4 documents and the first sequence is a single document.
All inputs are finite; a program needn't handle non-finite values.
Results may differ from a plain program's by a relative error of at most 0.023.
The roundings to bfloat16 on the way count: a program that leaves them out, or rounds other values in their place, can miss the bound.
Values may be sent and summed in bfloat16 or wider, within the bound.
No kernel may reach another device: no remote copies, remote signals or barrier semaphores. Data moves between devices by JAX's collectives and lax.ppermute only.
A program may use at most 256 MiB of HBM per device.

v0:
```python
import math

import jax
import jax.numpy as jnp
from jax import lax
from jax.sharding import PartitionSpec as P

QUERY_HEAD_COUNT = 8
KEY_VALUE_HEADS = 4
HEAD_SIZE = 256


EPS = 1e-06
CAP = 50.0
BASE = 10000.0


def norm_gain(vector, gain):
    return vector * lax.rsqrt(jnp.mean(vector * vector, axis=-1, keepdims=True) + EPS) * gain


def geglu(gate_in, up_in):
    return jax.nn.gelu(gate_in, approximate=True) * up_in


def rounded(value):
    return lax.optimization_barrier(value.astype(jnp.bfloat16)).astype(jnp.float32)


def angle_tables(block_pos):
    half = HEAD_SIZE // 2
    freq = BASE ** (-jnp.arange(half, dtype=jnp.float32) * 2.0 / HEAD_SIZE)
    angle = block_pos.astype(jnp.float32)[..., None] * freq
    return (jnp.cos(angle)[:, :, None, :], jnp.sin(angle)[:, :, None, :])


def turn(vector, cosine, sine):
    half = HEAD_SIZE // 2
    lower = vector[..., :half]
    upper = vector[..., half:]
    return jnp.concatenate([lower * cosine - upper * sine, upper * cosine + lower * sine], axis=-1)


def turn_back(grad, cosine, sine):
    half = HEAD_SIZE // 2
    lower = grad[..., :half]
    upper = grad[..., half:]
    return jnp.concatenate([lower * cosine + upper * sine, upper * cosine - lower * sine], axis=-1)


def load_attention(
    query_weight, key_weight, value_weight, output_weight, gain_table, key_value_begin, kv_cols
):
    key_full, value_full = (
        lax.all_gather(key_weight, ("dp", "ctx", "seq"), axis=0, tiled=True),
        lax.all_gather(value_weight, ("dp", "ctx", "seq"), axis=0, tiled=True),
    )
    key_part = lax.dynamic_slice_in_dim(key_full, key_value_begin, kv_cols, 1)
    value_part = lax.dynamic_slice_in_dim(value_full, key_value_begin, kv_cols, 1)
    w_query, w_output, gain_full = (
        lax.all_gather(query_weight, ("dp", "ctx"), axis=0, tiled=True),
        lax.all_gather(output_weight, ("dp", "ctx"), axis=1, tiled=True),
        lax.all_gather(gain_table, ("dp", "ctx"), axis=0, tiled=True),
    )
    return (w_query, key_part, value_part, w_output, gain_full)


def load_ffn(w_gate, w_up, w_down):
    return (
        lax.all_gather(w_gate, ("dp", "ctx"), axis=0, tiled=True),
        lax.all_gather(w_up, ("dp", "ctx"), axis=0, tiled=True),
        lax.all_gather(w_down, ("dp", "ctx"), axis=1, tiled=True),
    )


def full_output(output_part):
    return lax.all_gather(output_part, "seq", axis=0, tiled=True)


def block_rows(local_rows):
    return lax.all_gather(local_rows, "seq", axis=1, tiled=True)


def row_total(partial_rows):
    return lax.psum_scatter(
        partial_rows.astype(jnp.bfloat16), "seq", scatter_dimension=1, tiled=True
    ).astype(jnp.float32)


def visible_mask(first_row, row_count, key_count, query_pos):
    query_idx = first_row + jnp.arange(row_count, dtype=jnp.int32)
    key_idx = jnp.arange(key_count, dtype=jnp.int32)
    return (key_idx[None, :] <= query_idx[:, None]) & (
        key_idx[None, :] >= (query_idx - query_pos)[:, None]
    )


def scores_of(queries, key_rows, first_row, query_pos):
    row_count = queries.shape[0]
    head_count = queries.shape[1] // HEAD_SIZE
    query_heads = queries.reshape(row_count, head_count, HEAD_SIZE)
    key_heads = key_rows.reshape(key_rows.shape[0], head_count, HEAD_SIZE)
    scores = jnp.einsum(
        "qhd,khd->hqk", query_heads, key_heads, preferred_element_type=jnp.float32
    ) * HEAD_SIZE ** (-0.5)
    bent = jnp.tanh(scores / CAP)
    visible = visible_mask(first_row, row_count, key_rows.shape[0], query_pos)
    masked = jnp.where(visible[None], CAP * bent, -1e30)
    return (query_heads, key_heads, bent, masked)


def attend_forward(queries, key_rows, value_rows, query_pos, first_row):
    query_heads, key_heads, bent, masked = scores_of(queries, key_rows, first_row, query_pos)
    head_count = query_heads.shape[1]
    value_heads = value_rows.reshape(value_rows.shape[0], head_count, HEAD_SIZE)
    row_max = jnp.max(masked, axis=-1, keepdims=True)
    exponent = jnp.exp(masked - row_max)
    row_sum = jnp.sum(exponent, axis=-1, keepdims=True)
    probability = (exponent / row_sum).astype(jnp.bfloat16)
    log_total = (row_max + jnp.log(row_sum))[..., 0]
    result = jnp.einsum(
        "hqk,khd->qhd", probability, value_heads, preferred_element_type=jnp.float32
    )
    return (
        result.astype(jnp.bfloat16).reshape(queries.shape[0], head_count * HEAD_SIZE),
        log_total,
    )


def attend_backward(queries, key_rows, value_rows, query_pos, first_row, log_total, grad_rows):
    query_heads, key_heads, bent, masked = scores_of(queries, key_rows, first_row, query_pos)
    head_count = query_heads.shape[1]
    value_heads = value_rows.reshape(value_rows.shape[0], head_count, HEAD_SIZE)
    grad_heads = grad_rows.reshape(queries.shape[0], head_count, HEAD_SIZE)
    probability = jnp.exp(masked - log_total[..., None])
    prob_low = probability.astype(jnp.bfloat16)
    grad_value = jnp.einsum(
        "hqk,qhd->khd", prob_low, grad_heads, preferred_element_type=jnp.float32
    )
    grad_prob = jnp.einsum(
        "qhd,khd->hqk", grad_heads, value_heads, preferred_element_type=jnp.float32
    )
    delta = jnp.sum(probability * grad_prob, axis=-1, keepdims=True)
    grad_scores = (probability * (grad_prob - delta) * (1.0 - bent * bent)).astype(jnp.bfloat16)
    grad_query = jnp.einsum(
        "hqk,khd->qhd", grad_scores, key_heads, preferred_element_type=jnp.float32
    ) * HEAD_SIZE ** (-0.5)
    grad_key = jnp.einsum(
        "hqk,qhd->khd", grad_scores, query_heads, preferred_element_type=jnp.float32
    ) * HEAD_SIZE ** (-0.5)
    key_count = key_rows.shape[0]
    return (
        grad_query.reshape(queries.shape[0], head_count * HEAD_SIZE),
        grad_key.reshape(key_count, head_count * HEAD_SIZE),
        grad_value.reshape(key_count, head_count * HEAD_SIZE),
    )


def local(
    inputs,
    positions,
    query_weight,
    key_weight,
    value_weight,
    output_weight,
    gate_weight,
    up_weight,
    down_weight,
    pre_attn_gain,
    post_attn_gain,
    pre_ffn_gain,
    post_ffn_gain,
    cotangent,
):
    seqs, tokens, width = inputs.shape
    block_len = positions.shape[1]
    full_len = block_len * lax.axis_size("ctx")
    offset = lax.axis_index("ctx") * block_len
    head_count = QUERY_HEAD_COUNT // lax.axis_size("seq")
    key_value_group = QUERY_HEAD_COUNT // KEY_VALUE_HEADS
    kv_heads = max(head_count // key_value_group, 1)
    kv_cols = kv_heads * HEAD_SIZE
    repeat_by = head_count // kv_heads
    head_cols = head_count * HEAD_SIZE
    key_value_begin = lax.axis_index("seq") * head_count // key_value_group * HEAD_SIZE
    cosine, sine = angle_tables(positions)
    gain_table = jnp.stack([pre_attn_gain, post_attn_gain, pre_ffn_gain, post_ffn_gain], axis=1)
    fwd_attn = load_attention(
        query_weight, key_weight, value_weight, output_weight, gain_table, key_value_begin, kv_cols
    )
    fwd_ffn = load_ffn(gate_weight, up_weight, down_weight)
    w_query, key_matrix, value_matrix, w_output, gain_full = fwd_attn
    w_gate, w_up, w_down = fwd_ffn
    gain_float = gain_full.astype(jnp.float32)
    gain_one = gain_float[:, 0]
    gain_two = gain_float[:, 1]
    gain_three = gain_float[:, 2]
    gain_four = gain_float[:, 3]
    x_float = inputs.astype(jnp.float32)
    normed_one = norm_gain(x_float, gain_one).astype(jnp.bfloat16)
    block_one = block_rows(normed_one)
    query_raw = jnp.einsum("srd,de->sre", block_one, w_query, preferred_element_type=jnp.float32)
    key_raw = jnp.einsum("srd,de->sre", block_one, key_matrix, preferred_element_type=jnp.float32)
    value_raw = jnp.einsum(
        "srd,de->sre", block_one, value_matrix, preferred_element_type=jnp.float32
    )
    query_rot = (
        turn(query_raw.reshape(seqs, block_len, head_count, HEAD_SIZE), cosine, sine)
        .astype(jnp.bfloat16)
        .reshape(seqs, block_len, head_cols)
    )
    key_rot = (
        turn(key_raw.reshape(seqs, block_len, kv_heads, HEAD_SIZE), cosine, sine)
        .astype(jnp.bfloat16)
        .reshape(seqs, block_len, kv_cols)
    )
    key_all, value_all = (
        lax.all_gather(key_rot, "ctx", axis=1, tiled=True),
        lax.all_gather(value_raw.astype(jnp.bfloat16), "ctx", axis=1, tiled=True),
    )
    key_broadcast = jnp.repeat(
        key_all.reshape(seqs, full_len, kv_heads, HEAD_SIZE), repeat_by, axis=2
    ).reshape(seqs, full_len, head_cols)
    value_broadcast = jnp.repeat(
        value_all.reshape(seqs, full_len, kv_heads, HEAD_SIZE), repeat_by, axis=2
    ).reshape(seqs, full_len, head_cols)
    query_block = math.gcd(block_len, 512)
    block_count = block_len // query_block
    item_count = seqs * block_count
    item_index = jnp.arange(item_count, dtype=jnp.int32)
    block_starts = offset + item_index % block_count * query_block
    seq_owner = item_index // block_count

    def forward_item(pieces):
        queries, query_pos, first_row, seq_id = pieces
        key_rows = lax.dynamic_index_in_dim(key_broadcast, seq_id, 0, keepdims=False)
        value_rows = lax.dynamic_index_in_dim(value_broadcast, seq_id, 0, keepdims=False)
        return attend_forward(queries, key_rows, value_rows, query_pos, first_row)

    head_items, log_total = lax.map(forward_item, (query_rot, positions, block_starts, seq_owner))
    out_full = full_output(w_output)
    heads_tok = lax.all_to_all(head_items, "seq", split_axis=1, concat_axis=2, tiled=True)
    project = jnp.einsum("ste,ed->std", heads_tok, out_full, preferred_element_type=jnp.float32)
    middle = x_float + norm_gain(project, gain_two)
    normed_two = norm_gain(middle, gain_three).astype(jnp.bfloat16)
    ffn_input = block_rows(normed_two)
    gate = jnp.einsum("srd,df->srf", ffn_input, w_gate, preferred_element_type=jnp.float32)
    upper = jnp.einsum("srd,df->srf", ffn_input, w_up, preferred_element_type=jnp.float32)
    hidden = geglu(gate, upper).astype(jnp.bfloat16)
    feed = row_total(jnp.einsum("srf,fd->srd", hidden, w_down, preferred_element_type=jnp.float32))
    layer_output = (middle + norm_gain(feed, gain_four)).astype(jnp.bfloat16)
    back_attn = load_attention(
        query_weight, key_weight, value_weight, output_weight, gain_table, key_value_begin, kv_cols
    )
    back_ffn = load_ffn(gate_weight, up_weight, down_weight)
    bq_weight, bk_weight, bv_weight, bo_weight = (
        back_attn[0],
        back_attn[1],
        back_attn[2],
        back_attn[3],
    )
    bgate_weight, bup_weight, bdown_weight = back_ffn
    grad_top = cotangent.astype(jnp.float32)
    unused, pull_four = jax.vjp(norm_gain, feed, gain_four)
    grad_feed, grad_g_four = pull_four(grad_top)
    grad_feed_rows = block_rows(grad_feed.astype(jnp.bfloat16))
    grad_hidden = jnp.einsum(
        "srd,fd->srf", grad_feed_rows, bdown_weight, preferred_element_type=jnp.float32
    )
    grad_down_part = jnp.einsum(
        "srf,srd->fd", hidden, grad_feed_rows, preferred_element_type=jnp.float32
    )
    unused, pull_act = jax.vjp(geglu, gate, upper)
    grad_gate_act, grad_up_act = pull_act(grad_hidden)
    grad_gate_act = grad_gate_act.astype(jnp.bfloat16)
    grad_up_act = grad_up_act.astype(jnp.bfloat16)
    grad_rows_part = jnp.einsum(
        "srf,df->srd", grad_gate_act, bgate_weight, preferred_element_type=jnp.float32
    ) + jnp.einsum("srf,df->srd", grad_up_act, bup_weight, preferred_element_type=jnp.float32)
    grad_gate_part = jnp.einsum(
        "srd,srf->df", ffn_input, grad_gate_act, preferred_element_type=jnp.float32
    )
    grad_up_part = jnp.einsum(
        "srd,srf->df", ffn_input, grad_up_act, preferred_element_type=jnp.float32
    )
    ffn_grads = (
        lax.psum_scatter(
            grad_gate_part.astype(jnp.bfloat16), ("dp", "ctx"), scatter_dimension=0, tiled=True
        ).astype(jnp.float32),
        lax.psum_scatter(
            grad_up_part.astype(jnp.bfloat16), ("dp", "ctx"), scatter_dimension=0, tiled=True
        ).astype(jnp.float32),
        lax.psum_scatter(
            grad_down_part.astype(jnp.bfloat16), ("dp", "ctx"), scatter_dimension=1, tiled=True
        ).astype(jnp.float32),
    )
    grad_normed_two = row_total(grad_rows_part)
    unused, pull_three = jax.vjp(norm_gain, middle, gain_three)
    grad_mid_norm, grad_g_three = pull_three(grad_normed_two)
    grad_middle = grad_top + grad_mid_norm
    unused, pull_two = jax.vjp(norm_gain, project, gain_two)
    grad_project, grad_g_two = pull_two(grad_middle)
    grad_project = grad_project.astype(jnp.bfloat16)
    out_back = full_output(bo_weight)
    grad_heads_tok = jnp.einsum(
        "std,ed->ste", grad_project, out_back, preferred_element_type=jnp.float32
    ).astype(jnp.bfloat16)
    grad_output_part = lax.psum_scatter(
        jnp.einsum(
            "ste,std->ed", heads_tok, grad_project, preferred_element_type=jnp.float32
        ).astype(jnp.bfloat16),
        "seq",
        scatter_dimension=0,
        tiled=True,
    )
    grad_heads = lax.all_to_all(grad_heads_tok, "seq", split_axis=2, concat_axis=1, tiled=True)

    def backward_item(carry, pieces):
        key_acc, value_acc = carry
        queries, query_pos, first_row, seq_id, log_part, grad_part = pieces
        key_rows = lax.dynamic_index_in_dim(key_broadcast, seq_id, 0, keepdims=False)
        value_rows = lax.dynamic_index_in_dim(value_broadcast, seq_id, 0, keepdims=False)
        grad_query, grad_key, grad_value = attend_backward(
            queries, key_rows, value_rows, query_pos, first_row, log_part, grad_part
        )
        key_acc = lax.dynamic_update_index_in_dim(
            key_acc,
            lax.dynamic_index_in_dim(key_acc, seq_id, 0, keepdims=False) + grad_key,
            seq_id,
            0,
        )
        value_acc = lax.dynamic_update_index_in_dim(
            value_acc,
            lax.dynamic_index_in_dim(value_acc, seq_id, 0, keepdims=False) + grad_value,
            seq_id,
            0,
        )
        return ((key_acc, value_acc), grad_query)

    empty = jnp.zeros((seqs, full_len, head_cols), jnp.float32)
    (key_terms, value_terms), grad_query_items = lax.scan(
        backward_item,
        (empty, empty),
        (query_rot, positions, block_starts, seq_owner, log_total, grad_heads),
    )
    key_sums, value_sums = (
        lax.psum_scatter(
            key_terms.astype(jnp.bfloat16), "ctx", scatter_dimension=1, tiled=True
        ).astype(jnp.float32),
        lax.psum_scatter(
            value_terms.astype(jnp.bfloat16), "ctx", scatter_dimension=1, tiled=True
        ).astype(jnp.float32),
    )
    grad_query_rot = rounded(grad_query_items.reshape(seqs, block_len, head_count, HEAD_SIZE))
    grad_query_raw = (
        turn_back(grad_query_rot, cosine, sine)
        .astype(jnp.bfloat16)
        .reshape(seqs, block_len, head_cols)
    )
    grad_key_rot = rounded(key_sums.reshape(seqs, block_len, head_count, HEAD_SIZE))
    grad_key_raw = (
        turn_back(grad_key_rot, cosine, sine)
        .astype(jnp.bfloat16)
        .reshape(seqs, block_len, head_cols)
    )
    grad_value_raw = value_sums.astype(jnp.bfloat16)
    key_expand = jnp.repeat(
        bk_weight.reshape(width, kv_heads, HEAD_SIZE), repeat_by, axis=1
    ).reshape(width, head_cols)
    value_expand = jnp.repeat(
        bv_weight.reshape(width, kv_heads, HEAD_SIZE), repeat_by, axis=1
    ).reshape(width, head_cols)
    grad_block_one = jnp.einsum(
        "sre,de->srd", grad_query_raw, bq_weight, preferred_element_type=jnp.float32
    )
    grad_block_one = grad_block_one + jnp.einsum(
        "sre,de->srd", grad_key_raw, key_expand, preferred_element_type=jnp.float32
    )
    grad_block_one = grad_block_one + jnp.einsum(
        "sre,de->srd", grad_value_raw, value_expand, preferred_element_type=jnp.float32
    )
    grad_normed_one = row_total(grad_block_one)
    grad_query_part = jnp.einsum(
        "srd,sre->de", block_one, grad_query_raw, preferred_element_type=jnp.float32
    )
    grad_key_wide = jnp.einsum(
        "srd,sre->de", block_one, grad_key_raw, preferred_element_type=jnp.float32
    )
    grad_value_wide = jnp.einsum(
        "srd,sre->de", block_one, grad_value_raw, preferred_element_type=jnp.float32
    )
    grad_key_part = jnp.sum(
        grad_key_wide.reshape(width, kv_heads, repeat_by, HEAD_SIZE), axis=2
    ).reshape(width, kv_cols)
    grad_value_part = jnp.sum(
        grad_value_wide.reshape(width, kv_heads, repeat_by, HEAD_SIZE), axis=2
    ).reshape(width, kv_cols)
    unused, pull_one = jax.vjp(norm_gain, x_float, gain_one)
    grad_input_norm, grad_g_one = pull_one(grad_normed_one)
    input_grad = (grad_middle + grad_input_norm).astype(jnp.bfloat16)
    gain_grads = jnp.stack([grad_g_one, grad_g_two, grad_g_three, grad_g_four], axis=1)
    attention_gradients = (
        lax.psum_scatter(
            grad_query_part.astype(jnp.bfloat16), ("dp", "ctx"), scatter_dimension=0, tiled=True
        ).astype(jnp.float32),
        lax.psum_scatter(grad_output_part, ("dp", "ctx"), scatter_dimension=1, tiled=True).astype(
            jnp.float32
        ),
    )
    key_spread = lax.dynamic_update_slice_in_dim(
        jnp.zeros((width, KEY_VALUE_HEADS * HEAD_SIZE), jnp.float32),
        grad_key_part,
        key_value_begin,
        1,
    )
    value_spread = lax.dynamic_update_slice_in_dim(
        jnp.zeros((width, KEY_VALUE_HEADS * HEAD_SIZE), jnp.float32),
        grad_value_part,
        key_value_begin,
        1,
    )
    kv_sums = (
        lax.psum_scatter(key_spread, ("dp", "ctx", "seq"), scatter_dimension=0, tiled=True),
        lax.psum_scatter(value_spread, ("dp", "ctx", "seq"), scatter_dimension=0, tiled=True),
        lax.psum_scatter(gain_grads, ("dp", "ctx", "seq"), scatter_dimension=0, tiled=True),
    )
    gain_out = kv_sums[2]
    return (
        layer_output,
        input_grad,
        attention_gradients[0],
        kv_sums[0],
        kv_sums[1],
        attention_gradients[1],
        ffn_grads[0],
        ffn_grads[1],
        ffn_grads[2],
        gain_out[:, 0],
        gain_out[:, 1],
        gain_out[:, 2],
        gain_out[:, 3],
    )


def solution(mesh):
    placed = (
        P("dp", ("ctx", "seq"), None),
        P("dp", "ctx"),
        P(("dp", "ctx"), "seq"),
        P(("dp", "ctx", "seq"), None),
        P(("dp", "ctx", "seq"), None),
        P("seq", ("dp", "ctx")),
        P(("dp", "ctx"), "seq"),
        P(("dp", "ctx"), "seq"),
        P("seq", ("dp", "ctx")),
        P(("dp", "ctx")),
        P(("dp", "ctx")),
        P(("dp", "ctx")),
        P(("dp", "ctx")),
        P("dp", ("ctx", "seq"), None),
    )
    return jax.shard_map(
        local,
        mesh=mesh,
        in_specs=placed,
        out_specs=(
            P("dp", ("ctx", "seq"), None),
            P("dp", ("ctx", "seq"), None),
            P(("dp", "ctx"), "seq"),
            P(("dp", "ctx", "seq"), None),
            P(("dp", "ctx", "seq"), None),
            P("seq", ("dp", "ctx")),
            P(("dp", "ctx"), "seq"),
            P(("dp", "ctx"), "seq"),
            P("seq", ("dp", "ctx")),
            P(("dp", "ctx", "seq")),
            P(("dp", "ctx", "seq")),
            P(("dp", "ctx", "seq")),
            P(("dp", "ctx", "seq")),
        ),
        check_vma=False,
    )
```

profile of v0, /device:TPU:0, one launch (start us, length us, event | category | flops | bytes accessed | tf_op | source)
XLA Modules:
  0.0 1959.0 jit_solution(7823633622664403679)
XLA Ops:
  10.7 10.5 all-gather
  28.5 48.8 %all-gather.17.cloned.1.call-done = bf16[2304,1024]{1,0:T(8,128)(2,1)} async-done(((bf16[72,1024]{1,0:T(8,128)(2,1)}), bf16[2304,1024]{1,0:T(8,128)(2,1)}) %all-gather.17.cloned.1.call-update) | async-done | bytes 4718608 | tf_op jit(solution)/shard_map/all_gather | solution.py:56
  78.6 50.1 %all-gather.15.cloned.1.call-done = bf16[2,256,2304]{2,1,0:T(8,128)(2,1)} async-done(((bf16[2,64,2304]{2,1,0:T(8,128)(2,1)}), bf16[2,256,2304]{2,1,0:T(8,128)(2,1)}) %all-gather.15.cloned.1.call-update) | async-done | bytes 2359312 | tf_op jit(solution)/shard_map/all_gather | solution.py:81
  128.7 3.1 convolution_convert_fusion.1
  132.0 62.1 %all-gather.23.cloned.1.call-done = bf16[2304,1024]{1,0:T(8,128)(2,1)} async-done(((bf16[72,1024]{1,0:T(8,128)(2,1)}), bf16[2304,1024]{1,0:T(8,128)(2,1)}) %all-gather.23.cloned.1.call-update) | async-done | bytes 4718608 | tf_op jit(solution)/shard_map/all_gather | solution.py:55
  198.4 25.3 %all-gather.27.cloned.1.call-done = bf16[512,2304]{0,1:T(8,128)(2,1)} async-done(((bf16[512,288]{0,1:T(8,128)(2,1)}), bf16[512,2304]{0,1:T(8,128)(2,1)}) %all-gather.27.cloned.1.call-update) | async-done | bytes 2359312 | tf_op jit(solution)/shard_map/all_gather | solution.py:62
  223.7 4.3 copy.161
  229.8 24.7 %all-gather.21.cloned.1.call-done = bf16[2304,512]{1,0:T(8,128)(2,1)} async-done(((bf16[288,512]{1,0:T(8,128)(2,1)}), bf16[2304,512]{1,0:T(8,128)(2,1)}) %all-gather.21.cloned.1.call-update) | async-done | bytes 2359312 | tf_op jit(solution)/shard_map/all_gather | solution.py:61
  254.4 3.8 fusion.100
  260.5 12.7 all-gather.19.cloned.1.call-done
  274.7 17.5 all-gather.25.cloned.1.call-done
  296.6 18.2 while.30
  315.4 35.5 %all_to_all.36 = bf16[2,256,512]{2,0,1:T(2,128)(2,1)S(1)} all-to-all(bf16[2,256,512]{2,0,1:T(2,128)(2,1)S(1)} %copy.158), channel_id=1, replica_groups=mesh['dp'=2,'ctx'=4,'seq'=4] {'seq'}, dimensions={1} | all-to-all | bytes 1048576 | tf_op jit(solution)/shard_map/all_to_all | solution.py:242
  351.1 121.2 %all-gather.29.cloned.1.call-done = bf16[2048,2304]{1,0:T(8,128)(2,1)} async-done(((bf16[512,2304]{1,0:T(8,128)(2,1)}), bf16[2048,2304]{1,0:T(8,128)(2,1)}) %all-gather.29.cloned.1.call-update) | async-done | bytes 9437200 | tf_op jit(solution)/shard_map/all_gather | solution.py:77
  472.3 5.2 multiply_reduce_fusion.4
  480.9 55.3 %all-gather.33.cloned.1.call-done = bf16[2304,2304]{1,0:T(8,128)(2,1)} async-done(((bf16[288,2304]{1,0:T(8,128)(2,1)}), bf16[2304,2304]{1,0:T(8,128)(2,1)}) %all-gather.33.cloned.1.call-update) | async-done | bytes 10616848 | tf_op jit(solution)/shard_map/all_gather | solution.py:70
  536.2 52.5 %all-gather.31.cloned.1.call-done = bf16[2,256,2304]{2,1,0:T(8,128)(2,1)} async-done(((bf16[2,64,2304]{2,1,0:T(8,128)(2,1)}), bf16[2,256,2304]{2,1,0:T(8,128)(2,1)}) %all-gather.31.cloned.1.call-update) | async-done | bytes 2359312 | tf_op jit(solution)/shard_map/all_gather | solution.py:81
  588.7 11.7 fusion.71
  600.3 52.9 %all-gather.35.cloned.1.call-done = bf16[2304,2304]{1,0:T(8,128)(2,1)} async-done(((bf16[288,2304]{1,0:T(8,128)(2,1)}), bf16[2304,2304]{1,0:T(8,128)(2,1)}) %all-gather.35.cloned.1.call-update) | async-done | bytes 10616848 | tf_op jit(solution)/shard_map/all_gather | solution.py:71
  653.2 12.9 multiply_convert_fusion.2
  666.1 52.7 %all-gather.37.cloned.1.call-done = bf16[2304,2304]{0,1:T(8,128)(2,1)} async-done(((bf16[2304,288]{0,1:T(8,128)(2,1)}), bf16[2304,2304]{0,1:T(8,128)(2,1)}) %all-gather.37.cloned.1.call-update) | async-done | bytes 10616848 | tf_op jit(solution)/shard_map/all_gather | solution.py:72
  718.8 11.3 fusion.92
  730.2 48.1 %reduce-scatter.17.cloned.1.call-done = bf16[2,64,2304]{2,1,0:T(8,128)(2,1)} async-done(((bf16[2,256,2304]{2,1,0:T(8,128)(2,1)}), bf16[2,64,2304]{2,1,0:T(8,128)(2,1)}) %reduce-scatter.17.cloned.1.call-update) | async-done | bytes 589840 | tf_op jit(solution)/shard_map/reduce_scatter | solution.py:85
  784.3 49.7 %all-gather.39.cloned.1.call-done = bf16[2,256,2304]{2,1,0:T(8,128)(2,1)} async-done(((bf16[2,64,2304]{2,1,0:T(8,128)(2,1)}), bf16[2,256,2304]{2,1,0:T(8,128)(2,1)}) %all-gather.39.cloned.1.call-update) | async-done | bytes 2359312 | tf_op jit(solution)/shard_map/all_gather | solution.py:81
  834.0 14.4 fusion.86
  848.5 9.8 fusion.65
  858.3 11.0 fusion.89
  869.3 47.0 %reduce-scatter.19.cloned.1.call-done = bf16[2,64,2304]{2,1,0:T(8,128)(2,1)} async-done(((bf16[2,256,2304]{2,1,0:T(8,128)(2,1)}), bf16[2,64,2304]{2,1,0:T(8,128)(2,1)}) %reduce-scatter.19.cloned.1.call-update) | async-done | bytes 589840 | tf_op jit(solution)/shard_map/reduce_scatter | solution.py:85
  919.2 3.2 multiply_reduce_fusion.1
  924.5 6.8 fusion.95
  933.7 3.5 all-to-all-start.1
  937.4 14.3 all-to-all-done.1
  959.3 74.0 %while.31 = (s32[]{:T(128)}, f32[2,1024,512]{1,2,0:T(8,128)}, f32[2,1024,512]{1,2,0:T(8,128)}, bf16[2,256,512]{1,2,0:T(8,128)(2,1)}, s32[2]{0:T(128)S(1)}, /*ind...) while((s32[]{:T(128)}, f32[2,1024,512]{1,2,0:T(8,128)}, ...), condition=%wide.region_15.16_spmd, body=%wide.region_13.15_spmd.sunk | while | flops 1361055488 | bytes 79972184 | solution.py:341
  975.5 6.5 fusion.230
  984.2 4.5 constant_dynamic-update-slice_fusion.10
  990.7 4.8 fusion.231
  1012.4 6.5 fusion.230
  1021.2 4.5 constant_dynamic-update-slice_fusion.10
  1027.7 4.8 fusion.231
  1033.3 3.8 convert_element_type.190
  1037.2 3.8 convert_element_type.194
  1042.3 5.1 bitcast_convert_fusion.3
  1057.1 5.3 reshape.409
  1062.4 5.3 reduce-scatter.21.cloned.1.call-done
  1073.6 3.6 convolution_add_fusion.1
  1077.2 24.5 %reduce-scatter.23.cloned.1.call-done = bf16[2,256,512]{1,2,0:T(8,128)(2,1)} async-done(((bf16[2,1024,512]{1,2,0:T(8,128)(2,1)}), bf16[2,256,512]{1,2,0:T(8,128)(2,1)}) %reduce-scatter.23.cloned.1.call-update) | async-done | bytes 524304 | tf_op jit(solution)/shard_map/reduce_scatter | solution.py:350
  1101.7 5.4 fusion.88
  1108.8 10.6 bitcast_convert_fusion
  1121.1 9.9 bitcast_convert_fusion.2
  1131.1 10.0 bitcast_convert_fusion.1
  1141.2 124.0 %reduce-scatter.33.cloned.1.call-done = bf16[512,2304]{1,0:T(8,128)(2,1)} async-done(((bf16[2048,2304]{1,0:T(8,128)(2,1)}), bf16[512,2304]{1,0:T(8,128)(2,1)}) %reduce-scatter.33.cloned.1.call-update) | async-done | bytes 2359312 | tf_op jit(solution)/shard_map/reduce_scatter | solution.py:308
  1265.3 4.3 copy.186
  1272.7 4.8 broadcast.331.clone
  1280.3 3.5 fusion.149
  1288.7 4.8 broadcast.331.clone.1
  1295.9 16.7 reduce-scatter.27.cloned.1.call-done
  1314.4 49.0 %reduce-scatter.25.cloned.1.call-done = bf16[2,64,2304]{2,1,0:T(8,128)(2,1)} async-done(((bf16[2,256,2304]{2,1,0:T(8,128)(2,1)}), bf16[2,64,2304]{2,1,0:T(8,128)(2,1)}) %reduce-scatter.25.cloned.1.call-update) | async-done | bytes 589840 | tf_op jit(solution)/shard_map/reduce_scatter | solution.py:85
  1365.2 40.3 %all-reduce = f32[2304,4]{0,1:T(4,128)S(1)} all-reduce(f32[2304,4]{0,1:T(4,128)S(1)} %pad_maximum_fusion.2), channel_id=15, replica_groups=mesh['dp'=2,'ctx'=4,'seq'=4] {'dp','ctx','seq'}, use_global_device_ids=true, to_apply=%region_34.35.clone | all-reduce | flops 9216 | bytes 73728
  1408.4 41.3 %reduce-scatter.39.cloned.1.call-done = bf16[2304,288]{0,1:T(8,128)(2,1)} async-done(((bf16[2304,2304]{0,1:T(8,128)(2,1)}), bf16[2304,288]{0,1:T(8,128)(2,1)}) %reduce-scatter.39.cloned.1.call-update) | async-done | bytes 1327120 | tf_op jit(solution)/shard_map/reduce_scatter | solution.py:293
  1452.7 83.1 %reduce-scatter.35.cloned.1.call-done = bf16[288,2304]{1,0:T(8,128)(2,1)} async-done(((bf16[2304,2304]{1,0:T(8,128)(2,1)}), bf16[288,2304]{1,0:T(8,128)(2,1)}) %reduce-scatter.35.cloned.1.call-update) | async-done | bytes 1327120 | tf_op jit(solution)/shard_map/reduce_scatter | solution.py:287
  1538.8 83.1 %reduce-scatter.37.cloned.1.call-done = bf16[288,2304]{1,0:T(8,128)(2,1)} async-done(((bf16[2304,2304]{1,0:T(8,128)(2,1)}), bf16[288,2304]{1,0:T(8,128)(2,1)}) %reduce-scatter.37.cloned.1.call-update) | async-done | bytes 1327120 | tf_op jit(solution)/shard_map/reduce_scatter | solution.py:290
  1624.9 43.1 %reduce-scatter.41.cloned.1.call-done = bf16[288,512]{1,0:T(8,128)(2,1)} async-done(((bf16[2304,512]{1,0:T(8,128)(2,1)}), bf16[288,512]{1,0:T(8,128)(2,1)}) %reduce-scatter.41.cloned.1.call-update) | async-done | bytes 294928
  1670.2 139.8 %reduce-scatter.29.cloned.1.call-done = f32[72,1024]{1,0:T(8,128)} async-done(((f32[2304,1024]{1,0:T(8,128)}), f32[72,1024]{1,0:T(8,128)}) %reduce-scatter.29.cloned.1.call-update) | async-done | bytes 294928 | tf_op jit(solution)/shard_map/reduce_scatter | solution.py:423
  1809.9 142.0 %reduce-scatter.31.cloned.1.call-done = f32[72,1024]{1,0:T(8,128)} async-done(((f32[2304,1024]{1,0:T(8,128)}), f32[72,1024]{1,0:T(8,128)}) %reduce-scatter.31.cloned.1.call-update) | async-done | bytes 294928 | tf_op jit(solution)/shard_map/reduce_scatter | solution.py:424
  (324 shorter events, 154.6 us)
Async XLA Ops:
  7.2 70.1 %all-gather.17.cloned.1.call-start = ((), (), s32[]{:S(2)}) async-start(), calls=%async_computation.16 | async-start | bytes 4866048 | tf_op jit(solution)/shard_map/all_gather | solution.py:56
  7.9 120.8 %all-gather.15.cloned.1.call-start = ((), (), s32[]{:S(2)}) async-start(), calls=%async_computation.15 | async-start | bytes 2949120 | tf_op jit(solution)/shard_map/all_gather | solution.py:81
  26.5 167.6 %all-gather.23.cloned.1.call-start = ((), (), s32[]{:S(2)}) async-start(), calls=%async_computation.19 | async-start | bytes 4866048 | tf_op jit(solution)/shard_map/all_gather | solution.py:55
  27.2 196.4 %all-gather.27.cloned.1.call-start = ((), (), s32[]{:S(2)}) async-start(), calls=%async_computation.21 | async-start | bytes 2654208 | tf_op jit(solution)/shard_map/all_gather | solution.py:62
  27.8 226.6 %all-gather.21.cloned.1.call-start = ((), (), s32[]{:S(2)}) async-start(), calls=%async_computation.18 | async-start | bytes 2654208 | tf_op jit(solution)/shard_map/all_gather | solution.py:61
  28.4 244.8 %all-gather.19.cloned.1.call-start = ((), (), s32[]{:S(2)}) async-start(), calls=%async_computation.17 | async-start | bytes 1310720 | tf_op jit(solution)/shard_map/all_gather | solution.py:219
  78.6 53.3 %copy-start.15 = (bf16[2304,256]{1,0:T(8,128)(2,1)}, bf16[2304,256]{1,0:T(8,128)(2,1)S(1)}, u32[]{:S(2)}) copy-start(bf16[2304,256]{1,0:T(8,128)(2,1)S(1)} %constant_dynamic-slice_fusion.11) | copy-start | bytes 3538948
  78.6 53.3 %copy-start.37 = (s32[2,256]{1,0:T(2,128)S(1)}, s32[2,256]{1,0:T(2,128)}, u32[]{:S(2)}) copy-start(s32[2,256]{1,0:T(2,128)} %param.19) | copy-start | bytes 6148
  131.9 63.5 %copy-start.21 = (bf16[2,256,2304]{2,1,0:T(8,128)(2,1)S(1)}, bf16[2,256,2304]{2,1,0:T(8,128)(2,1)}, u32[]{:S(2)}) copy-start(bf16[2,256,2304]{2,1,0:T(8,128)(2,1)} %all-gather.15.cloned.1.call-done) | copy-start | bytes 7077892
  131.9 160.3 %all-gather.25.cloned.1.call-start = ((), (), s32[]{:S(2)}) async-start(), calls=%async_computation.20 | async-start | bytes 1310720 | tf_op jit(solution)/shard_map/all_gather | solution.py:218
  198.3 273.9 %all-gather.29.cloned.1.call-start = ((), (), s32[]{:S(2)}) async-start(), calls=%async_computation.22 | async-start | bytes 11796480 | tf_op jit(solution)/shard_map/all_gather | solution.py:77
  228.0 308.2 %all-gather.33.cloned.1.call-start = ((), (), s32[]{:S(2)}) async-start(), calls=%async_computation.24 | async-start | bytes 11943936 | tf_op jit(solution)/shard_map/all_gather | solution.py:70
  228.7 360.0 %all-gather.31.cloned.1.call-start = ((), (), s32[]{:S(2)}) async-start(), calls=%async_computation.23 | async-start | bytes 2949120 | tf_op jit(solution)/shard_map/all_gather | solution.py:81
  229.7 29.5 %copy-start.17 = (f32[2,256,128]{2,1,0:T(8,128)}, f32[2,256,128]{2,1,0:T(8,128)S(1)}, u32[]{:S(2)}) copy-start(f32[2,256,128]{2,1,0:T(8,128)S(1)} %get-tuple-element.496) | copy-start | bytes 786436
  229.8 29.5 %copy-start.19 = (f32[2,256,128]{2,1,0:T(8,128)}, f32[2,256,128]{2,1,0:T(8,128)S(1)}, u32[]{:S(2)}) copy-start(f32[2,256,128]{2,1,0:T(8,128)S(1)} %get-tuple-element.497) | copy-start | bytes 786436
  314.9 36.2 %copy-start.41 = (f32[2,2,256]{2,1,0:T(2,128)}, f32[2,2,256]{2,1,0:T(2,128)S(1)}, u32[]{:S(2)}) copy-start(f32[2,2,256]{2,1,0:T(2,128)S(1)} %get-tuple-element.695) | copy-start | bytes 12292
  314.9 36.2 %copy-start.56 = (s32[2]{0:T(128)}, s32[2]{0:T(128)S(1)}, u32[]{:S(2)}) copy-start(s32[2]{0:T(128)S(1)} %get-tuple-element.833) | copy-start | bytes 28
  351.1 126.5 %copy-start.11 = (bf16[2,4,8,8,512]{4,3,1,2,0:T(8,128)(2,1)}, bf16[2,4,8,8,512]{4,3,1,2,0:T(8,128)(2,1)S(1)}, u32[]{:S(2)}) copy-start(bf16[2,4,8,8,512]{4,3,1,2,0:T(8,128)(2,1)S(1)} %copy.194) | copy-start | bytes 1572868
  472.3 5.8 copy-start.3
  477.6 1.9 copy-start.45
  478.5 2.3 copy-start.49
  478.5 2.3 copy-start.47
  479.5 173.7 %all-gather.35.cloned.1.call-start = ((), (), s32[]{:S(2)}) async-start(), calls=%async_computation.25 | async-start | bytes 11943936 | tf_op jit(solution)/shard_map/all_gather | solution.py:71
  480.2 238.6 %all-gather.37.cloned.1.call-start = ((), (), s32[]{:S(2)}) async-start(), calls=%async_computation.26 | async-start | bytes 11943936 | tf_op jit(solution)/shard_map/all_gather | solution.py:72
  480.8 297.5 %reduce-scatter.17.cloned.1.call-start = ((), (), s32[]{:S(2)}) async-start(), calls=%async_computation.27 | async-start | bytes 2949120 | tf_op jit(solution)/shard_map/reduce_scatter | solution.py:85
  730.1 49.6 %copy-start.14 = (bf16[2,64,2304]{2,1,0:T(8,128)(2,1)S(1)}, bf16[2,64,2304]{2,1,0:T(8,128)(2,1)}, u32[]{:S(2)}) copy-start(bf16[2,64,2304]{2,1,0:T(8,128)(2,1)} %param.31) | copy-start | bytes 1769476
  730.2 103.9 %all-gather.39.cloned.1.call-start = ((), (), s32[]{:S(2)}) async-start(), calls=%async_computation.28 | async-start | bytes 2949120 | tf_op jit(solution)/shard_map/all_gather | solution.py:81
  778.4 3.6 copy-start.8
  779.7 2.3 copy-start.48
  783.9 132.4 %reduce-scatter.19.cloned.1.call-start = ((), (), s32[]{:S(2)}) async-start(), calls=%async_computation.29 | async-start | bytes 2949120 | tf_op jit(solution)/shard_map/reduce_scatter | solution.py:85
  848.5 9.8 copy-start.58
  848.5 9.8 copy-start.59
  916.3 2.8 copy-start.25
  919.2 3.2 copy-start.53
  919.2 4.3 copy-start.46
  933.7 18.0 all-to-all-start.1
  937.2 130.6 %reduce-scatter.21.cloned.1.call-start = ((), (), s32[]{:S(2)}) async-start(), calls=%async_computation.30 | async-start | bytes 2621440 | tf_op jit(solution)/shard_map/reduce_scatter | solution.py:347
  956.7 2.5 copy-start.42
  956.7 2.5 copy-start.57
  964.8 2.8 copy-start.13
  981.9 2.3 copy-start
  988.7 2.0 copy-start.1
  1001.8 2.8 copy-start.13
  1018.9 2.3 copy-start
  1025.7 2.0 copy-start.1
  1037.1 64.6 %reduce-scatter.23.cloned.1.call-start = ((), (), s32[]{:S(2)}) async-start(), calls=%async_computation.31 | async-start | bytes 2621440 | tf_op jit(solution)/shard_map/reduce_scatter | solution.py:350
  1041.0 224.2 %reduce-scatter.33.cloned.1.call-start = ((), (), s32[]{:S(2)}) async-start(), calls=%async_computation.36 | async-start | bytes 11796480 | tf_op jit(solution)/shard_map/reduce_scatter | solution.py:308
  1047.4 265.1 %reduce-scatter.27.cloned.1.call-start = ((), (), s32[]{:S(2)}) async-start(), calls=%async_computation.33 | async-start | bytes 2654208 | tf_op jit(solution)/shard_map/reduce_scatter | solution.py:403
  1053.3 310.2 %reduce-scatter.25.cloned.1.call-start = ((), (), s32[]{:S(2)}) async-start(), calls=%async_computation.32 | async-start | bytes 2949120 | tf_op jit(solution)/shard_map/reduce_scatter | solution.py:85
  1069.8 2.2 copy-start.28
  1107.1 342.6 %reduce-scatter.39.cloned.1.call-start = ((), (), s32[]{:S(2)}) async-start(), calls=%async_computation.39 | async-start | bytes 11943936 | tf_op jit(solution)/shard_map/reduce_scatter | solution.py:293
  1119.4 416.4 %reduce-scatter.35.cloned.1.call-start = ((), (), s32[]{:S(2)}) async-start(), calls=%async_computation.37 | async-start | bytes 11943936 | tf_op jit(solution)/shard_map/reduce_scatter | solution.py:287
  1131.1 490.9 %reduce-scatter.37.cloned.1.call-start = ((), (), s32[]{:S(2)}) async-start(), calls=%async_computation.38 | async-start | bytes 11943936 | tf_op jit(solution)/shard_map/reduce_scatter | solution.py:290
  1141.2 526.8 %reduce-scatter.41.cloned.1.call-start = ((), (), s32[]{:S(2)}) async-start(), calls=%async_computation.40 | async-start | bytes 2654208
  1265.3 4.4 copy-start.31
  1265.3 4.4 copy-start.33
  1269.6 540.3 %reduce-scatter.29.cloned.1.call-start = ((), (), s32[]{:S(2)}) async-start(), calls=%async_computation.34 | async-start | bytes 9732096 | tf_op jit(solution)/shard_map/reduce_scatter | solution.py:423
  1279.2 672.7 %reduce-scatter.31.cloned.1.call-start = ((), (), s32[]{:S(2)}) async-start(), calls=%async_computation.35 | async-start | bytes 9732096 | tf_op jit(solution)/shard_map/reduce_scatter | solution.py:424
  1288.7 4.8 copy-start.7
  1295.2 68.3 %copy-start.4 = (bf16[2,64,2304]{2,1,0:T(8,128)(2,1)S(1)}, bf16[2,64,2304]{2,1,0:T(8,128)(2,1)}, u32[]{:S(2)}) copy-start(bf16[2,64,2304]{2,1,0:T(8,128)(2,1)} %param.18) | copy-start | bytes 1769476
  1295.2 68.3 %copy-start.35 = (f32[2304]{0:T(1024)S(1)}, f32[2304]{0:T(1024)}, u32[]{:S(2)}) copy-start(f32[2304]{0:T(1024)} %copy-done.34) | copy-start | bytes 27652
  1295.2 68.3 %copy-start.44 = (f32[2,64]{1,0:T(2,128)S(1)}, f32[2,64]{1,0:T(2,128)}, u32[]{:S(2)}) copy-start(f32[2,64]{1,0:T(2,128)} %copy-done.43) | copy-start | bytes 1540
  1295.2 110.4 %copy-start.51 = (f32[2,64]{1,0:T(2,128)S(1)}, f32[2,64]{1,0:T(2,128)}, u32[]{:S(2)}) copy-start(f32[2,64]{1,0:T(2,128)} %copy-done.50) | copy-start | bytes 1540
  1295.2 110.9 %copy-start.6 = (f32[2,64,2304]{2,1,0:T(8,128)S(1)}, f32[2,64,2304]{2,1,0:T(8,128)}, u32[]{:S(2)}) copy-start(f32[2,64,2304]{2,1,0:T(8,128)} %copy-done.5) | copy-start | bytes 3538948
  (27 other events, 29.3 us)
Sparse Core Ops, SparseCore 0:
  10.9 66.2 all-gather.16
  79.4 49.2 all-gather.14
  131.6 62.3 all-gather.22
  195.8 27.8 all-gather.26
  225.4 29.0 all-gather.20
  256.4 16.7 all-gather.18
  275.3 16.8 all-gather.24
  294.3 177.9 all-gather.28
  474.2 61.9 all-gather.32
  538.2 50.4 all-gather.30
  590.6 62.6 all-gather.34
  655.0 63.8 all-gather.36
  730.3 48.0 reduce-scatter.16
  784.0 49.9 all-gather.38
  869.4 46.8 reduce-scatter.18
  1037.2 30.4 reduce-scatter.20
  1070.3 31.4 reduce-scatter.22
  1104.0 161.2 reduce-scatter.32
  1269.2 43.3 reduce-scatter.26
  1315.4 48.0 reduce-scatter.24
  1367.4 82.2 reduce-scatter.38
  1453.6 82.1 reduce-scatter.34
  1539.7 82.1 reduce-scatter.36
  1625.5 42.4 reduce-scatter.40
  1674.5 135.3 reduce-scatter.28
  1817.3 134.6 reduce-scatter.30
where the time goes:
time: 1970 us; the launch traced here: 1960 us
  waiting for transfers between devices  1490 us (76%)
  matrix products  181 us (9%)
  local copies, waits for them, and re-layouts  107 us (5%)
  blocking collectives  86.3 us (4%)
  other arithmetic  63.6 us (3%)
    all_gather x3, waiting for transfers between devices, block_rows(): return lax.all_gather(local_rows, 'seq', axis=1, tiled=True)  152 us
    reduce_scatter x3, waiting for transfers between devices, row_total(): lax.psum_scatter(partial_rows.astype(jnp.bfloat16), 'seq', scatter_dimens...  144 us
    reduce_scatter x1, waiting for transfers between devices, local(): lax.psum_scatter(value_spread, ('dp', 'ctx', 'seq'), scatter_dimension=0,...  142 us
    reduce_scatter x1, waiting for transfers between devices, local(): lax.psum_scatter(key_spread, ('dp', 'ctx', 'seq'), scatter_dimension=0, t...  140 us
    reduce_scatter x1, waiting for transfers between devices, local(): lax.psum_scatter(jnp.einsum('ste,std->ed', heads_tok, grad_project, prefe...  124 us
    all_gather x1, waiting for transfers between devices, full_output(): return lax.all_gather(output_part, 'seq', axis=0, tiled=True)  121 us
    reduce_scatter x1, waiting for transfers between devices, local(): lax.psum_scatter(grad_up_part.astype(jnp.bfloat16), ('dp', 'ctx'), scatte...  83.1 us
    reduce_scatter x1, waiting for transfers between devices, local(): lax.psum_scatter(grad_gate_part.astype(jnp.bfloat16), ('dp', 'ctx'), scat...  83.1 us
  transfers between devices with their start and end apart: 27, of which 27 were waited for; matrix products, arithmetic and copies ran while one was open for 10% of the time, Pallas kernels for 0%

commit v1 on v0

--- a/solution.py
+++ b/solution.py
@@ -156,7 +156,7 @@
     )
 
 
-def local(
+def general_local(
     inputs,
     positions,
     query_weight,
@@ -442,41 +442,279 @@
     )
 
 
+def flip(value, axis):
+    return lax.ppermute(value, axis, [(0, 1), (1, 0)])
+
+
+def ordered(index, own, other, axis=0):
+    return jnp.where(
+        index == 0, jnp.stack([own, other], axis=axis), jnp.stack([other, own], axis=axis)
+    )
+
+
+def pick(value, index, axis=0):
+    return lax.dynamic_index_in_dim(value, index, axis, keepdims=False)
+
+
+def trade_sequences(value):
+    cy = lax.axis_index("cy")
+    return ordered(cy, pick(value, cy), flip(pick(value, 1 - cy), "cy"))
+
+
+def gather_weight(local_rows):
+    x, y, c = lax.axis_index("dp"), lax.axis_index("cy"), lax.axis_index("core")
+    own = pick(local_rows, c, 1)
+    got = flip(pick(local_rows, 1 - c, 1), "core")
+    first = jnp.where(c == 0, own, got)
+    second = jnp.where(c == 0, got, own)
+    first_y = flip(first, "cy")
+    second_x = flip(second, "dp")
+    first_pair = ordered(y, first, first_y)
+    second_pair = ordered(x, second, second_x)
+    first_x = flip(first_pair, "dp")
+    second_y = flip(second_pair, "cy")
+    first_all = ordered(x, first_pair, first_x)
+    second_all = ordered(y, second_pair, second_y, axis=1)
+    return jnp.stack([first_all, second_all], axis=2).reshape(-1, own.shape[-1])
+
+
+def scatter_weight_grad(grad):
+    x, y, c = lax.axis_index("dp"), lax.axis_index("cy"), lax.axis_index("core")
+    cols = grad.shape[-1]
+    parts = grad.reshape(2, 2, 2, -1, cols)
+    first, second = parts[:, :, 0], parts[:, :, 1]
+    first_x = flip(pick(first, 1 - x), "dp")
+    second_y = flip(pick(second, 1 - y, 1), "cy")
+    first_sum = (pick(first, x).astype(jnp.float32) + first_x.astype(jnp.float32)).astype(
+        jnp.bfloat16
+    )
+    second_sum = (pick(second, y, 1).astype(jnp.float32) + second_y.astype(jnp.float32)).astype(
+        jnp.bfloat16
+    )
+    first_y = flip(pick(first_sum, 1 - y), "cy")
+    second_x = flip(pick(second_sum, 1 - x), "dp")
+    first_total = pick(first_sum, y).astype(jnp.float32) + first_y.astype(jnp.float32)
+    second_total = pick(second_sum, x).astype(jnp.float32) + second_x.astype(jnp.float32)
+    keep = jnp.where(c == 0, first_total, second_total)
+    got = flip(jnp.where(c == 0, second_total, first_total).astype(jnp.bfloat16), "core")
+    return ordered(c, keep, got.astype(jnp.float32), axis=1)
+
+
+def gather_rows(local_rows):
+    width = local_rows.shape[-1]
+    return lax.all_gather(local_rows, ("core", "seq"), axis=1, tiled=True).reshape(-1, width)
+
+
+def scatter_rows(partial_rows):
+    c = lax.axis_index("core")
+    parts = partial_rows.astype(jnp.bfloat16).reshape(2, 2, -1, partial_rows.shape[-1])
+    got = flip(pick(parts, 1 - c, 1), "core")
+    both = pick(parts, c, 1).astype(jnp.float32) + got.astype(jnp.float32)
+    return lax.psum_scatter(
+        both.astype(jnp.bfloat16), "seq", scatter_dimension=1, tiled=True
+    ).astype(jnp.float32)
+
+
+def dot(left, right, dims):
+    return lax.dot_general(left, right, ((dims[:1], dims[1:]), ((), ())), preferred_element_type=jnp.float32)
+
+
+def head_scores(queries, keys, visible):
+    bent = jnp.tanh(dot(queries, keys, (1, 1)) * (HEAD_SIZE ** (-0.5) / CAP))
+    return bent, jnp.where(visible, CAP * bent, -1e30)
+
+
+def head_local(
+    inputs,
+    positions,
+    query_weight,
+    key_weight,
+    value_weight,
+    output_weight,
+    gate_weight,
+    up_weight,
+    down_weight,
+    pre_attn_gain,
+    post_attn_gain,
+    pre_ffn_gain,
+    post_ffn_gain,
+    cotangent,
+):
+    width = inputs.shape[-1]
+    c, cy = lax.axis_index("core"), lax.axis_index("cy")
+    low = jnp.bfloat16
+    rows_own = query_weight.shape[0]
+    kv_stack = jnp.stack([key_weight, value_weight], axis=1).reshape(-1, 2, KEY_VALUE_HEADS, HEAD_SIZE)
+    kv_rows = lax.all_to_all(
+        kv_stack.transpose(2, 0, 1, 3), "seq", split_axis=0, concat_axis=0, tiled=True
+    ).reshape(rows_own, 2, HEAD_SIZE)
+    attn_share = jnp.concatenate(
+        [
+            query_weight.reshape(rows_own, 2, HEAD_SIZE),
+            kv_rows,
+            output_weight.T.reshape(rows_own, 2, HEAD_SIZE),
+        ],
+        axis=2,
+    )
+    ffn_cols = gate_weight.shape[1] // 2
+    gate_up_share = jnp.concatenate(
+        [gate_weight.reshape(rows_own, 2, ffn_cols), up_weight.reshape(rows_own, 2, ffn_cols)],
+        axis=2,
+    )
+    down_share = down_weight.T.reshape(rows_own, 2, ffn_cols)
+    gain_table = jnp.stack([pre_attn_gain, post_attn_gain, pre_ffn_gain, post_ffn_gain], axis=0)
+    gain_full = lax.all_gather(gain_table, ("dp", "cy", "core"), axis=1, tiled=True).astype(jnp.float32)
+    gain_one, gain_two, gain_three, gain_four = gain_full[0], gain_full[1], gain_full[2], gain_full[3]
+
+    x_float = trade_sequences(inputs).astype(jnp.float32)
+    grad_top = trade_sequences(cotangent).astype(jnp.float32)
+    seq_pos = lax.all_gather(positions, ("cy", "core"), axis=1, tiled=True)
+    seq_pos = pick(seq_pos, cy)
+    half = HEAD_SIZE // 2
+    freq = BASE ** (-jnp.arange(half, dtype=jnp.float32) * 2.0 / HEAD_SIZE)
+    angle = seq_pos.astype(jnp.float32)[:, None] * freq
+    cosine, sine = jnp.cos(angle), jnp.sin(angle)
+    kv_cosine = jnp.where(c == 0, cosine, 1.0)
+    kv_sine = jnp.where(c == 0, sine, 0.0)
+
+    attn_weight = gather_weight(attn_share)
+    in_weight = attn_weight[:, : 2 * HEAD_SIZE]
+    out_weight = attn_weight[:, 2 * HEAD_SIZE :]
+    gate_up_share, down_share, attn_weight_late = lax.optimization_barrier(
+        (gate_up_share, down_share, attn_weight[:8])
+    )
+    gate_up_weight = gather_weight(gate_up_share)
+    down_back = gather_weight(down_share)
+
+    block_one = gather_rows(norm_gain(x_float, gain_one).astype(low))
+    raw = dot(block_one, in_weight, (1, 0))
+    queries = turn(raw[:, :HEAD_SIZE], cosine, sine).astype(low)
+    kv_own = turn(raw[:, HEAD_SIZE:], kv_cosine, kv_sine).astype(low)
+    kv_other = flip(kv_own, "core")
+    keys = jnp.where(c == 0, kv_own, kv_other)
+    values = jnp.where(c == 0, kv_other, kv_own)
+    token = jnp.arange(seq_pos.shape[0], dtype=jnp.int32)
+    visible = (token[None, :] <= token[:, None]) & (token[None, :] >= (token - seq_pos)[:, None])
+    bent, masked = head_scores(queries, keys, visible)
+    row_max = jnp.max(masked, axis=-1, keepdims=True)
+    exponent = jnp.exp(masked - row_max)
+    row_sum = jnp.sum(exponent, axis=-1, keepdims=True)
+    heads = dot((exponent / row_sum).astype(low), values, (1, 0)).astype(low)
+    log_total = row_max + jnp.log(row_sum)
+
+    project = scatter_rows(dot(heads, out_weight, (1, 1)))
+    middle = x_float + norm_gain(project, gain_two)
+    block_two = gather_rows(norm_gain(middle, gain_three).astype(low))
+    gate_up = dot(block_two, gate_up_weight, (1, 0))
+    gate, upper = gate_up[:, :ffn_cols], gate_up[:, ffn_cols:]
+    hidden = geglu(gate, upper).astype(low)
+    feed = scatter_rows(dot(hidden, down_back, (1, 1)))
+    layer_output = trade_sequences((middle + norm_gain(feed, gain_four)).astype(low))
+
+    unused, pull_four = jax.vjp(norm_gain, feed, gain_four)
+    grad_feed, grad_g_four = pull_four(grad_top)
+    grad_feed_rows = gather_rows(grad_feed.astype(low))
+    grad_hidden = dot(grad_feed_rows, down_back, (1, 0))
+    unused, pull_act = jax.vjp(geglu, gate, upper)
+    grad_gate_act, grad_up_act = pull_act(grad_hidden)
+    grad_gate_up = jnp.concatenate([grad_gate_act.astype(low), grad_up_act.astype(low)], axis=1)
+    grad_normed_two = scatter_rows(dot(grad_gate_up, gate_up_weight, (1, 1)))
+    grad_down = scatter_weight_grad(dot(grad_feed_rows, hidden, (0, 0)).astype(low))
+    grad_gu = scatter_weight_grad(dot(block_two, grad_gate_up, (0, 0)).astype(low))
+
+    unused, pull_three = jax.vjp(norm_gain, middle, gain_three)
+    grad_mid_norm, grad_g_three = pull_three(grad_normed_two)
+    grad_middle = grad_top + grad_mid_norm
+    unused, pull_two = jax.vjp(norm_gain, project, gain_two)
+    grad_project, grad_g_two = pull_two(grad_middle)
+    grad_project_rows = gather_rows(grad_project.astype(low))
+    grad_heads = dot(grad_project_rows, out_weight, (1, 0)).astype(low)
+    grad_output_part = dot(grad_project_rows, heads, (0, 0)).astype(low)
+
+    bent, masked = head_scores(queries, keys, visible)
+    probability = jnp.exp(masked - log_total)
+    grad_value = dot(probability.astype(low), grad_heads, (0, 0)).astype(low)
+    grad_prob = dot(grad_heads, values, (1, 1))
+    delta = jnp.sum(probability * grad_prob, axis=-1, keepdims=True)
+    grad_scores = (probability * (grad_prob - delta) * (1.0 - bent * bent)).astype(low)
+    scale = HEAD_SIZE ** (-0.5)
+    grad_query_rot = rounded(dot(grad_scores, keys, (1, 0)) * scale)
+    grad_key_rot = rounded(dot(grad_scores, queries, (0, 0)) * scale)
+    grad_query_raw = turn_back(grad_query_rot, cosine, sine).astype(low)
+    grad_key_raw = turn_back(grad_key_rot, cosine, sine).astype(low)
+    kv_grad_own = jnp.where(c == 0, grad_key_raw, grad_value)
+    kv_grad_got = flip(jnp.where(c == 0, grad_value, grad_key_raw), "core")
+    kv_grad = (kv_grad_own.astype(jnp.float32) + kv_grad_got.astype(jnp.float32)).astype(low)
+    grad_in = jnp.concatenate([grad_query_raw, kv_grad], axis=1)
+    grad_normed_one = scatter_rows(dot(grad_in, in_weight, (1, 1)))
+    grad_in_part = dot(block_one, grad_in, (0, 0)).astype(low)
+    attn_grads = scatter_weight_grad(jnp.concatenate([grad_in_part, grad_output_part], axis=1))
+
+    unused, pull_one = jax.vjp(norm_gain, x_float, gain_one)
+    grad_input_norm, grad_g_one = pull_one(grad_normed_one)
+    input_grad = trade_sequences((grad_middle + grad_input_norm).astype(low))
+    gain_grads = jnp.stack([grad_g_one, grad_g_two, grad_g_three, grad_g_four], axis=0)
+    everyone = ("dp", "cy", "core", "seq")
+    device_count = lax.axis_size(everyone)
+    gain_out = jnp.sum(
+        lax.all_to_all(
+            gain_grads.reshape(4, device_count, -1).transpose(1, 0, 2),
+            everyone,
+            split_axis=0,
+            concat_axis=0,
+            tiled=True,
+        ),
+        axis=0,
+    )
+    grad_query_out = attn_grads[:, :, :HEAD_SIZE].reshape(rows_own, 2 * HEAD_SIZE)
+    grad_output_out = attn_grads[:, :, 2 * HEAD_SIZE :].reshape(rows_own, 2 * HEAD_SIZE).T
+    kv_back = lax.all_to_all(
+        attn_grads[:, :, HEAD_SIZE : 2 * HEAD_SIZE].astype(low), "seq", split_axis=0, concat_axis=0, tiled=True
+    ).reshape(KEY_VALUE_HEADS, -1, 2, HEAD_SIZE).transpose(2, 1, 0, 3).reshape(2, -1, KEY_VALUE_HEADS * HEAD_SIZE).astype(jnp.float32)
+    return (
+        layer_output,
+        input_grad,
+        grad_query_out,
+        kv_back[0],
+        kv_back[1],
+        grad_output_out,
+        grad_gu[:, :, :ffn_cols].reshape(rows_own, 2 * ffn_cols),
+        grad_gu[:, :, ffn_cols:].reshape(rows_own, 2 * ffn_cols),
+        grad_down.reshape(rows_own, 2 * ffn_cols).T,
+        gain_out[0],
+        gain_out[1],
+        gain_out[2],
+        gain_out[3],
+    )
+
+
+def one_head_each(mesh):
+    sizes = mesh.shape
+    return (
+        sizes["dp"] == 2
+        and sizes["ctx"] == 4
+        and sizes["seq"] == KEY_VALUE_HEADS
+        and QUERY_HEAD_COUNT == 2 * KEY_VALUE_HEADS
+    )
+
+
 def solution(mesh):
-    placed = (
-        P("dp", ("ctx", "seq"), None),
-        P("dp", "ctx"),
-        P(("dp", "ctx"), "seq"),
-        P(("dp", "ctx", "seq"), None),
-        P(("dp", "ctx", "seq"), None),
-        P("seq", ("dp", "ctx")),
-        P(("dp", "ctx"), "seq"),
-        P(("dp", "ctx"), "seq"),
-        P("seq", ("dp", "ctx")),
-        P(("dp", "ctx")),
-        P(("dp", "ctx")),
-        P(("dp", "ctx")),
-        P(("dp", "ctx")),
-        P("dp", ("ctx", "seq"), None),
-    )
+    if one_head_each(mesh):
+        body, ctx = head_local, ("cy", "core")
+        grid = jax.sharding.Mesh(
+            mesh.devices.reshape(mesh.shape["dp"], -1, 2, mesh.shape["seq"]),
+            ("dp", "cy", "core", "seq"),
+        )
+    else:
+        body, ctx, grid = general_local, ("ctx",), mesh
+    owners, everyone = ("dp", *ctx), ("dp", *ctx, "seq")
+    rows = P("dp", (*ctx, "seq"), None)
+    tall, flat, wide = P(owners, "seq"), P(everyone, None), P("seq", owners)
+    gains = (P(owners),) * 4
     return jax.shard_map(
-        local,
-        mesh=mesh,
-        in_specs=placed,
-        out_specs=(
-            P("dp", ("ctx", "seq"), None),
-            P("dp", ("ctx", "seq"), None),
-            P(("dp", "ctx"), "seq"),
-            P(("dp", "ctx", "seq"), None),
-            P(("dp", "ctx", "seq"), None),
-            P("seq", ("dp", "ctx")),
-            P(("dp", "ctx"), "seq"),
-            P(("dp", "ctx"), "seq"),
-            P("seq", ("dp", "ctx")),
-            P(("dp", "ctx", "seq")),
-            P(("dp", "ctx", "seq")),
-            P(("dp", "ctx", "seq")),
-            P(("dp", "ctx", "seq")),
-        ),
+        body,
+        mesh=grid,
+        in_specs=(rows, P("dp", ctx), tall, flat, flat, wide, tall, tall, wide, *gains, rows),
+        out_specs=(rows, rows, tall, flat, flat, wide, tall, tall, wide, *((P(everyone),) * 4)),
         check_vma=False,
     )

time: 1970 us -> 817 us (0.41)
  waiting for transfers between devices: 1490 us -> 417 us
  matrix products: 181 us -> 107 us
  blocking collectives: 86.3 us -> 29.6 us
  starting transfers between devices: 5.86 us -> 45.7 us
  other arithmetic: 63.6 us -> 94.7 us
    reduce_scatter x12 -> x4, waiting for transfers between devices: 804 us -> 87 us  [scatter_rows(): lax.psum_scatter(both.astype(jnp.bfloat16), 'seq', scatter_dimension=1, t...]
    all_gather x13 -> x4, waiting for transfers between devices: 625 us -> 51.3 us  [gather_rows(): lax.all_gather(local_rows, ('core', 'seq'), axis=1, tiled=True)]
    ppermute x0 -> x40, waiting for transfers between devices: none -> 256 us  [flip(): return lax.ppermute(value, axis, [(0, 1), (1, 0)])]
    dot_general x35 -> x18, matrix products: 181 us -> 107 us  [dot(): lax.dot_general(left, right, ((dims[:1], dims[1:]), ((), ())), preferred_...]
    unnamed x27 -> x8, waiting for transfers between devices: 47.7 us -> 0.13 us
    unnamed x1 -> x0, blocking collectives: 40.3 us -> none
    all_to_all x1 -> x0, blocking collectives: 35.5 us -> none  [local(): lax.all_to_all(head_items, 'seq', split_axis=1, concat_axis=2, tiled=True)]
    ppermute x0 -> x40, starting transfers between devices: none -> 34.3 us  [flip(): return lax.ppermute(value, axis, [(0, 1), (1, 0)])]
  transfers between devices with their start and end apart: 27 -> 51, of which waited for: 27 -> 28; matrix products, arithmetic and copies ran while one was open for 10% -> 25% of each run, Pallas kernels for 0% -> 0%
where the time goes in v1:
time: 817 us; the launch traced here: 810 us
  waiting for transfers between devices  417 us (51%)
  matrix products  107 us (13%)
  local copies, waits for them, and re-layouts  101 us (12%)
  other arithmetic  94.7 us (12%)
  starting transfers between devices  45.7 us (6%)
  blocking collectives  29.6 us (4%)
  between operations  16.1 us (2%)
    ppermute x40, waiting for transfers between devices, flip(): return lax.ppermute(value, axis, [(0, 1), (1, 0)])  256 us
    dot_general x18, matrix products, dot(): lax.dot_general(left, right, ((dims[:1], dims[1:]), ((), ())), preferred_...  107 us
    reduce_scatter x4, waiting for transfers between devices, scatter_rows(): lax.psum_scatter(both.astype(jnp.bfloat16), 'seq', scatter_dimension=1, t...  87 us
    all_gather x4, waiting for transfers between devices, gather_rows(): lax.all_gather(local_rows, ('core', 'seq'), axis=1, tiled=True)  51.3 us
    ppermute x40, starting transfers between devices, flip(): return lax.ppermute(value, axis, [(0, 1), (1, 0)])  34.3 us
    all_gather x1, blocking collectives, head_local(): seq_pos = lax.all_gather(positions, ('cy', 'core'), axis=1, tiled=True)  20.5 us
    all_to_all x1, waiting for transfers between devices, head_local(): lax.all_to_all(kv_stack.transpose(2, 0, 1, 3), 'seq', split_axis=0, conca...  17.3 us
    unnamed x173, local copies, waits for them, and re-layouts  17.2 us
  transfers between devices with their start and end apart: 51, of which 28 were waited for; matrix products, arithmetic and copies ran while one was open for 25% of the time, Pallas kernels for 0%

profile of v1, /device:TPU:0, one launch (start us, length us, event | category | flops | bytes accessed | tf_op | source)
XLA Modules:
  0.0 810.2 jit_solution(7075839232544310207)
XLA Ops:
  8.4 3.0 collective-permute-start
  14.2 9.0 %all-gather = bf16[8,288,4]{1,2,0:T(4,128)(2,1)S(1)} all-gather(bf16[1,288,4]{1,2,0:T(4,128)(2,1)S(1)} %maximum_bitcast_fusion.2), channel_id=1, replica_groups=mesh['dp'=2,'cy'=2,'core'=2,'seq'=4] {'dp','cy','core'}, dimensions={0}, use_global_device_ids=true | all-gather | bytes 20736 | tf_op jit(solution)/shard_map/all_gather | solution.py:566
  25.9 4.9 all-to-all-start
  31.2 17.3 %all-to-all-done = bf16[4,72,2,256]{3,1,2,0:T(8,128)(2,1)S(1)} async-done(((bf16[4,72,2,256]{3,1,2,0:T(8,128)(2,1)}), bf16[4,72,2,256]{3,1,2,0:T(8,128)(2,1)S(1)}, u32[]{:S(2)}, u32[]{:S(2)}) %all-to-all-start) | async-done | bytes 294944 | tf_op jit(solution)/shard_map/all_to_all | solution.py:548
  54.1 11.2 %collective-permute-done.2 = bf16[288,768]{1,0:T(8,128)(2,1)S(1)} collective-permute-done((bf16[288,768]{1,0:T(8,128)(2,1)S(1)}, bf16[288,768]{1,0:T(8,128)(2,1)S(1)}, u32[]{:S(2)}, u32[]{:S(2)}) %collective-permute-start.2) | collective-permute-done | bytes 442400 | tf_op jit(solution)/shard_map/ppermute | solution.py:446
  67.3 20.5 %all_gather.18 = s32[2,1024]{1,0:T(2,128)S(1)} all-gather(s32[2,256]{1,0:T(2,128)S(1)} %copy-done.67), channel_id=1, replica_groups=mesh['dp'=2,'cy'=2,'core'=2,'seq'=4] {'cy','core'}, dimensions={1}, use_global_device_ids=true | all-gather | bytes 10240 | tf_op jit(solution)/shard_map/all_gather | solution.py:571
  92.8 5.3 fusion.26
  98.1 2.5 fusion.87
  107.4 2.9 convolution_convert_fusion.5
  110.8 4.2 collective-permute-done.7
  118.7 3.9 reshape.1360
  122.6 3.4 reshape.1361
  126.0 3.7 pad_maximum_fusion.7
  129.7 3.8 constant_dynamic-slice_fusion.4
  134.8 5.5 constant_dynamic-slice_fusion.6
  141.6 22.2 %reduce-scatter.5.cloned.1.call-done = bf16[2,64,2304]{2,1,0:T(8,128)(2,1)} async-done(((bf16[2,256,2304]{2,1,0:T(8,128)(2,1)}), bf16[2,64,2304]{2,1,0:T(8,128)(2,1)}) %reduce-scatter.5.cloned.1.call-update) | async-done | bytes 589840 | tf_op jit(solution)/shard_map/reduce_scatter | solution.py:513
  166.9 2.4 multiply_convert_fusion.3
  176.8 12.1 %collective-permute-done.14 = bf16[288,1152]{1,0:T(8,128)(2,1)S(1)} collective-permute-done((bf16[288,1152]{1,0:T(8,128)(2,1)S(1)}, bf16[288,1152]{1,0:T(8,128)(2,1)S(1)}, u32[]{:S(2)}, u32[]{:S(2)}) %collective-permute-start.14) | collective-permute-done | bytes 663584 | tf_op jit(solution)/shard_map/ppermute | solution.py:446
  193.1 24.2 %collective-permute-done.9 = bf16[288,2304]{1,0:T(8,128)(2,1)S(1)} collective-permute-done((bf16[288,2304]{1,0:T(8,128)(2,1)S(1)}, bf16[288,2304]{1,0:T(8,128)(2,1)S(1)}, u32[]{:S(2)}, u32[]{:S(2)}) %collective-permute-start.9) | collective-permute-done | bytes 1327136 | tf_op jit(solution)/shard_map/ppermute | solution.py:446
  221.3 26.0 %collective-permute-done.15 = bf16[2,288,1152]{2,1,0:T(8,128)(2,1)S(1)} collective-permute-done((bf16[2,288,1152]{2,1,0:T(8,128)(2,1)S(1)}, bf16[2,288,1152]{2,1,0:T(8,128)(2,1)S(1)}, u32[]{:S(2)}, u32[]{:S(2)}) %collective-permute-start.15) | collective-permute-done | bytes 1327136 | tf_op jit(solution)/shard_map/ppermute | solution.py:446
  248.9 2.7 copy.206
  252.5 50.1 %collective-permute-done.10 = bf16[2,288,2304]{2,1,0:T(8,128)(2,1)} collective-permute-done((bf16[2,288,2304]{2,1,0:T(8,128)(2,1)S(1)}, bf16[2,288,2304]{2,1,0:T(8,128)(2,1)}, u32[]{:S(2)}, u32[]{:S(2)}) %collective-permute-start.10) | collective-permute-done | bytes 2654240 | tf_op jit(solution)/shard_map/ppermute | solution.py:446
  302.6 3.6 maximum_select_fusion
  306.2 3.6 maximum_select_fusion.1
  310.9 4.7 copy.205
  315.6 15.1 %fusion.119 = f32[1024,2304]{1,0:T(8,128)S(1)} fusion(bf16[1024,2304]{1,0:T(8,128)(2,1)} %bitcast.378, bf16[2304,2304]{1,0:T(8,128)(2,1)} %bitcast.315), kind=kOutput, calls=%fused_computation.305 | convolution fusion | flops 10871635968 | bytes 24772608 | tf_op jit(solution)/shard_map/dot_general | solution.py:519
  334.3 6.6 convolution_convert_fusion.4
  341.2 4.5 collective-permute-done.18
  349.5 45.3 %reduce-scatter.7.cloned.1.call-done = bf16[2,64,2304]{2,1,0:T(8,128)(2,1)} async-done(((bf16[2,256,2304]{2,1,0:T(8,128)(2,1)}), bf16[2,64,2304]{2,1,0:T(8,128)(2,1)}) %reduce-scatter.7.cloned.1.call-update) | async-done | bytes 589840 | tf_op jit(solution)/shard_map/reduce_scatter | solution.py:513
  397.8 2.3 fusion.54
  400.2 51.3 %all-gather.10.cloned.1.call-done = bf16[2,512,2304]{2,1,0:T(8,128)(2,1)} async-done(((bf16[2,64,2304]{2,1,0:T(8,128)(2,1)}), bf16[2,512,2304]{2,1,0:T(8,128)(2,1)}) %all-gather.10.cloned.1.call-update) | async-done | bytes 4718608 | tf_op jit(solution)/shard_map/all_gather | solution.py:505
  451.5 15.1 %fusion.8 = (bf16[1024,1152]{1,0:T(8,128)(2,1)S(1)}, bf16[1024,1152]{1,0:T(8,128)(2,1)S(1)}) fusion(f32[1024,2304]{1,0:T(8,128)} %copy-done.15, bf16[1024,2304]{1,0:T(8,128)(2,1)} %bitcast.384, bf16[2304,1152]{1,0:T(8,128)(2,1)} %bitcast.326), kind=kOutput, calls=%fused_computation.23 | convolution fusion | flops 5464129536 | bytes 24182784 | tf_op jit(solution)/shard_map/dot_general | solution.py:519
  466.6 15.3 %convolution_convert_fusion.3 = bf16[1024,2304]{1,0:T(8,128)(2,1)S(1)} fusion(bf16[2304,2304]{1,0:T(8,128)(2,1)} %bitcast.316, bf16[1024,1152]{1,0:T(8,128)(2,1)S(1)} %get-tuple-element.28, bf16[1024,1152]{1,0:T(8,128)(2,1)S(1)} %get-tuple-element.27), kind=kOutput, calls=%fused_computation.6 | convolution fusion | flops 10883432448 | bytes 20054016 | tf_op jit(solution)/shard_map/dot_general | solution.py:519
  482.5 4.3 collective-permute-done.21
  488.9 17.5 %convolution_convert_fusion = bf16[2304,2304]{1,0:T(8,128)(2,1)} fusion(bf16[1024,2304]{1,0:T(8,128)(2,1)} %bitcast.379, bf16[1024,1152]{1,0:T(8,128)(2,1)} %copy-done.73, bf16[1024,1152]{1,0:T(8,128)(2,1)} %copy-done.72), kind=kOutput, calls=%fused_computation | convolution fusion | flops 10886381568 | bytes 20054016 | tf_op jit(solution)/shard_map/dot_general | solution.py:519
  506.4 10.0 %convolution_convert_fusion.1 = bf16[2304,1152]{1,0:T(8,128)(2,1)} fusion(bf16[1024,2304]{1,0:T(8,128)(2,1)} %bitcast.385, bf16[1024,1152]{1,0:T(8,128)(2,1)S(1)} %copy-done.26), kind=kOutput, calls=%fused_computation.1 | convolution fusion | flops 5438472192 | bytes 12386304 | tf_op jit(solution)/shard_map/dot_general | solution.py:519
  516.4 19.5 %reduce-scatter.9.cloned.1.call-done = bf16[2,64,2304]{2,1,0:T(8,128)(2,1)} async-done(((bf16[2,256,2304]{2,1,0:T(8,128)(2,1)}), bf16[2,64,2304]{2,1,0:T(8,128)(2,1)}) %reduce-scatter.9.cloned.1.call-update) | async-done | bytes 589840 | tf_op jit(solution)/shard_map/reduce_scatter | solution.py:513
  535.9 3.5 fusion.51
  542.4 3.0 fusion.116
  550.7 8.8 %fusion.115 = (bf16[2,2,1,288,2304]{4,3,2,1,0:T(8,128)(2,1)}, bf16[2,2,1,288,2304]{4,3,2,1,0:T(8,128)(2,1)}) fusion(bf16[2,2,2,288,2304]{4,3,2,1,0:T(8,128)(2,1)} %bitcast.317), kind=kLoop, calls=%fused_computation.301 | loop fusion | bytes 21233664 | tf_op jit(solution)/shard_map/slice | solution.py:485
  559.5 3.6 dynamic-slice_bitcast_fusion
  566.6 12.4 %collective-permute-done.37 = bf16[2,288,1152]{2,1,0:T(8,128)(2,1)} collective-permute-done((bf16[2,288,1152]{2,1,0:T(8,128)(2,1)}, bf16[2,288,1152]{2,1,0:T(8,128)(2,1)}, u32[]{:S(2)}, u32[]{:S(2)}) %collective-permute-start.37) | collective-permute-done | bytes 1327136 | tf_op jit(solution)/shard_map/ppermute | solution.py:446
  587.4 63.7 %collective-permute-done.38 = bf16[288,1152]{1,0:T(8,128)(2,1)} collective-permute-done((bf16[288,1152]{1,0:T(8,128)(2,1)S(1)}, bf16[288,1152]{1,0:T(8,128)(2,1)}, u32[]{:S(2)}, u32[]{:S(2)}) %collective-permute-start.38) | collective-permute-done | bytes 663584 | tf_op jit(solution)/shard_map/ppermute | solution.py:446
  651.1 3.5 select_bitcast_fusion.1
  654.7 3.3 fusion
  660.7 2.4 fusion.1
  666.1 4.2 convolution_convert_fusion.8
  671.9 2.7 multiply_convert_fusion.2
  676.4 2.4 fusion.95
  684.6 3.0 convolution_convert_fusion.2
  691.0 5.6 collective-permute-done.31
  696.6 4.5 select_bitcast_fusion
  702.7 3.5 convolution_convert_fusion.6
  708.2 6.0 copy.212
  714.2 3.5 fusion.117
  720.9 4.4 fusion.9
  729.2 12.9 %collective-permute-done.27 = bf16[2,288,768]{2,1,0:T(8,128)(2,1)S(1)} collective-permute-done((bf16[2,288,768]{2,1,0:T(8,128)(2,1)}, bf16[2,288,768]{2,1,0:T(8,128)(2,1)S(1)}, u32[]{:S(2)}, u32[]{:S(2)}) %collective-permute-start.27) | collective-permute-done | bytes 884768 | tf_op jit(solution)/shard_map/ppermute | solution.py:446
  743.1 7.7 collective-permute-done.25
  755.8 3.7 collective-permute-done.28
  759.5 2.4 collective-permute-done.26
  771.5 3.5 all-to-all-start.1
  781.8 3.4 all-to-all-done.1
  787.8 2.6 all-to-all-start.2
  798.4 3.7 collective-permute-done.24
  (394 shorter events, 151.0 us)
Async XLA Ops:
  7.2 17.6 %copy-start.45 = (bf16[72,1024]{1,0:T(8,128)(2,1)S(1)}, bf16[72,1024]{1,0:T(8,128)(2,1)}, u32[]{:S(2)}) copy-start(bf16[72,1024]{1,0:T(8,128)(2,1)} %param.17) | copy-start | bytes 442372
  7.2 17.7 %copy-start.46 = (bf16[72,1024]{1,0:T(8,128)(2,1)S(1)}, bf16[72,1024]{1,0:T(8,128)(2,1)}, u32[]{:S(2)}) copy-start(bf16[72,1024]{1,0:T(8,128)(2,1)} %param.18) | copy-start | bytes 442372
  7.2 85.6 %all-gather.6.cloned.1.call-start = ((), (), s32[]{:S(2)}) async-start(), calls=%async_computation.7 | async-start | bytes 5308416 | tf_op jit(solution)/shard_map/all_gather | solution.py:505
  8.4 22.4 %copy-start.37 = (bf16[288,512]{1,0:T(8,128)(2,1)S(1)}, bf16[288,512]{1,0:T(8,128)(2,1)}, u32[]{:S(2)}) copy-start(bf16[288,512]{1,0:T(8,128)(2,1)} %param.16) | copy-start | bytes 884740
  8.4 15.0 %collective-permute-start = (bf16[64,2304]{1,0:T(8,128)(2,1)S(1)}, bf16[64,2304]{1,0:T(8,128)(2,1)S(1)}, u32[]{:S(2)}, u32[]{:S(2)}) collective-permute-start(bf16[64,2304]{1,0:T(8,128)(2,1)S(1)} %get-tuple-element.74), channel_id=1, source_target_pairs={{0,8},{8,0},{1,9},{9,1},{2,10},{10,2},{3,11},{11,3},{4,12},{12,4},... | collective-permute-start | bytes 884744 | tf_op jit(solution)/shard_map/ppermute | solution.py:446
  23.4 739.5 %copy-start.34 = (f32[2304]{0:T(1024)}, f32[2304]{0:T(1024)S(1)}, u32[]{:S(2)}) copy-start(f32[2304]{0:T(1024)S(1)} %get-tuple-element.24) | copy-start | bytes 27652
  25.9 22.6 %all-to-all-start = ((bf16[4,72,2,256]{3,1,2,0:T(8,128)(2,1)}), bf16[4,72,2,256]{3,1,2,0:T(8,128)(2,1)S(1)}, u32[]{:S(2)}, u32[]{:S(2)}) async-start(bf16[4,72,2,256]{3,1,2,0:T(8,128)(2,1)} %copy.200), calls=%async_computation | async-start | bytes 589824 | tf_op jit(solution)/shard_map/all_to_all | solution.py:548
  30.8 133.1 %reduce-scatter.5.cloned.1.call-start = ((), (), s32[]{:S(2)}) async-start(), calls=%async_computation.8 | async-start | bytes 2949120 | tf_op jit(solution)/shard_map/reduce_scatter | solution.py:513
  51.1 1.9 collective-permute-start.1
  53.1 12.3 %collective-permute-start.2 = (bf16[288,768]{1,0:T(8,128)(2,1)S(1)}, bf16[288,768]{1,0:T(8,128)(2,1)S(1)}, u32[]{:S(2)}, u32[]{:S(2)}) collective-permute-start(bf16[288,768]{1,0:T(8,128)(2,1)S(1)} %get-tuple-element.57), channel_id=1, source_target_pairs={{0,8},{8,0},{1,9},{9,1},{2,10},{10,2},{3,11},{11,3},{4,12},{12,4},... | collective-permute-start | bytes 1327112 | tf_op jit(solution)/shard_map/ppermute | solution.py:446
  54.1 11.9 %collective-permute-start.4 = (bf16[288,768]{1,0:T(8,128)(2,1)S(1)}, bf16[288,768]{1,0:T(8,128)(2,1)S(1)}, u32[]{:S(2)}, u32[]{:S(2)}) collective-permute-start(bf16[288,768]{1,0:T(8,128)(2,1)S(1)} %get-tuple-element.58), channel_id=1, source_target_pairs={{0,16},{16,0},{1,17},{17,1},{2,18},{18,2},{3,19},{19,3},{4,20},{20... | collective-permute-start | bytes 1327112 | tf_op jit(solution)/shard_map/ppermute | solution.py:446
  65.5 22.7 %collective-permute-start.3 = (bf16[2,288,768]{2,1,0:T(8,128)(2,1)S(1)}, bf16[2,288,768]{2,1,0:T(8,128)(2,1)}, u32[]{:S(2)}, u32[]{:S(2)}) collective-permute-start(bf16[2,288,768]{2,1,0:T(8,128)(2,1)S(1)} %maximum_select_fusion.18), channel_id=1, source_target_pairs={{0,16},{16,0},{1,17},{17,1},{2,18},{18,2},{3,19},{19,3},{4,20},{20... | collective-permute-start | bytes 2654216 | tf_op jit(solution)/shard_map/ppermute | solution.py:446
  66.2 23.9 %collective-permute-start.5 = (bf16[2,288,768]{2,1,0:T(8,128)(2,1)S(1)}, bf16[2,288,768]{2,1,0:T(8,128)(2,1)S(1)}, u32[]{:S(2)}, u32[]{:S(2)}) collective-permute-start(bf16[2,288,768]{2,1,0:T(8,128)(2,1)S(1)} %maximum_select_fusion.20), channel_id=1, source_target_pairs={{0,8},{8,0},{1,9},{9,1},{2,10},{10,2},{3,11},{11,3},{4,12},{12,4},... | collective-permute-start | bytes 2654216 | tf_op jit(solution)/shard_map/ppermute | solution.py:446
  100.6 2.0 collective-permute-start.6
  110.5 4.6 collective-permute-start.7
  117.0 198.5 %all-gather.8.cloned.1.call-start = ((), (), s32[]{:S(2)}) async-start(), calls=%async_computation.9 | async-start | bytes 5308416 | tf_op jit(solution)/shard_map/all_gather | solution.py:505
  134.5 34.8 %collective-permute-start.13 = (bf16[288,1152]{1,0:T(8,128)(2,1)}, bf16[288,1152]{1,0:T(8,128)(2,1)}, u32[]{:S(2)}, u32[]{:S(2)}) collective-permute-start(bf16[288,1152]{1,0:T(8,128)(2,1)} %bitcast.288), channel_id=1, source_target_pairs={{0,4},{4,0},{1,5},{5,1},{2,6},{6,2},{3,7},{7,3},{8,12},{12,8},{9,1... | collective-permute-start | bytes 1990664 | tf_op jit(solution)/shard_map/ppermute | solution.py:446
  141.4 32.6 %collective-permute-start.8 = (bf16[288,2304]{1,0:T(8,128)(2,1)}, bf16[288,2304]{1,0:T(8,128)(2,1)}, u32[]{:S(2)}, u32[]{:S(2)}) collective-permute-start(bf16[288,2304]{1,0:T(8,128)(2,1)} %bitcast.287), channel_id=1, source_target_pairs={{0,4},{4,0},{1,5},{5,1},{2,6},{6,2},{3,7},{7,3},{8,12},{12,8},{9,1... | collective-permute-start | bytes 3981320 | tf_op jit(solution)/shard_map/ppermute | solution.py:446
  166.9 596.1 %copy-start.50 = (f32[2,64]{1,0:T(2,128)}, f32[2,64]{1,0:T(2,128)S(1)}, u32[]{:S(2)}) copy-start(f32[2,64]{1,0:T(2,128)S(1)} %fusion.106) | copy-start | bytes 1540
  169.2 225.6 %reduce-scatter.7.cloned.1.call-start = ((), (), s32[]{:S(2)}) async-start(), calls=%async_computation.10 | async-start | bytes 2949120 | tf_op jit(solution)/shard_map/reduce_scatter | solution.py:513
  171.0 17.9 %collective-permute-start.14 = (bf16[288,1152]{1,0:T(8,128)(2,1)S(1)}, bf16[288,1152]{1,0:T(8,128)(2,1)S(1)}, u32[]{:S(2)}, u32[]{:S(2)}) collective-permute-start(bf16[288,1152]{1,0:T(8,128)(2,1)S(1)} %get-tuple-element.51), channel_id=1, source_target_pairs={{0,8},{8,0},{1,9},{9,1},{2,10},{10,2},{3,11},{11,3},{4,12},{12,4},... | collective-permute-start | bytes 1990664 | tf_op jit(solution)/shard_map/ppermute | solution.py:446
  172.5 18.2 %collective-permute-start.16 = (bf16[288,1152]{1,0:T(8,128)(2,1)S(1)}, bf16[288,1152]{1,0:T(8,128)(2,1)S(1)}, u32[]{:S(2)}, u32[]{:S(2)}) collective-permute-start(bf16[288,1152]{1,0:T(8,128)(2,1)S(1)} %get-tuple-element.52), channel_id=1, source_target_pairs={{0,16},{16,0},{1,17},{17,1},{2,18},{18,2},{3,19},{19,3},{4,20},{20... | collective-permute-start | bytes 1990664 | tf_op jit(solution)/shard_map/ppermute | solution.py:446
  175.6 41.7 %collective-permute-start.9 = (bf16[288,2304]{1,0:T(8,128)(2,1)S(1)}, bf16[288,2304]{1,0:T(8,128)(2,1)S(1)}, u32[]{:S(2)}, u32[]{:S(2)}) collective-permute-start(bf16[288,2304]{1,0:T(8,128)(2,1)S(1)} %get-tuple-element.39), channel_id=1, source_target_pairs={{0,8},{8,0},{1,9},{9,1},{2,10},{10,2},{3,11},{11,3},{4,12},{12,4},... | collective-permute-start | bytes 3981320 | tf_op jit(solution)/shard_map/ppermute | solution.py:446
  176.2 43.1 %collective-permute-start.11 = (bf16[288,2304]{1,0:T(8,128)(2,1)S(1)}, bf16[288,2304]{1,0:T(8,128)(2,1)S(1)}, u32[]{:S(2)}, u32[]{:S(2)}) collective-permute-start(bf16[288,2304]{1,0:T(8,128)(2,1)S(1)} %get-tuple-element.40), channel_id=1, source_target_pairs={{0,16},{16,0},{1,17},{17,1},{2,18},{18,2},{3,19},{19,3},{4,20},{20... | collective-permute-start | bytes 3981320 | tf_op jit(solution)/shard_map/ppermute | solution.py:446
  189.2 58.1 %collective-permute-start.15 = (bf16[2,288,1152]{2,1,0:T(8,128)(2,1)S(1)}, bf16[2,288,1152]{2,1,0:T(8,128)(2,1)S(1)}, u32[]{:S(2)}, u32[]{:S(2)}) collective-permute-start(bf16[2,288,1152]{2,1,0:T(8,128)(2,1)S(1)} %maximum_select_fusion.14), channel_id=1, source_target_pairs={{0,16},{16,0},{1,17},{17,1},{2,18},{18,2},{3,19},{19,3},{4,20},{20... | collective-permute-start | bytes 3981320 | tf_op jit(solution)/shard_map/ppermute | solution.py:446
  191.0 56.8 %collective-permute-start.17 = (bf16[2,288,1152]{2,1,0:T(8,128)(2,1)S(1)}, bf16[2,288,1152]{2,1,0:T(8,128)(2,1)S(1)}, u32[]{:S(2)}, u32[]{:S(2)}) collective-permute-start(bf16[2,288,1152]{2,1,0:T(8,128)(2,1)S(1)} %maximum_select_fusion.16), channel_id=1, source_target_pairs={{0,8},{8,0},{1,9},{9,1},{2,10},{10,2},{3,11},{11,3},{4,12},{12,4},... | collective-permute-start | bytes 3981320 | tf_op jit(solution)/shard_map/ppermute | solution.py:446
  217.8 84.8 %collective-permute-start.10 = (bf16[2,288,2304]{2,1,0:T(8,128)(2,1)S(1)}, bf16[2,288,2304]{2,1,0:T(8,128)(2,1)}, u32[]{:S(2)}, u32[]{:S(2)}) collective-permute-start(bf16[2,288,2304]{2,1,0:T(8,128)(2,1)S(1)} %maximum_select_fusion.4), channel_id=1, source_target_pairs={{0,16},{16,0},{1,17},{17,1},{2,18},{18,2},{3,19},{19,3},{4,20},{20... | collective-permute-start | bytes 7962632 | tf_op jit(solution)/shard_map/ppermute | solution.py:446
  219.8 86.4 %collective-permute-start.12 = (bf16[2,288,2304]{2,1,0:T(8,128)(2,1)S(1)}, bf16[2,288,2304]{2,1,0:T(8,128)(2,1)}, u32[]{:S(2)}, u32[]{:S(2)}) collective-permute-start(bf16[2,288,2304]{2,1,0:T(8,128)(2,1)S(1)} %maximum_select_fusion.6), channel_id=1, source_target_pairs={{0,8},{8,0},{1,9},{9,1},{2,10},{10,2},{3,11},{11,3},{4,12},{12,4},... | collective-permute-start | bytes 7962632 | tf_op jit(solution)/shard_map/ppermute | solution.py:446
  310.9 23.4 %slice-start.2 = ((s8[5308416]{0:T(1024)(128)(4,1)}), s8[1114112]{0:T(1024)(128)(4,1)S(1)}, s32[]{:S(2)}) async-start(s8[5308416]{0:T(1024)(128)(4,1)} %bitcast.327), calls=%async_computation.17 | async-start | bytes 2228224
  315.6 18.8 %slice-start.3 = ((s8[5308416]{0:T(1024)(128)(4,1)}), s8[4194304]{0:T(1024)(128)(4,1)S(1)}, s32[]{:S(2)}) async-start(s8[5308416]{0:T(1024)(128)(4,1)} %bitcast.327), calls=%async_computation.18 | async-start | bytes 8388608
  341.1 4.6 collective-permute-start.18
  347.8 103.7 %all-gather.10.cloned.1.call-start = ((), (), s32[]{:S(2)}) async-start(), calls=%async_computation.11 | async-start | bytes 5308416 | tf_op jit(solution)/shard_map/all_gather | solution.py:505
  348.9 47.2 %collective-permute-start.20 = (bf16[64,2304]{1,0:T(8,128)(2,1)S(1)}, bf16[64,2304]{1,0:T(8,128)(2,1)S(1)}, u32[]{:S(2)}, u32[]{:S(2)}) collective-permute-start(bf16[64,2304]{1,0:T(8,128)(2,1)S(1)} %get-tuple-element.70), channel_id=1, source_target_pairs={{0,8},{8,0},{1,9},{9,1},{2,10},{10,2},{3,11},{11,3},{4,12},{12,4},... | collective-permute-start | bytes 884744 | tf_op jit(solution)/shard_map/ppermute | solution.py:446
  400.2 135.7 %reduce-scatter.9.cloned.1.call-start = ((), (), s32[]{:S(2)}) async-start(), calls=%async_computation.12 | async-start | bytes 2949120 | tf_op jit(solution)/shard_map/reduce_scatter | solution.py:513
  482.2 4.6 collective-permute-start.21
  488.8 177.3 %all-gather.12.cloned.1.call-start = ((), (), s32[]{:S(2)}) async-start(), calls=%async_computation.13 | async-start | bytes 5308416 | tf_op jit(solution)/shard_map/all_gather | solution.py:505
  488.9 17.5 %copy-start.26 = (bf16[1024,1152]{1,0:T(8,128)(2,1)S(1)}, bf16[1024,1152]{1,0:T(8,128)(2,1)}, u32[]{:S(2)}) copy-start(bf16[1024,1152]{1,0:T(8,128)(2,1)} %copy-done.25) | copy-start | bytes 7077892
  506.4 29.5 %copy-start = (bf16[2,64,2304]{2,1,0:T(8,128)(2,1)S(1)}, bf16[2,64,2304]{2,1,0:T(8,128)(2,1)}, u32[]{:S(2)}) copy-start(bf16[2,64,2304]{2,1,0:T(8,128)(2,1)} %reduce-scatter.5.cloned.1.call-done) | copy-start | bytes 1769476
  506.4 29.5 %copy-start.14 = (bf16[2,64,2304]{2,1,0:T(8,128)(2,1)S(1)}, bf16[2,64,2304]{2,1,0:T(8,128)(2,1)}, u32[]{:S(2)}) copy-start(bf16[2,64,2304]{2,1,0:T(8,128)(2,1)} %reduce-scatter.7.cloned.1.call-done) | copy-start | bytes 1769476
  539.4 223.5 %copy-start.57 = (f32[2,64]{1,0:T(2,128)}, f32[2,64]{1,0:T(2,128)S(1)}, u32[]{:S(2)}) copy-start(f32[2,64]{1,0:T(2,128)S(1)} %multiply_multiply_fusion.5) | copy-start | bytes 1540
  542.1 243.1 %reduce-scatter.11.cloned.1.call-start = ((), (), s32[]{:S(2)}) async-start(), calls=%async_computation.14 | async-start | bytes 2949120 | tf_op jit(solution)/shard_map/reduce_scatter | solution.py:513
  546.6 32.4 %collective-permute-start.37 = (bf16[2,288,1152]{2,1,0:T(8,128)(2,1)}, bf16[2,288,1152]{2,1,0:T(8,128)(2,1)}, u32[]{:S(2)}, u32[]{:S(2)}) collective-permute-start(bf16[2,288,1152]{2,1,0:T(8,128)(2,1)} %dynamic-slice_bitcast_fusion.6), channel_id=1, source_target_pairs={{0,8},{8,0},{1,9},{9,1},{2,10},{10,2},{3,11},{11,3},{4,12},{12,4},... | collective-permute-start | bytes 3981320 | tf_op jit(solution)/shard_map/ppermute | solution.py:446
  549.3 33.0 %collective-permute-start.35 = (bf16[2,288,1152]{2,1,0:T(8,128)(2,1)}, bf16[2,288,1152]{2,1,0:T(8,128)(2,1)}, u32[]{:S(2)}, u32[]{:S(2)}) collective-permute-start(bf16[2,288,1152]{2,1,0:T(8,128)(2,1)} %dynamic-slice_bitcast_fusion.7), channel_id=1, source_target_pairs={{0,16},{16,0},{1,17},{17,1},{2,18},{18,2},{3,19},{19,3},{4,20},{20... | collective-permute-start | bytes 3981320 | tf_op jit(solution)/shard_map/ppermute | solution.py:446
  563.1 91.6 %collective-permute-start.32 = (bf16[2,288,2304]{2,1,0:T(8,128)(2,1)}, bf16[2,288,2304]{2,1,0:T(8,128)(2,1)}, u32[]{:S(2)}, u32[]{:S(2)}) collective-permute-start(bf16[2,288,2304]{2,1,0:T(8,128)(2,1)} %dynamic-slice_bitcast_fusion), channel_id=1, source_target_pairs={{0,8},{8,0},{1,9},{9,1},{2,10},{10,2},{3,11},{11,3},{4,12},{12,4},... | collective-permute-start | bytes 7962632 | tf_op jit(solution)/shard_map/ppermute | solution.py:446
  565.9 94.8 %collective-permute-start.30 = (bf16[2,288,2304]{2,1,0:T(8,128)(2,1)}, bf16[2,288,2304]{2,1,0:T(8,128)(2,1)}, u32[]{:S(2)}, u32[]{:S(2)}) collective-permute-start(bf16[2,288,2304]{2,1,0:T(8,128)(2,1)} %dynamic-slice_bitcast_fusion.1), channel_id=1, source_target_pairs={{0,16},{16,0},{1,17},{17,1},{2,18},{18,2},{3,19},{19,3},{4,20},{20... | collective-permute-start | bytes 7962632 | tf_op jit(solution)/shard_map/ppermute | solution.py:446
  580.7 70.4 %collective-permute-start.38 = (bf16[288,1152]{1,0:T(8,128)(2,1)S(1)}, bf16[288,1152]{1,0:T(8,128)(2,1)}, u32[]{:S(2)}, u32[]{:S(2)}) collective-permute-start(bf16[288,1152]{1,0:T(8,128)(2,1)S(1)} %dynamic-slice_bitcast_fusion.12), channel_id=1, source_target_pairs={{0,16},{16,0},{1,17},{17,1},{2,18},{18,2},{3,19},{19,3},{4,20},{20... | collective-permute-start | bytes 1990664 | tf_op jit(solution)/shard_map/ppermute | solution.py:446
  585.2 65.9 %collective-permute-start.36 = (bf16[288,1152]{1,0:T(8,128)(2,1)}, bf16[288,1152]{1,0:T(8,128)(2,1)}, u32[]{:S(2)}, u32[]{:S(2)}) collective-permute-start(bf16[288,1152]{1,0:T(8,128)(2,1)} %dynamic-slice_bitcast_fusion.13), channel_id=1, source_target_pairs={{0,8},{8,0},{1,9},{9,1},{2,10},{10,2},{3,11},{11,3},{4,12},{12,4},... | collective-permute-start | bytes 1990664 | tf_op jit(solution)/shard_map/ppermute | solution.py:446
  654.7 25.6 %collective-permute-start.39 = (bf16[288,1152]{1,0:T(8,128)(2,1)}, bf16[288,1152]{1,0:T(8,128)(2,1)S(1)}, u32[]{:S(2)}, u32[]{:S(2)}) collective-permute-start(bf16[288,1152]{1,0:T(8,128)(2,1)} %get-tuple-element.38), channel_id=1, source_target_pairs={{0,4},{4,0},{1,5},{5,1},{2,6},{6,2},{3,7},{7,3},{8,12},{12,8},{9,1... | collective-permute-start | bytes 1990664 | tf_op jit(solution)/shard_map/ppermute | solution.py:446
  659.2 31.8 %collective-permute-start.33 = (bf16[288,2304]{1,0:T(8,128)(2,1)}, bf16[288,2304]{1,0:T(8,128)(2,1)}, u32[]{:S(2)}, u32[]{:S(2)}) collective-permute-start(bf16[288,2304]{1,0:T(8,128)(2,1)} %dynamic-slice_bitcast_fusion.8), channel_id=1, source_target_pairs={{0,16},{16,0},{1,17},{17,1},{2,18},{18,2},{3,19},{19,3},{4,20},{20... | collective-permute-start | bytes 3981320 | tf_op jit(solution)/shard_map/ppermute | solution.py:446
  665.1 31.5 %collective-permute-start.31 = (bf16[288,2304]{1,0:T(8,128)(2,1)}, bf16[288,2304]{1,0:T(8,128)(2,1)}, u32[]{:S(2)}, u32[]{:S(2)}) collective-permute-start(bf16[288,2304]{1,0:T(8,128)(2,1)} %dynamic-slice_bitcast_fusion.9), channel_id=1, source_target_pairs={{0,8},{8,0},{1,9},{9,1},{2,10},{10,2},{3,11},{11,3},{4,12},{12,4},... | collective-permute-start | bytes 3981320 | tf_op jit(solution)/shard_map/ppermute | solution.py:446
  680.1 3.2 collective-permute-start.22
  684.6 18.0 %slice-start.4 = ((s8[4718592]{0:T(1024)(128)(4,1)}), s8[4194304]{0:T(1024)(128)(4,1)S(1)}, s32[]{:S(2)}) async-start(s8[4718592]{0:T(1024)(128)(4,1)} %bitcast.375), calls=%async_computation.19 | async-start | bytes 8388608
  689.2 31.7 %collective-permute-start.23 = (bf16[2,256,2304]{2,1,0:T(8,128)(2,1)}, bf16[2,256,2304]{2,1,0:T(8,128)(2,1)}, u32[]{:S(2)}, u32[]{:S(2)}) collective-permute-start(bf16[2,256,2304]{2,1,0:T(8,128)(2,1)} %dynamic-slice_bitcast_fusion.2), channel_id=1, source_target_pairs={{0,4},{4,0},{1,5},{5,1},{2,6},{6,2},{3,7},{7,3},{8,12},{12,8},{9,1... | collective-permute-start | bytes 7077896 | tf_op jit(solution)/shard_map/ppermute | solution.py:446
  701.1 24.2 %collective-permute-start.34 = (bf16[288,2304]{1,0:T(8,128)(2,1)}, bf16[288,2304]{1,0:T(8,128)(2,1)}, u32[]{:S(2)}, u32[]{:S(2)}) collective-permute-start(bf16[288,2304]{1,0:T(8,128)(2,1)} %get-tuple-element.32), channel_id=1, source_target_pairs={{0,4},{4,0},{1,5},{5,1},{2,6},{6,2},{3,7},{7,3},{8,12},{12,8},{9,1... | collective-permute-start | bytes 3981320 | tf_op jit(solution)/shard_map/ppermute | solution.py:446
  719.9 22.3 %collective-permute-start.27 = (bf16[2,288,768]{2,1,0:T(8,128)(2,1)}, bf16[2,288,768]{2,1,0:T(8,128)(2,1)S(1)}, u32[]{:S(2)}, u32[]{:S(2)}) collective-permute-start(bf16[2,288,768]{2,1,0:T(8,128)(2,1)} %dynamic-slice_bitcast_fusion.10), channel_id=1, source_target_pairs={{0,8},{8,0},{1,9},{9,1},{2,10},{10,2},{3,11},{11,3},{4,12},{12,4},... | collective-permute-start | bytes 2654216 | tf_op jit(solution)/shard_map/ppermute | solution.py:446
  728.2 22.6 %collective-permute-start.25 = (bf16[2,288,768]{2,1,0:T(8,128)(2,1)S(1)}, bf16[2,288,768]{2,1,0:T(8,128)(2,1)S(1)}, u32[]{:S(2)}, u32[]{:S(2)}) collective-permute-start(bf16[2,288,768]{2,1,0:T(8,128)(2,1)S(1)} %dynamic-slice_bitcast_fusion.11), channel_id=1, source_target_pairs={{0,16},{16,0},{1,17},{17,1},{2,18},{18,2},{3,19},{19,3},{4,20},{20... | collective-permute-start | bytes 2654216 | tf_op jit(solution)/shard_map/ppermute | solution.py:446
  729.2 21.6 %copy-start.16 = (bf16[2,2,1,288,768]{4,3,2,1,0:T(8,128)(2,1)S(1)}, bf16[2,2,1,288,768]{4,3,2,1,0:T(8,128)(2,1)}, u32[]{:S(2)}) copy-start(bf16[2,2,1,288,768]{4,3,2,1,0:T(8,128)(2,1)} %get-tuple-element.42) | copy-start | bytes 5308420
  742.4 17.1 %collective-permute-start.28 = (bf16[288,768]{1,0:T(8,128)(2,1)S(1)}, bf16[288,768]{1,0:T(8,128)(2,1)S(1)}, u32[]{:S(2)}, u32[]{:S(2)}) collective-permute-start(bf16[288,768]{1,0:T(8,128)(2,1)S(1)} %dynamic-slice_bitcast_fusion.14), channel_id=1, source_target_pairs={{0,16},{16,0},{1,17},{17,1},{2,18},{18,2},{3,19},{19,3},{4,20},{20... | collective-permute-start | bytes 1327112 | tf_op jit(solution)/shard_map/ppermute | solution.py:446
  751.0 10.9 %collective-permute-start.26 = (bf16[288,768]{1,0:T(8,128)(2,1)S(1)}, bf16[288,768]{1,0:T(8,128)(2,1)S(1)}, u32[]{:S(2)}, u32[]{:S(2)}) collective-permute-start(bf16[288,768]{1,0:T(8,128)(2,1)S(1)} %dynamic-slice_bitcast_fusion.15), channel_id=1, source_target_pairs={{0,8},{8,0},{1,9},{9,1},{2,10},{10,2},{3,11},{11,3},{4,12},{12,4},... | collective-permute-start | bytes 1327112 | tf_op jit(solution)/shard_map/ppermute | solution.py:446
  762.9 5.0 collective-permute-start.29
  766.9 9.7 %collective-permute-start.19 = (bf16[64,2304]{1,0:T(8,128)(2,1)}, bf16[64,2304]{1,0:T(8,128)(2,1)}, u32[]{:S(2)}, u32[]{:S(2)}) collective-permute-start(bf16[64,2304]{1,0:T(8,128)(2,1)} %get-tuple-element.73), channel_id=1, source_target_pairs={{0,8},{8,0},{1,9},{9,1},{2,10},{10,2},{3,11},{11,3},{4,12},{12,4},... | collective-permute-start | bytes 884744 | tf_op jit(solution)/shard_map/ppermute | solution.py:446
  771.5 13.6 %all-to-all-start.1 = ((bf16[288,2,256]{2,1,0:T(2,128)(2,1)}), bf16[288,2,256]{2,1,0:T(2,128)(2,1)S(1)}, u32[]{:S(2)}, u32[]{:S(2)}) async-start(bf16[288,2,256]{2,1,0:T(2,128)(2,1)} %copy.215), calls=%async_computation.5 | async-start | bytes 589824 | tf_op jit(solution)/shard_map/all_to_all | solution.py:671
  787.8 10.1 %all-to-all-start.2 = ((f32[32,4,72]{2,1,0:T(4,128)}), f32[32,4,72]{2,1,0:T(4,128)S(1)}, u32[]{:S(2)}, u32[]{:S(2)}) async-start(f32[32,4,72]{2,1,0:T(4,128)} %maximum_bitcast_fusion.1), calls=%async_computation.6 | async-start | bytes 131072 | tf_op jit(solution)/shard_map/all_to_all | solution.py:660
  792.7 9.4 %collective-permute-start.24 = (bf16[64,2304]{1,0:T(8,128)(2,1)S(1)}, bf16[64,2304]{1,0:T(8,128)(2,1)S(1)}, u32[]{:S(2)}, u32[]{:S(2)}) collective-permute-start(bf16[64,2304]{1,0:T(8,128)(2,1)S(1)} %get-tuple-element.69), channel_id=1, source_target_pairs={{0,8},{8,0},{1,9},{9,1},{2,10},{10,2},{3,11},{11,3},{4,12},{12,4},... | collective-permute-start | bytes 884744 | tf_op jit(solution)/shard_map/ppermute | solution.py:446
  (69 other events, 443.4 us)
Sparse Core Ops, SparseCore 0:
  24.9 55.8 all-gather.5
  117.2 46.6 reduce-scatter.4
  169.4 51.1 all-gather.7
  347.9 46.8 reduce-scatter.6
  400.3 51.1 all-gather.9
  488.9 46.8 reduce-scatter.8
  542.3 51.1 all-gather.11
  725.4 46.3 reduce-scatter.10

commit v2 on v1

--- a/solution.py
+++ b/solution.py
@@ -1,8 +1,11 @@
+import functools
 import math
 
 import jax
 import jax.numpy as jnp
 from jax import lax
+from jax.experimental import pallas as pl
+from jax.experimental.pallas import tpu as pltpu
 from jax.sharding import PartitionSpec as P
 
 QUERY_HEAD_COUNT = 8
@@ -456,48 +459,114 @@
     return lax.dynamic_index_in_dim(value, index, axis, keepdims=False)
 
 
+def after(value, *earlier):
+    return lax.optimization_barrier((value, *earlier))[0]
+
+
+def total(kept, *got):
+    value = kept.astype(jnp.float32)
+    for more in got:
+        value = value + more.astype(jnp.float32)
+    return value
+
+
 def trade_sequences(value):
     cy = lax.axis_index("cy")
     return ordered(cy, pick(value, cy), flip(pick(value, 1 - cy), "cy"))
 
 
-def gather_weight(local_rows):
-    x, y, c = lax.axis_index("dp"), lax.axis_index("cy"), lax.axis_index("core")
-    own = pick(local_rows, c, 1)
-    got = flip(pick(local_rows, 1 - c, 1), "core")
-    first = jnp.where(c == 0, own, got)
-    second = jnp.where(c == 0, got, own)
-    first_y = flip(first, "cy")
-    second_x = flip(second, "dp")
-    first_pair = ordered(y, first, first_y)
-    second_pair = ordered(x, second, second_x)
-    first_x = flip(first_pair, "dp")
-    second_y = flip(second_pair, "cy")
-    first_all = ordered(x, first_pair, first_x)
-    second_all = ordered(y, second_pair, second_y, axis=1)
-    return jnp.stack([first_all, second_all], axis=2).reshape(-1, own.shape[-1])
-
-
-def scatter_weight_grad(grad):
-    x, y, c = lax.axis_index("dp"), lax.axis_index("cy"), lax.axis_index("core")
-    cols = grad.shape[-1]
-    parts = grad.reshape(2, 2, 2, -1, cols)
-    first, second = parts[:, :, 0], parts[:, :, 1]
-    first_x = flip(pick(first, 1 - x), "dp")
-    second_y = flip(pick(second, 1 - y, 1), "cy")
-    first_sum = (pick(first, x).astype(jnp.float32) + first_x.astype(jnp.float32)).astype(
-        jnp.bfloat16
-    )
-    second_sum = (pick(second, y, 1).astype(jnp.float32) + second_y.astype(jnp.float32)).astype(
-        jnp.bfloat16
-    )
-    first_y = flip(pick(first_sum, 1 - y), "cy")
-    second_x = flip(pick(second_sum, 1 - x), "dp")
-    first_total = pick(first_sum, y).astype(jnp.float32) + first_y.astype(jnp.float32)
-    second_total = pick(second_sum, x).astype(jnp.float32) + second_x.astype(jnp.float32)
-    keep = jnp.where(c == 0, first_total, second_total)
-    got = flip(jnp.where(c == 0, second_total, first_total).astype(jnp.bfloat16), "core")
-    return ordered(c, keep, got.astype(jnp.float32), axis=1)
+def core_columns(matrices, core):
+    parts = []
+    for matrix in matrices:
+        cols = matrix.shape[1] // 2
+        parts.append(lax.dynamic_slice_in_dim(matrix, core * cols, cols, 1))
+    return jnp.concatenate(parts, axis=1) if len(parts) > 1 else parts[0]
+
+
+def start_gather(matrices):
+    c = lax.axis_index("core")
+    got = flip(core_columns(matrices, 1 - c), "core")
+    rows = ordered(c, core_columns(matrices, c), got)
+    return rows, flip(rows, "cy"), flip(rows, "dp")
+
+
+def next_gather(rows, rows_y, rows_x):
+    return rows, rows_y, rows_x, flip(rows_y[0], "dp"), flip(rows_x[1], "cy")
+
+
+def place_kernel(splits, *refs):
+    sources, outs = refs[:5], refs[5 : 5 + len(splits)]
+    held, sem_in, sem_out = refs[5 + len(splits) : -2], refs[-2], refs[-1]
+    x, y = lax.axis_index("dp"), lax.axis_index("cy")
+    loads = [
+        pltpu.make_async_copy(source, buffer, sem_in.at[i])
+        for i, (source, buffer) in enumerate(zip(sources, held))
+    ]
+    for load in loads:
+        load.start()
+    stores = []
+    for i, (load, buffer) in enumerate(zip(loads, held)):
+        load.wait()
+        begin = 0
+        for out, cols in zip(outs, splits):
+            at = pl.ds(begin, cols)
+            target = (
+                out.at[x, y],
+                out.at[x, 1 - y],
+                out.at[1 - x, y],
+                out.at[1 - x, 1 - y, 0],
+                out.at[1 - x, 1 - y, 1],
+            )[i]
+            piece = buffer.at[:, :, at] if i < 3 else buffer.at[:, at]
+            stores.append(pltpu.make_async_copy(piece, target, sem_out.at[len(stores)]))
+            stores[-1].start()
+            begin += cols
+    for store in stores:
+        store.wait()
+
+
+def end_gather(begun, splits):
+    rows = begun[0]
+    size = 8 * rows.shape[1] * rows.shape[2] * rows.dtype.itemsize
+    anywhere = pl.BlockSpec(memory_space=pl.ANY)
+    outs = pl.pallas_call(
+        functools.partial(place_kernel, splits),
+        out_shape=[
+            jax.ShapeDtypeStruct((2, 2, 2, rows.shape[1], cols), rows.dtype) for cols in splits
+        ],
+        in_specs=[anywhere] * 5,
+        out_specs=[anywhere] * len(splits),
+        scratch_shapes=[pltpu.VMEM(piece.shape, piece.dtype) for piece in begun]
+        + [pltpu.SemaphoreType.DMA((5,)), pltpu.SemaphoreType.DMA((5 * len(splits),))],
+        compiler_params=pltpu.CompilerParams(vmem_limit_bytes=size + (2 << 20)),
+        cost_estimate=pl.CostEstimate(flops=0, bytes_accessed=2 * size, transcendentals=0),
+        name="place_rows",
+    )(*begun)
+    return [out.reshape(-1, out.shape[-1]) for out in outs]
+
+
+def start_scatter(grad):
+    x, y = lax.axis_index("dp"), lax.axis_index("cy")
+    parts = grad.reshape(2, 2, 2, -1, grad.shape[-1])
+    far = pick(pick(parts, 1 - x), 1 - y)
+    return parts, flip(far[0], "dp"), flip(far[1], "cy")
+
+
+def next_scatter(parts, far_first, far_second):
+    x, y = lax.axis_index("dp"), lax.axis_index("cy")
+    low = parts.dtype
+    by_y, by_x = pick(pick(parts, x), 1 - y), pick(pick(parts, 1 - x), y)
+    by_y = jnp.stack([total(by_y[0], far_first).astype(low), by_y[1]])
+    by_x = jnp.stack([by_x[0], total(by_x[1], far_second).astype(low)])
+    return pick(pick(parts, x), y), flip(by_y, "cy"), flip(by_x, "dp")
+
+
+def end_scatter(own, from_y, from_x):
+    c = lax.axis_index("core")
+    sums = total(own, from_y, from_x)
+    keep = pick(sums, c)
+    got = flip(pick(sums, 1 - c).astype(jnp.bfloat16), "core").astype(jnp.float32)
+    return jnp.where(c == 0, keep, got), jnp.where(c == 0, got, keep)
 
 
 def gather_rows(local_rows):
@@ -505,18 +574,28 @@
     return lax.all_gather(local_rows, ("core", "seq"), axis=1, tiled=True).reshape(-1, width)
 
 
-def scatter_rows(partial_rows):
+def core_rows(left, right, dims):
     c = lax.axis_index("core")
-    parts = partial_rows.astype(jnp.bfloat16).reshape(2, 2, -1, partial_rows.shape[-1])
-    got = flip(pick(parts, 1 - c, 1), "core")
-    both = pick(parts, c, 1).astype(jnp.float32) + got.astype(jnp.float32)
-    return lax.psum_scatter(
-        both.astype(jnp.bfloat16), "seq", scatter_dimension=1, tiled=True
-    ).astype(jnp.float32)
+    parts = left.reshape(2, 2, -1, left.shape[-1])
+
+    def rows_of(core):
+        rows = dot(pick(parts, core, 1).reshape(-1, left.shape[-1]), right, dims)
+        return rows.astype(jnp.bfloat16).reshape(2, -1, rows.shape[-1])
+
+    away = rows_of(1 - c)
+    got = flip(away, "core")
+    kept = lax.optimization_barrier(rows_of(c))
+    return total(kept, got).astype(jnp.bfloat16)
+
+
+def scatter_rows(core_sums):
+    return lax.psum_scatter(core_sums, "seq", scatter_dimension=1, tiled=True).astype(jnp.float32)
 
 
 def dot(left, right, dims):
-    return lax.dot_general(left, right, ((dims[:1], dims[1:]), ((), ())), preferred_element_type=jnp.float32)
+    return lax.dot_general(
+        left, right, ((dims[:1], dims[1:]), ((), ())), preferred_element_type=jnp.float32
+    )
 
 
 def head_scores(queries, keys, visible):
@@ -540,36 +619,24 @@
     post_ffn_gain,
     cotangent,
 ):
-    width = inputs.shape[-1]
     c, cy = lax.axis_index("core"), lax.axis_index("cy")
     low = jnp.bfloat16
     rows_own = query_weight.shape[0]
-    kv_stack = jnp.stack([key_weight, value_weight], axis=1).reshape(-1, 2, KEY_VALUE_HEADS, HEAD_SIZE)
-    kv_rows = lax.all_to_all(
-        kv_stack.transpose(2, 0, 1, 3), "seq", split_axis=0, concat_axis=0, tiled=True
-    ).reshape(rows_own, 2, HEAD_SIZE)
-    attn_share = jnp.concatenate(
-        [
-            query_weight.reshape(rows_own, 2, HEAD_SIZE),
-            kv_rows,
-            output_weight.T.reshape(rows_own, 2, HEAD_SIZE),
-        ],
-        axis=2,
-    )
     ffn_cols = gate_weight.shape[1] // 2
-    gate_up_share = jnp.concatenate(
-        [gate_weight.reshape(rows_own, 2, ffn_cols), up_weight.reshape(rows_own, 2, ffn_cols)],
-        axis=2,
-    )
-    down_share = down_weight.T.reshape(rows_own, 2, ffn_cols)
+
+    x_local = trade_sequences(inputs)
+    block_x = gather_rows(x_local)
+    x_float = x_local.astype(jnp.float32)
+    kv_stack = jnp.stack([key_weight, value_weight], axis=1)
+    kv_stack = kv_stack.reshape(-1, 2, KEY_VALUE_HEADS, HEAD_SIZE).transpose(2, 0, 1, 3)
+    kv_rows = lax.all_to_all(kv_stack, "seq", split_axis=0, concat_axis=0, tiled=True)
     gain_table = jnp.stack([pre_attn_gain, post_attn_gain, pre_ffn_gain, post_ffn_gain], axis=0)
-    gain_full = lax.all_gather(gain_table, ("dp", "cy", "core"), axis=1, tiled=True).astype(jnp.float32)
-    gain_one, gain_two, gain_three, gain_four = gain_full[0], gain_full[1], gain_full[2], gain_full[3]
-
-    x_float = trade_sequences(inputs).astype(jnp.float32)
-    grad_top = trade_sequences(cotangent).astype(jnp.float32)
-    seq_pos = lax.all_gather(positions, ("cy", "core"), axis=1, tiled=True)
-    seq_pos = pick(seq_pos, cy)
+    gain_full = lax.all_gather(gain_table, ("dp", "cy", "core"), axis=1, tiled=True)
+    kv_rows = after(kv_rows.reshape(rows_own, 2 * HEAD_SIZE), gain_full)
+    gain_one, gain_two, gain_three, gain_four = gain_full.astype(jnp.float32)
+
+    pos_own = trade_sequences(positions)
+    seq_pos = ordered(c, pos_own, flip(pos_own, "core"), axis=1).reshape(-1)
     half = HEAD_SIZE // 2
     freq = BASE ** (-jnp.arange(half, dtype=jnp.float32) * 2.0 / HEAD_SIZE)
     angle = seq_pos.astype(jnp.float32)[:, None] * freq
@@ -577,16 +644,14 @@
     kv_cosine = jnp.where(c == 0, cosine, 1.0)
     kv_sine = jnp.where(c == 0, sine, 0.0)
 
-    attn_weight = gather_weight(attn_share)
-    in_weight = attn_weight[:, : 2 * HEAD_SIZE]
-    out_weight = attn_weight[:, 2 * HEAD_SIZE :]
-    gate_up_share, down_share, attn_weight_late = lax.optimization_barrier(
-        (gate_up_share, down_share, attn_weight[:8])
-    )
-    gate_up_weight = gather_weight(gate_up_share)
-    down_back = gather_weight(down_share)
-
-    block_one = gather_rows(norm_gain(x_float, gain_one).astype(low))
+    attn_begun = next_gather(*start_gather([query_weight, kv_rows, output_weight.T]))
+    in_weight, out_weight = end_gather(attn_begun, (2 * HEAD_SIZE, HEAD_SIZE))
+    down_begun = start_gather([after(down_weight.T, attn_begun)])
+    gate_up_begun = start_gather(after([gate_weight, up_weight], attn_begun))
+    cotangent = after(cotangent, attn_begun)
+    grad_top = trade_sequences(cotangent)
+
+    block_one = norm_gain(block_x.astype(jnp.float32), gain_one).astype(low)
     raw = dot(block_one, in_weight, (1, 0))
     queries = turn(raw[:, :HEAD_SIZE], cosine, sine).astype(low)
     kv_own = turn(raw[:, HEAD_SIZE:], kv_cosine, kv_sine).astype(low)
@@ -601,35 +666,50 @@
     row_sum = jnp.sum(exponent, axis=-1, keepdims=True)
     heads = dot((exponent / row_sum).astype(low), values, (1, 0)).astype(low)
     log_total = row_max + jnp.log(row_sum)
-
-    project = scatter_rows(dot(heads, out_weight, (1, 1)))
+    heads = after(heads, grad_top, down_begun)
+    grad_top = grad_top.astype(jnp.float32)
+
+    project_core = core_rows(heads, out_weight, (1, 1))
+    project = scatter_rows(project_core)
     middle = x_float + norm_gain(project, gain_two)
-    block_two = gather_rows(norm_gain(middle, gain_three).astype(low))
+    normed_two = norm_gain(middle, gain_three).astype(low)
+    normed_two = after(normed_two, gate_up_begun)
+    gate_up_begun = next_gather(*after(gate_up_begun, normed_two))
+    down_begun = next_gather(*after(down_begun, normed_two))
+    block_two = gather_rows(normed_two)
+    (gate_up_weight,) = end_gather(gate_up_begun, (2 * ffn_cols,))
+    (down_back,) = end_gather(down_begun, (ffn_cols,))
     gate_up = dot(block_two, gate_up_weight, (1, 0))
     gate, upper = gate_up[:, :ffn_cols], gate_up[:, ffn_cols:]
     hidden = geglu(gate, upper).astype(low)
-    feed = scatter_rows(dot(hidden, down_back, (1, 1)))
-    layer_output = trade_sequences((middle + norm_gain(feed, gain_four)).astype(low))
-
+    feed = scatter_rows(core_rows(hidden, down_back, (1, 1)))
     unused, pull_four = jax.vjp(norm_gain, feed, gain_four)
     grad_feed, grad_g_four = pull_four(grad_top)
-    grad_feed_rows = gather_rows(grad_feed.astype(low))
+    grad_feed = grad_feed.astype(low)
+    layer_output = after((middle + norm_gain(feed, gain_four)).astype(low), grad_feed)
+    layer_output = trade_sequences(layer_output)
+
+    grad_feed_rows = after(gather_rows(grad_feed), layer_output)
     grad_hidden = dot(grad_feed_rows, down_back, (1, 0))
     unused, pull_act = jax.vjp(geglu, gate, upper)
     grad_gate_act, grad_up_act = pull_act(grad_hidden)
     grad_gate_up = jnp.concatenate([grad_gate_act.astype(low), grad_up_act.astype(low)], axis=1)
-    grad_normed_two = scatter_rows(dot(grad_gate_up, gate_up_weight, (1, 1)))
-    grad_down = scatter_weight_grad(dot(grad_feed_rows, hidden, (0, 0)).astype(low))
-    grad_gu = scatter_weight_grad(dot(block_two, grad_gate_up, (0, 0)).astype(low))
+    normed_two_core = core_rows(grad_gate_up, gate_up_weight, (1, 1))
+    grad_normed_two = scatter_rows(normed_two_core)
+    hidden, block_two = after((hidden, block_two), normed_two_core)
+    grad_down_begun = start_scatter(dot(grad_feed_rows, hidden, (0, 0)).astype(low))
+    grad_gu_begun = start_scatter(dot(block_two, grad_gate_up, (0, 0)).astype(low))
 
     unused, pull_three = jax.vjp(norm_gain, middle, gain_three)
     grad_mid_norm, grad_g_three = pull_three(grad_normed_two)
     grad_middle = grad_top + grad_mid_norm
     unused, pull_two = jax.vjp(norm_gain, project, gain_two)
     grad_project, grad_g_two = pull_two(grad_middle)
-    grad_project_rows = gather_rows(grad_project.astype(low))
+    grad_project = grad_project.astype(low)
+    grad_down_begun = next_scatter(*after(grad_down_begun, grad_project))
+    grad_gu_begun = next_scatter(*after(grad_gu_begun, grad_project))
+    grad_project_rows = gather_rows(grad_project)
     grad_heads = dot(grad_project_rows, out_weight, (1, 0)).astype(low)
-    grad_output_part = dot(grad_project_rows, heads, (0, 0)).astype(low)
 
     bent, masked = head_scores(queries, keys, visible)
     probability = jnp.exp(masked - log_total)
@@ -644,43 +724,45 @@
     grad_key_raw = turn_back(grad_key_rot, cosine, sine).astype(low)
     kv_grad_own = jnp.where(c == 0, grad_key_raw, grad_value)
     kv_grad_got = flip(jnp.where(c == 0, grad_value, grad_key_raw), "core")
-    kv_grad = (kv_grad_own.astype(jnp.float32) + kv_grad_got.astype(jnp.float32)).astype(low)
-    grad_in = jnp.concatenate([grad_query_raw, kv_grad], axis=1)
-    grad_normed_one = scatter_rows(dot(grad_in, in_weight, (1, 1)))
+    grad_in = jnp.concatenate([grad_query_raw, total(kv_grad_own, kv_grad_got).astype(low)], axis=1)
+    normed_one_core = core_rows(grad_in, in_weight, (1, 1))
+    grad_normed_one = scatter_rows(normed_one_core)
+    block_one, heads = after((block_one, heads), normed_one_core)
     grad_in_part = dot(block_one, grad_in, (0, 0)).astype(low)
-    attn_grads = scatter_weight_grad(jnp.concatenate([grad_in_part, grad_output_part], axis=1))
+    grad_output_part = dot(grad_project_rows, heads, (0, 0)).astype(low)
+    attn_grad_begun = start_scatter(jnp.concatenate([grad_in_part, grad_output_part], axis=1))
+    attn_grad_begun = next_scatter(*attn_grad_begun)
+    grad_down = end_scatter(*after(grad_down_begun, normed_one_core))
+    grad_gu = end_scatter(*after(grad_gu_begun, normed_one_core))
+    attn_grads = end_scatter(*attn_grad_begun)
 
     unused, pull_one = jax.vjp(norm_gain, x_float, gain_one)
     grad_input_norm, grad_g_one = pull_one(grad_normed_one)
     input_grad = trade_sequences((grad_middle + grad_input_norm).astype(low))
     gain_grads = jnp.stack([grad_g_one, grad_g_two, grad_g_three, grad_g_four], axis=0)
     everyone = ("dp", "cy", "core", "seq")
-    device_count = lax.axis_size(everyone)
+    gain_parts = gain_grads.reshape(4, lax.axis_size(everyone), -1).transpose(1, 0, 2)
     gain_out = jnp.sum(
-        lax.all_to_all(
-            gain_grads.reshape(4, device_count, -1).transpose(1, 0, 2),
-            everyone,
-            split_axis=0,
-            concat_axis=0,
-            tiled=True,
-        ),
-        axis=0,
-    )
-    grad_query_out = attn_grads[:, :, :HEAD_SIZE].reshape(rows_own, 2 * HEAD_SIZE)
-    grad_output_out = attn_grads[:, :, 2 * HEAD_SIZE :].reshape(rows_own, 2 * HEAD_SIZE).T
-    kv_back = lax.all_to_all(
-        attn_grads[:, :, HEAD_SIZE : 2 * HEAD_SIZE].astype(low), "seq", split_axis=0, concat_axis=0, tiled=True
-    ).reshape(KEY_VALUE_HEADS, -1, 2, HEAD_SIZE).transpose(2, 1, 0, 3).reshape(2, -1, KEY_VALUE_HEADS * HEAD_SIZE).astype(jnp.float32)
+        lax.all_to_all(gain_parts, everyone, split_axis=0, concat_axis=0, tiled=True), axis=0
+    )
+
+    def whole(pair, begin, cols):
+        return jnp.concatenate([part[:, begin : begin + cols] for part in pair], axis=1)
+
+    kv_back = whole(attn_grads, HEAD_SIZE, HEAD_SIZE).astype(low)
+    kv_back = lax.all_to_all(kv_back, "seq", split_axis=0, concat_axis=0, tiled=True)
+    kv_back = kv_back.reshape(KEY_VALUE_HEADS, -1, 2, HEAD_SIZE).transpose(2, 1, 0, 3)
+    kv_back = kv_back.reshape(2, -1, KEY_VALUE_HEADS * HEAD_SIZE).astype(jnp.float32)
     return (
         layer_output,
         input_grad,
-        grad_query_out,
+        whole(attn_grads, 0, HEAD_SIZE),
         kv_back[0],
         kv_back[1],
-        grad_output_out,
-        grad_gu[:, :, :ffn_cols].reshape(rows_own, 2 * ffn_cols),
-        grad_gu[:, :, ffn_cols:].reshape(rows_own, 2 * ffn_cols),
-        grad_down.reshape(rows_own, 2 * ffn_cols).T,
+        whole(attn_grads, 2 * HEAD_SIZE, HEAD_SIZE).T,
+        whole(grad_gu, 0, ffn_cols),
+        whole(grad_gu, ffn_cols, ffn_cols),
+        whole(grad_down, 0, ffn_cols).T,
         gain_out[0],
         gain_out[1],
         gain_out[2],

time: 817 us -> 751 us (0.919)
  local copies, waits for them, and re-layouts: 101 us -> 72.7 us
  waiting for transfers between devices: 417 us -> 391 us
  blocking collectives: 29.6 us -> 9.01 us
    ppermute x40 -> x42, waiting for transfers between devices: 256 us -> 188 us  [flip(): return lax.ppermute(value, axis, [(0, 1), (1, 0)])]
    reduce_scatter x4, waiting for transfers between devices: 87 us -> 132 us  [scatter_rows(): lax.psum_scatter(core_sums, 'seq', scatter_dimension=1, tiled=True)]
    all_gather x1 -> x0, blocking collectives: 20.5 us -> none  [head_local(): seq_pos = lax.all_gather(positions, ('cy', 'core'), axis=1, tiled=True)]
    another operation x12 -> x2, other arithmetic: 13.6 us -> 0.12 us  [ordered(): jnp.stack([own, other], axis=axis)]
    unnamed x173 -> x208, local copies, waits for them, and re-layouts: 17.2 us -> 29.6 us
    slice x7 -> x8, local copies, waits for them, and re-layouts: 16.4 us -> 4.18 us  [the longest x2 3.72 us: next_scatter(): by_x = jnp.stack([by_x[0], total(by_x[1], far_second).astype(low)])]
    reshape x9 -> x1, local copies, waits for them, and re-layouts: 13 us -> 1.72 us  [core_rows(): parts = left.reshape(2, 2, -1, left.shape[-1])]
    all_gather x4, waiting for transfers between devices: 51.3 us -> 40.3 us  [gather_rows(): lax.all_gather(local_rows, ('core', 'seq'), axis=1, tiled=True)]
  transfers between devices with their start and end apart: 51 -> 53, of which waited for: 28 -> 28; matrix products, arithmetic and copies ran while one was open for 25% -> 24% of each run, Pallas kernels for 0% -> 1%
where the time goes in v2:
time: 751 us; the launch traced here: 746 us
  waiting for transfers between devices  391 us (52%)
  matrix products  106 us (14%)
  other arithmetic  95 us (13%)
  local copies, waits for them, and re-layouts  72.7 us (10%)
  starting transfers between devices  50 us (7%)
  between operations  16.1 us (2%)
  blocking collectives  9.01 us (1%)
    ppermute x42, waiting for transfers between devices, flip(): return lax.ppermute(value, axis, [(0, 1), (1, 0)])  188 us
    reduce_scatter x4, waiting for transfers between devices, scatter_rows(): lax.psum_scatter(core_sums, 'seq', scatter_dimension=1, tiled=True)  132 us
    dot_general x22, matrix products, dot(): lax.dot_general(left, right, ((dims[:1], dims[1:]), ((), ())), preferred_...  106 us
    all_gather x4, waiting for transfers between devices, gather_rows(): lax.all_gather(local_rows, ('core', 'seq'), axis=1, tiled=True)  40.3 us
    ppermute x42, starting transfers between devices, flip(): return lax.ppermute(value, axis, [(0, 1), (1, 0)])  36.6 us
    unnamed x208, local copies, waits for them, and re-layouts  29.6 us
    all_to_all x1, waiting for transfers between devices, head_local(): lax.all_to_all(kv_stack, 'seq', split_axis=0, concat_axis=0, tiled=True)  16.3 us
  transfers between devices with their start and end apart: 53, of which 28 were waited for; matrix products, arithmetic and copies ran while one was open for 24% of the time, Pallas kernels for 1%

profile of v2, /device:TPU:0, one launch (start us, length us, event | category | flops | bytes accessed | tf_op | source)
XLA Modules:
  0.0 745.5 jit_solution(9397329864049054968)
XLA Ops:
  8.4 3.0 collective-permute-start
  11.4 7.0 collective-permute-done
  21.5 5.1 all-to-all-start
  26.6 16.3 %all-to-all-done = bf16[4,72,2,256]{3,2,1,0:T(2,128)(2,1)S(1)} async-done(((bf16[4,72,2,256]{3,2,1,0:T(2,128)(2,1)}), bf16[4,72,2,256]{3,2,1,0:T(2,128)(2,1)S(1)}, u32[]{:S(2)}, u32[]{:S(2)}) %all-to-all-start) | async-done | bytes 294944 | tf_op jit(solution)/shard_map/all_to_all | solution.py:632
  44.9 9.0 %all-gather = bf16[8,288,4]{1,2,0:T(4,128)(2,1)S(1)} all-gather(bf16[1,288,4]{1,2,0:T(4,128)(2,1)S(1)} %maximum_bitcast_fusion.6), channel_id=1, replica_groups=mesh['dp'=2,'cy'=2,'core'=2,'seq'=4] {'dp','cy','core'}, dimensions={0}, use_global_device_ids=true | all-gather | bytes 20736 | tf_op jit(solution)/shard_map/all_gather | solution.py:634
  57.6 18.5 %collective-permute-done.4.refs_1_ = bf16[2,288,768]{2,1,0:T(8,128)(2,1)S(1)} collective-permute-done((bf16[2,288,768]{2,1,0:T(8,128)(2,1)S(1)}, bf16[2,288,768]{2,1,0:T(8,128)(2,1)S(1)}, u32[]{:S(2)}, u32[]{:S(2)}) %collective-permute-start.4) | collective-permute-done | bytes 884768 | tf_op jit(solution)/shard_map/ppermute | solution.py:449
  79.0 8.8 %collective-permute-done.6.refs_3_ = bf16[288,768]{1,0:T(8,128)(2,1)S(1)} collective-permute-done((bf16[288,768]{1,0:T(8,128)(2,1)S(1)}, bf16[288,768]{1,0:T(8,128)(2,1)S(1)}, u32[]{:S(2)}, u32[]{:S(2)}) %collective-permute-start.6) | collective-permute-done | bytes 442400 | tf_op jit(solution)/shard_map/ppermute | solution.py:449
  97.0 3.8 multiply_reduce_fusion
  103.1 2.6 fusion.111
  105.8 2.5 fusion.78
  116.4 25.4 %collective-permute-done.11.refs_1_ = bf16[2,288,1152]{2,1,0:T(8,128)(2,1)S(1)} collective-permute-done((bf16[2,288,1152]{2,1,0:T(8,128)(2,1)S(1)}, bf16[2,288,1152]{2,1,0:T(8,128)(2,1)S(1)}, u32[]{:S(2)}, u32[]{:S(2)}) %collective-permute-start.11) | collective-permute-done | bytes 1327136 | tf_op jit(solution)/shard_map/ppermute | solution.py:449
  144.1 3.7 collective-permute-done.13
  152.0 2.9 collective-permute-done.14
  157.5 38.5 %reduce-scatter.5.cloned.1.call-done = bf16[2,64,2304]{2,1,0:T(8,128)(2,1)} async-done(((bf16[2,256,2304]{2,1,0:T(8,128)(2,1)}), bf16[2,64,2304]{2,1,0:T(8,128)(2,1)}) %reduce-scatter.5.cloned.1.call-update) | async-done | bytes 589840 | tf_op jit(solution)/shard_map/reduce_scatter | solution.py:592
  199.3 2.4 multiply_convert_fusion.4
  201.7 13.5 %collective-permute-done.15.refs_1_ = bf16[2,288,2304]{2,1,0:T(8,128)(2,1)} collective-permute-done((bf16[2,288,2304]{2,1,0:T(8,128)(2,1)S(1)}, bf16[2,288,2304]{2,1,0:T(8,128)(2,1)}, u32[]{:S(2)}, u32[]{:S(2)}) %collective-permute-start.15) | collective-permute-done | bytes 2654240 | tf_op jit(solution)/shard_map/ppermute | solution.py:449
  223.7 38.5 %collective-permute-done.19.refs_3_ = bf16[288,1152]{1,0:T(8,128)(2,1)S(1)} collective-permute-done((bf16[288,1152]{1,0:T(8,128)(2,1)S(1)}, bf16[288,1152]{1,0:T(8,128)(2,1)S(1)}, u32[]{:S(2)}, u32[]{:S(2)}) %collective-permute-start.19) | collective-permute-done | bytes 663584 | tf_op jit(solution)/shard_map/ppermute | solution.py:449
  265.9 2.4 copy-done.1
  268.3 3.3 place_rows.4
  271.6 3.9 copy-done
  275.6 15.0 %fusion.112 = f32[1024,2304]{1,0:T(8,128)S(1)} fusion(bf16[1024,2304]{1,0:T(8,128)(2,1)} %bitcast.322, bf16[2304,2304]{1,0:T(8,128)(2,1)} %bitcast.248), kind=kOutput, calls=%fused_computation.311 | convolution fusion | flops 10871635968 | bytes 24772608 | tf_op jit(solution)/shard_map/dot_general | solution.py:596
  292.3 3.1 copy-done.28
  296.9 3.5 convolution_convert_fusion.2
  300.5 3.5 convolution_convert_fusion.3
  307.1 46.1 %reduce-scatter.7.cloned.1.call-done = bf16[2,64,2304]{2,1,0:T(8,128)(2,1)} async-done(((bf16[2,256,2304]{2,1,0:T(8,128)(2,1)}), bf16[2,64,2304]{2,1,0:T(8,128)(2,1)}) %reduce-scatter.7.cloned.1.call-update) | async-done | bytes 589840 | tf_op jit(solution)/shard_map/reduce_scatter | solution.py:592
  354.4 2.5 fusion.43
  356.9 3.0 fusion.44
  363.0 7.1 collective-permute-done.22
  371.0 40.3 %all-gather.10.cloned.1.call-done = bf16[2,512,2304]{2,1,0:T(8,128)(2,1)} async-done(((bf16[2,64,2304]{2,1,0:T(8,128)(2,1)}), bf16[2,512,2304]{2,1,0:T(8,128)(2,1)}) %all-gather.10.cloned.1.call-update) | async-done | bytes 4718608 | tf_op jit(solution)/shard_map/all_gather | solution.py:574
  411.3 15.0 %fusion.8 = (bf16[1024,1152]{1,0:T(8,128)(2,1)S(1)}, bf16[1024,1152]{1,0:T(8,128)(2,1)S(1)}) fusion(f32[1024,2304]{1,0:T(8,128)} %copy-done.28, bf16[1024,2304]{1,0:T(8,128)(2,1)} %bitcast.326, bf16[2304,1152]{1,0:T(8,128)(2,1)} %bitcast.253), kind=kOutput, calls=%fused_computation.16 | convolution fusion | flops 5464129536 | bytes 24182784 | tf_op jit(solution)/shard_map/dot_general | solution.py:596
  428.9 7.0 convolution_convert_fusion.7
  436.1 6.9 convolution_convert_fusion.8
  443.0 3.7 add_convert_fusion.1
  446.8 47.0 %reduce-scatter.9.cloned.1.call-done = bf16[2,64,2304]{2,1,0:T(8,128)(2,1)} async-done(((bf16[2,256,2304]{2,1,0:T(8,128)(2,1)}), bf16[2,64,2304]{2,1,0:T(8,128)(2,1)}) %reduce-scatter.9.cloned.1.call-update) | async-done | bytes 589840 | tf_op jit(solution)/shard_map/reduce_scatter | solution.py:592
  495.5 3.4 fusion.39
  498.9 2.8 fusion.45
  502.0 5.9 fusion.1
  509.9 13.9 %convolution_convert_fusion = bf16[2304,2304]{1,0:T(8,128)(2,1)S(1)} fusion(bf16[1024,2304]{1,0:T(8,128)(2,1)} %bitcast.323, bf16[1024,1152]{1,0:T(8,128)(2,1)} %copy-done.40, bf16[1024,1152]{1,0:T(8,128)(2,1)S(1)} %copy-done.39), kind=kOutput, calls=%fused_computation | convolution fusion | flops 10886381568 | bytes 20054016 | tf_op jit(solution)/shard_map/dot_general | solution.py:596
  527.3 9.7 %convolution_convert_fusion.1 = bf16[2304,1152]{1,0:T(8,128)(2,1)S(1)} fusion(bf16[1024,2304]{1,0:T(8,128)(2,1)} %bitcast.327, bf16[1024,1152]{1,0:T(8,128)(2,1)S(1)} %copy-done.30), kind=kOutput, calls=%fused_computation.1 | convolution fusion | flops 5438472192 | bytes 12386304 | tf_op jit(solution)/shard_map/dot_general | solution.py:596
  541.4 14.7 %collective-permute-done.32 = bf16[288,2304]{1,0:T(8,128)(2,1)S(1)} collective-permute-done((bf16[288,2304]{1,0:T(8,128)(2,1)S(1)}, bf16[288,2304]{1,0:T(8,128)(2,1)S(1)}, u32[]{:S(2)}, u32[]{:S(2)}) %collective-permute-start.32) | collective-permute-done | bytes 1327136 | tf_op jit(solution)/shard_map/ppermute | solution.py:449
  563.9 3.9 convolution_convert_fusion.12
  569.3 2.5 multiply_convert_fusion.3
  574.1 2.4 fusion.86
  580.7 2.5 dynamic-slice_bitcast_fusion.9
  586.0 5.2 constant_dynamic-slice_fusion.2
  591.2 3.5 copy.68
  594.7 3.9 convolution_convert_fusion.5
  609.2 2.6 dynamic-slice_bitcast_fusion.7
  611.7 3.4 dynamic-slice_bitcast_fusion
  615.2 3.5 copy.67
  618.6 2.5 convolution_convert_fusion.6
  621.1 3.6 add_convert_fusion
  625.8 3.9 convolution_convert_fusion.11
  629.7 5.8 convolution_convert_fusion.4
  637.5 6.0 copy.63
  647.6 9.7 %collective-permute-done.39 = bf16[2,288,1152]{2,1,0:T(8,128)(2,1)} collective-permute-done((bf16[2,288,1152]{2,1,0:T(8,128)(2,1)}, bf16[2,288,1152]{2,1,0:T(8,128)(2,1)}, u32[]{:S(2)}, u32[]{:S(2)}) %collective-permute-start.39) | collective-permute-done | bytes 1327136 | tf_op jit(solution)/shard_map/ppermute | solution.py:449
  657.4 12.0 %collective-permute-done.40 = bf16[2,288,1152]{2,1,0:T(8,128)(2,1)} collective-permute-done((bf16[2,288,1152]{2,1,0:T(8,128)(2,1)}, bf16[2,288,1152]{2,1,0:T(8,128)(2,1)}, u32[]{:S(2)}, u32[]{:S(2)}) %collective-permute-start.40) | collective-permute-done | bytes 1327136 | tf_op jit(solution)/shard_map/ppermute | solution.py:449
  671.7 3.7 convert_add_fusion
  681.2 17.6 %collective-permute-done.30 = bf16[2,288,768]{2,1,0:T(8,128)(2,1)S(1)} collective-permute-done((bf16[2,288,768]{2,1,0:T(8,128)(2,1)S(1)}, bf16[2,288,768]{2,1,0:T(8,128)(2,1)S(1)}, u32[]{:S(2)}, u32[]{:S(2)}) %collective-permute-start.30) | collective-permute-done | bytes 884768 | tf_op jit(solution)/shard_map/ppermute | solution.py:449
  704.8 3.5 all-to-all-start.1
  710.1 8.6 %all-to-all-done.1 = bf16[4,72,512]{2,1,0:T(8,128)(2,1)S(1)} async-done(((bf16[4,72,512]{2,1,0:T(8,128)(2,1)}), bf16[4,72,512]{2,1,0:T(8,128)(2,1)S(1)}, u32[]{:S(2)}, u32[]{:S(2)}) %all-to-all-start.1) | async-done | bytes 294944 | tf_op jit(solution)/shard_map/all_to_all | solution.py:753
  721.9 2.4 fusion.47
  725.7 3.8 all-to-all-start.2
  731.1 5.8 all-to-all-done.2
  (424 shorter events, 142.4 us)
Async XLA Ops:
  7.2 89.8 %all-gather.6.cloned.1.call-start = ((), (), s32[]{:S(2)}) async-start(), calls=%async_computation.7 | async-start | bytes 5308416 | tf_op jit(solution)/shard_map/all_gather | solution.py:574
  8.4 10.0 %collective-permute-start = (bf16[64,2304]{1,0:T(8,128)(2,1)S(1)}, bf16[64,2304]{1,0:T(8,128)(2,1)S(1)}, u32[]{:S(2)}, u32[]{:S(2)}) collective-permute-start(bf16[64,2304]{1,0:T(8,128)(2,1)S(1)} %get-tuple-element.156), channel_id=1, source_target_pairs={{0,8},{8,0},{1,9},{9,1},{2,10},{10,2},{3,11},{11,3},{4,12},{12,4},... | collective-permute-start | bytes 884744 | tf_op jit(solution)/shard_map/ppermute | solution.py:449
  21.5 21.4 %all-to-all-start = ((bf16[4,72,2,256]{3,2,1,0:T(2,128)(2,1)}), bf16[4,72,2,256]{3,2,1,0:T(2,128)(2,1)S(1)}, u32[]{:S(2)}, u32[]{:S(2)}) async-start(bf16[4,72,2,256]{3,2,1,0:T(2,128)(2,1)} %maximum_bitcast_fusion.4), calls=%async_computation | async-start | bytes 589824 | tf_op jit(solution)/shard_map/all_to_all | solution.py:632
  26.6 169.3 %reduce-scatter.5.cloned.1.call-start = ((), (), s32[]{:S(2)}) async-start(), calls=%async_computation.8 | async-start | bytes 2949120 | tf_op jit(solution)/shard_map/reduce_scatter | solution.py:592
  43.1 11.0 %collective-permute-start.3 = (bf16[288,768]{1,0:T(8,128)(2,1)S(1)}, bf16[288,768]{1,0:T(8,128)(2,1)S(1)}, u32[]{:S(2)}, u32[]{:S(2)}) collective-permute-start(bf16[288,768]{1,0:T(8,128)(2,1)S(1)} %pad_maximum_fusion.16), channel_id=1, source_target_pairs={{0,4},{4,0},{1,5},{5,1},{2,6},{6,2},{3,7},{7,3},{8,12},{12,8},{9,1... | collective-permute-start | bytes 1327112 | tf_op jit(solution)/shard_map/ppermute | solution.py:449
  43.2 14.3 %collective-permute-start.1 = (s32[256]{0:T(256)S(1)}, s32[256]{0:T(256)S(1)}, u32[]{:S(2)}, u32[]{:S(2)}) collective-permute-start(s32[256]{0:T(256)S(1)} %bitcast.321), channel_id=1, source_target_pairs={{0,8},{8,0},{1,9},{9,1},{2,10},{10,2},{3,11},{11,3},{4,12},{12,4},... | collective-permute-start | bytes 3080 | tf_op jit(solution)/shard_map/ppermute | solution.py:449
  54.2 21.9 %collective-permute-start.4 = (bf16[2,288,768]{2,1,0:T(8,128)(2,1)S(1)}, bf16[2,288,768]{2,1,0:T(8,128)(2,1)S(1)}, u32[]{:S(2)}, u32[]{:S(2)}) collective-permute-start(bf16[2,288,768]{2,1,0:T(8,128)(2,1)S(1)} %maximum_select_fusion.2.refs_0_), channel_id=1, source_target_pairs={{0,8},{8,0},{1,9},{9,1},{2,10},{10,2},{3,11},{11,3},{4,12},{12,4},... | collective-permute-start | bytes 2654216 | tf_op jit(solution)/shard_map/ppermute | solution.py:449
  54.8 22.0 %collective-permute-start.5 = (bf16[2,288,768]{2,1,0:T(8,128)(2,1)S(1)}, bf16[2,288,768]{2,1,0:T(8,128)(2,1)S(1)}, u32[]{:S(2)}, u32[]{:S(2)}) collective-permute-start(bf16[2,288,768]{2,1,0:T(8,128)(2,1)S(1)} %maximum_select_fusion.2.refs_0_), channel_id=1, source_target_pairs={{0,16},{16,0},{1,17},{17,1},{2,18},{18,2},{3,19},{19,3},{4,20},{20... | collective-permute-start | bytes 2654216 | tf_op jit(solution)/shard_map/ppermute | solution.py:449
  57.5 20.9 %collective-permute-start.2 = (s32[2,256]{1,0:T(2,128)S(1)}, s32[2,256]{1,0:T(2,128)S(1)}, u32[]{:S(2)}, u32[]{:S(2)}) collective-permute-start(s32[2,256]{1,0:T(2,128)S(1)} %add_select_fusion.2), channel_id=1, source_target_pairs={{0,4},{4,0},{1,5},{5,1},{2,6},{6,2},{3,7},{7,3},{8,12},{12,8},{9,1... | collective-permute-start | bytes 6152 | tf_op jit(solution)/shard_map/ppermute | solution.py:449
  76.2 11.7 %collective-permute-start.6 = (bf16[288,768]{1,0:T(8,128)(2,1)S(1)}, bf16[288,768]{1,0:T(8,128)(2,1)S(1)}, u32[]{:S(2)}, u32[]{:S(2)}) collective-permute-start(bf16[288,768]{1,0:T(8,128)(2,1)S(1)} %slice_bitcast_fusion.5), channel_id=1, source_target_pairs={{0,16},{16,0},{1,17},{17,1},{2,18},{18,2},{3,19},{19,3},{4,20},{20... | collective-permute-start | bytes 1327112 | tf_op jit(solution)/shard_map/ppermute | solution.py:449
  76.8 11.4 %collective-permute-start.7 = (bf16[288,768]{1,0:T(8,128)(2,1)S(1)}, bf16[288,768]{1,0:T(8,128)(2,1)S(1)}, u32[]{:S(2)}, u32[]{:S(2)}) collective-permute-start(bf16[288,768]{1,0:T(8,128)(2,1)S(1)} %slice_bitcast_fusion.4), channel_id=1, source_target_pairs={{0,8},{8,0},{1,9},{9,1},{2,10},{10,2},{3,11},{11,3},{4,12},{12,4},... | collective-permute-start | bytes 1327112 | tf_op jit(solution)/shard_map/ppermute | solution.py:449
  90.1 18.8 %collective-permute-start.9 = (bf16[64,2304]{1,0:T(8,128)(2,1)}, bf16[64,2304]{1,0:T(8,128)(2,1)}, u32[]{:S(2)}, u32[]{:S(2)}) collective-permute-start(bf16[64,2304]{1,0:T(8,128)(2,1)} %get-tuple-element.154), channel_id=1, source_target_pairs={{0,8},{8,0},{1,9},{9,1},{2,10},{10,2},{3,11},{11,3},{4,12},{12,4},... | collective-permute-start | bytes 884744 | tf_op jit(solution)/shard_map/ppermute | solution.py:449
  92.8 16.1 %collective-permute-start.10 = (bf16[288,1152]{1,0:T(8,128)(2,1)}, bf16[288,1152]{1,0:T(8,128)(2,1)}, u32[]{:S(2)}, u32[]{:S(2)}) collective-permute-start(bf16[288,1152]{1,0:T(8,128)(2,1)} %get-tuple-element.134), channel_id=1, source_target_pairs={{0,4},{4,0},{1,5},{5,1},{2,6},{6,2},{3,7},{7,3},{8,12},{12,8},{9,1... | collective-permute-start | bytes 1990664 | tf_op jit(solution)/shard_map/ppermute | solution.py:449
  97.0 46.3 %copy-start.5 = (bf16[2,2,2,288,256]{4,3,2,1,0:T(8,128)(2,1)}, bf16[2,2,2,288,256]{4,3,2,1,0:T(8,128)(2,1)S(1)}, u32[]{:S(2)}) copy-start(bf16[2,2,2,288,256]{4,3,2,1,0:T(8,128)(2,1)S(1)} %get-tuple-element.51) | copy-start | bytes 3538948
  108.3 4.3 collective-permute-start.8
  110.5 31.3 %collective-permute-start.11 = (bf16[2,288,1152]{2,1,0:T(8,128)(2,1)S(1)}, bf16[2,288,1152]{2,1,0:T(8,128)(2,1)S(1)}, u32[]{:S(2)}, u32[]{:S(2)}) collective-permute-start(bf16[2,288,1152]{2,1,0:T(8,128)(2,1)S(1)} %maximum_select_fusion.1.refs_0_), channel_id=1, source_target_pairs={{0,8},{8,0},{1,9},{9,1},{2,10},{10,2},{3,11},{11,3},{4,12},{12,4},... | collective-permute-start | bytes 3981320 | tf_op jit(solution)/shard_map/ppermute | solution.py:449
  111.1 31.0 %collective-permute-start.12 = (bf16[2,288,1152]{2,1,0:T(8,128)(2,1)S(1)}, bf16[2,288,1152]{2,1,0:T(8,128)(2,1)S(1)}, u32[]{:S(2)}, u32[]{:S(2)}) collective-permute-start(bf16[2,288,1152]{2,1,0:T(8,128)(2,1)S(1)} %maximum_select_fusion.1.refs_0_), channel_id=1, source_target_pairs={{0,16},{16,0},{1,17},{17,1},{2,18},{18,2},{3,19},{19,3},{4,20},{20... | collective-permute-start | bytes 3981320 | tf_op jit(solution)/shard_map/ppermute | solution.py:449
  143.3 4.5 collective-permute-start.13
  149.8 125.7 %all-gather.8.cloned.1.call-start = ((), (), s32[]{:S(2)}) async-start(), calls=%async_computation.9 | async-start | bytes 5308416 | tf_op jit(solution)/shard_map/all_gather | solution.py:574
  151.8 3.1 collective-permute-start.14
  155.4 59.8 %collective-permute-start.15 = (bf16[2,288,2304]{2,1,0:T(8,128)(2,1)S(1)}, bf16[2,288,2304]{2,1,0:T(8,128)(2,1)}, u32[]{:S(2)}, u32[]{:S(2)}) collective-permute-start(bf16[2,288,2304]{2,1,0:T(8,128)(2,1)S(1)} %maximum_select_fusion.refs_0_), channel_id=1, source_target_pairs={{0,8},{8,0},{1,9},{9,1},{2,10},{10,2},{3,11},{11,3},{4,12},{12,4},... | collective-permute-start | bytes 7962632 | tf_op jit(solution)/shard_map/ppermute | solution.py:449
  156.8 59.4 %collective-permute-start.16 = (bf16[2,288,2304]{2,1,0:T(8,128)(2,1)S(1)}, bf16[2,288,2304]{2,1,0:T(8,128)(2,1)}, u32[]{:S(2)}, u32[]{:S(2)}) collective-permute-start(bf16[2,288,2304]{2,1,0:T(8,128)(2,1)S(1)} %maximum_select_fusion.refs_0_), channel_id=1, source_target_pairs={{0,16},{16,0},{1,17},{17,1},{2,18},{18,2},{3,19},{19,3},{4,20},{20... | collective-permute-start | bytes 7962632 | tf_op jit(solution)/shard_map/ppermute | solution.py:449
  216.2 136.9 %reduce-scatter.7.cloned.1.call-start = ((), (), s32[]{:S(2)}) async-start(), calls=%async_computation.10 | async-start | bytes 2949120 | tf_op jit(solution)/shard_map/reduce_scatter | solution.py:592
  217.8 46.4 %copy-start.4 = (bf16[2,288,1152]{2,1,0:T(8,128)(2,1)S(1)}, bf16[2,288,1152]{2,1,0:T(8,128)(2,1)}, u32[]{:S(2)}) copy-start(bf16[2,288,1152]{2,1,0:T(8,128)(2,1)} %copy-done.3) | copy-start | bytes 3981316
  217.8 50.5 %collective-permute-start.17 = (bf16[288,2304]{1,0:T(8,128)(2,1)S(1)}, bf16[288,2304]{1,0:T(8,128)(2,1)S(1)}, u32[]{:S(2)}, u32[]{:S(2)}) collective-permute-start(bf16[288,2304]{1,0:T(8,128)(2,1)S(1)} %slice_bitcast_fusion.1), channel_id=1, source_target_pairs={{0,16},{16,0},{1,17},{17,1},{2,18},{18,2},{3,19},{19,3},{4,20},{20... | collective-permute-start | bytes 3981320 | tf_op jit(solution)/shard_map/ppermute | solution.py:449
  220.0 48.3 %collective-permute-start.18 = (bf16[288,2304]{1,0:T(8,128)(2,1)S(1)}, bf16[288,2304]{1,0:T(8,128)(2,1)S(1)}, u32[]{:S(2)}, u32[]{:S(2)}) collective-permute-start(bf16[288,2304]{1,0:T(8,128)(2,1)S(1)} %slice_bitcast_fusion), channel_id=1, source_target_pairs={{0,8},{8,0},{1,9},{9,1},{2,10},{10,2},{3,11},{11,3},{4,12},{12,4},... | collective-permute-start | bytes 3981320 | tf_op jit(solution)/shard_map/ppermute | solution.py:449
  221.5 40.7 %collective-permute-start.19 = (bf16[288,1152]{1,0:T(8,128)(2,1)S(1)}, bf16[288,1152]{1,0:T(8,128)(2,1)S(1)}, u32[]{:S(2)}, u32[]{:S(2)}) collective-permute-start(bf16[288,1152]{1,0:T(8,128)(2,1)S(1)} %slice_bitcast_fusion.3), channel_id=1, source_target_pairs={{0,16},{16,0},{1,17},{17,1},{2,18},{18,2},{3,19},{19,3},{4,20},{20... | collective-permute-start | bytes 1990664 | tf_op jit(solution)/shard_map/ppermute | solution.py:449
  222.3 42.0 %collective-permute-start.20 = (bf16[288,1152]{1,0:T(8,128)(2,1)S(1)}, bf16[288,1152]{1,0:T(8,128)(2,1)S(1)}, u32[]{:S(2)}, u32[]{:S(2)}) collective-permute-start(bf16[288,1152]{1,0:T(8,128)(2,1)S(1)} %slice_bitcast_fusion.2), channel_id=1, source_target_pairs={{0,8},{8,0},{1,9},{9,1},{2,10},{10,2},{3,11},{11,3},{4,12},{12,4},... | collective-permute-start | bytes 1990664 | tf_op jit(solution)/shard_map/ppermute | solution.py:449
  300.4 4.6 collective-permute-start.21
  307.0 47.4 %copy-start.23 = (bf16[1,64,2304]{2,1,0:T(8,128)(2,1)S(1)}, bf16[1,64,2304]{2,1,0:T(8,128)(2,1)}, u32[]{:S(2)}) copy-start(bf16[1,64,2304]{2,1,0:T(8,128)(2,1)} %get-tuple-element.153) | copy-start | bytes 884740
  307.0 47.4 %copy-start.67 = (f32[2304]{0:T(1024)S(1)}, f32[2304]{0:T(1024)}, u32[]{:S(2)}) copy-start(f32[2304]{0:T(1024)} %get-tuple-element.87) | copy-start | bytes 27652
  307.0 49.9 %copy-start.17 = (bf16[2,64,2304]{2,1,0:T(8,128)(2,1)S(1)}, bf16[2,64,2304]{2,1,0:T(8,128)(2,1)}, u32[]{:S(2)}) copy-start(bf16[2,64,2304]{2,1,0:T(8,128)(2,1)} %reduce-scatter.5.cloned.1.call-done) | copy-start | bytes 1769476
  307.0 104.3 %all-gather.10.cloned.1.call-start = ((), (), s32[]{:S(2)}) async-start(), calls=%async_computation.11 | async-start | bytes 5308416 | tf_op jit(solution)/shard_map/all_gather | solution.py:574
  359.9 133.8 %reduce-scatter.9.cloned.1.call-start = ((), (), s32[]{:S(2)}) async-start(), calls=%async_computation.12 | async-start | bytes 2949120 | tf_op jit(solution)/shard_map/reduce_scatter | solution.py:592
  360.2 68.7 %slice-start = ((s8[10616832]{0:T(1024)(128)(4,1)}), s8[2228224]{0:T(1024)(128)(4,1)S(1)}, s32[]{:S(2)}) async-start(s8[10616832]{0:T(1024)(128)(4,1)} %bitcast.249), calls=%async_computation.15 | async-start | bytes 4456448
  361.4 8.7 %collective-permute-start.22 = (bf16[64,2304]{1,0:T(8,128)(2,1)S(1)}, bf16[64,2304]{1,0:T(8,128)(2,1)S(1)}, u32[]{:S(2)}, u32[]{:S(2)}) collective-permute-start(bf16[64,2304]{1,0:T(8,128)(2,1)S(1)} %get-tuple-element.152), channel_id=1, source_target_pairs={{0,8},{8,0},{1,9},{9,1},{2,10},{10,2},{3,11},{11,3},{4,12},{12,4},... | collective-permute-start | bytes 884744 | tf_op jit(solution)/shard_map/ppermute | solution.py:449
  435.8 7.2 collective-permute-start.23
  446.7 47.1 %copy-start.57 = (f32[2304]{0:T(1024)S(1)}, f32[2304]{0:T(1024)}, u32[]{:S(2)}) copy-start(f32[2304]{0:T(1024)} %get-tuple-element.88) | copy-start | bytes 27652
  446.7 48.8 %copy-start.87 = (f32[2,64]{1,0:T(2,128)S(1)}, f32[2,64]{1,0:T(2,128)}, u32[]{:S(2)}) copy-start(f32[2,64]{1,0:T(2,128)} %copy-done.86) | copy-start | bytes 1540
  446.7 48.8 %copy-start.24 = (bf16[1,64,2304]{2,1,0:T(8,128)(2,1)S(1)}, bf16[1,64,2304]{2,1,0:T(8,128)(2,1)}, u32[]{:S(2)}) copy-start(bf16[1,64,2304]{2,1,0:T(8,128)(2,1)} %get-tuple-element.153) | copy-start | bytes 884740
  446.7 48.8 %copy-start.76 = (f32[2,64]{1,0:T(2,128)S(1)}, f32[2,64]{1,0:T(2,128)}, u32[]{:S(2)}) copy-start(f32[2,64]{1,0:T(2,128)} %copy-done.75) | copy-start | bytes 1540
  446.7 52.2 %copy-start.85 = (f32[2,64]{1,0:T(2,128)S(1)}, f32[2,64]{1,0:T(2,128)}, u32[]{:S(2)}) copy-start(f32[2,64]{1,0:T(2,128)} %copy-done.84) | copy-start | bytes 1540
  446.7 117.1 %all-gather.12.cloned.1.call-start = ((), (), s32[]{:S(2)}) async-start(), calls=%async_computation.13 | async-start | bytes 5308416 | tf_op jit(solution)/shard_map/all_gather | solution.py:574
  501.7 217.8 %reduce-scatter.11.cloned.1.call-start = ((), (), s32[]{:S(2)}) async-start(), calls=%async_computation.14 | async-start | bytes 2949120 | tf_op jit(solution)/shard_map/reduce_scatter | solution.py:592
  524.0 32.1 %collective-permute-start.32 = (bf16[288,2304]{1,0:T(8,128)(2,1)S(1)}, bf16[288,2304]{1,0:T(8,128)(2,1)S(1)}, u32[]{:S(2)}, u32[]{:S(2)}) collective-permute-start(bf16[288,2304]{1,0:T(8,128)(2,1)S(1)} %get-tuple-element.98), channel_id=1, source_target_pairs={{0,16},{16,0},{1,17},{17,1},{2,18},{18,2},{3,19},{19,3},{4,20},{20... | collective-permute-start | bytes 3981320 | tf_op jit(solution)/shard_map/ppermute | solution.py:449
  525.7 32.0 %collective-permute-start.33 = (bf16[288,2304]{1,0:T(8,128)(2,1)S(1)}, bf16[288,2304]{1,0:T(8,128)(2,1)S(1)}, u32[]{:S(2)}, u32[]{:S(2)}) collective-permute-start(bf16[288,2304]{1,0:T(8,128)(2,1)S(1)} %get-tuple-element.97), channel_id=1, source_target_pairs={{0,8},{8,0},{1,9},{9,1},{2,10},{10,2},{3,11},{11,3},{4,12},{12,4},... | collective-permute-start | bytes 3981320 | tf_op jit(solution)/shard_map/ppermute | solution.py:449
  538.4 42.4 %collective-permute-start.37 = (bf16[288,1152]{1,0:T(8,128)(2,1)}, bf16[288,1152]{1,0:T(8,128)(2,1)}, u32[]{:S(2)}, u32[]{:S(2)}) collective-permute-start(bf16[288,1152]{1,0:T(8,128)(2,1)} %get-tuple-element.106), channel_id=1, source_target_pairs={{0,16},{16,0},{1,17},{17,1},{2,18},{18,2},{3,19},{19,3},{4,20},{20... | collective-permute-start | bytes 1990664 | tf_op jit(solution)/shard_map/ppermute | solution.py:449
  539.9 40.8 %collective-permute-start.38 = (bf16[288,1152]{1,0:T(8,128)(2,1)}, bf16[288,1152]{1,0:T(8,128)(2,1)}, u32[]{:S(2)}, u32[]{:S(2)}) collective-permute-start(bf16[288,1152]{1,0:T(8,128)(2,1)} %get-tuple-element.105), channel_id=1, source_target_pairs={{0,8},{8,0},{1,9},{9,1},{2,10},{10,2},{3,11},{11,3},{4,12},{12,4},... | collective-permute-start | bytes 1990664 | tf_op jit(solution)/shard_map/ppermute | solution.py:449
  562.4 83.7 %collective-permute-start.34 = (bf16[2,288,2304]{2,1,0:T(8,128)(2,1)}, bf16[2,288,2304]{2,1,0:T(8,128)(2,1)}, u32[]{:S(2)}, u32[]{:S(2)}) collective-permute-start(bf16[2,288,2304]{2,1,0:T(8,128)(2,1)} %pad_maximum_fusion.2), channel_id=1, source_target_pairs={{0,8},{8,0},{1,9},{9,1},{2,10},{10,2},{3,11},{11,3},{4,12},{12,4},... | collective-permute-start | bytes 7962632 | tf_op jit(solution)/shard_map/ppermute | solution.py:449
  577.8 5.4 collective-permute-start.24
  580.2 67.5 %collective-permute-start.35 = (bf16[2,288,2304]{2,1,0:T(8,128)(2,1)}, bf16[2,288,2304]{2,1,0:T(8,128)(2,1)}, u32[]{:S(2)}, u32[]{:S(2)}) collective-permute-start(bf16[2,288,2304]{2,1,0:T(8,128)(2,1)} %pad_maximum_fusion.3), channel_id=1, source_target_pairs={{0,16},{16,0},{1,17},{17,1},{2,18},{18,2},{3,19},{19,3},{4,20},{20... | collective-permute-start | bytes 7962632 | tf_op jit(solution)/shard_map/ppermute | solution.py:449
  598.6 22.5 %collective-permute-start.25 = (bf16[2,256,2304]{2,1,0:T(8,128)(2,1)}, bf16[2,256,2304]{2,1,0:T(8,128)(2,1)}, u32[]{:S(2)}, u32[]{:S(2)}) collective-permute-start(bf16[2,256,2304]{2,1,0:T(8,128)(2,1)} %bitcast.56), channel_id=1, source_target_pairs={{0,4},{4,0},{1,5},{5,1},{2,6},{6,2},{3,7},{7,3},{8,12},{12,8},{9,1... | collective-permute-start | bytes 7077896 | tf_op jit(solution)/shard_map/ppermute | solution.py:449
  601.9 55.4 %collective-permute-start.39 = (bf16[2,288,1152]{2,1,0:T(8,128)(2,1)}, bf16[2,288,1152]{2,1,0:T(8,128)(2,1)}, u32[]{:S(2)}, u32[]{:S(2)}) collective-permute-start(bf16[2,288,1152]{2,1,0:T(8,128)(2,1)} %pad_maximum_fusion.7), channel_id=1, source_target_pairs={{0,8},{8,0},{1,9},{9,1},{2,10},{10,2},{3,11},{11,3},{4,12},{12,4},... | collective-permute-start | bytes 3981320 | tf_op jit(solution)/shard_map/ppermute | solution.py:449
  603.6 65.8 %collective-permute-start.40 = (bf16[2,288,1152]{2,1,0:T(8,128)(2,1)}, bf16[2,288,1152]{2,1,0:T(8,128)(2,1)}, u32[]{:S(2)}, u32[]{:S(2)}) collective-permute-start(bf16[2,288,1152]{2,1,0:T(8,128)(2,1)} %pad_maximum_fusion.8), channel_id=1, source_target_pairs={{0,16},{16,0},{1,17},{17,1},{2,18},{18,2},{3,19},{19,3},{4,20},{20... | collective-permute-start | bytes 3981320 | tf_op jit(solution)/shard_map/ppermute | solution.py:449
  645.2 32.6 %collective-permute-start.27 = (bf16[288,768]{1,0:T(8,128)(2,1)S(1)}, bf16[288,768]{1,0:T(8,128)(2,1)S(1)}, u32[]{:S(2)}, u32[]{:S(2)}) collective-permute-start(bf16[288,768]{1,0:T(8,128)(2,1)S(1)} %get-tuple-element.111), channel_id=1, source_target_pairs={{0,16},{16,0},{1,17},{17,1},{2,18},{18,2},{3,19},{19,3},{4,20},{20... | collective-permute-start | bytes 1327112 | tf_op jit(solution)/shard_map/ppermute | solution.py:449
  646.0 31.7 %collective-permute-start.29 = (bf16[288,768]{1,0:T(8,128)(2,1)S(1)}, bf16[288,768]{1,0:T(8,128)(2,1)S(1)}, u32[]{:S(2)}, u32[]{:S(2)}) collective-permute-start(bf16[288,768]{1,0:T(8,128)(2,1)S(1)} %get-tuple-element.113), channel_id=1, source_target_pairs={{0,8},{8,0},{1,9},{9,1},{2,10},{10,2},{3,11},{11,3},{4,12},{12,4},... | collective-permute-start | bytes 1327112 | tf_op jit(solution)/shard_map/ppermute | solution.py:449
  671.6 7.7 %collective-permute-start.41 = (bf16[288,1152]{1,0:T(8,128)(2,1)S(1)}, bf16[288,1152]{1,0:T(8,128)(2,1)S(1)}, u32[]{:S(2)}, u32[]{:S(2)}) collective-permute-start(bf16[288,1152]{1,0:T(8,128)(2,1)S(1)} %fusion.74), channel_id=1, source_target_pairs={{0,4},{4,0},{1,5},{5,1},{2,6},{6,2},{3,7},{7,3},{8,12},{12,8},{9,1... | collective-permute-start | bytes 1990664 | tf_op jit(solution)/shard_map/ppermute | solution.py:449
  675.6 24.1 %collective-permute-start.36 = (bf16[288,2304]{1,0:T(8,128)(2,1)S(1)}, bf16[288,2304]{1,0:T(8,128)(2,1)S(1)}, u32[]{:S(2)}, u32[]{:S(2)}) collective-permute-start(bf16[288,2304]{1,0:T(8,128)(2,1)S(1)} %fusion.26), channel_id=1, source_target_pairs={{0,4},{4,0},{1,5},{5,1},{2,6},{6,2},{3,7},{7,3},{8,12},{12,8},{9,1... | collective-permute-start | bytes 3981320 | tf_op jit(solution)/shard_map/ppermute | solution.py:449
  678.1 20.7 %collective-permute-start.30 = (bf16[2,288,768]{2,1,0:T(8,128)(2,1)S(1)}, bf16[2,288,768]{2,1,0:T(8,128)(2,1)S(1)}, u32[]{:S(2)}, u32[]{:S(2)}) collective-permute-start(bf16[2,288,768]{2,1,0:T(8,128)(2,1)S(1)} %pad_maximum_fusion.11), channel_id=1, source_target_pairs={{0,16},{16,0},{1,17},{17,1},{2,18},{18,2},{3,19},{19,3},{4,20},{20... | collective-permute-start | bytes 2654216 | tf_op jit(solution)/shard_map/ppermute | solution.py:449
  678.8 20.5 %collective-permute-start.28 = (bf16[2,288,768]{2,1,0:T(8,128)(2,1)S(1)}, bf16[2,288,768]{2,1,0:T(8,128)(2,1)S(1)}, u32[]{:S(2)}, u32[]{:S(2)}) collective-permute-start(bf16[2,288,768]{2,1,0:T(8,128)(2,1)S(1)} %pad_maximum_fusion.10), channel_id=1, source_target_pairs={{0,8},{8,0},{1,9},{9,1},{2,10},{10,2},{3,11},{11,3},{4,12},{12,4},... | collective-permute-start | bytes 2654216 | tf_op jit(solution)/shard_map/ppermute | solution.py:449
  699.6 4.2 collective-permute-start.31
  704.8 13.9 %all-to-all-start.1 = ((bf16[4,72,512]{2,1,0:T(8,128)(2,1)}), bf16[4,72,512]{2,1,0:T(8,128)(2,1)S(1)}, u32[]{:S(2)}, u32[]{:S(2)}) async-start(bf16[4,72,512]{2,1,0:T(8,128)(2,1)} %pad_maximum_fusion.19), calls=%async_computation.5 | async-start | bytes 589824 | tf_op jit(solution)/shard_map/all_to_all | solution.py:753
  724.4 13.2 %collective-permute-start.26 = (bf16[64,2304]{1,0:T(8,128)(2,1)S(1)}, bf16[64,2304]{1,0:T(8,128)(2,1)S(1)}, u32[]{:S(2)}, u32[]{:S(2)}) collective-permute-start(bf16[64,2304]{1,0:T(8,128)(2,1)S(1)} %get-tuple-element.150), channel_id=1, source_target_pairs={{0,8},{8,0},{1,9},{9,1},{2,10},{10,2},{3,11},{11,3},{4,12},{12,4},... | collective-permute-start | bytes 884744 | tf_op jit(solution)/shard_map/ppermute | solution.py:449
  725.7 11.3 %all-to-all-start.2 = ((f32[32,4,72]{2,1,0:T(4,128)}), f32[32,4,72]{2,1,0:T(4,128)S(1)}, u32[]{:S(2)}, u32[]{:S(2)}) async-start(f32[32,4,72]{2,1,0:T(4,128)} %maximum_bitcast_fusion.5), calls=%async_computation.6 | async-start | bytes 131072 | tf_op jit(solution)/shard_map/all_to_all | solution.py:746
  (89 other events, 768.1 us)
Sparse Core Ops, SparseCore 0:
  19.5 55.6 all-gather.5
  149.9 45.9 reduce-scatter.4
  216.3 49.5 all-gather.7
  307.1 45.9 reduce-scatter.6
  360.1 51.1 all-gather.9
  446.8 46.8 reduce-scatter.8
  501.8 51.1 all-gather.11
  624.9 46.9 reduce-scatter.10

commit v3 on v2

--- a/solution.py
+++ b/solution.py
@@ -477,13 +477,13 @@
 
 def core_columns(matrices, core):
     parts = []
-    for matrix in matrices:
-        cols = matrix.shape[1] // 2
-        parts.append(lax.dynamic_slice_in_dim(matrix, core * cols, cols, 1))
+    for matrix, begin, width in matrices:
+        at = core * (matrix.shape[1] // 2) + begin
+        parts.append(lax.dynamic_slice_in_dim(matrix, at, width, 1))
     return jnp.concatenate(parts, axis=1) if len(parts) > 1 else parts[0]
 
 
-def start_gather(matrices):
+def start_gather(*matrices):
     c = lax.axis_index("core")
     got = flip(core_columns(matrices, 1 - c), "core")
     rows = ordered(c, core_columns(matrices, c), got)
@@ -494,9 +494,9 @@
     return rows, rows_y, rows_x, flip(rows_y[0], "dp"), flip(rows_x[1], "cy")
 
 
-def place_kernel(splits, *refs):
-    sources, outs = refs[:5], refs[5 : 5 + len(splits)]
-    held, sem_in, sem_out = refs[5 + len(splits) : -2], refs[-2], refs[-1]
+def place_kernel(moves, count, *refs):
+    sources, outs = refs[:count], refs[count : len(refs) - count - 2]
+    held, sem_in, sem_out = refs[-count - 2 : -2], refs[-2], refs[-1]
     x, y = lax.axis_index("dp"), lax.axis_index("cy")
     loads = [
         pltpu.make_async_copy(source, buffer, sem_in.at[i])
@@ -507,89 +507,171 @@
     stores = []
     for i, (load, buffer) in enumerate(zip(loads, held)):
         load.wait()
-        begin = 0
-        for out, cols in zip(outs, splits):
+        for out, begin, to, cols in moves[i // 5]:
+            out, to = outs[out], pl.ds(to, cols)
+            target = (
+                out.at[x, y, :, :, to],
+                out.at[x, 1 - y, :, :, to],
+                out.at[1 - x, y, :, :, to],
+                out.at[1 - x, 1 - y, 0, :, to],
+                out.at[1 - x, 1 - y, 1, :, to],
+            )[i % 5]
             at = pl.ds(begin, cols)
-            target = (
-                out.at[x, y],
-                out.at[x, 1 - y],
-                out.at[1 - x, y],
-                out.at[1 - x, 1 - y, 0],
-                out.at[1 - x, 1 - y, 1],
-            )[i]
-            piece = buffer.at[:, :, at] if i < 3 else buffer.at[:, at]
+            piece = buffer.at[:, :, at] if i % 5 < 3 else buffer.at[:, at]
             stores.append(pltpu.make_async_copy(piece, target, sem_out.at[len(stores)]))
             stores[-1].start()
-            begin += cols
     for store in stores:
         store.wait()
 
 
-def end_gather(begun, splits):
-    rows = begun[0]
-    size = 8 * rows.shape[1] * rows.shape[2] * rows.dtype.itemsize
+def end_gather(gathers, moves, widths):
+    pieces = [piece for begun in gathers for piece in begun]
+    rows, low = pieces[0].shape[1], pieces[0].dtype
+    size = 8 * rows * sum(widths) * low.itemsize
     anywhere = pl.BlockSpec(memory_space=pl.ANY)
+    stores = 5 * sum(len(some) for some in moves)
     outs = pl.pallas_call(
-        functools.partial(place_kernel, splits),
-        out_shape=[
-            jax.ShapeDtypeStruct((2, 2, 2, rows.shape[1], cols), rows.dtype) for cols in splits
-        ],
-        in_specs=[anywhere] * 5,
-        out_specs=[anywhere] * len(splits),
-        scratch_shapes=[pltpu.VMEM(piece.shape, piece.dtype) for piece in begun]
-        + [pltpu.SemaphoreType.DMA((5,)), pltpu.SemaphoreType.DMA((5 * len(splits),))],
+        functools.partial(place_kernel, moves, len(pieces)),
+        out_shape=[jax.ShapeDtypeStruct((2, 2, 2, rows, width), low) for width in widths],
+        in_specs=[anywhere] * len(pieces),
+        out_specs=[anywhere] * len(widths),
+        scratch_shapes=[pltpu.VMEM(piece.shape, low) for piece in pieces]
+        + [pltpu.SemaphoreType.DMA((len(pieces),)), pltpu.SemaphoreType.DMA((stores,))],
         compiler_params=pltpu.CompilerParams(vmem_limit_bytes=size + (2 << 20)),
         cost_estimate=pl.CostEstimate(flops=0, bytes_accessed=2 * size, transcendentals=0),
         name="place_rows",
-    )(*begun)
+    )(*pieces)
     return [out.reshape(-1, out.shape[-1]) for out in outs]
 
 
 def start_scatter(grad):
     x, y = lax.axis_index("dp"), lax.axis_index("cy")
     parts = grad.reshape(2, 2, 2, -1, grad.shape[-1])
-    far = pick(pick(parts, 1 - x), 1 - y)
-    return parts, flip(far[0], "dp"), flip(far[1], "cy")
-
-
-def next_scatter(parts, far_first, far_second):
+    return parts, pick(parts, 1 - x)[:, 0], pick(parts, 1 - y, 1)[:, 1]
+
+
+def send_scatter(parts, by_x, by_y):
+    return parts, flip(by_x, "dp"), flip(by_y, "cy")
+
+
+def next_scatter(parts, from_x, from_y):
     x, y = lax.axis_index("dp"), lax.axis_index("cy")
-    low = parts.dtype
-    by_y, by_x = pick(pick(parts, x), 1 - y), pick(pick(parts, 1 - x), y)
-    by_y = jnp.stack([total(by_y[0], far_first).astype(low), by_y[1]])
-    by_x = jnp.stack([by_x[0], total(by_x[1], far_second).astype(low)])
-    return pick(pick(parts, x), y), flip(by_y, "cy"), flip(by_x, "dp")
-
-
-def end_scatter(own, from_y, from_x):
+    by_y = total(pick(pick(parts, x), 1 - y)[0], pick(from_x, 1 - y)).astype(parts.dtype)
+    by_x = total(pick(pick(parts, 1 - x), y)[1], pick(from_y, 1 - x)).astype(parts.dtype)
+    return parts, from_x, from_y, flip(by_y, "cy"), flip(by_x, "dp")
+
+
+def end_scatter(parts, from_x, from_y, last_y, last_x):
+    x, y, c = lax.axis_index("dp"), lax.axis_index("cy"), lax.axis_index("core")
+    own = pick(pick(parts, x), y)
+    first = total(own[0], pick(from_x, y), last_y)
+    second = total(own[1], pick(from_y, x), last_x)
+    keep = jnp.where(c == 0, first, second)
+    away = jnp.where(c == 0, second, first).astype(jnp.bfloat16)
+    got = flip(away, "core").astype(jnp.float32)
+    return jnp.where(c == 0, keep, got), jnp.where(c == 0, got, keep)
+
+
+def gather_gains(table):
+    table = ordered(lax.axis_index("core"), table, flip(table, "core"), axis=1)
+    table = ordered(lax.axis_index("cy"), table, flip(table, "cy"), axis=1)
+    table = ordered(lax.axis_index("dp"), table, flip(table, "dp"), axis=1)
+    return table.reshape(table.shape[0], -1)
+
+
+def exchange_seq(parts):
+    z, size = lax.axis_index("seq"), lax.axis_size("seq")
+    got = [pick(parts, z)]
+    for step in range(1, size):
+        ring = [(i, (i + step) % size) for i in range(size)]
+        got.insert(0, lax.ppermute(pick(parts, lax.rem(z + step, size)), "seq", ring))
+    got = jnp.stack(got + got[:-1])
+    return lax.dynamic_slice_in_dim(got, size - 1 - z, size, 0)
+
+
+def shift(value, step):
+    size = lax.axis_size("seq")
+    return lax.ppermute(value, "seq", [(i, (i + step) % size) for i in range(size)])
+
+
+def gather_rows(local_rows):
+    size = lax.axis_size("seq")
+    got = {step: shift(local_rows, step) for step in (2, 1, 3)}
+    pieces = [local_rows] + [got[size - ahead] for ahead in range(1, size)]
+    return jnp.concatenate(pieces + [flip(piece, "core") for piece in pieces])
+
+
+def gather_first(local_rows):
+    c, z, size = lax.axis_index("core"), lax.axis_index("seq"), lax.axis_size("seq")
+    whole = lax.all_gather(local_rows, ("core", "seq"), axis=0)
+    order = [(core, ahead) for core in (c, 1 - c) for ahead in range(size)]
+    return jnp.concatenate([pick(whole, core * size + lax.rem(z + i, size)) for core, i in order])
+
+
+def row_tokens(rows, length):
+    c, z, size = lax.axis_index("core"), lax.axis_index("seq"), lax.axis_size("seq")
+    shape = (2, size, 2, rows // 2)
+    core = jnp.where(lax.broadcasted_iota(jnp.int32, shape, 0) == 0, c, 1 - c)
+    owner = lax.rem(z + lax.broadcasted_iota(jnp.int32, shape, 1), size)
+    begin = lax.broadcasted_iota(jnp.int32, shape, 2) * (length // 2)
+    row = lax.broadcasted_iota(jnp.int32, shape, 3)
+    return (begin + (core * size + owner) * (rows // 2) + row).reshape(-1)
+
+
+def row_order(values):
+    c, z, size = lax.axis_index("core"), lax.axis_index("seq"), lax.axis_size("seq")
+    parts = values.reshape(2, 2, size, -1).transpose(1, 2, 0, 3)
+    parts = jnp.stack([pick(parts, c), pick(parts, 1 - c)])
+    parts = jnp.concatenate([parts, parts], axis=1)
+    return lax.dynamic_slice_in_dim(parts, z, size, 1).reshape(-1)
+
+
+def core_swap(value):
+    half = value.shape[0] // 2
+    got = flip(value, "core")
+    return jnp.concatenate([got[half:], got[:half]])
+
+
+def core_rows(left, right, dims):
+    half = left.shape[0] // 2
+    got = flip(dot(left[half:], right, dims).astype(jnp.bfloat16), "core")
+    kept = lax.optimization_barrier(dot(left[:half], right, dims).astype(jnp.bfloat16))
+    return total(kept, got).astype(jnp.bfloat16)
+
+
+def core_sums(partial_rows):
+    half = partial_rows.shape[0] // 2
+    return total(partial_rows[:half], flip(partial_rows[half:], "core")).astype(jnp.bfloat16)
+
+
+def scatter_rows(sums):
+    size = lax.axis_size("seq")
+    parts = sums.reshape(size, -1, sums.shape[-1])
+    got = [shift(parts[step], step) for step in (2, 1, 3)]
+    return total(parts[0], *got)
+
+
+def chip_rows(*matrices):
     c = lax.axis_index("core")
-    sums = total(own, from_y, from_x)
-    keep = pick(sums, c)
-    got = flip(pick(sums, 1 - c).astype(jnp.bfloat16), "core").astype(jnp.float32)
+    got = flip(core_columns(matrices, 1 - c), "core")
+    return ordered(c, core_columns(matrices, c), got)
+
+
+def gather_chips(rows):
+    whole = lax.all_gather(rows.reshape(-1, rows.shape[-1]), ("dp", "cy"), axis=0, tiled=True)
+    return whole
+
+
+def scatter_chips(grad):
+    sums = lax.psum_scatter(grad, ("dp", "cy"), scatter_dimension=0, tiled=True)
+    return sums.reshape(2, -1, sums.shape[-1])
+
+
+def both_columns(sums):
+    c = lax.axis_index("core")
+    keep = pick(sums, c).astype(jnp.float32)
+    got = flip(pick(sums, 1 - c), "core").astype(jnp.float32)
     return jnp.where(c == 0, keep, got), jnp.where(c == 0, got, keep)
-
-
-def gather_rows(local_rows):
-    width = local_rows.shape[-1]
-    return lax.all_gather(local_rows, ("core", "seq"), axis=1, tiled=True).reshape(-1, width)
-
-
-def core_rows(left, right, dims):
-    c = lax.axis_index("core")
-    parts = left.reshape(2, 2, -1, left.shape[-1])
-
-    def rows_of(core):
-        rows = dot(pick(parts, core, 1).reshape(-1, left.shape[-1]), right, dims)
-        return rows.astype(jnp.bfloat16).reshape(2, -1, rows.shape[-1])
-
-    away = rows_of(1 - c)
-    got = flip(away, "core")
-    kept = lax.optimization_barrier(rows_of(c))
-    return total(kept, got).astype(jnp.bfloat16)
-
-
-def scatter_rows(core_sums):
-    return lax.psum_scatter(core_sums, "seq", scatter_dimension=1, tiled=True).astype(jnp.float32)
 
 
 def dot(left, right, dims):
@@ -624,41 +706,49 @@
     rows_own = query_weight.shape[0]
     ffn_cols = gate_weight.shape[1] // 2
 
-    x_local = trade_sequences(inputs)
-    block_x = gather_rows(x_local)
-    x_float = x_local.astype(jnp.float32)
     kv_stack = jnp.stack([key_weight, value_weight], axis=1)
     kv_stack = kv_stack.reshape(-1, 2, KEY_VALUE_HEADS, HEAD_SIZE).transpose(2, 0, 1, 3)
-    kv_rows = lax.all_to_all(kv_stack, "seq", split_axis=0, concat_axis=0, tiled=True)
+    kv_rows = exchange_seq(kv_stack).reshape(rows_own, 2 * HEAD_SIZE)
+    x_local = after(trade_sequences(inputs), kv_rows)
+    own_shape = x_local.shape
+    x_local = x_local.reshape(-1, x_local.shape[-1])
+    block_x = gather_first(x_local)
+    x_float = x_local.astype(jnp.float32)
     gain_table = jnp.stack([pre_attn_gain, post_attn_gain, pre_ffn_gain, post_ffn_gain], axis=0)
-    gain_full = lax.all_gather(gain_table, ("dp", "cy", "core"), axis=1, tiled=True)
-    kv_rows = after(kv_rows.reshape(rows_own, 2 * HEAD_SIZE), gain_full)
-    gain_one, gain_two, gain_three, gain_four = gain_full.astype(jnp.float32)
+    gain_one, gain_two, gain_three, gain_four = gather_gains(gain_table).astype(jnp.float32)
 
     pos_own = trade_sequences(positions)
     seq_pos = ordered(c, pos_own, flip(pos_own, "core"), axis=1).reshape(-1)
     half = HEAD_SIZE // 2
     freq = BASE ** (-jnp.arange(half, dtype=jnp.float32) * 2.0 / HEAD_SIZE)
+    token = row_tokens(x_local.shape[0], seq_pos.shape[0])
+    seq_pos = row_order(seq_pos)
     angle = seq_pos.astype(jnp.float32)[:, None] * freq
     cosine, sine = jnp.cos(angle), jnp.sin(angle)
     kv_cosine = jnp.where(c == 0, cosine, 1.0)
     kv_sine = jnp.where(c == 0, sine, 0.0)
 
-    attn_begun = next_gather(*start_gather([query_weight, kv_rows, output_weight.T]))
-    in_weight, out_weight = end_gather(attn_begun, (2 * HEAD_SIZE, HEAD_SIZE))
-    down_begun = start_gather([after(down_weight.T, attn_begun)])
-    gate_up_begun = start_gather(after([gate_weight, up_weight], attn_begun))
-    cotangent = after(cotangent, attn_begun)
-    grad_top = trade_sequences(cotangent)
+    attn_begun = next_gather(
+        *start_gather(
+            (query_weight, 0, HEAD_SIZE), (kv_rows, 0, HEAD_SIZE), (output_weight.T, 0, HEAD_SIZE)
+        )
+    )
+    split = 2 * HEAD_SIZE
+    in_weight, out_weight = end_gather(
+        [attn_begun], [((0, 0, 0, split), (1, split, 0, HEAD_SIZE))], (split, HEAD_SIZE)
+    )
+    gate_up_rows = chip_rows((gate_weight, 0, ffn_cols), (up_weight, 0, ffn_cols))
+    gate_up_weight = gather_chips(after(gate_up_rows, attn_begun[:3]))
+    down_back = gather_chips(chip_rows((down_weight.T, 0, ffn_cols)))
+    grad_top = trade_sequences(after(cotangent, attn_begun))
 
     block_one = norm_gain(block_x.astype(jnp.float32), gain_one).astype(low)
     raw = dot(block_one, in_weight, (1, 0))
     queries = turn(raw[:, :HEAD_SIZE], cosine, sine).astype(low)
     kv_own = turn(raw[:, HEAD_SIZE:], kv_cosine, kv_sine).astype(low)
-    kv_other = flip(kv_own, "core")
+    kv_other = core_swap(kv_own)
     keys = jnp.where(c == 0, kv_own, kv_other)
     values = jnp.where(c == 0, kv_other, kv_own)
-    token = jnp.arange(seq_pos.shape[0], dtype=jnp.int32)
     visible = (token[None, :] <= token[:, None]) & (token[None, :] >= (token - seq_pos)[:, None])
     bent, masked = head_scores(queries, keys, visible)
     row_max = jnp.max(masked, axis=-1, keepdims=True)
@@ -666,19 +756,14 @@
     row_sum = jnp.sum(exponent, axis=-1, keepdims=True)
     heads = dot((exponent / row_sum).astype(low), values, (1, 0)).astype(low)
     log_total = row_max + jnp.log(row_sum)
-    heads = after(heads, grad_top, down_begun)
-    grad_top = grad_top.astype(jnp.float32)
+    heads = after(heads, grad_top)
+    grad_top = grad_top.reshape(x_local.shape).astype(jnp.float32)
 
     project_core = core_rows(heads, out_weight, (1, 1))
     project = scatter_rows(project_core)
     middle = x_float + norm_gain(project, gain_two)
     normed_two = norm_gain(middle, gain_three).astype(low)
-    normed_two = after(normed_two, gate_up_begun)
-    gate_up_begun = next_gather(*after(gate_up_begun, normed_two))
-    down_begun = next_gather(*after(down_begun, normed_two))
     block_two = gather_rows(normed_two)
-    (gate_up_weight,) = end_gather(gate_up_begun, (2 * ffn_cols,))
-    (down_back,) = end_gather(down_begun, (ffn_cols,))
     gate_up = dot(block_two, gate_up_weight, (1, 0))
     gate, upper = gate_up[:, :ffn_cols], gate_up[:, ffn_cols:]
     hidden = geglu(gate, upper).astype(low)
@@ -687,7 +772,7 @@
     grad_feed, grad_g_four = pull_four(grad_top)
     grad_feed = grad_feed.astype(low)
     layer_output = after((middle + norm_gain(feed, gain_four)).astype(low), grad_feed)
-    layer_output = trade_sequences(layer_output)
+    layer_output = trade_sequences(layer_output.reshape(own_shape))
 
     grad_feed_rows = after(gather_rows(grad_feed), layer_output)
     grad_hidden = dot(grad_feed_rows, down_back, (1, 0))
@@ -696,9 +781,11 @@
     grad_gate_up = jnp.concatenate([grad_gate_act.astype(low), grad_up_act.astype(low)], axis=1)
     normed_two_core = core_rows(grad_gate_up, gate_up_weight, (1, 1))
     grad_normed_two = scatter_rows(normed_two_core)
-    hidden, block_two = after((hidden, block_two), normed_two_core)
-    grad_down_begun = start_scatter(dot(grad_feed_rows, hidden, (0, 0)).astype(low))
-    grad_gu_begun = start_scatter(dot(block_two, grad_gate_up, (0, 0)).astype(low))
+    late = after((hidden, block_two), normed_two_core)
+    grad_down = dot(grad_feed_rows, late[0], (0, 0)).astype(low)
+    grad_gu = dot(late[1], grad_gate_up, (0, 0)).astype(low)
+    grad_normed_two = after(grad_normed_two, grad_down, grad_gu)
+    grad_down, grad_gu = scatter_chips(grad_down), scatter_chips(grad_gu)
 
     unused, pull_three = jax.vjp(norm_gain, middle, gain_three)
     grad_mid_norm, grad_g_three = pull_three(grad_normed_two)
@@ -706,8 +793,6 @@
     unused, pull_two = jax.vjp(norm_gain, project, gain_two)
     grad_project, grad_g_two = pull_two(grad_middle)
     grad_project = grad_project.astype(low)
-    grad_down_begun = next_scatter(*after(grad_down_begun, grad_project))
-    grad_gu_begun = next_scatter(*after(grad_gu_begun, grad_project))
     grad_project_rows = gather_rows(grad_project)
     grad_heads = dot(grad_project_rows, out_weight, (1, 0)).astype(low)
 
@@ -723,34 +808,42 @@
     grad_query_raw = turn_back(grad_query_rot, cosine, sine).astype(low)
     grad_key_raw = turn_back(grad_key_rot, cosine, sine).astype(low)
     kv_grad_own = jnp.where(c == 0, grad_key_raw, grad_value)
-    kv_grad_got = flip(jnp.where(c == 0, grad_value, grad_key_raw), "core")
+    kv_grad_got = core_swap(jnp.where(c == 0, grad_value, grad_key_raw))
     grad_in = jnp.concatenate([grad_query_raw, total(kv_grad_own, kv_grad_got).astype(low)], axis=1)
-    normed_one_core = core_rows(grad_in, in_weight, (1, 1))
+    normed_one_part = dot(grad_in, in_weight, (1, 1)).astype(low)
+    normed_one_core = core_sums(normed_one_part)
     grad_normed_one = scatter_rows(normed_one_core)
     block_one, heads = after((block_one, heads), normed_one_core)
     grad_in_part = dot(block_one, grad_in, (0, 0)).astype(low)
     grad_output_part = dot(grad_project_rows, heads, (0, 0)).astype(low)
     attn_grad_begun = start_scatter(jnp.concatenate([grad_in_part, grad_output_part], axis=1))
+    attn_grad_begun = send_scatter(*attn_grad_begun)
+    grad_normed_one = after(grad_normed_one, attn_grad_begun)
     attn_grad_begun = next_scatter(*attn_grad_begun)
-    grad_down = end_scatter(*after(grad_down_begun, normed_one_core))
-    grad_gu = end_scatter(*after(grad_gu_begun, normed_one_core))
     attn_grads = end_scatter(*attn_grad_begun)
-
-    unused, pull_one = jax.vjp(norm_gain, x_float, gain_one)
-    grad_input_norm, grad_g_one = pull_one(grad_normed_one)
-    input_grad = trade_sequences((grad_middle + grad_input_norm).astype(low))
+    grad_down, grad_gu = after((grad_down, grad_gu), attn_grad_begun)
+    grad_down, grad_gu = both_columns(grad_down), both_columns(grad_gu)
+
+    block_x = after(block_x, attn_grad_begun[0]).astype(jnp.float32)
+    unused, pull_gain = jax.vjp(lambda gain: norm_gain(block_x, gain), gain_one)
+    (grad_g_one,) = pull_gain(normed_one_part.astype(jnp.float32))
+    everyone = ("dp", "cy", "core", "seq")
     gain_grads = jnp.stack([grad_g_one, grad_g_two, grad_g_three, grad_g_four], axis=0)
-    everyone = ("dp", "cy", "core", "seq")
+    gain_grads = after(gain_grads, grad_normed_one)
     gain_parts = gain_grads.reshape(4, lax.axis_size(everyone), -1).transpose(1, 0, 2)
     gain_out = jnp.sum(
         lax.all_to_all(gain_parts, everyone, split_axis=0, concat_axis=0, tiled=True), axis=0
     )
 
+    unused, pull_one = jax.vjp(lambda rows: norm_gain(rows, gain_one), x_float)
+    (grad_input_norm,) = pull_one(grad_normed_one)
+    input_grad = trade_sequences((grad_middle + grad_input_norm).astype(low).reshape(own_shape))
+
     def whole(pair, begin, cols):
         return jnp.concatenate([part[:, begin : begin + cols] for part in pair], axis=1)
 
     kv_back = whole(attn_grads, HEAD_SIZE, HEAD_SIZE).astype(low)
-    kv_back = lax.all_to_all(kv_back, "seq", split_axis=0, concat_axis=0, tiled=True)
+    kv_back = exchange_seq(kv_back.reshape(KEY_VALUE_HEADS, -1, 2 * HEAD_SIZE))
     kv_back = kv_back.reshape(KEY_VALUE_HEADS, -1, 2, HEAD_SIZE).transpose(2, 1, 0, 3)
     kv_back = kv_back.reshape(2, -1, KEY_VALUE_HEADS * HEAD_SIZE).astype(jnp.float32)
     return (

time: 751 us -> 704 us (0.937)
  waiting for transfers between devices: 391 us -> 355 us
  other arithmetic: 95 us -> 78.6 us
  starting transfers between devices: 50 us -> 62.5 us
  blocking collectives: 9.01 us -> 0 us
    ppermute x0 -> x27, waiting for transfers between devices: none -> 295 us  [the longest x21 289 us: shift(): lax.ppermute(value, 'seq', [(i, (i + step) % size) for i in range(size)])]
    reduce_scatter x4 -> x2, waiting for transfers between devices: 132 us -> 0.04 us  [scatter_chips(): sums = lax.psum_scatter(grad, ('dp', 'cy'), scatter_dimension=0, tiled=True)]
    ppermute x42 -> x41, waiting for transfers between devices: 188 us -> 58.5 us  [flip(): return lax.ppermute(value, axis, [(0, 1), (1, 0)])]
    all_gather x4 -> x3, waiting for transfers between devices: 40.3 us -> 0.01 us  [the longest x2 0.01 us: gather_chips(): lax.all_gather(rows.reshape(-1, rows.shape[-1]), ('dp', 'cy'), axis=0, ti...]
    ppermute x0 -> x27, starting transfers between devices: none -> 38 us  [the longest x21 27 us: shift(): lax.ppermute(value, 'seq', [(i, (i + step) % size) for i in range(size)])]
    all_to_all x2 -> x0, waiting for transfers between devices: 24.9 us -> none  [the longest x1 16.3 us: head_local(): lax.all_to_all(kv_stack, 'seq', split_axis=0, concat_axis=0, tiled=True)]
    ppermute x42 -> x41, starting transfers between devices: 36.6 us -> 20.5 us  [flip(): return lax.ppermute(value, axis, [(0, 1), (1, 0)])]
    another operation x11 -> x4, other arithmetic: 14.9 us -> 5.55 us  [the longest x5 6.83 us: next_scatter(): by_x = jnp.stack([by_x[0], total(by_x[1], far_second).astype(low)])]
  transfers between devices with their start and end apart: 53 -> 74, of which waited for: 28 -> 35; matrix products, arithmetic and copies ran while one was open for 24% -> 28% of each run, Pallas kernels for 1% -> 0%
where the time goes in v3:
time: 704 us; the launch traced here: 699 us
  waiting for transfers between devices  355 us (50%)
  matrix products  107 us (15%)
  other arithmetic  78.6 us (11%)
  local copies, waits for them, and re-layouts  77.6 us (11%)
  starting transfers between devices  62.5 us (9%)
  between operations  16.3 us (2%)
    ppermute x21, waiting for transfers between devices, shift(): lax.ppermute(value, 'seq', [(i, (i + step) % size) for i in range(size)])  289 us
    dot_general x21, matrix products, dot(): lax.dot_general(left, right, ((dims[:1], dims[1:]), ((), ())), preferred_...  107 us
    ppermute x41, waiting for transfers between devices, flip(): return lax.ppermute(value, axis, [(0, 1), (1, 0)])  58.5 us
    unnamed x239, local copies, waits for them, and re-layouts  36.8 us
    ppermute x21, starting transfers between devices, shift(): lax.ppermute(value, 'seq', [(i, (i + step) % size) for i in range(size)])  27 us
    ppermute x41, starting transfers between devices, flip(): return lax.ppermute(value, axis, [(0, 1), (1, 0)])  20.5 us
  transfers between devices with their start and end apart: 74, of which 35 were waited for; matrix products, arithmetic and copies ran while one was open for 28% of the time, Pallas kernels for 0%

profile of v3, /device:TPU:0, one launch (start us, length us, event | category | flops | bytes accessed | tf_op | source)
XLA Modules:
  0.0 699.4 jit_solution(13951455670780656844)
XLA Ops:
  10.3 5.1 collective-permute-start.1
  20.1 2.5 collective-permute-done.2
  23.2 3.5 collective-permute-done
  32.1 2.9 collective-permute-done.9
  39.7 3.3 maximum_select_fusion
  43.1 13.8 %collective-permute-done.10.refs_1_ = bf16[2,288,768]{2,1,0:T(8,128)(2,1)S(1)} collective-permute-done((bf16[2,288,768]{2,1,0:T(8,128)(2,1)S(1)}, bf16[2,288,768]{2,1,0:T(8,128)(2,1)S(1)}, u32[]{:S(2)}, u32[]{:S(2)}) %collective-permute-start.10) | collective-permute-done | bytes 884768 | tf_op jit(solution)/shard_map/ppermute | solution.py:449
  61.2 2.4 collective-permute-done.4
  69.8 8.7 %collective-permute-done.8 = bf16[4,2,2,288]{3,0,2,1:T(4,128)(2,1)S(1)} collective-permute-done((bf16[4,2,2,288]{3,0,2,1:T(4,128)(2,1)S(1)}, bf16[4,2,2,288]{3,0,2,1:T(4,128)(2,1)S(1)}, u32[]{:S(2)}, u32[]{:S(2)}) %collective-permute-start.8) | collective-permute-done | bytes 9248 | tf_op jit(solution)/shard_map/ppermute | solution.py:449
  94.8 2.6 fusion.134
  97.5 2.5 fusion.65
  110.7 2.8 collective-permute-done.15
  116.6 3.1 collective-permute-start.18
  121.1 2.7 maximum_select_fusion.1
  123.9 9.9 %collective-permute-done.18 = bf16[128,2304]{1,0:T(8,128)(2,1)} collective-permute-done((bf16[128,2304]{1,0:T(8,128)(2,1)}, bf16[128,2304]{1,0:T(8,128)(2,1)}, u32[]{:S(2)}, u32[]{:S(2)}) %collective-permute-start.18) | collective-permute-done | bytes 589856 | tf_op jit(solution)/shard_map/ppermute | solution.py:594
  133.8 13.7 %collective-permute-done.17 = bf16[128,2304]{1,0:T(8,128)(2,1)} collective-permute-done((bf16[128,2304]{1,0:T(8,128)(2,1)}, bf16[128,2304]{1,0:T(8,128)(2,1)}, u32[]{:S(2)}, u32[]{:S(2)}) %collective-permute-start.17) | collective-permute-done | bytes 589856 | tf_op jit(solution)/shard_map/ppermute | solution.py:594
  147.6 24.7 %collective-permute-done.16 = bf16[128,2304]{1,0:T(8,128)(2,1)} collective-permute-done((bf16[128,2304]{1,0:T(8,128)(2,1)}, bf16[128,2304]{1,0:T(8,128)(2,1)}, u32[]{:S(2)}, u32[]{:S(2)}) %collective-permute-start.16) | collective-permute-done | bytes 589856 | tf_op jit(solution)/shard_map/ppermute | solution.py:594
  175.8 2.6 collective-permute-start.19
  179.0 13.2 %collective-permute-done.19 = bf16[128,2304]{1,0:T(8,128)(2,1)S(1)} collective-permute-done((bf16[128,2304]{1,0:T(8,128)(2,1)S(1)}, bf16[128,2304]{1,0:T(8,128)(2,1)S(1)}, u32[]{:S(2)}, u32[]{:S(2)}) %collective-permute-start.19) | collective-permute-done | bytes 589856 | tf_op jit(solution)/shard_map/ppermute | solution.py:594
  192.3 35.6 %collective-permute-done.20 = bf16[128,2304]{1,0:T(8,128)(2,1)S(1)} collective-permute-done((bf16[128,2304]{1,0:T(8,128)(2,1)S(1)}, bf16[128,2304]{1,0:T(8,128)(2,1)S(1)}, u32[]{:S(2)}, u32[]{:S(2)}) %collective-permute-start.20) | collective-permute-done | bytes 589856 | tf_op jit(solution)/shard_map/ppermute | solution.py:594
  234.5 15.1 %fusion.135 = f32[1024,2304]{1,0:T(8,128)S(1)} fusion(bf16[1024,2304]{1,0:T(8,128)(2,1)} %constant_dynamic-update-slice_fusion.9, bf16[2304,2304]{1,0:T(8,128)(2,1)} %all-gather.6.cloned.1.call-done), kind=kOutput, calls=%fused_computation.374 | convolution fusion | flops 10871635968 | bytes 24772608 | tf_op jit(solution)/shard_map/dot_general | solution.py:678
  249.6 3.6 copy-done.17
  253.2 2.7 multiply_convert_fusion.1
  255.9 6.3 convolution_convert_fusion.3
  264.3 3.5 convolution_convert_fusion.4
  273.0 3.4 collective-permute-start.29
  279.2 7.6 %collective-permute-done.31 = bf16[128,2304]{1,0:T(8,128)(2,1)} collective-permute-done((bf16[128,2304]{1,0:T(8,128)(2,1)}, bf16[128,2304]{1,0:T(8,128)(2,1)}, u32[]{:S(2)}, u32[]{:S(2)}) %collective-permute-start.31) | collective-permute-done | bytes 589856 | tf_op jit(solution)/shard_map/ppermute | solution.py:594
  286.8 16.4 %collective-permute-done.30 = bf16[128,2304]{1,0:T(8,128)(2,1)} collective-permute-done((bf16[128,2304]{1,0:T(8,128)(2,1)}, bf16[128,2304]{1,0:T(8,128)(2,1)}, u32[]{:S(2)}, u32[]{:S(2)}) %collective-permute-start.30) | collective-permute-done | bytes 589856 | tf_op jit(solution)/shard_map/ppermute | solution.py:594
  303.1 22.8 %collective-permute-done.29 = bf16[128,2304]{1,0:T(8,128)(2,1)} collective-permute-done((bf16[128,2304]{1,0:T(8,128)(2,1)}, bf16[128,2304]{1,0:T(8,128)(2,1)}, u32[]{:S(2)}, u32[]{:S(2)}) %collective-permute-start.29) | collective-permute-done | bytes 589856 | tf_op jit(solution)/shard_map/ppermute | solution.py:594
  332.8 8.5 %collective-permute-done.33 = bf16[64,2304]{1,0:T(8,128)(2,1)S(1)} collective-permute-done((bf16[64,2304]{1,0:T(8,128)(2,1)S(1)}, bf16[64,2304]{1,0:T(8,128)(2,1)S(1)}, u32[]{:S(2)}, u32[]{:S(2)}) %collective-permute-start.33) | collective-permute-done | bytes 294944 | tf_op jit(solution)/shard_map/ppermute | solution.py:449
  342.2 3.7 collective-permute-done.34
  345.9 34.5 %collective-permute-done.35 = bf16[128,2304]{1,0:T(8,128)(2,1)S(1)} collective-permute-done((bf16[128,2304]{1,0:T(8,128)(2,1)S(1)}, bf16[128,2304]{1,0:T(8,128)(2,1)S(1)}, u32[]{:S(2)}, u32[]{:S(2)}) %collective-permute-start.35) | collective-permute-done | bytes 589856 | tf_op jit(solution)/shard_map/ppermute | solution.py:594
  383.4 11.0 %multiply_convert_fusion = (bf16[1024,1152]{1,0:T(8,128)(2,1)}, bf16[1024,1152]{1,0:T(8,128)(2,1)}) fusion(f32[1024,2304]{1,0:T(8,128)S(1)} %bitcast.256, bf16[1024,2304]{1,0:T(8,128)(2,1)S(1)} %constant_dynamic-update-slice_fusion.17, bf16[2304,1152]{1,0:T(8,128)(2,1)S(1)} %bitcast.295), kind=kOutput, calls=%fused_computation.29 | convolution fusion | flops 5464129536 | bytes 24182784 | tf_op jit(solution)/shard_map/dot_general | solution.py:678
  394.3 10.4 %convolution_convert_fusion.6 = bf16[512,2304]{1,0:T(8,128)(2,1)S(1)} fusion(bf16[2304,2304]{1,0:T(8,128)(2,1)} %all-gather.6.cloned.1.call-done, bf16[1024,1152]{1,0:T(8,128)(2,1)} %get-tuple-element.75, bf16[1024,1152]{1,0:T(8,128)(2,1)} %get-tuple-element.74), kind=kOutput, calls=%fused_computation.36 | convolution fusion | flops 5441716224 | bytes 17694720 | tf_op jit(solution)/shard_map/dot_general | solution.py:678
  405.0 10.1 %convolution_convert_fusion.7 = bf16[512,2304]{1,0:T(8,128)(2,1)S(1)} fusion(bf16[2304,2304]{1,0:T(8,128)(2,1)} %all-gather.6.cloned.1.call-done, bf16[1024,1152]{1,0:T(8,128)(2,1)} %get-tuple-element.75, bf16[1024,1152]{1,0:T(8,128)(2,1)S(1)} %copy-done.87), kind=kOutput, calls=%fused_computation.37 | convolution fusion | flops 5441716224 | bytes 17694720 | tf_op jit(solution)/shard_map/dot_general | solution.py:678
  419.1 8.0 %convolution_convert_fusion.1 = bf16[2304,1152]{1,0:T(8,128)(2,1)} fusion(bf16[1024,2304]{1,0:T(8,128)(2,1)S(1)} %copy-done.58, bf16[1024,1152]{1,0:T(8,128)(2,1)S(1)} %copy-done.22), kind=kOutput, calls=%fused_computation.5 | convolution fusion | flops 5438472192 | bytes 12386304 | tf_op jit(solution)/shard_map/dot_general | solution.py:678
  427.2 2.7 fusion.125
  431.9 2.6 collective-permute-start.42
  434.5 17.1 %convolution_convert_fusion = bf16[2304,2304]{1,0:T(8,128)(2,1)} fusion(bf16[1024,2304]{1,0:T(8,128)(2,1)} %constant_dynamic-update-slice_fusion.9, bf16[1024,1152]{1,0:T(8,128)(2,1)} %get-tuple-element.74, bf16[1024,1152]{1,0:T(8,128)(2,1)} %get-tuple-element.75), kind=kOutput, calls=%fused_computation | convolution fusion | flops 10886381568 | bytes 20054016 | tf_op jit(solution)/shard_map/dot_general | solution.py:678
  451.7 9.5 %collective-permute-done.43 = bf16[128,2304]{1,0:T(8,128)(2,1)} collective-permute-done((bf16[128,2304]{1,0:T(8,128)(2,1)}, bf16[128,2304]{1,0:T(8,128)(2,1)}, u32[]{:S(2)}, u32[]{:S(2)}) %collective-permute-start.43) | collective-permute-done | bytes 589856 | tf_op jit(solution)/shard_map/ppermute | solution.py:594
  461.1 23.5 %collective-permute-done.42 = bf16[128,2304]{1,0:T(8,128)(2,1)} collective-permute-done((bf16[128,2304]{1,0:T(8,128)(2,1)}, bf16[128,2304]{1,0:T(8,128)(2,1)}, u32[]{:S(2)}, u32[]{:S(2)}) %collective-permute-start.42) | collective-permute-done | bytes 589856 | tf_op jit(solution)/shard_map/ppermute | solution.py:594
  493.0 14.7 %collective-permute-done.45 = bf16[128,2304]{1,0:T(8,128)(2,1)} collective-permute-done((bf16[128,2304]{1,0:T(8,128)(2,1)S(1)}, bf16[128,2304]{1,0:T(8,128)(2,1)}, u32[]{:S(2)}, u32[]{:S(2)}) %collective-permute-start.45) | collective-permute-done | bytes 589856 | tf_op jit(solution)/shard_map/ppermute | solution.py:594
  509.6 32.1 %collective-permute-done.46 = bf16[128,2304]{1,0:T(8,128)(2,1)S(1)} collective-permute-done((bf16[128,2304]{1,0:T(8,128)(2,1)S(1)}, bf16[128,2304]{1,0:T(8,128)(2,1)S(1)}, u32[]{:S(2)}, u32[]{:S(2)}) %collective-permute-start.46) | collective-permute-done | bytes 589856 | tf_op jit(solution)/shard_map/ppermute | solution.py:594
  547.6 4.0 convolution_convert_fusion.11
  553.6 2.8 multiply_convert_fusion.2
  558.4 2.4 fusion.73
  560.9 2.5 broadcast_select_fusion
  565.7 2.9 convolution_convert_fusion.2
  568.7 2.2 copy-done.9
  572.9 4.3 collective-permute-done.53
  577.3 2.9 add_convert_fusion
  583.5 3.3 collective-permute-start.54
  588.3 3.7 convolution_convert_fusion.5
  594.0 5.8 copy.75
  605.0 4.0 fusion.5
  609.7 3.7 collective-permute-done.55
  613.4 23.5 %collective-permute-done.54 = bf16[128,2304]{1,0:T(8,128)(2,1)} collective-permute-done((bf16[128,2304]{1,0:T(8,128)(2,1)}, bf16[128,2304]{1,0:T(8,128)(2,1)}, u32[]{:S(2)}, u32[]{:S(2)}) %collective-permute-start.54) | collective-permute-done | bytes 589856 | tf_op jit(solution)/shard_map/ppermute | solution.py:594
  636.9 2.5 convert_add_fusion.1
  646.0 3.3 all-to-all-start
  651.0 2.2 fusion.35
  660.2 3.2 collective-permute-done.59
  663.3 2.2 maximum_select_fusion.6
  667.3 3.7 collective-permute-start.63
  673.9 3.7 collective-permute-done.64
  679.7 2.5 dynamic-slice_bitcast_fusion
  (523 shorter events, 166.3 us)
Async XLA Ops:
  7.2 77.7 %all-gather.4.cloned.1.call-start = ((), (), s32[]{:S(2)}) async-start(), calls=%async_computation.3 | async-start | bytes 5308416 | tf_op jit(solution)/shard_map/all_gather | solution.py:606
  10.3 9.7 %collective-permute-start.1 = (bf16[72,2,256]{2,1,0:T(2,128)(2,1)S(1)}, bf16[72,2,256]{2,1,0:T(2,128)(2,1)S(1)}, u32[]{:S(2)}, u32[]{:S(2)}) collective-permute-start(bf16[72,2,256]{2,1,0:T(2,128)(2,1)S(1)} %bitcast.283), channel_id=1, source_target_pairs={{0,3},{1,0},{2,1},{3,2},{4,7},{5,4},{6,5},{7,6},{8,11},{9,8},{10,9... | collective-permute-start | bytes 221192 | tf_op jit(solution)/shard_map/ppermute | solution.py:587
  15.5 7.1 %collective-permute-start.2 = (bf16[72,2,256]{2,1,0:T(2,128)(2,1)S(1)}, bf16[72,2,256]{2,1,0:T(2,128)(2,1)S(1)}, u32[]{:S(2)}, u32[]{:S(2)}) collective-permute-start(bf16[72,2,256]{2,1,0:T(2,128)(2,1)S(1)} %bitcast.284), channel_id=1, source_target_pairs={{0,2},{1,3},{2,0},{3,1},{4,6},{5,7},{6,4},{7,5},{8,10},{9,11},{10,... | collective-permute-start | bytes 221192 | tf_op jit(solution)/shard_map/ppermute | solution.py:587
  15.6 7.0 collective-permute-start.3
  18.5 8.2 %collective-permute-start = (bf16[64,2304]{1,0:T(8,128)(2,1)}, bf16[64,2304]{1,0:T(8,128)(2,1)}, u32[]{:S(2)}, u32[]{:S(2)}) collective-permute-start(bf16[64,2304]{1,0:T(8,128)(2,1)} %get-tuple-element.127), channel_id=1, source_target_pairs={{0,8},{8,0},{1,9},{9,1},{2,10},{10,2},{3,11},{11,3},{4,12},{12,4},... | collective-permute-start | bytes 884744 | tf_op jit(solution)/shard_map/ppermute | solution.py:449
  28.7 205.8 %all-gather.6.cloned.1.call-start = ((), (), s32[]{:S(2)}) async-start(), calls=%async_computation.4 | async-start | bytes 13271040 | tf_op jit(solution)/shard_map/all_gather | solution.py:661
  31.3 8.4 %collective-permute-start.26 = (bf16[288,2304]{1,0:T(8,128)(2,1)}, bf16[288,2304]{1,0:T(8,128)(2,1)}, u32[]{:S(2)}, u32[]{:S(2)}) collective-permute-start(bf16[288,2304]{1,0:T(8,128)(2,1)} %pad_maximum_fusion.5), channel_id=1, source_target_pairs={{0,4},{4,0},{1,5},{5,1},{2,6},{6,2},{3,7},{7,3},{8,12},{12,8},{9,1... | collective-permute-start | bytes 3981320 | tf_op jit(solution)/shard_map/ppermute | solution.py:449
  35.1 21.8 %collective-permute-start.10 = (bf16[2,288,768]{2,1,0:T(8,128)(2,1)S(1)}, bf16[2,288,768]{2,1,0:T(8,128)(2,1)S(1)}, u32[]{:S(2)}, u32[]{:S(2)}) collective-permute-start(bf16[2,288,768]{2,1,0:T(8,128)(2,1)S(1)} %maximum_select_fusion.2.refs_0_), channel_id=1, source_target_pairs={{0,8},{8,0},{1,9},{9,1},{2,10},{10,2},{3,11},{11,3},{4,12},{12,4},... | collective-permute-start | bytes 2654216 | tf_op jit(solution)/shard_map/ppermute | solution.py:449
  36.7 21.4 %collective-permute-start.11 = (bf16[2,288,768]{2,1,0:T(8,128)(2,1)S(1)}, bf16[2,288,768]{2,1,0:T(8,128)(2,1)S(1)}, u32[]{:S(2)}, u32[]{:S(2)}) collective-permute-start(bf16[2,288,768]{2,1,0:T(8,128)(2,1)S(1)} %maximum_select_fusion.2.refs_0_), channel_id=1, source_target_pairs={{0,16},{16,0},{1,17},{17,1},{2,18},{18,2},{3,19},{19,3},{4,20},{20... | collective-permute-start | bytes 2654216 | tf_op jit(solution)/shard_map/ppermute | solution.py:449
  38.2 25.4 %collective-permute-start.6 = (bf16[4,288]{1,0:T(4,128)(2,1)S(1)}, bf16[4,288]{1,0:T(4,128)(2,1)S(1)}, u32[]{:S(2)}, u32[]{:S(2)}) collective-permute-start(bf16[4,288]{1,0:T(4,128)(2,1)S(1)} %pad_maximum_fusion.18), channel_id=1, source_target_pairs={{0,4},{4,0},{1,5},{5,1},{2,6},{6,2},{3,7},{7,3},{8,12},{12,8},{9,1... | collective-permute-start | bytes 6920 | tf_op jit(solution)/shard_map/ppermute | solution.py:449
  58.2 197.7 %all-gather.8.cloned.1.call-start = ((), (), s32[]{:S(2)}) async-start(), calls=%async_computation.5 | async-start | bytes 6635520 | tf_op jit(solution)/shard_map/all_gather | solution.py:661
  63.7 5.4 collective-permute-start.7
  65.8 13.5 %collective-permute-start.12 = (bf16[288,768]{1,0:T(8,128)(2,1)}, bf16[288,768]{1,0:T(8,128)(2,1)S(1)}, u32[]{:S(2)}, u32[]{:S(2)}) collective-permute-start(bf16[288,768]{1,0:T(8,128)(2,1)} %slice_bitcast_fusion.3), channel_id=1, source_target_pairs={{0,16},{16,0},{1,17},{17,1},{2,18},{18,2},{3,19},{19,3},{4,20},{20... | collective-permute-start | bytes 1327112 | tf_op jit(solution)/shard_map/ppermute | solution.py:449
  68.0 12.3 %collective-permute-start.13 = (bf16[288,768]{1,0:T(8,128)(2,1)}, bf16[288,768]{1,0:T(8,128)(2,1)}, u32[]{:S(2)}, u32[]{:S(2)}) collective-permute-start(bf16[288,768]{1,0:T(8,128)(2,1)} %slice_bitcast_fusion.2), channel_id=1, source_target_pairs={{0,8},{8,0},{1,9},{9,1},{2,10},{10,2},{3,11},{11,3},{4,12},{12,4},... | collective-permute-start | bytes 1327112 | tf_op jit(solution)/shard_map/ppermute | solution.py:449
  69.2 9.3 %collective-permute-start.8 = (bf16[4,2,2,288]{3,0,2,1:T(4,128)(2,1)S(1)}, bf16[4,2,2,288]{3,0,2,1:T(4,128)(2,1)S(1)}, u32[]{:S(2)}, u32[]{:S(2)}) collective-permute-start(bf16[4,2,2,288]{3,0,2,1:T(4,128)(2,1)S(1)} %maximum_select_fusion.9), channel_id=1, source_target_pairs={{0,16},{16,0},{1,17},{17,1},{2,18},{18,2},{3,19},{19,3},{4,20},{20... | collective-permute-start | bytes 27656 | tf_op jit(solution)/shard_map/ppermute | solution.py:449
  109.7 11.4 %collective-permute-start.27 = (bf16[288,1152]{1,0:T(8,128)(2,1)S(1)}, bf16[288,1152]{1,0:T(8,128)(2,1)}, u32[]{:S(2)}, u32[]{:S(2)}) collective-permute-start(bf16[288,1152]{1,0:T(8,128)(2,1)S(1)} %get-tuple-element.107), channel_id=1, source_target_pairs={{0,4},{4,0},{1,5},{5,1},{2,6},{6,2},{3,7},{7,3},{8,12},{12,8},{9,1... | collective-permute-start | bytes 1990664 | tf_op jit(solution)/shard_map/ppermute | solution.py:449
  116.6 17.2 %collective-permute-start.18 = (bf16[128,2304]{1,0:T(8,128)(2,1)}, bf16[128,2304]{1,0:T(8,128)(2,1)}, u32[]{:S(2)}, u32[]{:S(2)}) collective-permute-start(bf16[128,2304]{1,0:T(8,128)(2,1)} %get-tuple-element.94), channel_id=1, source_target_pairs={{0,3},{1,0},{2,1},{3,2},{4,7},{5,4},{6,5},{7,6},{8,11},{9,8},{10,9... | collective-permute-start | bytes 1769480 | tf_op jit(solution)/shard_map/ppermute | solution.py:594
  119.8 27.8 %collective-permute-start.17 = (bf16[128,2304]{1,0:T(8,128)(2,1)}, bf16[128,2304]{1,0:T(8,128)(2,1)}, u32[]{:S(2)}, u32[]{:S(2)}) collective-permute-start(bf16[128,2304]{1,0:T(8,128)(2,1)} %get-tuple-element.95), channel_id=1, source_target_pairs={{0,1},{1,2},{2,3},{3,0},{4,5},{5,6},{6,7},{7,4},{8,9},{9,10},{10,1... | collective-permute-start | bytes 1769480 | tf_op jit(solution)/shard_map/ppermute | solution.py:594
  119.8 52.4 %collective-permute-start.16 = (bf16[128,2304]{1,0:T(8,128)(2,1)}, bf16[128,2304]{1,0:T(8,128)(2,1)}, u32[]{:S(2)}, u32[]{:S(2)}) collective-permute-start(bf16[128,2304]{1,0:T(8,128)(2,1)} %get-tuple-element.93), channel_id=1, source_target_pairs={{0,2},{1,3},{2,0},{3,1},{4,6},{5,7},{6,4},{7,5},{8,10},{9,11},{10,... | collective-permute-start | bytes 1769480 | tf_op jit(solution)/shard_map/ppermute | solution.py:594
  123.9 553.8 %reduce-scatter.3.cloned.1.call-start = ((), (), s32[]{:S(2)}) async-start(), calls=%async_computation.6 | async-start | bytes 6635520 | tf_op jit(solution)/shard_map/reduce_scatter | solution.py:666
  175.8 16.4 %collective-permute-start.19 = (bf16[128,2304]{1,0:T(8,128)(2,1)S(1)}, bf16[128,2304]{1,0:T(8,128)(2,1)S(1)}, u32[]{:S(2)}, u32[]{:S(2)}) collective-permute-start(bf16[128,2304]{1,0:T(8,128)(2,1)S(1)} %get-tuple-element.65), channel_id=1, source_target_pairs={{0,3},{1,0},{2,1},{3,2},{4,7},{5,4},{6,5},{7,6},{8,11},{9,8},{10,9... | collective-permute-start | bytes 1769480 | tf_op jit(solution)/shard_map/ppermute | solution.py:594
  178.5 49.5 %collective-permute-start.20 = (bf16[128,2304]{1,0:T(8,128)(2,1)S(1)}, bf16[128,2304]{1,0:T(8,128)(2,1)S(1)}, u32[]{:S(2)}, u32[]{:S(2)}) collective-permute-start(bf16[128,2304]{1,0:T(8,128)(2,1)S(1)} %get-tuple-element.65), channel_id=1, source_target_pairs={{0,2},{1,3},{2,0},{3,1},{4,6},{5,7},{6,4},{7,5},{8,10},{9,11},{10,... | collective-permute-start | bytes 1769480 | tf_op jit(solution)/shard_map/ppermute | solution.py:594
  178.5 49.5 %collective-permute-start.21 = (bf16[128,2304]{1,0:T(8,128)(2,1)S(1)}, bf16[128,2304]{1,0:T(8,128)(2,1)S(1)}, u32[]{:S(2)}, u32[]{:S(2)}) collective-permute-start(bf16[128,2304]{1,0:T(8,128)(2,1)S(1)} %get-tuple-element.65), channel_id=1, source_target_pairs={{0,1},{1,2},{2,3},{3,0},{4,5},{5,6},{6,7},{7,4},{8,9},{9,10},{10,1... | collective-permute-start | bytes 1769480 | tf_op jit(solution)/shard_map/ppermute | solution.py:594
  179.0 52.0 %collective-permute-start.22 = (bf16[128,2304]{1,0:T(8,128)(2,1)S(1)}, bf16[128,2304]{1,0:T(8,128)(2,1)S(1)}, u32[]{:S(2)}, u32[]{:S(2)}) collective-permute-start(bf16[128,2304]{1,0:T(8,128)(2,1)S(1)} %get-tuple-element.65), channel_id=1, source_target_pairs={{0,4},{4,0},{1,5},{5,1},{2,6},{6,2},{3,7},{7,3},{8,12},{12,8},{9,1... | collective-permute-start | bytes 1769480 | tf_op jit(solution)/shard_map/ppermute | solution.py:449
  192.3 39.6 %collective-permute-start.23 = (bf16[128,2304]{1,0:T(8,128)(2,1)S(1)}, bf16[128,2304]{1,0:T(8,128)(2,1)S(1)}, u32[]{:S(2)}, u32[]{:S(2)}) collective-permute-start(bf16[128,2304]{1,0:T(8,128)(2,1)S(1)} %collective-permute-done.19), channel_id=1, source_target_pairs={{0,4},{4,0},{1,5},{5,1},{2,6},{6,2},{3,7},{7,3},{8,12},{12,8},{9,1... | collective-permute-start | bytes 1769480 | tf_op jit(solution)/shard_map/ppermute | solution.py:449
  227.9 5.7 collective-permute-start.25
  262.2 5.6 collective-permute-start.28
  263.1 14.0 %collective-permute-start.32 = (bf16[64,2304]{1,0:T(8,128)(2,1)}, bf16[64,2304]{1,0:T(8,128)(2,1)S(1)}, u32[]{:S(2)}, u32[]{:S(2)}) collective-permute-start(bf16[64,2304]{1,0:T(8,128)(2,1)} %get-tuple-element.125), channel_id=1, source_target_pairs={{0,8},{8,0},{1,9},{9,1},{2,10},{10,2},{3,11},{11,3},{4,12},{12,4},... | collective-permute-start | bytes 884744 | tf_op jit(solution)/shard_map/ppermute | solution.py:449
  271.0 15.7 %collective-permute-start.31 = (bf16[128,2304]{1,0:T(8,128)(2,1)}, bf16[128,2304]{1,0:T(8,128)(2,1)}, u32[]{:S(2)}, u32[]{:S(2)}) collective-permute-start(bf16[128,2304]{1,0:T(8,128)(2,1)} %get-tuple-element.91), channel_id=1, source_target_pairs={{0,3},{1,0},{2,1},{3,2},{4,7},{5,4},{6,5},{7,6},{8,11},{9,8},{10,9... | collective-permute-start | bytes 1769480 | tf_op jit(solution)/shard_map/ppermute | solution.py:594
  271.3 31.8 %collective-permute-start.30 = (bf16[128,2304]{1,0:T(8,128)(2,1)}, bf16[128,2304]{1,0:T(8,128)(2,1)}, u32[]{:S(2)}, u32[]{:S(2)}) collective-permute-start(bf16[128,2304]{1,0:T(8,128)(2,1)} %get-tuple-element.92), channel_id=1, source_target_pairs={{0,1},{1,2},{2,3},{3,0},{4,5},{5,6},{6,7},{7,4},{8,9},{9,10},{10,1... | collective-permute-start | bytes 1769480 | tf_op jit(solution)/shard_map/ppermute | solution.py:594
  273.0 52.8 %collective-permute-start.29 = (bf16[128,2304]{1,0:T(8,128)(2,1)}, bf16[128,2304]{1,0:T(8,128)(2,1)}, u32[]{:S(2)}, u32[]{:S(2)}) collective-permute-start(bf16[128,2304]{1,0:T(8,128)(2,1)} %get-tuple-element.90), channel_id=1, source_target_pairs={{0,2},{1,3},{2,0},{3,1},{4,6},{5,7},{6,4},{7,5},{8,10},{9,11},{10,... | collective-permute-start | bytes 1769480 | tf_op jit(solution)/shard_map/ppermute | solution.py:594
  329.7 16.2 %collective-permute-start.34 = (bf16[128,2304]{1,0:T(8,128)(2,1)S(1)}, bf16[128,2304]{1,0:T(8,128)(2,1)S(1)}, u32[]{:S(2)}, u32[]{:S(2)}) collective-permute-start(bf16[128,2304]{1,0:T(8,128)(2,1)S(1)} %get-tuple-element.108), channel_id=1, source_target_pairs={{0,3},{1,0},{2,1},{3,2},{4,7},{5,4},{6,5},{7,6},{8,11},{9,8},{10,9... | collective-permute-start | bytes 1769480 | tf_op jit(solution)/shard_map/ppermute | solution.py:594
  330.6 49.8 %collective-permute-start.35 = (bf16[128,2304]{1,0:T(8,128)(2,1)S(1)}, bf16[128,2304]{1,0:T(8,128)(2,1)S(1)}, u32[]{:S(2)}, u32[]{:S(2)}) collective-permute-start(bf16[128,2304]{1,0:T(8,128)(2,1)S(1)} %get-tuple-element.108), channel_id=1, source_target_pairs={{0,2},{1,3},{2,0},{3,1},{4,6},{5,7},{6,4},{7,5},{8,10},{9,11},{10,... | collective-permute-start | bytes 1769480 | tf_op jit(solution)/shard_map/ppermute | solution.py:594
  330.6 49.8 %collective-permute-start.36 = (bf16[128,2304]{1,0:T(8,128)(2,1)S(1)}, bf16[128,2304]{1,0:T(8,128)(2,1)S(1)}, u32[]{:S(2)}, u32[]{:S(2)}) collective-permute-start(bf16[128,2304]{1,0:T(8,128)(2,1)S(1)} %get-tuple-element.108), channel_id=1, source_target_pairs={{0,1},{1,2},{2,3},{3,0},{4,5},{5,6},{6,7},{7,4},{8,9},{9,10},{10,1... | collective-permute-start | bytes 1769480 | tf_op jit(solution)/shard_map/ppermute | solution.py:594
  331.7 49.4 %collective-permute-start.37 = (bf16[128,2304]{1,0:T(8,128)(2,1)S(1)}, bf16[128,2304]{1,0:T(8,128)(2,1)S(1)}, u32[]{:S(2)}, u32[]{:S(2)}) collective-permute-start(bf16[128,2304]{1,0:T(8,128)(2,1)S(1)} %get-tuple-element.108), channel_id=1, source_target_pairs={{0,4},{4,0},{1,5},{5,1},{2,6},{6,2},{3,7},{7,3},{8,12},{12,8},{9,1... | collective-permute-start | bytes 1769480 | tf_op jit(solution)/shard_map/ppermute | solution.py:449
  331.8 9.5 %collective-permute-start.33 = (bf16[64,2304]{1,0:T(8,128)(2,1)S(1)}, bf16[64,2304]{1,0:T(8,128)(2,1)S(1)}, u32[]{:S(2)}, u32[]{:S(2)}) collective-permute-start(bf16[64,2304]{1,0:T(8,128)(2,1)S(1)} %get-tuple-element.123), channel_id=1, source_target_pairs={{0,8},{8,0},{1,9},{9,1},{2,10},{10,2},{3,11},{11,3},{4,12},{12,4},... | collective-permute-start | bytes 884744 | tf_op jit(solution)/shard_map/ppermute | solution.py:449
  345.9 35.3 %collective-permute-start.38 = (bf16[128,2304]{1,0:T(8,128)(2,1)S(1)}, bf16[128,2304]{1,0:T(8,128)(2,1)S(1)}, u32[]{:S(2)}, u32[]{:S(2)}) collective-permute-start(bf16[128,2304]{1,0:T(8,128)(2,1)S(1)} %collective-permute-done.34), channel_id=1, source_target_pairs={{0,4},{4,0},{1,5},{5,1},{2,6},{6,2},{3,7},{7,3},{8,12},{12,8},{9,1... | collective-permute-start | bytes 1769480 | tf_op jit(solution)/shard_map/ppermute | solution.py:449
  404.8 10.4 %collective-permute-start.41 = (bf16[512,2304]{1,0:T(8,128)(2,1)S(1)}, bf16[512,2304]{1,0:T(8,128)(2,1)S(1)}, u32[]{:S(2)}, u32[]{:S(2)}) collective-permute-start(bf16[512,2304]{1,0:T(8,128)(2,1)S(1)} %convolution_convert_fusion.6), channel_id=1, source_target_pairs={{0,4},{4,0},{1,5},{5,1},{2,6},{6,2},{3,7},{7,3},{8,12},{12,8},{9,1... | collective-permute-start | bytes 7077896 | tf_op jit(solution)/shard_map/ppermute | solution.py:449
  427.1 250.6 %reduce-scatter.5.cloned.1.call-start = ((), (), s32[]{:S(2)}) async-start(), calls=%async_computation.7 | async-start | bytes 13271040 | tf_op jit(solution)/shard_map/reduce_scatter | solution.py:666
  429.8 21.8 %collective-permute-start.44 = (bf16[128,2304]{1,0:T(8,128)(2,1)}, bf16[128,2304]{1,0:T(8,128)(2,1)}, u32[]{:S(2)}, u32[]{:S(2)}) collective-permute-start(bf16[128,2304]{1,0:T(8,128)(2,1)} %get-tuple-element.88), channel_id=1, source_target_pairs={{0,3},{1,0},{2,1},{3,2},{4,7},{5,4},{6,5},{7,6},{8,11},{9,8},{10,9... | collective-permute-start | bytes 1769480 | tf_op jit(solution)/shard_map/ppermute | solution.py:594
  429.8 31.3 %collective-permute-start.43 = (bf16[128,2304]{1,0:T(8,128)(2,1)}, bf16[128,2304]{1,0:T(8,128)(2,1)}, u32[]{:S(2)}, u32[]{:S(2)}) collective-permute-start(bf16[128,2304]{1,0:T(8,128)(2,1)} %get-tuple-element.89), channel_id=1, source_target_pairs={{0,1},{1,2},{2,3},{3,0},{4,5},{5,6},{6,7},{7,4},{8,9},{9,10},{10,1... | collective-permute-start | bytes 1769480 | tf_op jit(solution)/shard_map/ppermute | solution.py:594
  431.9 52.7 %collective-permute-start.42 = (bf16[128,2304]{1,0:T(8,128)(2,1)}, bf16[128,2304]{1,0:T(8,128)(2,1)}, u32[]{:S(2)}, u32[]{:S(2)}) collective-permute-start(bf16[128,2304]{1,0:T(8,128)(2,1)} %get-tuple-element.87), channel_id=1, source_target_pairs={{0,2},{1,3},{2,0},{3,1},{4,6},{5,7},{6,4},{7,5},{8,10},{9,11},{10,... | collective-permute-start | bytes 1769480 | tf_op jit(solution)/shard_map/ppermute | solution.py:594
  490.8 16.9 %collective-permute-start.45 = (bf16[128,2304]{1,0:T(8,128)(2,1)S(1)}, bf16[128,2304]{1,0:T(8,128)(2,1)}, u32[]{:S(2)}, u32[]{:S(2)}) collective-permute-start(bf16[128,2304]{1,0:T(8,128)(2,1)S(1)} %get-tuple-element.60), channel_id=1, source_target_pairs={{0,3},{1,0},{2,1},{3,2},{4,7},{5,4},{6,5},{7,6},{8,11},{9,8},{10,9... | collective-permute-start | bytes 1769480 | tf_op jit(solution)/shard_map/ppermute | solution.py:594
  491.9 49.8 %collective-permute-start.46 = (bf16[128,2304]{1,0:T(8,128)(2,1)S(1)}, bf16[128,2304]{1,0:T(8,128)(2,1)S(1)}, u32[]{:S(2)}, u32[]{:S(2)}) collective-permute-start(bf16[128,2304]{1,0:T(8,128)(2,1)S(1)} %get-tuple-element.60), channel_id=1, source_target_pairs={{0,2},{1,3},{2,0},{3,1},{4,6},{5,7},{6,4},{7,5},{8,10},{9,11},{10,... | collective-permute-start | bytes 1769480 | tf_op jit(solution)/shard_map/ppermute | solution.py:594
  492.0 49.8 %collective-permute-start.47 = (bf16[128,2304]{1,0:T(8,128)(2,1)S(1)}, bf16[128,2304]{1,0:T(8,128)(2,1)S(1)}, u32[]{:S(2)}, u32[]{:S(2)}) collective-permute-start(bf16[128,2304]{1,0:T(8,128)(2,1)S(1)} %get-tuple-element.60), channel_id=1, source_target_pairs={{0,1},{1,2},{2,3},{3,0},{4,5},{5,6},{6,7},{7,4},{8,9},{9,10},{10,1... | collective-permute-start | bytes 1769480 | tf_op jit(solution)/shard_map/ppermute | solution.py:594
  492.9 51.2 %collective-permute-start.48 = (bf16[128,2304]{1,0:T(8,128)(2,1)S(1)}, bf16[128,2304]{1,0:T(8,128)(2,1)S(1)}, u32[]{:S(2)}, u32[]{:S(2)}) collective-permute-start(bf16[128,2304]{1,0:T(8,128)(2,1)S(1)} %get-tuple-element.60), channel_id=1, source_target_pairs={{0,4},{4,0},{1,5},{5,1},{2,6},{6,2},{3,7},{7,3},{8,12},{12,8},{9,1... | collective-permute-start | bytes 1769480 | tf_op jit(solution)/shard_map/ppermute | solution.py:449
  507.7 37.3 %collective-permute-start.49 = (bf16[128,2304]{1,0:T(8,128)(2,1)}, bf16[128,2304]{1,0:T(8,128)(2,1)S(1)}, u32[]{:S(2)}, u32[]{:S(2)}) collective-permute-start(bf16[128,2304]{1,0:T(8,128)(2,1)} %collective-permute-done.45), channel_id=1, source_target_pairs={{0,4},{4,0},{1,5},{5,1},{2,6},{6,2},{3,7},{7,3},{8,12},{12,8},{9,1... | collective-permute-start | bytes 1769480 | tf_op jit(solution)/shard_map/ppermute | solution.py:449
  541.8 4.9 collective-permute-start.51
  572.4 4.9 collective-permute-start.53
  581.5 28.2 %collective-permute-start.56 = (bf16[128,2304]{1,0:T(8,128)(2,1)}, bf16[128,2304]{1,0:T(8,128)(2,1)S(1)}, u32[]{:S(2)}, u32[]{:S(2)}) collective-permute-start(bf16[128,2304]{1,0:T(8,128)(2,1)} %get-tuple-element.85), channel_id=1, source_target_pairs={{0,3},{1,0},{2,1},{3,2},{4,7},{5,4},{6,5},{7,6},{8,11},{9,8},{10,9... | collective-permute-start | bytes 1769480 | tf_op jit(solution)/shard_map/ppermute | solution.py:594
  581.5 31.9 %collective-permute-start.55 = (bf16[128,2304]{1,0:T(8,128)(2,1)}, bf16[128,2304]{1,0:T(8,128)(2,1)}, u32[]{:S(2)}, u32[]{:S(2)}) collective-permute-start(bf16[128,2304]{1,0:T(8,128)(2,1)} %get-tuple-element.86), channel_id=1, source_target_pairs={{0,1},{1,2},{2,3},{3,0},{4,5},{5,6},{6,7},{7,4},{8,9},{9,10},{10,1... | collective-permute-start | bytes 1769480 | tf_op jit(solution)/shard_map/ppermute | solution.py:594
  583.5 53.4 %collective-permute-start.54 = (bf16[128,2304]{1,0:T(8,128)(2,1)}, bf16[128,2304]{1,0:T(8,128)(2,1)}, u32[]{:S(2)}, u32[]{:S(2)}) collective-permute-start(bf16[128,2304]{1,0:T(8,128)(2,1)} %get-tuple-element.84), channel_id=1, source_target_pairs={{0,2},{1,3},{2,0},{3,1},{4,6},{5,7},{6,4},{7,5},{8,10},{9,11},{10,... | collective-permute-start | bytes 1769480 | tf_op jit(solution)/shard_map/ppermute | solution.py:594
  601.7 37.8 %collective-permute-start.57 = (bf16[2,288,768]{2,1,0:T(8,128)(2,1)S(1)}, bf16[2,288,768]{2,1,0:T(8,128)(2,1)S(1)}, u32[]{:S(2)}, u32[]{:S(2)}) collective-permute-start(bf16[2,288,768]{2,1,0:T(8,128)(2,1)S(1)} %slice_bitcast_fusion.1), channel_id=1, source_target_pairs={{0,16},{16,0},{1,17},{17,1},{2,18},{18,2},{3,19},{19,3},{4,20},{20... | collective-permute-start | bytes 2654216 | tf_op jit(solution)/shard_map/ppermute | solution.py:449
  602.6 36.9 %collective-permute-start.58 = (bf16[2,288,768]{2,1,0:T(8,128)(2,1)S(1)}, bf16[2,288,768]{2,1,0:T(8,128)(2,1)S(1)}, u32[]{:S(2)}, u32[]{:S(2)}) collective-permute-start(bf16[2,288,768]{2,1,0:T(8,128)(2,1)S(1)} %slice_bitcast_fusion), channel_id=1, source_target_pairs={{0,8},{8,0},{1,9},{9,1},{2,10},{10,2},{3,11},{11,3},{4,12},{12,4},... | collective-permute-start | bytes 2654216 | tf_op jit(solution)/shard_map/ppermute | solution.py:449
  641.0 16.7 %collective-permute-start.60 = (bf16[288,768]{1,0:T(8,128)(2,1)}, bf16[288,768]{1,0:T(8,128)(2,1)}, u32[]{:S(2)}, u32[]{:S(2)}) collective-permute-start(bf16[288,768]{1,0:T(8,128)(2,1)} %get-tuple-element.79), channel_id=1, source_target_pairs={{0,8},{8,0},{1,9},{9,1},{2,10},{10,2},{3,11},{11,3},{4,12},{12,4},... | collective-permute-start | bytes 1327112 | tf_op jit(solution)/shard_map/ppermute | solution.py:449
  641.9 15.7 %collective-permute-start.61 = (bf16[288,768]{1,0:T(8,128)(2,1)}, bf16[288,768]{1,0:T(8,128)(2,1)}, u32[]{:S(2)}, u32[]{:S(2)}) collective-permute-start(bf16[288,768]{1,0:T(8,128)(2,1)} %get-tuple-element.78), channel_id=1, source_target_pairs={{0,16},{16,0},{1,17},{17,1},{2,18},{18,2},{3,19},{19,3},{4,20},{20... | collective-permute-start | bytes 1327112 | tf_op jit(solution)/shard_map/ppermute | solution.py:449
  646.0 10.8 %all-to-all-start = ((f32[32,4,72]{2,1,0:T(4,128)}), f32[32,4,72]{2,1,0:T(4,128)}, u32[]{:S(2)}, u32[]{:S(2)}) async-start(f32[32,4,72]{2,1,0:T(4,128)} %copy.79), calls=%async_computation.2 | async-start | bytes 131072 | tf_op jit(solution)/shard_map/all_to_all | solution.py:835
  654.1 9.3 %collective-permute-start.59 = (bf16[64,2304]{1,0:T(8,128)(2,1)}, bf16[64,2304]{1,0:T(8,128)(2,1)}, u32[]{:S(2)}, u32[]{:S(2)}) collective-permute-start(bf16[64,2304]{1,0:T(8,128)(2,1)} %get-tuple-element.121), channel_id=1, source_target_pairs={{0,8},{8,0},{1,9},{9,1},{2,10},{10,2},{3,11},{11,3},{4,12},{12,4},... | collective-permute-start | bytes 884744 | tf_op jit(solution)/shard_map/ppermute | solution.py:449
  659.5 6.0 collective-permute-start.62
  667.3 6.6 collective-permute-start.63
  671.0 6.6 collective-permute-start.64
  671.0 6.6 collective-permute-start.65
  679.7 5.5 collective-permute-start.67
  682.2 6.1 collective-permute-start.66
  (109 other events, 1437.3 us)
Sparse Core Ops, SparseCore 0:
  28.8 52.4 all-gather.3
  83.7 104.9 all-gather.5
  190.6 61.9 all-gather.7
  427.2 61.3 reduce-scatter.2
  493.0 104.2 reduce-scatter.4

commit v4 on v3

--- a/solution.py
+++ b/solution.py
@@ -596,16 +596,46 @@
 
 def gather_rows(local_rows):
     size = lax.axis_size("seq")
-    got = {step: shift(local_rows, step) for step in (2, 1, 3)}
+    got = {step: shift(local_rows, step) for step in (3, 1, 2)}
     pieces = [local_rows] + [got[size - ahead] for ahead in range(1, size)]
     return jnp.concatenate(pieces + [flip(piece, "core") for piece in pieces])
 
 
+def join_kernel(whole, out, held, sem):
+    c, z = lax.axis_index("core"), lax.axis_index("seq")
+    size, rows = whole.shape[0] // 2, whole.shape[1]
+    loads = []
+    for i in range(2 * size):
+        owner = (c if i < size else 1 - c) * size + lax.rem(z + i % size, size)
+        target = held.at[pl.ds(i * rows, rows)]
+        loads.append(pltpu.make_async_copy(whole.at[owner], target, sem.at[i]))
+    for load in loads:
+        load.start()
+    for load in loads:
+        load.wait()
+    store = pltpu.make_async_copy(held, out, sem.at[2 * size])
+    store.start()
+    store.wait()
+
+
 def gather_first(local_rows):
-    c, z, size = lax.axis_index("core"), lax.axis_index("seq"), lax.axis_size("seq")
     whole = lax.all_gather(local_rows, ("core", "seq"), axis=0)
-    order = [(core, ahead) for core in (c, 1 - c) for ahead in range(size)]
-    return jnp.concatenate([pick(whole, core * size + lax.rem(z + i, size)) for core, i in order])
+    shape, low = (whole.shape[0] * whole.shape[1], whole.shape[2]), whole.dtype
+    size = whole.size * low.itemsize
+    anywhere = pl.BlockSpec(memory_space=pl.ANY)
+    return pl.pallas_call(
+        join_kernel,
+        out_shape=jax.ShapeDtypeStruct(shape, low),
+        in_specs=[anywhere],
+        out_specs=anywhere,
+        scratch_shapes=[
+            pltpu.VMEM(shape, low),
+            pltpu.SemaphoreType.DMA((whole.shape[0] + 1,)),
+        ],
+        compiler_params=pltpu.CompilerParams(vmem_limit_bytes=size + (2 << 20)),
+        cost_estimate=pl.CostEstimate(flops=0, bytes_accessed=2 * size, transcendentals=0),
+        name="join_rows",
+    )(whole)
 
 
 def row_tokens(rows, length):
@@ -647,7 +677,7 @@
 def scatter_rows(sums):
     size = lax.axis_size("seq")
     parts = sums.reshape(size, -1, sums.shape[-1])
-    got = [shift(parts[step], step) for step in (2, 1, 3)]
+    got = [shift(parts[step], step) for step in (3, 1, 2)]
     return total(parts[0], *got)
 
 
@@ -738,7 +768,7 @@
         [attn_begun], [((0, 0, 0, split), (1, split, 0, HEAD_SIZE))], (split, HEAD_SIZE)
     )
     gate_up_rows = chip_rows((gate_weight, 0, ffn_cols), (up_weight, 0, ffn_cols))
-    gate_up_weight = gather_chips(after(gate_up_rows, attn_begun[:3]))
+    gate_up_weight = gather_chips(gate_up_rows)
     down_back = gather_chips(chip_rows((down_weight.T, 0, ffn_cols)))
     grad_top = trade_sequences(after(cotangent, attn_begun))
 
@@ -779,7 +809,7 @@
     unused, pull_act = jax.vjp(geglu, gate, upper)
     grad_gate_act, grad_up_act = pull_act(grad_hidden)
     grad_gate_up = jnp.concatenate([grad_gate_act.astype(low), grad_up_act.astype(low)], axis=1)
-    normed_two_core = core_rows(grad_gate_up, gate_up_weight, (1, 1))
+    normed_two_core = core_sums(dot(grad_gate_up, gate_up_weight, (1, 1)).astype(low))
     grad_normed_two = scatter_rows(normed_two_core)
     late = after((hidden, block_two), normed_two_core)
     grad_down = dot(grad_feed_rows, late[0], (0, 0)).astype(low)
@@ -829,7 +859,7 @@
     (grad_g_one,) = pull_gain(normed_one_part.astype(jnp.float32))
     everyone = ("dp", "cy", "core", "seq")
     gain_grads = jnp.stack([grad_g_one, grad_g_two, grad_g_three, grad_g_four], axis=0)
-    gain_grads = after(gain_grads, grad_normed_one)
+    gain_grads = after(gain_grads, grad_normed_one, attn_grad_begun)
     gain_parts = gain_grads.reshape(4, lax.axis_size(everyone), -1).transpose(1, 0, 2)
     gain_out = jnp.sum(
         lax.all_to_all(gain_parts, everyone, split_axis=0, concat_axis=0, tiled=True), axis=0

time: 704 us -> 690 us (0.980)
  starting transfers between devices: 62.5 us -> 118 us
  waiting for transfers between devices: 355 us -> 305 us
  other arithmetic: 78.6 us -> 65.2 us
    ppermute x21, waiting for transfers between devices: 289 us -> 222 us  [shift(): lax.ppermute(value, 'seq', [(i, (i + step) % size) for i in range(size)])]
    ppermute x21, starting transfers between devices: 27 us -> 81.1 us  [shift(): lax.ppermute(value, 'seq', [(i, (i + step) % size) for i in range(size)])]
    ppermute x41, waiting for transfers between devices: 58.5 us -> 69.5 us  [flip(): return lax.ppermute(value, axis, [(0, 1), (1, 0)])]
    unnamed x239 -> x230, local copies, waits for them, and re-layouts: 36.8 us -> 32.6 us
    dot_general x21 -> x20, matrix products: 107 us -> 105 us  [dot(): lax.dot_general(left, right, ((dims[:1], dims[1:]), ((), ())), preferred_...]
  transfers between devices with their start and end apart: 74 -> 74, of which waited for: 35 -> 32; matrix products, arithmetic and copies ran while one was open for 28% -> 25% of each run, Pallas kernels for 0% -> 0%
where the time goes in v4:
time: 690 us; the launch traced here: 686 us
  waiting for transfers between devices  305 us (44%)
  starting transfers between devices  118 us (17%)
  matrix products  105 us (15%)
  local copies, waits for them, and re-layouts  72.9 us (11%)
  other arithmetic  65.2 us (9%)
  between operations  16.2 us (2%)
    ppermute x21, waiting for transfers between devices, shift(): lax.ppermute(value, 'seq', [(i, (i + step) % size) for i in range(size)])  222 us
    dot_general x20, matrix products, dot(): lax.dot_general(left, right, ((dims[:1], dims[1:]), ((), ())), preferred_...  105 us
    ppermute x21, starting transfers between devices, shift(): lax.ppermute(value, 'seq', [(i, (i + step) % size) for i in range(size)])  81.1 us
    ppermute x41, waiting for transfers between devices, flip(): return lax.ppermute(value, axis, [(0, 1), (1, 0)])  69.5 us
    unnamed x230, local copies, waits for them, and re-layouts  32.6 us
    ppermute x41, starting transfers between devices, flip(): return lax.ppermute(value, axis, [(0, 1), (1, 0)])  20.9 us
  transfers between devices with their start and end apart: 74, of which 32 were waited for; matrix products, arithmetic and copies ran while one was open for 25% of the time, Pallas kernels for 0%

profile of v4, /device:TPU:0, one launch (start us, length us, event | category | flops | bytes accessed | tf_op | source)
XLA Modules:
  0.0 685.6 jit_solution(10594170456397407104)
XLA Ops:
  10.1 5.1 collective-permute-start.1
  19.3 3.1 collective-permute-done.2
  23.1 2.5 collective-permute-done
  28.4 3.1 collective-permute-done.26
  31.5 3.3 maximum_select_fusion
  44.9 18.2 %collective-permute-done.10.refs_1_ = bf16[2,288,768]{2,1,0:T(8,128)(2,1)S(1)} collective-permute-done((bf16[2,288,768]{2,1,0:T(8,128)(2,1)S(1)}, bf16[2,288,768]{2,1,0:T(8,128)(2,1)S(1)}, u32[]{:S(2)}, u32[]{:S(2)}) %collective-permute-start.10) | collective-permute-done | bytes 884768 | tf_op jit(solution)/shard_map/ppermute | solution.py:449
  68.3 7.8 %collective-permute-done.8 = bf16[4,2,2,288]{3,0,2,1:T(4,128)(2,1)S(1)} collective-permute-done((bf16[4,2,2,288]{3,0,2,1:T(4,128)(2,1)S(1)}, bf16[4,2,2,288]{3,0,2,1:T(4,128)(2,1)S(1)}, u32[]{:S(2)}, u32[]{:S(2)}) %collective-permute-start.8) | collective-permute-done | bytes 9248 | tf_op jit(solution)/shard_map/ppermute | solution.py:449
  82.6 2.3 copy-done.1
  89.0 2.2 copy-done.5
  91.2 2.6 fusion.129
  93.8 2.5 fusion.61
  99.9 2.2 fusion.13
  102.2 2.1 fusion.26
  107.0 2.8 collective-permute-done.15
  113.0 2.2 collective-permute-start.18
  116.7 2.4 collective-permute-start.16
  120.0 2.7 maximum_select_fusion.1
  122.8 32.9 %collective-permute-done.18 = bf16[128,2304]{1,0:T(8,128)(2,1)} collective-permute-done((bf16[128,2304]{1,0:T(8,128)(2,1)}, bf16[128,2304]{1,0:T(8,128)(2,1)}, u32[]{:S(2)}, u32[]{:S(2)}) %collective-permute-start.18) | collective-permute-done | bytes 589856 | tf_op jit(solution)/shard_map/ppermute | solution.py:594
  159.3 2.6 collective-permute-start.19
  161.9 24.1 %collective-permute-start.20 = (bf16[128,2304]{1,0:T(8,128)(2,1)S(1)}, bf16[128,2304]{1,0:T(8,128)(2,1)S(1)}, u32[]{:S(2)}, u32[]{:S(2)}) collective-permute-start(bf16[128,2304]{1,0:T(8,128)(2,1)S(1)} %get-tuple-element.63), channel_id=1, source_target_pairs={{0,2},{1,3},{2,0},{3,1},{4,6},{5,7},{6,4},{7,5},{8,10},{9,11},{10,... | collective-permute-start | bytes 1769480 | tf_op jit(solution)/shard_map/ppermute | solution.py:594
  188.0 9.6 %collective-permute-done.19 = bf16[128,2304]{1,0:T(8,128)(2,1)S(1)} collective-permute-done((bf16[128,2304]{1,0:T(8,128)(2,1)S(1)}, bf16[128,2304]{1,0:T(8,128)(2,1)S(1)}, u32[]{:S(2)}, u32[]{:S(2)}) %collective-permute-start.19) | collective-permute-done | bytes 589856 | tf_op jit(solution)/shard_map/ppermute | solution.py:594
  197.6 39.8 %collective-permute-done.20 = bf16[128,2304]{1,0:T(8,128)(2,1)S(1)} collective-permute-done((bf16[128,2304]{1,0:T(8,128)(2,1)S(1)}, bf16[128,2304]{1,0:T(8,128)(2,1)S(1)}, u32[]{:S(2)}, u32[]{:S(2)}) %collective-permute-start.20) | collective-permute-done | bytes 589856 | tf_op jit(solution)/shard_map/ppermute | solution.py:594
  244.0 15.1 %fusion.130 = f32[1024,2304]{1,0:T(8,128)S(1)} fusion(bf16[1024,2304]{1,0:T(8,128)(2,1)} %constant_dynamic-update-slice_fusion.9, bf16[2304,2304]{1,0:T(8,128)(2,1)} %all-gather.6.cloned.1.call-done), kind=kOutput, calls=%fused_computation.358 | convolution fusion | flops 10871635968 | bytes 24772608 | tf_op jit(solution)/shard_map/dot_general | solution.py:708
  259.1 3.6 copy-done.18
  262.7 2.7 multiply_convert_fusion.1
  265.4 6.3 convolution_convert_fusion.4
  274.1 3.5 convolution_convert_fusion.5
  280.9 3.8 collective-permute-start.29
  287.4 23.5 %collective-permute-done.31 = bf16[128,2304]{1,0:T(8,128)(2,1)} collective-permute-done((bf16[128,2304]{1,0:T(8,128)(2,1)}, bf16[128,2304]{1,0:T(8,128)(2,1)}, u32[]{:S(2)}, u32[]{:S(2)}) %collective-permute-start.31) | collective-permute-done | bytes 589856 | tf_op jit(solution)/shard_map/ppermute | solution.py:594
  310.9 11.9 %collective-permute-done.29 = bf16[128,2304]{1,0:T(8,128)(2,1)} collective-permute-done((bf16[128,2304]{1,0:T(8,128)(2,1)}, bf16[128,2304]{1,0:T(8,128)(2,1)}, u32[]{:S(2)}, u32[]{:S(2)}) %collective-permute-start.29) | collective-permute-done | bytes 589856 | tf_op jit(solution)/shard_map/ppermute | solution.py:594
  322.8 2.2 multiply_reduce_fusion.5
  329.3 8.9 %collective-permute-done.33 = bf16[64,2304]{1,0:T(8,128)(2,1)S(1)} collective-permute-done((bf16[64,2304]{1,0:T(8,128)(2,1)S(1)}, bf16[64,2304]{1,0:T(8,128)(2,1)S(1)}, u32[]{:S(2)}, u32[]{:S(2)}) %collective-permute-start.33) | collective-permute-done | bytes 294944 | tf_op jit(solution)/shard_map/ppermute | solution.py:449
  339.1 3.5 collective-permute-done.34
  342.6 36.6 %collective-permute-done.35 = bf16[128,2304]{1,0:T(8,128)(2,1)S(1)} collective-permute-done((bf16[128,2304]{1,0:T(8,128)(2,1)S(1)}, bf16[128,2304]{1,0:T(8,128)(2,1)S(1)}, u32[]{:S(2)}, u32[]{:S(2)}) %collective-permute-start.35) | collective-permute-done | bytes 589856 | tf_op jit(solution)/shard_map/ppermute | solution.py:594
  382.1 10.5 %fusion.12 = (bf16[1024,1152]{1,0:T(8,128)(2,1)S(1)}, bf16[1024,1152]{1,0:T(8,128)(2,1)}) fusion(f32[1024,2304]{1,0:T(8,128)S(1)} %bitcast.239, bf16[1024,2304]{1,0:T(8,128)(2,1)S(1)} %constant_dynamic-update-slice_fusion.17, bf16[2304,1152]{1,0:T(8,128)(2,1)S(1)} %bitcast.278), kind=kOutput, calls=%fused_computation.22 | convolution fusion | flops 5464129536 | bytes 24182784 | tf_op jit(solution)/shard_map/dot_general | solution.py:708
  392.6 15.2 %convolution_convert_fusion.3 = bf16[1024,2304]{1,0:T(8,128)(2,1)S(1)} fusion(bf16[2304,2304]{1,0:T(8,128)(2,1)} %all-gather.6.cloned.1.call-done, bf16[1024,1152]{1,0:T(8,128)(2,1)} %get-tuple-element.73, bf16[1024,1152]{1,0:T(8,128)(2,1)S(1)} %get-tuple-element.72), kind=kOutput, calls=%fused_computation.15 | convolution fusion | flops 10883432448 | bytes 20054016 | tf_op jit(solution)/shard_map/dot_general | solution.py:708
  408.3 4.4 collective-permute-done.41
  414.7 8.0 %convolution_convert_fusion.1 = bf16[2304,1152]{1,0:T(8,128)(2,1)} fusion(bf16[1024,2304]{1,0:T(8,128)(2,1)S(1)} %constant_dynamic-update-slice_fusion.17, bf16[1024,1152]{1,0:T(8,128)(2,1)S(1)} %copy-done.22), kind=kOutput, calls=%fused_computation.5 | convolution fusion | flops 5438472192 | bytes 12386304 | tf_op jit(solution)/shard_map/dot_general | solution.py:708
  422.8 2.8 fusion.120
  426.9 3.8 collective-permute-start.42
  430.7 16.4 %convolution_convert_fusion = bf16[2304,2304]{1,0:T(8,128)(2,1)} fusion(bf16[1024,2304]{1,0:T(8,128)(2,1)} %constant_dynamic-update-slice_fusion.9, bf16[1024,1152]{1,0:T(8,128)(2,1)} %get-tuple-element.73, bf16[1024,1152]{1,0:T(8,128)(2,1)S(1)} %copy-done.88), kind=kOutput, calls=%fused_computation | convolution fusion | flops 10886381568 | bytes 20054016 | tf_op jit(solution)/shard_map/dot_general | solution.py:708
  447.2 19.2 %collective-permute-done.44 = bf16[128,2304]{1,0:T(8,128)(2,1)} collective-permute-done((bf16[128,2304]{1,0:T(8,128)(2,1)}, bf16[128,2304]{1,0:T(8,128)(2,1)}, u32[]{:S(2)}, u32[]{:S(2)}) %collective-permute-start.44) | collective-permute-done | bytes 589856 | tf_op jit(solution)/shard_map/ppermute | solution.py:594
  475.3 27.5 %collective-permute-start.46 = (bf16[128,2304]{1,0:T(8,128)(2,1)S(1)}, bf16[128,2304]{1,0:T(8,128)(2,1)S(1)}, u32[]{:S(2)}, u32[]{:S(2)}) collective-permute-start(bf16[128,2304]{1,0:T(8,128)(2,1)S(1)} %get-tuple-element.58), channel_id=1, source_target_pairs={{0,2},{1,3},{2,0},{3,1},{4,6},{5,7},{6,4},{7,5},{8,10},{9,11},{10,... | collective-permute-start | bytes 1769480 | tf_op jit(solution)/shard_map/ppermute | solution.py:594
  507.3 30.3 %collective-permute-done.46 = bf16[128,2304]{1,0:T(8,128)(2,1)S(1)} collective-permute-done((bf16[128,2304]{1,0:T(8,128)(2,1)S(1)}, bf16[128,2304]{1,0:T(8,128)(2,1)S(1)}, u32[]{:S(2)}, u32[]{:S(2)}) %collective-permute-start.46) | collective-permute-done | bytes 589856 | tf_op jit(solution)/shard_map/ppermute | solution.py:594
  543.4 4.2 convolution_convert_fusion.10
  549.7 2.8 multiply_convert_fusion.2
  554.5 2.4 fusion.69
  556.9 2.5 broadcast_select_fusion
  561.8 4.4 convolution_convert_fusion.2
  566.2 3.3 slice.317
  571.1 3.1 collective-permute-done.53
  574.2 3.1 add_convert_fusion
  578.6 3.8 collective-permute-start.54
  582.4 3.8 convolution_convert_fusion.9
  586.2 3.7 convolution_convert_fusion.6
  591.9 5.8 copy.75
  602.6 4.1 fusion.5
  606.8 8.2 %collective-permute-done.56 = bf16[128,2304]{1,0:T(8,128)(2,1)S(1)} collective-permute-done((bf16[128,2304]{1,0:T(8,128)(2,1)}, bf16[128,2304]{1,0:T(8,128)(2,1)S(1)}, u32[]{:S(2)}, u32[]{:S(2)}) %collective-permute-start.56) | collective-permute-done | bytes 589856 | tf_op jit(solution)/shard_map/ppermute | solution.py:594
  615.0 5.7 collective-permute-done.54
  629.1 8.7 %collective-permute-done.60 = bf16[288,768]{1,0:T(8,128)(2,1)S(1)} collective-permute-done((bf16[288,768]{1,0:T(8,128)(2,1)S(1)}, bf16[288,768]{1,0:T(8,128)(2,1)S(1)}, u32[]{:S(2)}, u32[]{:S(2)}) %collective-permute-start.60) | collective-permute-done | bytes 442400 | tf_op jit(solution)/shard_map/ppermute | solution.py:449
  639.0 6.2 all-to-all-start
  647.2 5.5 all-to-all-done
  659.9 4.1 collective-permute-done.64
  666.1 2.5 dynamic-slice_bitcast_fusion
  (513 shorter events, 145.9 us)
Async XLA Ops:
  7.2 75.4 %all-gather.4.cloned.1.call-start = ((), (), s32[]{:S(2)}) async-start(), calls=%async_computation.3 | async-start | bytes 5308416 | tf_op jit(solution)/shard_map/all_gather | solution.py:622
  10.1 9.1 %collective-permute-start.1 = (bf16[72,2,256]{2,1,0:T(2,128)(2,1)S(1)}, bf16[72,2,256]{2,1,0:T(2,128)(2,1)S(1)}, u32[]{:S(2)}, u32[]{:S(2)}) collective-permute-start(bf16[72,2,256]{2,1,0:T(2,128)(2,1)S(1)} %bitcast.266), channel_id=1, source_target_pairs={{0,3},{1,0},{2,1},{3,2},{4,7},{5,4},{6,5},{7,6},{8,11},{9,8},{10,9... | collective-permute-start | bytes 221192 | tf_op jit(solution)/shard_map/ppermute | solution.py:587
  15.3 7.1 %collective-permute-start.2 = (bf16[72,2,256]{2,1,0:T(2,128)(2,1)S(1)}, bf16[72,2,256]{2,1,0:T(2,128)(2,1)S(1)}, u32[]{:S(2)}, u32[]{:S(2)}) collective-permute-start(bf16[72,2,256]{2,1,0:T(2,128)(2,1)S(1)} %bitcast.267), channel_id=1, source_target_pairs={{0,2},{1,3},{2,0},{3,1},{4,6},{5,7},{6,4},{7,5},{8,10},{9,11},{10,... | collective-permute-start | bytes 221192 | tf_op jit(solution)/shard_map/ppermute | solution.py:587
  15.5 7.0 %collective-permute-start.3 = (bf16[72,2,256]{2,1,0:T(2,128)(2,1)S(1)}, bf16[72,2,256]{2,1,0:T(2,128)(2,1)S(1)}, u32[]{:S(2)}, u32[]{:S(2)}) collective-permute-start(bf16[72,2,256]{2,1,0:T(2,128)(2,1)S(1)} %bitcast.268), channel_id=1, source_target_pairs={{0,1},{1,2},{2,3},{3,0},{4,5},{5,6},{6,7},{7,4},{8,9},{9,10},{10,1... | collective-permute-start | bytes 221192 | tf_op jit(solution)/shard_map/ppermute | solution.py:587
  17.6 8.0 %collective-permute-start = (bf16[64,2304]{1,0:T(8,128)(2,1)S(1)}, bf16[64,2304]{1,0:T(8,128)(2,1)S(1)}, u32[]{:S(2)}, u32[]{:S(2)}) collective-permute-start(bf16[64,2304]{1,0:T(8,128)(2,1)S(1)} %get-tuple-element.125), channel_id=1, source_target_pairs={{0,8},{8,0},{1,9},{9,1},{2,10},{10,2},{3,11},{11,3},{4,12},{12,4},... | collective-permute-start | bytes 884744 | tf_op jit(solution)/shard_map/ppermute | solution.py:449
  26.5 217.5 %all-gather.6.cloned.1.call-start = ((), (), s32[]{:S(2)}) async-start(), calls=%async_computation.4 | async-start | bytes 13271040 | tf_op jit(solution)/shard_map/all_gather | solution.py:691
  34.8 230.5 %all-gather.8.cloned.1.call-start = ((), (), s32[]{:S(2)}) async-start(), calls=%async_computation.5 | async-start | bytes 6635520 | tf_op jit(solution)/shard_map/all_gather | solution.py:691
  35.5 6.9 %collective-permute-start.6 = (bf16[4,288]{1,0:T(4,128)(2,1)S(1)}, bf16[4,288]{1,0:T(4,128)(2,1)S(1)}, u32[]{:S(2)}, u32[]{:S(2)}) collective-permute-start(bf16[4,288]{1,0:T(4,128)(2,1)S(1)} %pad_maximum_fusion.19), channel_id=1, source_target_pairs={{0,4},{4,0},{1,5},{5,1},{2,6},{6,2},{3,7},{7,3},{8,12},{12,8},{9,1... | collective-permute-start | bytes 6920 | tf_op jit(solution)/shard_map/ppermute | solution.py:449
  40.9 22.2 %collective-permute-start.10 = (bf16[2,288,768]{2,1,0:T(8,128)(2,1)S(1)}, bf16[2,288,768]{2,1,0:T(8,128)(2,1)S(1)}, u32[]{:S(2)}, u32[]{:S(2)}) collective-permute-start(bf16[2,288,768]{2,1,0:T(8,128)(2,1)S(1)} %maximum_select_fusion.2.refs_0_), channel_id=1, source_target_pairs={{0,8},{8,0},{1,9},{9,1},{2,10},{10,2},{3,11},{11,3},{4,12},{12,4},... | collective-permute-start | bytes 2654216 | tf_op jit(solution)/shard_map/ppermute | solution.py:449
  42.5 22.8 %collective-permute-start.11 = (bf16[2,288,768]{2,1,0:T(8,128)(2,1)S(1)}, bf16[2,288,768]{2,1,0:T(8,128)(2,1)S(1)}, u32[]{:S(2)}, u32[]{:S(2)}) collective-permute-start(bf16[2,288,768]{2,1,0:T(8,128)(2,1)S(1)} %maximum_select_fusion.2.refs_0_), channel_id=1, source_target_pairs={{0,16},{16,0},{1,17},{17,1},{2,18},{18,2},{3,19},{19,3},{4,20},{20... | collective-permute-start | bytes 2654216 | tf_op jit(solution)/shard_map/ppermute | solution.py:449
  44.1 23.6 %collective-permute-start.7 = (bf16[4,2,288]{2,0,1:T(4,128)(2,1)S(1)}, bf16[4,2,288]{2,0,1:T(4,128)(2,1)S(1)}, u32[]{:S(2)}, u32[]{:S(2)}) collective-permute-start(bf16[4,2,288]{2,0,1:T(4,128)(2,1)S(1)} %maximum_select_fusion.11), channel_id=1, source_target_pairs={{0,8},{8,0},{1,9},{9,1},{2,10},{10,2},{3,11},{11,3},{4,12},{12,4},... | collective-permute-start | bytes 13832 | tf_op jit(solution)/shard_map/ppermute | solution.py:449
  63.9 13.1 %collective-permute-start.12 = (bf16[288,768]{1,0:T(8,128)(2,1)}, bf16[288,768]{1,0:T(8,128)(2,1)S(1)}, u32[]{:S(2)}, u32[]{:S(2)}) collective-permute-start(bf16[288,768]{1,0:T(8,128)(2,1)} %slice_bitcast_fusion.3), channel_id=1, source_target_pairs={{0,16},{16,0},{1,17},{17,1},{2,18},{18,2},{3,19},{19,3},{4,20},{20... | collective-permute-start | bytes 1327112 | tf_op jit(solution)/shard_map/ppermute | solution.py:449
  66.2 11.9 %collective-permute-start.13 = (bf16[288,768]{1,0:T(8,128)(2,1)}, bf16[288,768]{1,0:T(8,128)(2,1)}, u32[]{:S(2)}, u32[]{:S(2)}) collective-permute-start(bf16[288,768]{1,0:T(8,128)(2,1)} %slice_bitcast_fusion.2), channel_id=1, source_target_pairs={{0,8},{8,0},{1,9},{9,1},{2,10},{10,2},{3,11},{11,3},{4,12},{12,4},... | collective-permute-start | bytes 1327112 | tf_op jit(solution)/shard_map/ppermute | solution.py:449
  67.7 8.4 %collective-permute-start.8 = (bf16[4,2,2,288]{3,0,2,1:T(4,128)(2,1)S(1)}, bf16[4,2,2,288]{3,0,2,1:T(4,128)(2,1)S(1)}, u32[]{:S(2)}, u32[]{:S(2)}) collective-permute-start(bf16[4,2,2,288]{3,0,2,1:T(4,128)(2,1)S(1)} %maximum_select_fusion.9), channel_id=1, source_target_pairs={{0,16},{16,0},{1,17},{17,1},{2,18},{18,2},{3,19},{19,3},{4,20},{20... | collective-permute-start | bytes 27656 | tf_op jit(solution)/shard_map/ppermute | solution.py:449
  105.2 4.6 collective-permute-start.15
  106.0 13.1 %collective-permute-start.27 = (bf16[288,1152]{1,0:T(8,128)(2,1)S(1)}, bf16[288,1152]{1,0:T(8,128)(2,1)S(1)}, u32[]{:S(2)}, u32[]{:S(2)}) collective-permute-start(bf16[288,1152]{1,0:T(8,128)(2,1)S(1)} %get-tuple-element.105), channel_id=1, source_target_pairs={{0,4},{4,0},{1,5},{5,1},{2,6},{6,2},{3,7},{7,3},{8,12},{12,8},{9,1... | collective-permute-start | bytes 1990664 | tf_op jit(solution)/shard_map/ppermute | solution.py:449
  113.0 42.7 %collective-permute-start.18 = (bf16[128,2304]{1,0:T(8,128)(2,1)}, bf16[128,2304]{1,0:T(8,128)(2,1)}, u32[]{:S(2)}, u32[]{:S(2)}) collective-permute-start(bf16[128,2304]{1,0:T(8,128)(2,1)} %get-tuple-element.92), channel_id=1, source_target_pairs={{0,2},{1,3},{2,0},{3,1},{4,6},{5,7},{6,4},{7,5},{8,10},{9,11},{10,... | collective-permute-start | bytes 1769480 | tf_op jit(solution)/shard_map/ppermute | solution.py:594
  115.2 40.5 %collective-permute-start.17 = (bf16[128,2304]{1,0:T(8,128)(2,1)}, bf16[128,2304]{1,0:T(8,128)(2,1)}, u32[]{:S(2)}, u32[]{:S(2)}) collective-permute-start(bf16[128,2304]{1,0:T(8,128)(2,1)} %get-tuple-element.93), channel_id=1, source_target_pairs={{0,1},{1,2},{2,3},{3,0},{4,5},{5,6},{6,7},{7,4},{8,9},{9,10},{10,1... | collective-permute-start | bytes 1769480 | tf_op jit(solution)/shard_map/ppermute | solution.py:594
  116.7 39.0 %collective-permute-start.16 = (bf16[128,2304]{1,0:T(8,128)(2,1)}, bf16[128,2304]{1,0:T(8,128)(2,1)}, u32[]{:S(2)}, u32[]{:S(2)}) collective-permute-start(bf16[128,2304]{1,0:T(8,128)(2,1)} %get-tuple-element.91), channel_id=1, source_target_pairs={{0,3},{1,0},{2,1},{3,2},{4,7},{5,4},{6,5},{7,6},{8,11},{9,8},{10,9... | collective-permute-start | bytes 1769480 | tf_op jit(solution)/shard_map/ppermute | solution.py:594
  122.7 541.3 %reduce-scatter.3.cloned.1.call-start = ((), (), s32[]{:S(2)}) async-start(), calls=%async_computation.6 | async-start | bytes 6635520 | tf_op jit(solution)/shard_map/reduce_scatter | solution.py:696
  159.3 38.3 %collective-permute-start.19 = (bf16[128,2304]{1,0:T(8,128)(2,1)S(1)}, bf16[128,2304]{1,0:T(8,128)(2,1)S(1)}, u32[]{:S(2)}, u32[]{:S(2)}) collective-permute-start(bf16[128,2304]{1,0:T(8,128)(2,1)S(1)} %get-tuple-element.63), channel_id=1, source_target_pairs={{0,3},{1,0},{2,1},{3,2},{4,7},{5,4},{6,5},{7,6},{8,11},{9,8},{10,9... | collective-permute-start | bytes 1769480 | tf_op jit(solution)/shard_map/ppermute | solution.py:594
  161.9 75.5 %collective-permute-start.20 = (bf16[128,2304]{1,0:T(8,128)(2,1)S(1)}, bf16[128,2304]{1,0:T(8,128)(2,1)S(1)}, u32[]{:S(2)}, u32[]{:S(2)}) collective-permute-start(bf16[128,2304]{1,0:T(8,128)(2,1)S(1)} %get-tuple-element.63), channel_id=1, source_target_pairs={{0,2},{1,3},{2,0},{3,1},{4,6},{5,7},{6,4},{7,5},{8,10},{9,11},{10,... | collective-permute-start | bytes 1769480 | tf_op jit(solution)/shard_map/ppermute | solution.py:594
  186.0 51.4 %collective-permute-start.21 = (bf16[128,2304]{1,0:T(8,128)(2,1)S(1)}, bf16[128,2304]{1,0:T(8,128)(2,1)S(1)}, u32[]{:S(2)}, u32[]{:S(2)}) collective-permute-start(bf16[128,2304]{1,0:T(8,128)(2,1)S(1)} %get-tuple-element.63), channel_id=1, source_target_pairs={{0,1},{1,2},{2,3},{3,0},{4,5},{5,6},{6,7},{7,4},{8,9},{9,10},{10,1... | collective-permute-start | bytes 1769480 | tf_op jit(solution)/shard_map/ppermute | solution.py:594
  188.0 52.5 %collective-permute-start.22 = (bf16[128,2304]{1,0:T(8,128)(2,1)S(1)}, bf16[128,2304]{1,0:T(8,128)(2,1)S(1)}, u32[]{:S(2)}, u32[]{:S(2)}) collective-permute-start(bf16[128,2304]{1,0:T(8,128)(2,1)S(1)} %get-tuple-element.63), channel_id=1, source_target_pairs={{0,4},{4,0},{1,5},{5,1},{2,6},{6,2},{3,7},{7,3},{8,12},{12,8},{9,1... | collective-permute-start | bytes 1769480 | tf_op jit(solution)/shard_map/ppermute | solution.py:449
  197.6 43.8 %collective-permute-start.23 = (bf16[128,2304]{1,0:T(8,128)(2,1)S(1)}, bf16[128,2304]{1,0:T(8,128)(2,1)S(1)}, u32[]{:S(2)}, u32[]{:S(2)}) collective-permute-start(bf16[128,2304]{1,0:T(8,128)(2,1)S(1)} %collective-permute-done.19), channel_id=1, source_target_pairs={{0,4},{4,0},{1,5},{5,1},{2,6},{6,2},{3,7},{7,3},{8,12},{12,8},{9,1... | collective-permute-start | bytes 1769480 | tf_op jit(solution)/shard_map/ppermute | solution.py:449
  237.4 4.8 collective-permute-start.24
  237.4 5.7 collective-permute-start.25
  271.6 6.0 collective-permute-start.28
  272.6 12.8 %collective-permute-start.32 = (bf16[64,2304]{1,0:T(8,128)(2,1)}, bf16[64,2304]{1,0:T(8,128)(2,1)S(1)}, u32[]{:S(2)}, u32[]{:S(2)}) collective-permute-start(bf16[64,2304]{1,0:T(8,128)(2,1)} %get-tuple-element.123), channel_id=1, source_target_pairs={{0,8},{8,0},{1,9},{9,1},{2,10},{10,2},{3,11},{11,3},{4,12},{12,4},... | collective-permute-start | bytes 884744 | tf_op jit(solution)/shard_map/ppermute | solution.py:449
  280.8 30.1 %collective-permute-start.31 = (bf16[128,2304]{1,0:T(8,128)(2,1)}, bf16[128,2304]{1,0:T(8,128)(2,1)}, u32[]{:S(2)}, u32[]{:S(2)}) collective-permute-start(bf16[128,2304]{1,0:T(8,128)(2,1)} %get-tuple-element.89), channel_id=1, source_target_pairs={{0,2},{1,3},{2,0},{3,1},{4,6},{5,7},{6,4},{7,5},{8,10},{9,11},{10,... | collective-permute-start | bytes 1769480 | tf_op jit(solution)/shard_map/ppermute | solution.py:594
  280.9 30.1 %collective-permute-start.30 = (bf16[128,2304]{1,0:T(8,128)(2,1)}, bf16[128,2304]{1,0:T(8,128)(2,1)}, u32[]{:S(2)}, u32[]{:S(2)}) collective-permute-start(bf16[128,2304]{1,0:T(8,128)(2,1)} %get-tuple-element.90), channel_id=1, source_target_pairs={{0,1},{1,2},{2,3},{3,0},{4,5},{5,6},{6,7},{7,4},{8,9},{9,10},{10,1... | collective-permute-start | bytes 1769480 | tf_op jit(solution)/shard_map/ppermute | solution.py:594
  280.9 41.9 %collective-permute-start.29 = (bf16[128,2304]{1,0:T(8,128)(2,1)}, bf16[128,2304]{1,0:T(8,128)(2,1)}, u32[]{:S(2)}, u32[]{:S(2)}) collective-permute-start(bf16[128,2304]{1,0:T(8,128)(2,1)} %get-tuple-element.88), channel_id=1, source_target_pairs={{0,3},{1,0},{2,1},{3,2},{4,7},{5,4},{6,5},{7,6},{8,11},{9,8},{10,9... | collective-permute-start | bytes 1769480 | tf_op jit(solution)/shard_map/ppermute | solution.py:594
  326.6 16.1 %collective-permute-start.34 = (bf16[128,2304]{1,0:T(8,128)(2,1)S(1)}, bf16[128,2304]{1,0:T(8,128)(2,1)S(1)}, u32[]{:S(2)}, u32[]{:S(2)}) collective-permute-start(bf16[128,2304]{1,0:T(8,128)(2,1)S(1)} %get-tuple-element.106), channel_id=1, source_target_pairs={{0,3},{1,0},{2,1},{3,2},{4,7},{5,4},{6,5},{7,6},{8,11},{9,8},{10,9... | collective-permute-start | bytes 1769480 | tf_op jit(solution)/shard_map/ppermute | solution.py:594
  327.8 51.3 %collective-permute-start.35 = (bf16[128,2304]{1,0:T(8,128)(2,1)S(1)}, bf16[128,2304]{1,0:T(8,128)(2,1)S(1)}, u32[]{:S(2)}, u32[]{:S(2)}) collective-permute-start(bf16[128,2304]{1,0:T(8,128)(2,1)S(1)} %get-tuple-element.106), channel_id=1, source_target_pairs={{0,2},{1,3},{2,0},{3,1},{4,6},{5,7},{6,4},{7,5},{8,10},{9,11},{10,... | collective-permute-start | bytes 1769480 | tf_op jit(solution)/shard_map/ppermute | solution.py:594
  328.7 50.5 %collective-permute-start.36 = (bf16[128,2304]{1,0:T(8,128)(2,1)S(1)}, bf16[128,2304]{1,0:T(8,128)(2,1)S(1)}, u32[]{:S(2)}, u32[]{:S(2)}) collective-permute-start(bf16[128,2304]{1,0:T(8,128)(2,1)S(1)} %get-tuple-element.106), channel_id=1, source_target_pairs={{0,1},{1,2},{2,3},{3,0},{4,5},{5,6},{6,7},{7,4},{8,9},{9,10},{10,1... | collective-permute-start | bytes 1769480 | tf_op jit(solution)/shard_map/ppermute | solution.py:594
  328.7 51.2 %collective-permute-start.37 = (bf16[128,2304]{1,0:T(8,128)(2,1)S(1)}, bf16[128,2304]{1,0:T(8,128)(2,1)S(1)}, u32[]{:S(2)}, u32[]{:S(2)}) collective-permute-start(bf16[128,2304]{1,0:T(8,128)(2,1)S(1)} %get-tuple-element.106), channel_id=1, source_target_pairs={{0,4},{4,0},{1,5},{5,1},{2,6},{6,2},{3,7},{7,3},{8,12},{12,8},{9,1... | collective-permute-start | bytes 1769480 | tf_op jit(solution)/shard_map/ppermute | solution.py:449
  328.7 9.5 %collective-permute-start.33 = (bf16[64,2304]{1,0:T(8,128)(2,1)S(1)}, bf16[64,2304]{1,0:T(8,128)(2,1)S(1)}, u32[]{:S(2)}, u32[]{:S(2)}) collective-permute-start(bf16[64,2304]{1,0:T(8,128)(2,1)S(1)} %get-tuple-element.121), channel_id=1, source_target_pairs={{0,8},{8,0},{1,9},{9,1},{2,10},{10,2},{3,11},{11,3},{4,12},{12,4},... | collective-permute-start | bytes 884744 | tf_op jit(solution)/shard_map/ppermute | solution.py:449
  342.6 37.3 %collective-permute-start.38 = (bf16[128,2304]{1,0:T(8,128)(2,1)S(1)}, bf16[128,2304]{1,0:T(8,128)(2,1)S(1)}, u32[]{:S(2)}, u32[]{:S(2)}) collective-permute-start(bf16[128,2304]{1,0:T(8,128)(2,1)S(1)} %collective-permute-done.34), channel_id=1, source_target_pairs={{0,4},{4,0},{1,5},{5,1},{2,6},{6,2},{3,7},{7,3},{8,12},{12,8},{9,1... | collective-permute-start | bytes 1769480 | tf_op jit(solution)/shard_map/ppermute | solution.py:449
  422.7 241.3 %reduce-scatter.5.cloned.1.call-start = ((), (), s32[]{:S(2)}) async-start(), calls=%async_computation.7 | async-start | bytes 13271040 | tf_op jit(solution)/shard_map/reduce_scatter | solution.py:696
  425.6 40.8 %collective-permute-start.44 = (bf16[128,2304]{1,0:T(8,128)(2,1)}, bf16[128,2304]{1,0:T(8,128)(2,1)}, u32[]{:S(2)}, u32[]{:S(2)}) collective-permute-start(bf16[128,2304]{1,0:T(8,128)(2,1)} %get-tuple-element.86), channel_id=1, source_target_pairs={{0,2},{1,3},{2,0},{3,1},{4,6},{5,7},{6,4},{7,5},{8,10},{9,11},{10,... | collective-permute-start | bytes 1769480 | tf_op jit(solution)/shard_map/ppermute | solution.py:594
  426.9 39.5 %collective-permute-start.43 = (bf16[128,2304]{1,0:T(8,128)(2,1)}, bf16[128,2304]{1,0:T(8,128)(2,1)}, u32[]{:S(2)}, u32[]{:S(2)}) collective-permute-start(bf16[128,2304]{1,0:T(8,128)(2,1)} %get-tuple-element.87), channel_id=1, source_target_pairs={{0,1},{1,2},{2,3},{3,0},{4,5},{5,6},{6,7},{7,4},{8,9},{9,10},{10,1... | collective-permute-start | bytes 1769480 | tf_op jit(solution)/shard_map/ppermute | solution.py:594
  426.9 40.9 %collective-permute-start.42 = (bf16[128,2304]{1,0:T(8,128)(2,1)}, bf16[128,2304]{1,0:T(8,128)(2,1)}, u32[]{:S(2)}, u32[]{:S(2)}) collective-permute-start(bf16[128,2304]{1,0:T(8,128)(2,1)} %get-tuple-element.85), channel_id=1, source_target_pairs={{0,3},{1,0},{2,1},{3,2},{4,7},{5,4},{6,5},{7,6},{8,11},{9,8},{10,9... | collective-permute-start | bytes 1769480 | tf_op jit(solution)/shard_map/ppermute | solution.py:594
  473.2 31.7 %collective-permute-start.45 = (bf16[128,2304]{1,0:T(8,128)(2,1)S(1)}, bf16[128,2304]{1,0:T(8,128)(2,1)}, u32[]{:S(2)}, u32[]{:S(2)}) collective-permute-start(bf16[128,2304]{1,0:T(8,128)(2,1)S(1)} %get-tuple-element.58), channel_id=1, source_target_pairs={{0,3},{1,0},{2,1},{3,2},{4,7},{5,4},{6,5},{7,6},{8,11},{9,8},{10,9... | collective-permute-start | bytes 1769480 | tf_op jit(solution)/shard_map/ppermute | solution.py:594
  475.3 62.3 %collective-permute-start.46 = (bf16[128,2304]{1,0:T(8,128)(2,1)S(1)}, bf16[128,2304]{1,0:T(8,128)(2,1)S(1)}, u32[]{:S(2)}, u32[]{:S(2)}) collective-permute-start(bf16[128,2304]{1,0:T(8,128)(2,1)S(1)} %get-tuple-element.58), channel_id=1, source_target_pairs={{0,2},{1,3},{2,0},{3,1},{4,6},{5,7},{6,4},{7,5},{8,10},{9,11},{10,... | collective-permute-start | bytes 1769480 | tf_op jit(solution)/shard_map/ppermute | solution.py:594
  502.7 34.9 %collective-permute-start.47 = (bf16[128,2304]{1,0:T(8,128)(2,1)S(1)}, bf16[128,2304]{1,0:T(8,128)(2,1)S(1)}, u32[]{:S(2)}, u32[]{:S(2)}) collective-permute-start(bf16[128,2304]{1,0:T(8,128)(2,1)S(1)} %get-tuple-element.58), channel_id=1, source_target_pairs={{0,1},{1,2},{2,3},{3,0},{4,5},{5,6},{6,7},{7,4},{8,9},{9,10},{10,1... | collective-permute-start | bytes 1769480 | tf_op jit(solution)/shard_map/ppermute | solution.py:594
  504.8 35.1 %collective-permute-start.48 = (bf16[128,2304]{1,0:T(8,128)(2,1)S(1)}, bf16[128,2304]{1,0:T(8,128)(2,1)S(1)}, u32[]{:S(2)}, u32[]{:S(2)}) collective-permute-start(bf16[128,2304]{1,0:T(8,128)(2,1)S(1)} %get-tuple-element.58), channel_id=1, source_target_pairs={{0,4},{4,0},{1,5},{5,1},{2,6},{6,2},{3,7},{7,3},{8,12},{12,8},{9,1... | collective-permute-start | bytes 1769480 | tf_op jit(solution)/shard_map/ppermute | solution.py:449
  504.9 35.9 %collective-permute-start.49 = (bf16[128,2304]{1,0:T(8,128)(2,1)}, bf16[128,2304]{1,0:T(8,128)(2,1)S(1)}, u32[]{:S(2)}, u32[]{:S(2)}) collective-permute-start(bf16[128,2304]{1,0:T(8,128)(2,1)} %collective-permute-done.45), channel_id=1, source_target_pairs={{0,4},{4,0},{1,5},{5,1},{2,6},{6,2},{3,7},{7,3},{8,12},{12,8},{9,1... | collective-permute-start | bytes 1769480 | tf_op jit(solution)/shard_map/ppermute | solution.py:449
  537.6 4.9 collective-permute-start.51
  569.4 4.7 collective-permute-start.53
  578.5 36.4 %collective-permute-start.56 = (bf16[128,2304]{1,0:T(8,128)(2,1)}, bf16[128,2304]{1,0:T(8,128)(2,1)S(1)}, u32[]{:S(2)}, u32[]{:S(2)}) collective-permute-start(bf16[128,2304]{1,0:T(8,128)(2,1)} %get-tuple-element.83), channel_id=1, source_target_pairs={{0,2},{1,3},{2,0},{3,1},{4,6},{5,7},{6,4},{7,5},{8,10},{9,11},{10,... | collective-permute-start | bytes 1769480 | tf_op jit(solution)/shard_map/ppermute | solution.py:594
  578.5 36.4 %collective-permute-start.55 = (bf16[128,2304]{1,0:T(8,128)(2,1)}, bf16[128,2304]{1,0:T(8,128)(2,1)}, u32[]{:S(2)}, u32[]{:S(2)}) collective-permute-start(bf16[128,2304]{1,0:T(8,128)(2,1)} %get-tuple-element.84), channel_id=1, source_target_pairs={{0,1},{1,2},{2,3},{3,0},{4,5},{5,6},{6,7},{7,4},{8,9},{9,10},{10,1... | collective-permute-start | bytes 1769480 | tf_op jit(solution)/shard_map/ppermute | solution.py:594
  578.6 42.1 %collective-permute-start.54 = (bf16[128,2304]{1,0:T(8,128)(2,1)}, bf16[128,2304]{1,0:T(8,128)(2,1)}, u32[]{:S(2)}, u32[]{:S(2)}) collective-permute-start(bf16[128,2304]{1,0:T(8,128)(2,1)} %get-tuple-element.82), channel_id=1, source_target_pairs={{0,3},{1,0},{2,1},{3,2},{4,7},{5,4},{6,5},{7,6},{8,11},{9,8},{10,9... | collective-permute-start | bytes 1769480 | tf_op jit(solution)/shard_map/ppermute | solution.py:594
  599.6 24.9 %collective-permute-start.57 = (bf16[2,288,768]{2,1,0:T(8,128)(2,1)S(1)}, bf16[2,288,768]{2,1,0:T(8,128)(2,1)S(1)}, u32[]{:S(2)}, u32[]{:S(2)}) collective-permute-start(bf16[2,288,768]{2,1,0:T(8,128)(2,1)S(1)} %slice_bitcast_fusion.1), channel_id=1, source_target_pairs={{0,16},{16,0},{1,17},{17,1},{2,18},{18,2},{3,19},{19,3},{4,20},{20... | collective-permute-start | bytes 2654216 | tf_op jit(solution)/shard_map/ppermute | solution.py:449
  600.5 23.9 %collective-permute-start.58 = (bf16[2,288,768]{2,1,0:T(8,128)(2,1)S(1)}, bf16[2,288,768]{2,1,0:T(8,128)(2,1)S(1)}, u32[]{:S(2)}, u32[]{:S(2)}) collective-permute-start(bf16[2,288,768]{2,1,0:T(8,128)(2,1)S(1)} %slice_bitcast_fusion), channel_id=1, source_target_pairs={{0,8},{8,0},{1,9},{9,1},{2,10},{10,2},{3,11},{11,3},{4,12},{12,4},... | collective-permute-start | bytes 2654216 | tf_op jit(solution)/shard_map/ppermute | solution.py:449
  624.6 13.1 %collective-permute-start.60 = (bf16[288,768]{1,0:T(8,128)(2,1)S(1)}, bf16[288,768]{1,0:T(8,128)(2,1)S(1)}, u32[]{:S(2)}, u32[]{:S(2)}) collective-permute-start(bf16[288,768]{1,0:T(8,128)(2,1)S(1)} %get-tuple-element.77), channel_id=1, source_target_pairs={{0,8},{8,0},{1,9},{9,1},{2,10},{10,2},{3,11},{11,3},{4,12},{12,4},... | collective-permute-start | bytes 1327112 | tf_op jit(solution)/shard_map/ppermute | solution.py:449
  626.2 11.6 %collective-permute-start.61 = (bf16[288,768]{1,0:T(8,128)(2,1)S(1)}, bf16[288,768]{1,0:T(8,128)(2,1)S(1)}, u32[]{:S(2)}, u32[]{:S(2)}) collective-permute-start(bf16[288,768]{1,0:T(8,128)(2,1)S(1)} %get-tuple-element.76), channel_id=1, source_target_pairs={{0,16},{16,0},{1,17},{17,1},{2,18},{18,2},{3,19},{19,3},{4,20},{20... | collective-permute-start | bytes 1327112 | tf_op jit(solution)/shard_map/ppermute | solution.py:449
  627.5 17.7 %collective-permute-start.59 = (bf16[64,2304]{1,0:T(8,128)(2,1)S(1)}, bf16[64,2304]{1,0:T(8,128)(2,1)}, u32[]{:S(2)}, u32[]{:S(2)}) collective-permute-start(bf16[64,2304]{1,0:T(8,128)(2,1)S(1)} %get-tuple-element.119), channel_id=1, source_target_pairs={{0,8},{8,0},{1,9},{9,1},{2,10},{10,2},{3,11},{11,3},{4,12},{12,4},... | collective-permute-start | bytes 884744 | tf_op jit(solution)/shard_map/ppermute | solution.py:449
  638.2 15.1 %collective-permute-start.62 = (bf16[288,768]{1,0:T(8,128)(2,1)S(1)}, bf16[288,768]{1,0:T(8,128)(2,1)S(1)}, u32[]{:S(2)}, u32[]{:S(2)}) collective-permute-start(bf16[288,768]{1,0:T(8,128)(2,1)S(1)} %select_convert_fusion), channel_id=1, source_target_pairs={{0,4},{4,0},{1,5},{5,1},{2,6},{6,2},{3,7},{7,3},{8,12},{12,8},{9,1... | collective-permute-start | bytes 1327112 | tf_op jit(solution)/shard_map/ppermute | solution.py:449
  639.0 13.7 %all-to-all-start = ((f32[32,4,72]{2,1,0:T(4,128)}), f32[32,4,72]{2,1,0:T(4,128)S(1)}, u32[]{:S(2)}, u32[]{:S(2)}) async-start(f32[32,4,72]{2,1,0:T(4,128)} %copy.79), calls=%async_computation.2 | async-start | bytes 131072 | tf_op jit(solution)/shard_map/all_to_all | solution.py:865
  655.1 4.8 collective-permute-start.63
  656.0 7.9 %collective-permute-start.64 = (bf16[72,512]{1,0:T(8,128)(2,1)S(1)}, bf16[72,512]{1,0:T(8,128)(2,1)S(1)}, u32[]{:S(2)}, u32[]{:S(2)}) collective-permute-start(bf16[72,512]{1,0:T(8,128)(2,1)S(1)} %get-tuple-element.132), channel_id=1, source_target_pairs={{0,2},{1,3},{2,0},{3,1},{4,6},{5,7},{6,4},{7,5},{8,10},{9,11},{10,... | collective-permute-start | bytes 221192 | tf_op jit(solution)/shard_map/ppermute | solution.py:587
  656.9 7.1 %collective-permute-start.65 = (bf16[72,512]{1,0:T(8,128)(2,1)S(1)}, bf16[72,512]{1,0:T(8,128)(2,1)S(1)}, u32[]{:S(2)}, u32[]{:S(2)}) collective-permute-start(bf16[72,512]{1,0:T(8,128)(2,1)S(1)} %get-tuple-element.130), channel_id=1, source_target_pairs={{0,1},{1,2},{2,3},{3,0},{4,5},{5,6},{6,7},{7,4},{8,9},{9,10},{10,1... | collective-permute-start | bytes 221192 | tf_op jit(solution)/shard_map/ppermute | solution.py:587
  666.1 5.5 collective-permute-start.67
  668.6 4.9 collective-permute-start.66
  (108 other events, 1484.0 us)
Sparse Core Ops, SparseCore 0:
  26.6 52.4 all-gather.3
  81.5 104.9 all-gather.5
  188.4 61.9 all-gather.7
  422.9 59.0 reduce-scatter.2
  504.9 105.5 reduce-scatter.4

commit v5 on v4

--- a/solution.py
+++ b/solution.py
@@ -789,7 +789,7 @@
     heads = after(heads, grad_top)
     grad_top = grad_top.reshape(x_local.shape).astype(jnp.float32)
 
-    project_core = core_rows(heads, out_weight, (1, 1))
+    project_core = core_sums(dot(heads, out_weight, (1, 1)).astype(low))
     project = scatter_rows(project_core)
     middle = x_float + norm_gain(project, gain_two)
     normed_two = norm_gain(middle, gain_three).astype(low)

time: 690 us -> 683 us (0.990)
  starting transfers between devices: 118 us -> 94.6 us
  waiting for transfers between devices: 305 us -> 318 us
    ppermute x21, starting transfers between devices: 81.1 us -> 58.2 us  [shift(): lax.ppermute(value, 'seq', [(i, (i + step) % size) for i in range(size)])]
    ppermute x21, waiting for transfers between devices: 222 us -> 243 us  [shift(): lax.ppermute(value, 'seq', [(i, (i + step) % size) for i in range(size)])]
    ppermute x41, waiting for transfers between devices: 69.5 us -> 60.5 us  [flip(): return lax.ppermute(value, axis, [(0, 1), (1, 0)])]
    dot_general x20 -> x19, matrix products: 105 us -> 104 us  [dot(): lax.dot_general(left, right, ((dims[:1], dims[1:]), ((), ())), preferred_...]
    unnamed x230 -> x234, local copies, waits for them, and re-layouts: 32.6 us -> 32.5 us
  transfers between devices with their start and end apart: 74 -> 74, of which waited for: 32 -> 33; matrix products, arithmetic and copies ran while one was open for 25% -> 25% of each run, Pallas kernels for 0% -> 0%
where the time goes in v5:
time: 683 us; the launch traced here: 679 us
  waiting for transfers between devices  318 us (47%)
  matrix products  104 us (15%)
  starting transfers between devices  94.6 us (14%)
  local copies, waits for them, and re-layouts  73.9 us (11%)
  other arithmetic  68.4 us (10%)
  between operations  16.3 us (2%)
    ppermute x21, waiting for transfers between devices, shift(): lax.ppermute(value, 'seq', [(i, (i + step) % size) for i in range(size)])  243 us
    dot_general x19, matrix products, dot(): lax.dot_general(left, right, ((dims[:1], dims[1:]), ((), ())), preferred_...  104 us
    ppermute x41, waiting for transfers between devices, flip(): return lax.ppermute(value, axis, [(0, 1), (1, 0)])  60.5 us
    ppermute x21, starting transfers between devices, shift(): lax.ppermute(value, 'seq', [(i, (i + step) % size) for i in range(size)])  58.2 us
    unnamed x234, local copies, waits for them, and re-layouts  32.5 us
    ppermute x41, starting transfers between devices, flip(): return lax.ppermute(value, axis, [(0, 1), (1, 0)])  21.8 us
  transfers between devices with their start and end apart: 74, of which 33 were waited for; matrix products, arithmetic and copies ran while one was open for 25% of the time, Pallas kernels for 0%

profile of v5, /device:TPU:0, one launch (start us, length us, event | category | flops | bytes accessed | tf_op | source)
XLA Modules:
  0.0 678.7 jit_solution(17508720388961090426)
XLA Ops:
  10.1 5.1 collective-permute-start.1
  19.3 4.3 collective-permute-done.2
  27.8 3.1 collective-permute-done.26
  30.9 3.3 maximum_select_fusion
  46.0 16.5 %collective-permute-done.10.refs_1_ = bf16[2,288,768]{2,1,0:T(8,128)(2,1)S(1)} collective-permute-done((bf16[2,288,768]{2,1,0:T(8,128)(2,1)S(1)}, bf16[2,288,768]{2,1,0:T(8,128)(2,1)S(1)}, u32[]{:S(2)}, u32[]{:S(2)}) %collective-permute-start.10) | collective-permute-done | bytes 884768 | tf_op jit(solution)/shard_map/ppermute | solution.py:449
  69.1 6.5 collective-permute-done.8
  81.2 2.4 copy-done.1
  87.5 2.1 copy-done.5
  89.7 2.6 fusion.127
  92.3 2.5 fusion.61
  98.4 2.2 fusion.13
  100.7 2.1 fusion.26
  106.8 3.1 collective-permute-done.15
  114.4 3.8 collective-permute-start.16
  119.2 2.7 maximum_select_fusion.1
  121.9 32.0 %collective-permute-done.18 = bf16[128,2304]{1,0:T(8,128)(2,1)} collective-permute-done((bf16[128,2304]{1,0:T(8,128)(2,1)}, bf16[128,2304]{1,0:T(8,128)(2,1)}, u32[]{:S(2)}, u32[]{:S(2)}) %collective-permute-start.18) | collective-permute-done | bytes 589856 | tf_op jit(solution)/shard_map/ppermute | solution.py:594
  160.9 22.8 %collective-permute-start.20 = (bf16[128,2304]{1,0:T(8,128)(2,1)S(1)}, bf16[128,2304]{1,0:T(8,128)(2,1)S(1)}, u32[]{:S(2)}, u32[]{:S(2)}) collective-permute-start(bf16[128,2304]{1,0:T(8,128)(2,1)S(1)} %get-tuple-element.63), channel_id=1, source_target_pairs={{0,2},{1,3},{2,0},{3,1},{4,6},{5,7},{6,4},{7,5},{8,10},{9,11},{10,... | collective-permute-start | bytes 1769480 | tf_op jit(solution)/shard_map/ppermute | solution.py:594
  185.7 8.9 %collective-permute-done.19 = bf16[128,2304]{1,0:T(8,128)(2,1)S(1)} collective-permute-done((bf16[128,2304]{1,0:T(8,128)(2,1)S(1)}, bf16[128,2304]{1,0:T(8,128)(2,1)S(1)}, u32[]{:S(2)}, u32[]{:S(2)}) %collective-permute-start.19) | collective-permute-done | bytes 589856 | tf_op jit(solution)/shard_map/ppermute | solution.py:594
  194.6 39.8 %collective-permute-done.20 = bf16[128,2304]{1,0:T(8,128)(2,1)S(1)} collective-permute-done((bf16[128,2304]{1,0:T(8,128)(2,1)S(1)}, bf16[128,2304]{1,0:T(8,128)(2,1)S(1)}, u32[]{:S(2)}, u32[]{:S(2)}) %collective-permute-start.20) | collective-permute-done | bytes 589856 | tf_op jit(solution)/shard_map/ppermute | solution.py:594
  241.0 15.1 %fusion.128 = f32[1024,2304]{1,0:T(8,128)S(1)} fusion(bf16[1024,2304]{1,0:T(8,128)(2,1)} %constant_dynamic-update-slice_fusion.9, bf16[2304,2304]{1,0:T(8,128)(2,1)} %all-gather.6.cloned.1.call-done), kind=kOutput, calls=%fused_computation.355 | convolution fusion | flops 10871635968 | bytes 24772608 | tf_op jit(solution)/shard_map/dot_general | solution.py:708
  256.2 3.6 copy-done.18
  259.7 2.7 multiply_convert_fusion.1
  262.4 6.3 convolution_convert_fusion.5
  270.6 3.5 convolution_convert_fusion.6
  277.3 3.8 collective-permute-start.29
  283.9 24.3 %collective-permute-done.31 = bf16[128,2304]{1,0:T(8,128)(2,1)} collective-permute-done((bf16[128,2304]{1,0:T(8,128)(2,1)}, bf16[128,2304]{1,0:T(8,128)(2,1)}, u32[]{:S(2)}, u32[]{:S(2)}) %collective-permute-start.31) | collective-permute-done | bytes 589856 | tf_op jit(solution)/shard_map/ppermute | solution.py:594
  308.2 11.3 %collective-permute-done.29 = bf16[128,2304]{1,0:T(8,128)(2,1)} collective-permute-done((bf16[128,2304]{1,0:T(8,128)(2,1)}, bf16[128,2304]{1,0:T(8,128)(2,1)}, u32[]{:S(2)}, u32[]{:S(2)}) %collective-permute-start.29) | collective-permute-done | bytes 589856 | tf_op jit(solution)/shard_map/ppermute | solution.py:594
  319.5 2.2 multiply_reduce_fusion.5
  324.4 2.2 collective-permute-start.35
  327.9 8.3 %collective-permute-done.33 = bf16[64,2304]{1,0:T(8,128)(2,1)S(1)} collective-permute-done((bf16[64,2304]{1,0:T(8,128)(2,1)S(1)}, bf16[64,2304]{1,0:T(8,128)(2,1)S(1)}, u32[]{:S(2)}, u32[]{:S(2)}) %collective-permute-start.33) | collective-permute-done | bytes 294944 | tf_op jit(solution)/shard_map/ppermute | solution.py:449
  338.7 39.1 %collective-permute-done.35 = bf16[128,2304]{1,0:T(8,128)(2,1)S(1)} collective-permute-done((bf16[128,2304]{1,0:T(8,128)(2,1)S(1)}, bf16[128,2304]{1,0:T(8,128)(2,1)S(1)}, u32[]{:S(2)}, u32[]{:S(2)}) %collective-permute-start.35) | collective-permute-done | bytes 589856 | tf_op jit(solution)/shard_map/ppermute | solution.py:594
  380.8 10.5 %fusion.12 = (bf16[1024,1152]{1,0:T(8,128)(2,1)S(1)}, bf16[1024,1152]{1,0:T(8,128)(2,1)}) fusion(f32[1024,2304]{1,0:T(8,128)S(1)} %bitcast.238, bf16[1024,2304]{1,0:T(8,128)(2,1)S(1)} %constant_dynamic-update-slice_fusion.17, bf16[2304,1152]{1,0:T(8,128)(2,1)S(1)} %bitcast.275), kind=kOutput, calls=%fused_computation.23 | convolution fusion | flops 5464129536 | bytes 24182784 | tf_op jit(solution)/shard_map/dot_general | solution.py:708
  391.3 15.2 %convolution_convert_fusion.3 = bf16[1024,2304]{1,0:T(8,128)(2,1)S(1)} fusion(bf16[2304,2304]{1,0:T(8,128)(2,1)} %all-gather.6.cloned.1.call-done, bf16[1024,1152]{1,0:T(8,128)(2,1)} %get-tuple-element.73, bf16[1024,1152]{1,0:T(8,128)(2,1)S(1)} %get-tuple-element.72), kind=kOutput, calls=%fused_computation.15 | convolution fusion | flops 10883432448 | bytes 20054016 | tf_op jit(solution)/shard_map/dot_general | solution.py:708
  406.9 4.4 collective-permute-done.41
  411.3 2.0 add_convert_fusion.1
  413.4 8.0 %convolution_convert_fusion.1 = bf16[2304,1152]{1,0:T(8,128)(2,1)} fusion(bf16[1024,2304]{1,0:T(8,128)(2,1)S(1)} %constant_dynamic-update-slice_fusion.17, bf16[1024,1152]{1,0:T(8,128)(2,1)S(1)} %copy-done.22), kind=kOutput, calls=%fused_computation.5 | convolution fusion | flops 5438472192 | bytes 12386304 | tf_op jit(solution)/shard_map/dot_general | solution.py:708
  421.5 2.8 fusion.118
  424.3 3.8 collective-permute-start.42
  428.1 16.5 %convolution_convert_fusion = bf16[2304,2304]{1,0:T(8,128)(2,1)} fusion(bf16[1024,2304]{1,0:T(8,128)(2,1)} %constant_dynamic-update-slice_fusion.9, bf16[1024,1152]{1,0:T(8,128)(2,1)} %get-tuple-element.73, bf16[1024,1152]{1,0:T(8,128)(2,1)S(1)} %copy-done.90), kind=kOutput, calls=%fused_computation | convolution fusion | flops 10886381568 | bytes 20054016 | tf_op jit(solution)/shard_map/dot_general | solution.py:708
  444.6 18.6 %collective-permute-done.44 = bf16[128,2304]{1,0:T(8,128)(2,1)} collective-permute-done((bf16[128,2304]{1,0:T(8,128)(2,1)}, bf16[128,2304]{1,0:T(8,128)(2,1)}, u32[]{:S(2)}, u32[]{:S(2)}) %collective-permute-start.44) | collective-permute-done | bytes 589856 | tf_op jit(solution)/shard_map/ppermute | solution.py:594
  463.3 3.1 collective-permute-done.42
  473.0 10.3 %collective-permute-start.46 = (bf16[128,2304]{1,0:T(8,128)(2,1)S(1)}, bf16[128,2304]{1,0:T(8,128)(2,1)S(1)}, u32[]{:S(2)}, u32[]{:S(2)}) collective-permute-start(bf16[128,2304]{1,0:T(8,128)(2,1)S(1)} %get-tuple-element.58), channel_id=1, source_target_pairs={{0,2},{1,3},{2,0},{3,1},{4,6},{5,7},{6,4},{7,5},{8,10},{9,11},{10,... | collective-permute-start | bytes 1769480 | tf_op jit(solution)/shard_map/ppermute | solution.py:594
  483.4 12.0 %collective-permute-done.45 = bf16[128,2304]{1,0:T(8,128)(2,1)} collective-permute-done((bf16[128,2304]{1,0:T(8,128)(2,1)S(1)}, bf16[128,2304]{1,0:T(8,128)(2,1)}, u32[]{:S(2)}, u32[]{:S(2)}) %collective-permute-start.45) | collective-permute-done | bytes 589856 | tf_op jit(solution)/shard_map/ppermute | solution.py:594
  497.4 37.1 %collective-permute-done.46 = bf16[128,2304]{1,0:T(8,128)(2,1)S(1)} collective-permute-done((bf16[128,2304]{1,0:T(8,128)(2,1)S(1)}, bf16[128,2304]{1,0:T(8,128)(2,1)S(1)}, u32[]{:S(2)}, u32[]{:S(2)}) %collective-permute-start.46) | collective-permute-done | bytes 589856 | tf_op jit(solution)/shard_map/ppermute | solution.py:594
  540.3 3.9 convolution_convert_fusion.9
  546.3 2.8 multiply_convert_fusion.2
  551.1 2.4 fusion.69
  553.5 2.5 broadcast_select_fusion
  558.4 4.4 convolution_convert_fusion.2
  562.8 3.4 slice.317
  568.0 2.9 collective-permute-done.53
  570.9 2.5 add_convert_fusion
  574.7 3.8 collective-permute-start.54
  578.5 3.8 convolution_convert_fusion.8
  582.3 3.7 convolution_convert_fusion.7
  588.0 5.9 copy.75
  599.3 4.0 fusion.5
  603.4 3.9 collective-permute-done.56
  607.2 9.6 %collective-permute-done.54 = bf16[128,2304]{1,0:T(8,128)(2,1)} collective-permute-done((bf16[128,2304]{1,0:T(8,128)(2,1)}, bf16[128,2304]{1,0:T(8,128)(2,1)}, u32[]{:S(2)}, u32[]{:S(2)}) %collective-permute-start.54) | collective-permute-done | bytes 589856 | tf_op jit(solution)/shard_map/ppermute | solution.py:594
  623.0 9.0 %collective-permute-done.60 = bf16[288,768]{1,0:T(8,128)(2,1)S(1)} collective-permute-done((bf16[288,768]{1,0:T(8,128)(2,1)S(1)}, bf16[288,768]{1,0:T(8,128)(2,1)S(1)}, u32[]{:S(2)}, u32[]{:S(2)}) %collective-permute-start.60) | collective-permute-done | bytes 442400 | tf_op jit(solution)/shard_map/ppermute | solution.py:449
  633.2 5.2 all-to-all-start
  640.4 5.5 all-to-all-done
  653.1 4.1 collective-permute-done.64
  659.3 2.5 dynamic-slice_bitcast_fusion
  (517 shorter events, 144.2 us)
Async XLA Ops:
  7.2 74.0 %all-gather.4.cloned.1.call-start = ((), (), s32[]{:S(2)}) async-start(), calls=%async_computation.3 | async-start | bytes 5308416 | tf_op jit(solution)/shard_map/all_gather | solution.py:622
  10.1 9.1 %collective-permute-start.1 = (bf16[72,2,256]{2,1,0:T(2,128)(2,1)S(1)}, bf16[72,2,256]{2,1,0:T(2,128)(2,1)S(1)}, u32[]{:S(2)}, u32[]{:S(2)}) collective-permute-start(bf16[72,2,256]{2,1,0:T(2,128)(2,1)S(1)} %bitcast.265), channel_id=1, source_target_pairs={{0,3},{1,0},{2,1},{3,2},{4,7},{5,4},{6,5},{7,6},{8,11},{9,8},{10,9... | collective-permute-start | bytes 221192 | tf_op jit(solution)/shard_map/ppermute | solution.py:587
  16.3 8.7 %collective-permute-start = (bf16[64,2304]{1,0:T(8,128)(2,1)S(1)}, bf16[64,2304]{1,0:T(8,128)(2,1)S(1)}, u32[]{:S(2)}, u32[]{:S(2)}) collective-permute-start(bf16[64,2304]{1,0:T(8,128)(2,1)S(1)} %get-tuple-element.125), channel_id=1, source_target_pairs={{0,8},{8,0},{1,9},{9,1},{2,10},{10,2},{3,11},{11,3},{4,12},{12,4},... | collective-permute-start | bytes 884744 | tf_op jit(solution)/shard_map/ppermute | solution.py:449
  18.0 5.5 collective-permute-start.2
  18.1 6.2 collective-permute-start.3
  25.9 215.1 %all-gather.6.cloned.1.call-start = ((), (), s32[]{:S(2)}) async-start(), calls=%async_computation.4 | async-start | bytes 13271040 | tf_op jit(solution)/shard_map/all_gather | solution.py:691
  34.3 228.1 %all-gather.8.cloned.1.call-start = ((), (), s32[]{:S(2)}) async-start(), calls=%async_computation.5 | async-start | bytes 6635520 | tf_op jit(solution)/shard_map/all_gather | solution.py:691
  35.0 6.8 %collective-permute-start.6 = (bf16[4,288]{1,0:T(4,128)(2,1)S(1)}, bf16[4,288]{1,0:T(4,128)(2,1)S(1)}, u32[]{:S(2)}, u32[]{:S(2)}) collective-permute-start(bf16[4,288]{1,0:T(4,128)(2,1)S(1)} %pad_maximum_fusion.19), channel_id=1, source_target_pairs={{0,4},{4,0},{1,5},{5,1},{2,6},{6,2},{3,7},{7,3},{8,12},{12,8},{9,1... | collective-permute-start | bytes 6920 | tf_op jit(solution)/shard_map/ppermute | solution.py:449
  40.0 5.1 collective-permute-start.5
  40.3 22.2 %collective-permute-start.10 = (bf16[2,288,768]{2,1,0:T(8,128)(2,1)S(1)}, bf16[2,288,768]{2,1,0:T(8,128)(2,1)S(1)}, u32[]{:S(2)}, u32[]{:S(2)}) collective-permute-start(bf16[2,288,768]{2,1,0:T(8,128)(2,1)S(1)} %maximum_select_fusion.2.refs_0_), channel_id=1, source_target_pairs={{0,8},{8,0},{1,9},{9,1},{2,10},{10,2},{3,11},{11,3},{4,12},{12,4},... | collective-permute-start | bytes 2654216 | tf_op jit(solution)/shard_map/ppermute | solution.py:449
  42.4 22.4 %collective-permute-start.11 = (bf16[2,288,768]{2,1,0:T(8,128)(2,1)S(1)}, bf16[2,288,768]{2,1,0:T(8,128)(2,1)S(1)}, u32[]{:S(2)}, u32[]{:S(2)}) collective-permute-start(bf16[2,288,768]{2,1,0:T(8,128)(2,1)S(1)} %maximum_select_fusion.2.refs_0_), channel_id=1, source_target_pairs={{0,16},{16,0},{1,17},{17,1},{2,18},{18,2},{3,19},{19,3},{4,20},{20... | collective-permute-start | bytes 2654216 | tf_op jit(solution)/shard_map/ppermute | solution.py:449
  44.5 22.5 %collective-permute-start.7 = (bf16[4,2,288]{2,0,1:T(4,128)(2,1)}, bf16[4,2,288]{2,0,1:T(4,128)(2,1)}, u32[]{:S(2)}, u32[]{:S(2)}) collective-permute-start(bf16[4,2,288]{2,0,1:T(4,128)(2,1)} %maximum_select_fusion.11), channel_id=1, source_target_pairs={{0,8},{8,0},{1,9},{9,1},{2,10},{10,2},{3,11},{11,3},{4,12},{12,4},... | collective-permute-start | bytes 13832 | tf_op jit(solution)/shard_map/ppermute | solution.py:449
  63.3 13.9 %collective-permute-start.12 = (bf16[288,768]{1,0:T(8,128)(2,1)}, bf16[288,768]{1,0:T(8,128)(2,1)S(1)}, u32[]{:S(2)}, u32[]{:S(2)}) collective-permute-start(bf16[288,768]{1,0:T(8,128)(2,1)} %slice_bitcast_fusion.3), channel_id=1, source_target_pairs={{0,16},{16,0},{1,17},{17,1},{2,18},{18,2},{3,19},{19,3},{4,20},{20... | collective-permute-start | bytes 1327112 | tf_op jit(solution)/shard_map/ppermute | solution.py:449
  65.6 11.8 %collective-permute-start.13 = (bf16[288,768]{1,0:T(8,128)(2,1)}, bf16[288,768]{1,0:T(8,128)(2,1)S(1)}, u32[]{:S(2)}, u32[]{:S(2)}) collective-permute-start(bf16[288,768]{1,0:T(8,128)(2,1)} %slice_bitcast_fusion.2), channel_id=1, source_target_pairs={{0,8},{8,0},{1,9},{9,1},{2,10},{10,2},{3,11},{11,3},{4,12},{12,4},... | collective-permute-start | bytes 1327112 | tf_op jit(solution)/shard_map/ppermute | solution.py:449
  67.7 7.8 %collective-permute-start.8 = (bf16[4,2,2,288]{3,0,2,1:T(4,128)(2,1)S(1)}, bf16[4,2,2,288]{3,0,2,1:T(4,128)(2,1)S(1)}, u32[]{:S(2)}, u32[]{:S(2)}) collective-permute-start(bf16[4,2,2,288]{3,0,2,1:T(4,128)(2,1)S(1)} %maximum_select_fusion.9), channel_id=1, source_target_pairs={{0,16},{16,0},{1,17},{17,1},{2,18},{18,2},{3,19},{19,3},{4,20},{20... | collective-permute-start | bytes 27656 | tf_op jit(solution)/shard_map/ppermute | solution.py:449
  106.6 11.7 %collective-permute-start.27 = (bf16[288,1152]{1,0:T(8,128)(2,1)S(1)}, bf16[288,1152]{1,0:T(8,128)(2,1)S(1)}, u32[]{:S(2)}, u32[]{:S(2)}) collective-permute-start(bf16[288,1152]{1,0:T(8,128)(2,1)S(1)} %get-tuple-element.105), channel_id=1, source_target_pairs={{0,4},{4,0},{1,5},{5,1},{2,6},{6,2},{3,7},{7,3},{8,12},{12,8},{9,1... | collective-permute-start | bytes 1990664 | tf_op jit(solution)/shard_map/ppermute | solution.py:449
  113.1 40.8 %collective-permute-start.18 = (bf16[128,2304]{1,0:T(8,128)(2,1)}, bf16[128,2304]{1,0:T(8,128)(2,1)}, u32[]{:S(2)}, u32[]{:S(2)}) collective-permute-start(bf16[128,2304]{1,0:T(8,128)(2,1)} %get-tuple-element.92), channel_id=1, source_target_pairs={{0,2},{1,3},{2,0},{3,1},{4,6},{5,7},{6,4},{7,5},{8,10},{9,11},{10,... | collective-permute-start | bytes 1769480 | tf_op jit(solution)/shard_map/ppermute | solution.py:594
  114.3 39.6 %collective-permute-start.17 = (bf16[128,2304]{1,0:T(8,128)(2,1)}, bf16[128,2304]{1,0:T(8,128)(2,1)}, u32[]{:S(2)}, u32[]{:S(2)}) collective-permute-start(bf16[128,2304]{1,0:T(8,128)(2,1)} %get-tuple-element.93), channel_id=1, source_target_pairs={{0,1},{1,2},{2,3},{3,0},{4,5},{5,6},{6,7},{7,4},{8,9},{9,10},{10,1... | collective-permute-start | bytes 1769480 | tf_op jit(solution)/shard_map/ppermute | solution.py:594
  114.4 40.8 %collective-permute-start.16 = (bf16[128,2304]{1,0:T(8,128)(2,1)}, bf16[128,2304]{1,0:T(8,128)(2,1)}, u32[]{:S(2)}, u32[]{:S(2)}) collective-permute-start(bf16[128,2304]{1,0:T(8,128)(2,1)} %get-tuple-element.91), channel_id=1, source_target_pairs={{0,3},{1,0},{2,1},{3,2},{4,7},{5,4},{6,5},{7,6},{8,11},{9,8},{10,9... | collective-permute-start | bytes 1769480 | tf_op jit(solution)/shard_map/ppermute | solution.py:594
  121.9 535.4 %reduce-scatter.3.cloned.1.call-start = ((), (), s32[]{:S(2)}) async-start(), calls=%async_computation.6 | async-start | bytes 6635520 | tf_op jit(solution)/shard_map/reduce_scatter | solution.py:696
  158.9 35.7 %collective-permute-start.19 = (bf16[128,2304]{1,0:T(8,128)(2,1)S(1)}, bf16[128,2304]{1,0:T(8,128)(2,1)S(1)}, u32[]{:S(2)}, u32[]{:S(2)}) collective-permute-start(bf16[128,2304]{1,0:T(8,128)(2,1)S(1)} %get-tuple-element.63), channel_id=1, source_target_pairs={{0,3},{1,0},{2,1},{3,2},{4,7},{5,4},{6,5},{7,6},{8,11},{9,8},{10,9... | collective-permute-start | bytes 1769480 | tf_op jit(solution)/shard_map/ppermute | solution.py:594
  160.9 73.6 %collective-permute-start.20 = (bf16[128,2304]{1,0:T(8,128)(2,1)S(1)}, bf16[128,2304]{1,0:T(8,128)(2,1)S(1)}, u32[]{:S(2)}, u32[]{:S(2)}) collective-permute-start(bf16[128,2304]{1,0:T(8,128)(2,1)S(1)} %get-tuple-element.63), channel_id=1, source_target_pairs={{0,2},{1,3},{2,0},{3,1},{4,6},{5,7},{6,4},{7,5},{8,10},{9,11},{10,... | collective-permute-start | bytes 1769480 | tf_op jit(solution)/shard_map/ppermute | solution.py:594
  183.7 50.7 %collective-permute-start.21 = (bf16[128,2304]{1,0:T(8,128)(2,1)S(1)}, bf16[128,2304]{1,0:T(8,128)(2,1)S(1)}, u32[]{:S(2)}, u32[]{:S(2)}) collective-permute-start(bf16[128,2304]{1,0:T(8,128)(2,1)S(1)} %get-tuple-element.63), channel_id=1, source_target_pairs={{0,1},{1,2},{2,3},{3,0},{4,5},{5,6},{6,7},{7,4},{8,9},{9,10},{10,1... | collective-permute-start | bytes 1769480 | tf_op jit(solution)/shard_map/ppermute | solution.py:594
  185.7 51.8 %collective-permute-start.22 = (bf16[128,2304]{1,0:T(8,128)(2,1)S(1)}, bf16[128,2304]{1,0:T(8,128)(2,1)S(1)}, u32[]{:S(2)}, u32[]{:S(2)}) collective-permute-start(bf16[128,2304]{1,0:T(8,128)(2,1)S(1)} %get-tuple-element.63), channel_id=1, source_target_pairs={{0,4},{4,0},{1,5},{5,1},{2,6},{6,2},{3,7},{7,3},{8,12},{12,8},{9,1... | collective-permute-start | bytes 1769480 | tf_op jit(solution)/shard_map/ppermute | solution.py:449
  194.6 43.8 %collective-permute-start.23 = (bf16[128,2304]{1,0:T(8,128)(2,1)S(1)}, bf16[128,2304]{1,0:T(8,128)(2,1)S(1)}, u32[]{:S(2)}, u32[]{:S(2)}) collective-permute-start(bf16[128,2304]{1,0:T(8,128)(2,1)S(1)} %collective-permute-done.19), channel_id=1, source_target_pairs={{0,4},{4,0},{1,5},{5,1},{2,6},{6,2},{3,7},{7,3},{8,12},{12,8},{9,1... | collective-permute-start | bytes 1769480 | tf_op jit(solution)/shard_map/ppermute | solution.py:449
  234.4 4.8 collective-permute-start.24
  234.4 5.7 collective-permute-start.25
  268.7 5.4 collective-permute-start.28
  269.6 12.2 %collective-permute-start.32 = (bf16[64,2304]{1,0:T(8,128)(2,1)}, bf16[64,2304]{1,0:T(8,128)(2,1)S(1)}, u32[]{:S(2)}, u32[]{:S(2)}) collective-permute-start(bf16[64,2304]{1,0:T(8,128)(2,1)} %get-tuple-element.123), channel_id=1, source_target_pairs={{0,8},{8,0},{1,9},{9,1},{2,10},{10,2},{3,11},{11,3},{4,12},{12,4},... | collective-permute-start | bytes 884744 | tf_op jit(solution)/shard_map/ppermute | solution.py:449
  277.3 30.9 %collective-permute-start.31 = (bf16[128,2304]{1,0:T(8,128)(2,1)}, bf16[128,2304]{1,0:T(8,128)(2,1)}, u32[]{:S(2)}, u32[]{:S(2)}) collective-permute-start(bf16[128,2304]{1,0:T(8,128)(2,1)} %get-tuple-element.89), channel_id=1, source_target_pairs={{0,2},{1,3},{2,0},{3,1},{4,6},{5,7},{6,4},{7,5},{8,10},{9,11},{10,... | collective-permute-start | bytes 1769480 | tf_op jit(solution)/shard_map/ppermute | solution.py:594
  277.3 30.9 %collective-permute-start.30 = (bf16[128,2304]{1,0:T(8,128)(2,1)}, bf16[128,2304]{1,0:T(8,128)(2,1)}, u32[]{:S(2)}, u32[]{:S(2)}) collective-permute-start(bf16[128,2304]{1,0:T(8,128)(2,1)} %get-tuple-element.90), channel_id=1, source_target_pairs={{0,1},{1,2},{2,3},{3,0},{4,5},{5,6},{6,7},{7,4},{8,9},{9,10},{10,1... | collective-permute-start | bytes 1769480 | tf_op jit(solution)/shard_map/ppermute | solution.py:594
  277.3 42.2 %collective-permute-start.29 = (bf16[128,2304]{1,0:T(8,128)(2,1)}, bf16[128,2304]{1,0:T(8,128)(2,1)}, u32[]{:S(2)}, u32[]{:S(2)}) collective-permute-start(bf16[128,2304]{1,0:T(8,128)(2,1)} %get-tuple-element.88), channel_id=1, source_target_pairs={{0,3},{1,0},{2,1},{3,2},{4,7},{5,4},{6,5},{7,6},{8,11},{9,8},{10,9... | collective-permute-start | bytes 1769480 | tf_op jit(solution)/shard_map/ppermute | solution.py:594
  323.3 15.4 %collective-permute-start.34 = (bf16[128,2304]{1,0:T(8,128)(2,1)S(1)}, bf16[128,2304]{1,0:T(8,128)(2,1)S(1)}, u32[]{:S(2)}, u32[]{:S(2)}) collective-permute-start(bf16[128,2304]{1,0:T(8,128)(2,1)S(1)} %get-tuple-element.106), channel_id=1, source_target_pairs={{0,3},{1,0},{2,1},{3,2},{4,7},{5,4},{6,5},{7,6},{8,11},{9,8},{10,9... | collective-permute-start | bytes 1769480 | tf_op jit(solution)/shard_map/ppermute | solution.py:594
  324.4 53.4 %collective-permute-start.35 = (bf16[128,2304]{1,0:T(8,128)(2,1)S(1)}, bf16[128,2304]{1,0:T(8,128)(2,1)S(1)}, u32[]{:S(2)}, u32[]{:S(2)}) collective-permute-start(bf16[128,2304]{1,0:T(8,128)(2,1)S(1)} %get-tuple-element.106), channel_id=1, source_target_pairs={{0,2},{1,3},{2,0},{3,1},{4,6},{5,7},{6,4},{7,5},{8,10},{9,11},{10,... | collective-permute-start | bytes 1769480 | tf_op jit(solution)/shard_map/ppermute | solution.py:594
  326.7 51.2 %collective-permute-start.36 = (bf16[128,2304]{1,0:T(8,128)(2,1)S(1)}, bf16[128,2304]{1,0:T(8,128)(2,1)S(1)}, u32[]{:S(2)}, u32[]{:S(2)}) collective-permute-start(bf16[128,2304]{1,0:T(8,128)(2,1)S(1)} %get-tuple-element.106), channel_id=1, source_target_pairs={{0,1},{1,2},{2,3},{3,0},{4,5},{5,6},{6,7},{7,4},{8,9},{9,10},{10,1... | collective-permute-start | bytes 1769480 | tf_op jit(solution)/shard_map/ppermute | solution.py:594
  326.7 51.9 %collective-permute-start.37 = (bf16[128,2304]{1,0:T(8,128)(2,1)S(1)}, bf16[128,2304]{1,0:T(8,128)(2,1)S(1)}, u32[]{:S(2)}, u32[]{:S(2)}) collective-permute-start(bf16[128,2304]{1,0:T(8,128)(2,1)S(1)} %get-tuple-element.106), channel_id=1, source_target_pairs={{0,4},{4,0},{1,5},{5,1},{2,6},{6,2},{3,7},{7,3},{8,12},{12,8},{9,1... | collective-permute-start | bytes 1769480 | tf_op jit(solution)/shard_map/ppermute | solution.py:449
  326.7 9.5 %collective-permute-start.33 = (bf16[64,2304]{1,0:T(8,128)(2,1)S(1)}, bf16[64,2304]{1,0:T(8,128)(2,1)S(1)}, u32[]{:S(2)}, u32[]{:S(2)}) collective-permute-start(bf16[64,2304]{1,0:T(8,128)(2,1)S(1)} %get-tuple-element.121), channel_id=1, source_target_pairs={{0,8},{8,0},{1,9},{9,1},{2,10},{10,2},{3,11},{11,3},{4,12},{12,4},... | collective-permute-start | bytes 884744 | tf_op jit(solution)/shard_map/ppermute | solution.py:449
  338.7 39.9 %collective-permute-start.38 = (bf16[128,2304]{1,0:T(8,128)(2,1)S(1)}, bf16[128,2304]{1,0:T(8,128)(2,1)S(1)}, u32[]{:S(2)}, u32[]{:S(2)}) collective-permute-start(bf16[128,2304]{1,0:T(8,128)(2,1)S(1)} %collective-permute-done.34), channel_id=1, source_target_pairs={{0,4},{4,0},{1,5},{5,1},{2,6},{6,2},{3,7},{7,3},{8,12},{12,8},{9,1... | collective-permute-start | bytes 1769480 | tf_op jit(solution)/shard_map/ppermute | solution.py:449
  421.4 235.9 %reduce-scatter.5.cloned.1.call-start = ((), (), s32[]{:S(2)}) async-start(), calls=%async_computation.7 | async-start | bytes 13271040 | tf_op jit(solution)/shard_map/reduce_scatter | solution.py:696
  424.3 39.0 %collective-permute-start.44 = (bf16[128,2304]{1,0:T(8,128)(2,1)}, bf16[128,2304]{1,0:T(8,128)(2,1)}, u32[]{:S(2)}, u32[]{:S(2)}) collective-permute-start(bf16[128,2304]{1,0:T(8,128)(2,1)} %get-tuple-element.86), channel_id=1, source_target_pairs={{0,2},{1,3},{2,0},{3,1},{4,6},{5,7},{6,4},{7,5},{8,10},{9,11},{10,... | collective-permute-start | bytes 1769480 | tf_op jit(solution)/shard_map/ppermute | solution.py:594
  424.3 39.0 %collective-permute-start.43 = (bf16[128,2304]{1,0:T(8,128)(2,1)}, bf16[128,2304]{1,0:T(8,128)(2,1)}, u32[]{:S(2)}, u32[]{:S(2)}) collective-permute-start(bf16[128,2304]{1,0:T(8,128)(2,1)} %get-tuple-element.87), channel_id=1, source_target_pairs={{0,1},{1,2},{2,3},{3,0},{4,5},{5,6},{6,7},{7,4},{8,9},{9,10},{10,1... | collective-permute-start | bytes 1769480 | tf_op jit(solution)/shard_map/ppermute | solution.py:594
  424.3 42.1 %collective-permute-start.42 = (bf16[128,2304]{1,0:T(8,128)(2,1)}, bf16[128,2304]{1,0:T(8,128)(2,1)}, u32[]{:S(2)}, u32[]{:S(2)}) collective-permute-start(bf16[128,2304]{1,0:T(8,128)(2,1)} %get-tuple-element.85), channel_id=1, source_target_pairs={{0,3},{1,0},{2,1},{3,2},{4,7},{5,4},{6,5},{7,6},{8,11},{9,8},{10,9... | collective-permute-start | bytes 1769480 | tf_op jit(solution)/shard_map/ppermute | solution.py:594
  471.9 23.6 %collective-permute-start.45 = (bf16[128,2304]{1,0:T(8,128)(2,1)S(1)}, bf16[128,2304]{1,0:T(8,128)(2,1)}, u32[]{:S(2)}, u32[]{:S(2)}) collective-permute-start(bf16[128,2304]{1,0:T(8,128)(2,1)S(1)} %get-tuple-element.58), channel_id=1, source_target_pairs={{0,3},{1,0},{2,1},{3,2},{4,7},{5,4},{6,5},{7,6},{8,11},{9,8},{10,9... | collective-permute-start | bytes 1769480 | tf_op jit(solution)/shard_map/ppermute | solution.py:594
  473.0 61.5 %collective-permute-start.46 = (bf16[128,2304]{1,0:T(8,128)(2,1)S(1)}, bf16[128,2304]{1,0:T(8,128)(2,1)S(1)}, u32[]{:S(2)}, u32[]{:S(2)}) collective-permute-start(bf16[128,2304]{1,0:T(8,128)(2,1)S(1)} %get-tuple-element.58), channel_id=1, source_target_pairs={{0,2},{1,3},{2,0},{3,1},{4,6},{5,7},{6,4},{7,5},{8,10},{9,11},{10,... | collective-permute-start | bytes 1769480 | tf_op jit(solution)/shard_map/ppermute | solution.py:594
  483.3 51.2 %collective-permute-start.47 = (bf16[128,2304]{1,0:T(8,128)(2,1)S(1)}, bf16[128,2304]{1,0:T(8,128)(2,1)S(1)}, u32[]{:S(2)}, u32[]{:S(2)}) collective-permute-start(bf16[128,2304]{1,0:T(8,128)(2,1)S(1)} %get-tuple-element.58), channel_id=1, source_target_pairs={{0,1},{1,2},{2,3},{3,0},{4,5},{5,6},{6,7},{7,4},{8,9},{9,10},{10,1... | collective-permute-start | bytes 1769480 | tf_op jit(solution)/shard_map/ppermute | solution.py:594
  483.4 53.4 %collective-permute-start.48 = (bf16[128,2304]{1,0:T(8,128)(2,1)S(1)}, bf16[128,2304]{1,0:T(8,128)(2,1)S(1)}, u32[]{:S(2)}, u32[]{:S(2)}) collective-permute-start(bf16[128,2304]{1,0:T(8,128)(2,1)S(1)} %get-tuple-element.58), channel_id=1, source_target_pairs={{0,4},{4,0},{1,5},{5,1},{2,6},{6,2},{3,7},{7,3},{8,12},{12,8},{9,1... | collective-permute-start | bytes 1769480 | tf_op jit(solution)/shard_map/ppermute | solution.py:449
  495.5 42.2 %collective-permute-start.49 = (bf16[128,2304]{1,0:T(8,128)(2,1)}, bf16[128,2304]{1,0:T(8,128)(2,1)S(1)}, u32[]{:S(2)}, u32[]{:S(2)}) collective-permute-start(bf16[128,2304]{1,0:T(8,128)(2,1)} %collective-permute-done.45), channel_id=1, source_target_pairs={{0,4},{4,0},{1,5},{5,1},{2,6},{6,2},{3,7},{7,3},{8,12},{12,8},{9,1... | collective-permute-start | bytes 1769480 | tf_op jit(solution)/shard_map/ppermute | solution.py:449
  534.5 4.9 collective-permute-start.51
  566.2 4.7 collective-permute-start.53
  574.7 32.6 %collective-permute-start.56 = (bf16[128,2304]{1,0:T(8,128)(2,1)}, bf16[128,2304]{1,0:T(8,128)(2,1)S(1)}, u32[]{:S(2)}, u32[]{:S(2)}) collective-permute-start(bf16[128,2304]{1,0:T(8,128)(2,1)} %get-tuple-element.83), channel_id=1, source_target_pairs={{0,2},{1,3},{2,0},{3,1},{4,6},{5,7},{6,4},{7,5},{8,10},{9,11},{10,... | collective-permute-start | bytes 1769480 | tf_op jit(solution)/shard_map/ppermute | solution.py:594
  574.7 32.6 %collective-permute-start.55 = (bf16[128,2304]{1,0:T(8,128)(2,1)}, bf16[128,2304]{1,0:T(8,128)(2,1)}, u32[]{:S(2)}, u32[]{:S(2)}) collective-permute-start(bf16[128,2304]{1,0:T(8,128)(2,1)} %get-tuple-element.84), channel_id=1, source_target_pairs={{0,1},{1,2},{2,3},{3,0},{4,5},{5,6},{6,7},{7,4},{8,9},{9,10},{10,1... | collective-permute-start | bytes 1769480 | tf_op jit(solution)/shard_map/ppermute | solution.py:594
  574.7 42.2 %collective-permute-start.54 = (bf16[128,2304]{1,0:T(8,128)(2,1)}, bf16[128,2304]{1,0:T(8,128)(2,1)}, u32[]{:S(2)}, u32[]{:S(2)}) collective-permute-start(bf16[128,2304]{1,0:T(8,128)(2,1)} %get-tuple-element.82), channel_id=1, source_target_pairs={{0,3},{1,0},{2,1},{3,2},{4,7},{5,4},{6,5},{7,6},{8,11},{9,8},{10,9... | collective-permute-start | bytes 1769480 | tf_op jit(solution)/shard_map/ppermute | solution.py:594
  595.7 22.9 %collective-permute-start.57 = (bf16[2,288,768]{2,1,0:T(8,128)(2,1)S(1)}, bf16[2,288,768]{2,1,0:T(8,128)(2,1)S(1)}, u32[]{:S(2)}, u32[]{:S(2)}) collective-permute-start(bf16[2,288,768]{2,1,0:T(8,128)(2,1)S(1)} %slice_bitcast_fusion.1), channel_id=1, source_target_pairs={{0,16},{16,0},{1,17},{17,1},{2,18},{18,2},{3,19},{19,3},{4,20},{20... | collective-permute-start | bytes 2654216 | tf_op jit(solution)/shard_map/ppermute | solution.py:449
  597.2 21.4 %collective-permute-start.58 = (bf16[2,288,768]{2,1,0:T(8,128)(2,1)S(1)}, bf16[2,288,768]{2,1,0:T(8,128)(2,1)S(1)}, u32[]{:S(2)}, u32[]{:S(2)}) collective-permute-start(bf16[2,288,768]{2,1,0:T(8,128)(2,1)S(1)} %slice_bitcast_fusion), channel_id=1, source_target_pairs={{0,8},{8,0},{1,9},{9,1},{2,10},{10,2},{3,11},{11,3},{4,12},{12,4},... | collective-permute-start | bytes 2654216 | tf_op jit(solution)/shard_map/ppermute | solution.py:449
  618.8 13.2 %collective-permute-start.60 = (bf16[288,768]{1,0:T(8,128)(2,1)S(1)}, bf16[288,768]{1,0:T(8,128)(2,1)S(1)}, u32[]{:S(2)}, u32[]{:S(2)}) collective-permute-start(bf16[288,768]{1,0:T(8,128)(2,1)S(1)} %get-tuple-element.77), channel_id=1, source_target_pairs={{0,8},{8,0},{1,9},{9,1},{2,10},{10,2},{3,11},{11,3},{4,12},{12,4},... | collective-permute-start | bytes 1327112 | tf_op jit(solution)/shard_map/ppermute | solution.py:449
  619.9 12.1 %collective-permute-start.61 = (bf16[288,768]{1,0:T(8,128)(2,1)S(1)}, bf16[288,768]{1,0:T(8,128)(2,1)S(1)}, u32[]{:S(2)}, u32[]{:S(2)}) collective-permute-start(bf16[288,768]{1,0:T(8,128)(2,1)S(1)} %get-tuple-element.76), channel_id=1, source_target_pairs={{0,16},{16,0},{1,17},{17,1},{2,18},{18,2},{3,19},{19,3},{4,20},{20... | collective-permute-start | bytes 1327112 | tf_op jit(solution)/shard_map/ppermute | solution.py:449
  621.9 16.5 %collective-permute-start.59 = (bf16[64,2304]{1,0:T(8,128)(2,1)S(1)}, bf16[64,2304]{1,0:T(8,128)(2,1)}, u32[]{:S(2)}, u32[]{:S(2)}) collective-permute-start(bf16[64,2304]{1,0:T(8,128)(2,1)S(1)} %get-tuple-element.119), channel_id=1, source_target_pairs={{0,8},{8,0},{1,9},{9,1},{2,10},{10,2},{3,11},{11,3},{4,12},{12,4},... | collective-permute-start | bytes 884744 | tf_op jit(solution)/shard_map/ppermute | solution.py:449
  632.4 14.1 %collective-permute-start.62 = (bf16[288,768]{1,0:T(8,128)(2,1)S(1)}, bf16[288,768]{1,0:T(8,128)(2,1)S(1)}, u32[]{:S(2)}, u32[]{:S(2)}) collective-permute-start(bf16[288,768]{1,0:T(8,128)(2,1)S(1)} %select_convert_fusion), channel_id=1, source_target_pairs={{0,4},{4,0},{1,5},{5,1},{2,6},{6,2},{3,7},{7,3},{8,12},{12,8},{9,1... | collective-permute-start | bytes 1327112 | tf_op jit(solution)/shard_map/ppermute | solution.py:449
  633.2 12.7 %all-to-all-start = ((f32[32,4,72]{2,1,0:T(4,128)}), f32[32,4,72]{2,1,0:T(4,128)S(1)}, u32[]{:S(2)}, u32[]{:S(2)}) async-start(f32[32,4,72]{2,1,0:T(4,128)} %copy.79), calls=%async_computation.2 | async-start | bytes 131072 | tf_op jit(solution)/shard_map/all_to_all | solution.py:865
  648.3 4.8 collective-permute-start.63
  649.2 7.9 %collective-permute-start.64 = (bf16[72,512]{1,0:T(8,128)(2,1)S(1)}, bf16[72,512]{1,0:T(8,128)(2,1)S(1)}, u32[]{:S(2)}, u32[]{:S(2)}) collective-permute-start(bf16[72,512]{1,0:T(8,128)(2,1)S(1)} %get-tuple-element.132), channel_id=1, source_target_pairs={{0,2},{1,3},{2,0},{3,1},{4,6},{5,7},{6,4},{7,5},{8,10},{9,11},{10,... | collective-permute-start | bytes 221192 | tf_op jit(solution)/shard_map/ppermute | solution.py:587
  650.1 7.1 %collective-permute-start.65 = (bf16[72,512]{1,0:T(8,128)(2,1)S(1)}, bf16[72,512]{1,0:T(8,128)(2,1)S(1)}, u32[]{:S(2)}, u32[]{:S(2)}) collective-permute-start(bf16[72,512]{1,0:T(8,128)(2,1)S(1)} %get-tuple-element.130), channel_id=1, source_target_pairs={{0,1},{1,2},{2,3},{3,0},{4,5},{5,6},{6,7},{7,4},{8,9},{9,10},{10,1... | collective-permute-start | bytes 221192 | tf_op jit(solution)/shard_map/ppermute | solution.py:587
  659.3 5.5 collective-permute-start.67
  661.7 4.9 collective-permute-start.66
  (110 other events, 1290.8 us)
Sparse Core Ops, SparseCore 0:
  26.0 49.8 all-gather.3
  78.4 104.9 all-gather.5
  185.2 61.9 all-gather.7
  421.5 59.4 reduce-scatter.2
  484.0 104.8 reduce-scatter.4

commit v6 on v5

--- a/solution.py
+++ b/solution.py
@@ -596,7 +596,7 @@
 
 def gather_rows(local_rows):
     size = lax.axis_size("seq")
-    got = {step: shift(local_rows, step) for step in (3, 1, 2)}
+    got = {step: shift(local_rows, step) for step in (1, 3, 2)}
     pieces = [local_rows] + [got[size - ahead] for ahead in range(1, size)]
     return jnp.concatenate(pieces + [flip(piece, "core") for piece in pieces])
 

time: 683 us -> 683 us (level)
  no operation moved by 1% of the time
where the time goes in v6:
time: 683 us; the launch traced here: 679 us
  waiting for transfers between devices  318 us (47%)
  matrix products  104 us (15%)
  starting transfers between devices  94.6 us (14%)
  local copies, waits for them, and re-layouts  73.9 us (11%)
  other arithmetic  68.4 us (10%)
  between operations  16.3 us (2%)
    ppermute x21, waiting for transfers between devices, shift(): lax.ppermute(value, 'seq', [(i, (i + step) % size) for i in range(size)])  243 us
    dot_general x19, matrix products, dot(): lax.dot_general(left, right, ((dims[:1], dims[1:]), ((), ())), preferred_...  104 us
    ppermute x41, waiting for transfers between devices, flip(): return lax.ppermute(value, axis, [(0, 1), (1, 0)])  60.5 us
    ppermute x21, starting transfers between devices, shift(): lax.ppermute(value, 'seq', [(i, (i + step) % size) for i in range(size)])  58.2 us
    unnamed x234, local copies, waits for them, and re-layouts  32.5 us
    ppermute x41, starting transfers between devices, flip(): return lax.ppermute(value, axis, [(0, 1), (1, 0)])  21.8 us
  transfers between devices with their start and end apart: 74, of which 33 were waited for; matrix products, arithmetic and copies ran while one was open for 25% of the time, Pallas kernels for 0%

profile of v6, /device:TPU:0, one launch (start us, length us, event | category | flops | bytes accessed | tf_op | source)
XLA Modules:
  0.0 678.7 jit_solution(17508720388961090426)
XLA Ops:
  10.1 5.1 collective-permute-start.1
  19.3 4.3 collective-permute-done.2
  27.8 3.1 collective-permute-done.26
  30.9 3.3 maximum_select_fusion
  46.0 16.5 %collective-permute-done.10.refs_1_ = bf16[2,288,768]{2,1,0:T(8,128)(2,1)S(1)} collective-permute-done((bf16[2,288,768]{2,1,0:T(8,128)(2,1)S(1)}, bf16[2,288,768]{2,1,0:T(8,128)(2,1)S(1)}, u32[]{:S(2)}, u32[]{:S(2)}) %collective-permute-start.10) | collective-permute-done | bytes 884768 | tf_op jit(solution)/shard_map/ppermute | solution.py:449
  69.1 6.5 collective-permute-done.8
  81.2 2.4 copy-done.1
  87.5 2.1 copy-done.5
  89.7 2.6 fusion.127
  92.3 2.5 fusion.61
  98.4 2.2 fusion.13
  100.7 2.1 fusion.26
  106.8 3.1 collective-permute-done.15
  114.4 3.8 collective-permute-start.16
  119.2 2.7 maximum_select_fusion.1
  121.9 32.0 %collective-permute-done.18 = bf16[128,2304]{1,0:T(8,128)(2,1)} collective-permute-done((bf16[128,2304]{1,0:T(8,128)(2,1)}, bf16[128,2304]{1,0:T(8,128)(2,1)}, u32[]{:S(2)}, u32[]{:S(2)}) %collective-permute-start.18) | collective-permute-done | bytes 589856 | tf_op jit(solution)/shard_map/ppermute | solution.py:594
  160.9 22.8 %collective-permute-start.20 = (bf16[128,2304]{1,0:T(8,128)(2,1)S(1)}, bf16[128,2304]{1,0:T(8,128)(2,1)S(1)}, u32[]{:S(2)}, u32[]{:S(2)}) collective-permute-start(bf16[128,2304]{1,0:T(8,128)(2,1)S(1)} %get-tuple-element.63), channel_id=1, source_target_pairs={{0,2},{1,3},{2,0},{3,1},{4,6},{5,7},{6,4},{7,5},{8,10},{9,11},{10,... | collective-permute-start | bytes 1769480 | tf_op jit(solution)/shard_map/ppermute | solution.py:594
  185.7 8.9 %collective-permute-done.19 = bf16[128,2304]{1,0:T(8,128)(2,1)S(1)} collective-permute-done((bf16[128,2304]{1,0:T(8,128)(2,1)S(1)}, bf16[128,2304]{1,0:T(8,128)(2,1)S(1)}, u32[]{:S(2)}, u32[]{:S(2)}) %collective-permute-start.19) | collective-permute-done | bytes 589856 | tf_op jit(solution)/shard_map/ppermute | solution.py:594
  194.6 39.8 %collective-permute-done.20 = bf16[128,2304]{1,0:T(8,128)(2,1)S(1)} collective-permute-done((bf16[128,2304]{1,0:T(8,128)(2,1)S(1)}, bf16[128,2304]{1,0:T(8,128)(2,1)S(1)}, u32[]{:S(2)}, u32[]{:S(2)}) %collective-permute-start.20) | collective-permute-done | bytes 589856 | tf_op jit(solution)/shard_map/ppermute | solution.py:594
  241.0 15.1 %fusion.128 = f32[1024,2304]{1,0:T(8,128)S(1)} fusion(bf16[1024,2304]{1,0:T(8,128)(2,1)} %constant_dynamic-update-slice_fusion.9, bf16[2304,2304]{1,0:T(8,128)(2,1)} %all-gather.6.cloned.1.call-done), kind=kOutput, calls=%fused_computation.355 | convolution fusion | flops 10871635968 | bytes 24772608 | tf_op jit(solution)/shard_map/dot_general | solution.py:708
  256.2 3.6 copy-done.18
  259.7 2.7 multiply_convert_fusion.1
  262.4 6.3 convolution_convert_fusion.5
  270.6 3.5 convolution_convert_fusion.6
  277.3 3.8 collective-permute-start.29
  283.9 24.3 %collective-permute-done.31 = bf16[128,2304]{1,0:T(8,128)(2,1)} collective-permute-done((bf16[128,2304]{1,0:T(8,128)(2,1)}, bf16[128,2304]{1,0:T(8,128)(2,1)}, u32[]{:S(2)}, u32[]{:S(2)}) %collective-permute-start.31) | collective-permute-done | bytes 589856 | tf_op jit(solution)/shard_map/ppermute | solution.py:594
  308.2 11.3 %collective-permute-done.29 = bf16[128,2304]{1,0:T(8,128)(2,1)} collective-permute-done((bf16[128,2304]{1,0:T(8,128)(2,1)}, bf16[128,2304]{1,0:T(8,128)(2,1)}, u32[]{:S(2)}, u32[]{:S(2)}) %collective-permute-start.29) | collective-permute-done | bytes 589856 | tf_op jit(solution)/shard_map/ppermute | solution.py:594
  319.5 2.2 multiply_reduce_fusion.5
  324.4 2.2 collective-permute-start.35
  327.9 8.3 %collective-permute-done.33 = bf16[64,2304]{1,0:T(8,128)(2,1)S(1)} collective-permute-done((bf16[64,2304]{1,0:T(8,128)(2,1)S(1)}, bf16[64,2304]{1,0:T(8,128)(2,1)S(1)}, u32[]{:S(2)}, u32[]{:S(2)}) %collective-permute-start.33) | collective-permute-done | bytes 294944 | tf_op jit(solution)/shard_map/ppermute | solution.py:449
  338.7 39.1 %collective-permute-done.35 = bf16[128,2304]{1,0:T(8,128)(2,1)S(1)} collective-permute-done((bf16[128,2304]{1,0:T(8,128)(2,1)S(1)}, bf16[128,2304]{1,0:T(8,128)(2,1)S(1)}, u32[]{:S(2)}, u32[]{:S(2)}) %collective-permute-start.35) | collective-permute-done | bytes 589856 | tf_op jit(solution)/shard_map/ppermute | solution.py:594
  380.8 10.5 %fusion.12 = (bf16[1024,1152]{1,0:T(8,128)(2,1)S(1)}, bf16[1024,1152]{1,0:T(8,128)(2,1)}) fusion(f32[1024,2304]{1,0:T(8,128)S(1)} %bitcast.238, bf16[1024,2304]{1,0:T(8,128)(2,1)S(1)} %constant_dynamic-update-slice_fusion.17, bf16[2304,1152]{1,0:T(8,128)(2,1)S(1)} %bitcast.275), kind=kOutput, calls=%fused_computation.23 | convolution fusion | flops 5464129536 | bytes 24182784 | tf_op jit(solution)/shard_map/dot_general | solution.py:708
  391.3 15.2 %convolution_convert_fusion.3 = bf16[1024,2304]{1,0:T(8,128)(2,1)S(1)} fusion(bf16[2304,2304]{1,0:T(8,128)(2,1)} %all-gather.6.cloned.1.call-done, bf16[1024,1152]{1,0:T(8,128)(2,1)} %get-tuple-element.73, bf16[1024,1152]{1,0:T(8,128)(2,1)S(1)} %get-tuple-element.72), kind=kOutput, calls=%fused_computation.15 | convolution fusion | flops 10883432448 | bytes 20054016 | tf_op jit(solution)/shard_map/dot_general | solution.py:708
  406.9 4.4 collective-permute-done.41
  411.3 2.0 add_convert_fusion.1
  413.4 8.0 %convolution_convert_fusion.1 = bf16[2304,1152]{1,0:T(8,128)(2,1)} fusion(bf16[1024,2304]{1,0:T(8,128)(2,1)S(1)} %constant_dynamic-update-slice_fusion.17, bf16[1024,1152]{1,0:T(8,128)(2,1)S(1)} %copy-done.22), kind=kOutput, calls=%fused_computation.5 | convolution fusion | flops 5438472192 | bytes 12386304 | tf_op jit(solution)/shard_map/dot_general | solution.py:708
  421.5 2.8 fusion.118
  424.3 3.8 collective-permute-start.42
  428.1 16.5 %convolution_convert_fusion = bf16[2304,2304]{1,0:T(8,128)(2,1)} fusion(bf16[1024,2304]{1,0:T(8,128)(2,1)} %constant_dynamic-update-slice_fusion.9, bf16[1024,1152]{1,0:T(8,128)(2,1)} %get-tuple-element.73, bf16[1024,1152]{1,0:T(8,128)(2,1)S(1)} %copy-done.90), kind=kOutput, calls=%fused_computation | convolution fusion | flops 10886381568 | bytes 20054016 | tf_op jit(solution)/shard_map/dot_general | solution.py:708
  444.6 18.6 %collective-permute-done.44 = bf16[128,2304]{1,0:T(8,128)(2,1)} collective-permute-done((bf16[128,2304]{1,0:T(8,128)(2,1)}, bf16[128,2304]{1,0:T(8,128)(2,1)}, u32[]{:S(2)}, u32[]{:S(2)}) %collective-permute-start.44) | collective-permute-done | bytes 589856 | tf_op jit(solution)/shard_map/ppermute | solution.py:594
  463.3 3.1 collective-permute-done.42
  473.0 10.3 %collective-permute-start.46 = (bf16[128,2304]{1,0:T(8,128)(2,1)S(1)}, bf16[128,2304]{1,0:T(8,128)(2,1)S(1)}, u32[]{:S(2)}, u32[]{:S(2)}) collective-permute-start(bf16[128,2304]{1,0:T(8,128)(2,1)S(1)} %get-tuple-element.58), channel_id=1, source_target_pairs={{0,2},{1,3},{2,0},{3,1},{4,6},{5,7},{6,4},{7,5},{8,10},{9,11},{10,... | collective-permute-start | bytes 1769480 | tf_op jit(solution)/shard_map/ppermute | solution.py:594
  483.4 12.0 %collective-permute-done.45 = bf16[128,2304]{1,0:T(8,128)(2,1)} collective-permute-done((bf16[128,2304]{1,0:T(8,128)(2,1)S(1)}, bf16[128,2304]{1,0:T(8,128)(2,1)}, u32[]{:S(2)}, u32[]{:S(2)}) %collective-permute-start.45) | collective-permute-done | bytes 589856 | tf_op jit(solution)/shard_map/ppermute | solution.py:594
  497.4 37.1 %collective-permute-done.46 = bf16[128,2304]{1,0:T(8,128)(2,1)S(1)} collective-permute-done((bf16[128,2304]{1,0:T(8,128)(2,1)S(1)}, bf16[128,2304]{1,0:T(8,128)(2,1)S(1)}, u32[]{:S(2)}, u32[]{:S(2)}) %collective-permute-start.46) | collective-permute-done | bytes 589856 | tf_op jit(solution)/shard_map/ppermute | solution.py:594
  540.3 3.9 convolution_convert_fusion.9
  546.3 2.8 multiply_convert_fusion.2
  551.1 2.4 fusion.69
  553.5 2.5 broadcast_select_fusion
  558.4 4.4 convolution_convert_fusion.2
  562.8 3.4 slice.317
  568.0 2.9 collective-permute-done.53
  570.9 2.5 add_convert_fusion
  574.7 3.8 collective-permute-start.54
  578.5 3.8 convolution_convert_fusion.8
  582.3 3.7 convolution_convert_fusion.7
  588.0 5.9 copy.75
  599.3 4.0 fusion.5
  603.4 3.9 collective-permute-done.56
  607.2 9.6 %collective-permute-done.54 = bf16[128,2304]{1,0:T(8,128)(2,1)} collective-permute-done((bf16[128,2304]{1,0:T(8,128)(2,1)}, bf16[128,2304]{1,0:T(8,128)(2,1)}, u32[]{:S(2)}, u32[]{:S(2)}) %collective-permute-start.54) | collective-permute-done | bytes 589856 | tf_op jit(solution)/shard_map/ppermute | solution.py:594
  623.0 9.0 %collective-permute-done.60 = bf16[288,768]{1,0:T(8,128)(2,1)S(1)} collective-permute-done((bf16[288,768]{1,0:T(8,128)(2,1)S(1)}, bf16[288,768]{1,0:T(8,128)(2,1)S(1)}, u32[]{:S(2)}, u32[]{:S(2)}) %collective-permute-start.60) | collective-permute-done | bytes 442400 | tf_op jit(solution)/shard_map/ppermute | solution.py:449
  633.2 5.2 all-to-all-start
  640.4 5.5 all-to-all-done
  653.1 4.1 collective-permute-done.64
  659.3 2.5 dynamic-slice_bitcast_fusion
  (517 shorter events, 144.2 us)
Async XLA Ops:
  7.2 74.0 %all-gather.4.cloned.1.call-start = ((), (), s32[]{:S(2)}) async-start(), calls=%async_computation.3 | async-start | bytes 5308416 | tf_op jit(solution)/shard_map/all_gather | solution.py:622
  10.1 9.1 %collective-permute-start.1 = (bf16[72,2,256]{2,1,0:T(2,128)(2,1)S(1)}, bf16[72,2,256]{2,1,0:T(2,128)(2,1)S(1)}, u32[]{:S(2)}, u32[]{:S(2)}) collective-permute-start(bf16[72,2,256]{2,1,0:T(2,128)(2,1)S(1)} %bitcast.265), channel_id=1, source_target_pairs={{0,3},{1,0},{2,1},{3,2},{4,7},{5,4},{6,5},{7,6},{8,11},{9,8},{10,9... | collective-permute-start | bytes 221192 | tf_op jit(solution)/shard_map/ppermute | solution.py:587
  16.3 8.7 %collective-permute-start = (bf16[64,2304]{1,0:T(8,128)(2,1)S(1)}, bf16[64,2304]{1,0:T(8,128)(2,1)S(1)}, u32[]{:S(2)}, u32[]{:S(2)}) collective-permute-start(bf16[64,2304]{1,0:T(8,128)(2,1)S(1)} %get-tuple-element.125), channel_id=1, source_target_pairs={{0,8},{8,0},{1,9},{9,1},{2,10},{10,2},{3,11},{11,3},{4,12},{12,4},... | collective-permute-start | bytes 884744 | tf_op jit(solution)/shard_map/ppermute | solution.py:449
  18.0 5.5 collective-permute-start.2
  18.1 6.2 collective-permute-start.3
  25.9 215.1 %all-gather.6.cloned.1.call-start = ((), (), s32[]{:S(2)}) async-start(), calls=%async_computation.4 | async-start | bytes 13271040 | tf_op jit(solution)/shard_map/all_gather | solution.py:691
  34.3 228.1 %all-gather.8.cloned.1.call-start = ((), (), s32[]{:S(2)}) async-start(), calls=%async_computation.5 | async-start | bytes 6635520 | tf_op jit(solution)/shard_map/all_gather | solution.py:691
  35.0 6.8 %collective-permute-start.6 = (bf16[4,288]{1,0:T(4,128)(2,1)S(1)}, bf16[4,288]{1,0:T(4,128)(2,1)S(1)}, u32[]{:S(2)}, u32[]{:S(2)}) collective-permute-start(bf16[4,288]{1,0:T(4,128)(2,1)S(1)} %pad_maximum_fusion.19), channel_id=1, source_target_pairs={{0,4},{4,0},{1,5},{5,1},{2,6},{6,2},{3,7},{7,3},{8,12},{12,8},{9,1... | collective-permute-start | bytes 6920 | tf_op jit(solution)/shard_map/ppermute | solution.py:449
  40.0 5.1 collective-permute-start.5
  40.3 22.2 %collective-permute-start.10 = (bf16[2,288,768]{2,1,0:T(8,128)(2,1)S(1)}, bf16[2,288,768]{2,1,0:T(8,128)(2,1)S(1)}, u32[]{:S(2)}, u32[]{:S(2)}) collective-permute-start(bf16[2,288,768]{2,1,0:T(8,128)(2,1)S(1)} %maximum_select_fusion.2.refs_0_), channel_id=1, source_target_pairs={{0,8},{8,0},{1,9},{9,1},{2,10},{10,2},{3,11},{11,3},{4,12},{12,4},... | collective-permute-start | bytes 2654216 | tf_op jit(solution)/shard_map/ppermute | solution.py:449
  42.4 22.4 %collective-permute-start.11 = (bf16[2,288,768]{2,1,0:T(8,128)(2,1)S(1)}, bf16[2,288,768]{2,1,0:T(8,128)(2,1)S(1)}, u32[]{:S(2)}, u32[]{:S(2)}) collective-permute-start(bf16[2,288,768]{2,1,0:T(8,128)(2,1)S(1)} %maximum_select_fusion.2.refs_0_), channel_id=1, source_target_pairs={{0,16},{16,0},{1,17},{17,1},{2,18},{18,2},{3,19},{19,3},{4,20},{20... | collective-permute-start | bytes 2654216 | tf_op jit(solution)/shard_map/ppermute | solution.py:449
  44.5 22.5 %collective-permute-start.7 = (bf16[4,2,288]{2,0,1:T(4,128)(2,1)}, bf16[4,2,288]{2,0,1:T(4,128)(2,1)}, u32[]{:S(2)}, u32[]{:S(2)}) collective-permute-start(bf16[4,2,288]{2,0,1:T(4,128)(2,1)} %maximum_select_fusion.11), channel_id=1, source_target_pairs={{0,8},{8,0},{1,9},{9,1},{2,10},{10,2},{3,11},{11,3},{4,12},{12,4},... | collective-permute-start | bytes 13832 | tf_op jit(solution)/shard_map/ppermute | solution.py:449
  63.3 13.9 %collective-permute-start.12 = (bf16[288,768]{1,0:T(8,128)(2,1)}, bf16[288,768]{1,0:T(8,128)(2,1)S(1)}, u32[]{:S(2)}, u32[]{:S(2)}) collective-permute-start(bf16[288,768]{1,0:T(8,128)(2,1)} %slice_bitcast_fusion.3), channel_id=1, source_target_pairs={{0,16},{16,0},{1,17},{17,1},{2,18},{18,2},{3,19},{19,3},{4,20},{20... | collective-permute-start | bytes 1327112 | tf_op jit(solution)/shard_map/ppermute | solution.py:449
  65.6 11.8 %collective-permute-start.13 = (bf16[288,768]{1,0:T(8,128)(2,1)}, bf16[288,768]{1,0:T(8,128)(2,1)S(1)}, u32[]{:S(2)}, u32[]{:S(2)}) collective-permute-start(bf16[288,768]{1,0:T(8,128)(2,1)} %slice_bitcast_fusion.2), channel_id=1, source_target_pairs={{0,8},{8,0},{1,9},{9,1},{2,10},{10,2},{3,11},{11,3},{4,12},{12,4},... | collective-permute-start | bytes 1327112 | tf_op jit(solution)/shard_map/ppermute | solution.py:449
  67.7 7.8 %collective-permute-start.8 = (bf16[4,2,2,288]{3,0,2,1:T(4,128)(2,1)S(1)}, bf16[4,2,2,288]{3,0,2,1:T(4,128)(2,1)S(1)}, u32[]{:S(2)}, u32[]{:S(2)}) collective-permute-start(bf16[4,2,2,288]{3,0,2,1:T(4,128)(2,1)S(1)} %maximum_select_fusion.9), channel_id=1, source_target_pairs={{0,16},{16,0},{1,17},{17,1},{2,18},{18,2},{3,19},{19,3},{4,20},{20... | collective-permute-start | bytes 27656 | tf_op jit(solution)/shard_map/ppermute | solution.py:449
  106.6 11.7 %collective-permute-start.27 = (bf16[288,1152]{1,0:T(8,128)(2,1)S(1)}, bf16[288,1152]{1,0:T(8,128)(2,1)S(1)}, u32[]{:S(2)}, u32[]{:S(2)}) collective-permute-start(bf16[288,1152]{1,0:T(8,128)(2,1)S(1)} %get-tuple-element.105), channel_id=1, source_target_pairs={{0,4},{4,0},{1,5},{5,1},{2,6},{6,2},{3,7},{7,3},{8,12},{12,8},{9,1... | collective-permute-start | bytes 1990664 | tf_op jit(solution)/shard_map/ppermute | solution.py:449
  113.1 40.8 %collective-permute-start.18 = (bf16[128,2304]{1,0:T(8,128)(2,1)}, bf16[128,2304]{1,0:T(8,128)(2,1)}, u32[]{:S(2)}, u32[]{:S(2)}) collective-permute-start(bf16[128,2304]{1,0:T(8,128)(2,1)} %get-tuple-element.92), channel_id=1, source_target_pairs={{0,2},{1,3},{2,0},{3,1},{4,6},{5,7},{6,4},{7,5},{8,10},{9,11},{10,... | collective-permute-start | bytes 1769480 | tf_op jit(solution)/shard_map/ppermute | solution.py:594
  114.3 39.6 %collective-permute-start.17 = (bf16[128,2304]{1,0:T(8,128)(2,1)}, bf16[128,2304]{1,0:T(8,128)(2,1)}, u32[]{:S(2)}, u32[]{:S(2)}) collective-permute-start(bf16[128,2304]{1,0:T(8,128)(2,1)} %get-tuple-element.93), channel_id=1, source_target_pairs={{0,1},{1,2},{2,3},{3,0},{4,5},{5,6},{6,7},{7,4},{8,9},{9,10},{10,1... | collective-permute-start | bytes 1769480 | tf_op jit(solution)/shard_map/ppermute | solution.py:594
  114.4 40.8 %collective-permute-start.16 = (bf16[128,2304]{1,0:T(8,128)(2,1)}, bf16[128,2304]{1,0:T(8,128)(2,1)}, u32[]{:S(2)}, u32[]{:S(2)}) collective-permute-start(bf16[128,2304]{1,0:T(8,128)(2,1)} %get-tuple-element.91), channel_id=1, source_target_pairs={{0,3},{1,0},{2,1},{3,2},{4,7},{5,4},{6,5},{7,6},{8,11},{9,8},{10,9... | collective-permute-start | bytes 1769480 | tf_op jit(solution)/shard_map/ppermute | solution.py:594
  121.9 535.4 %reduce-scatter.3.cloned.1.call-start = ((), (), s32[]{:S(2)}) async-start(), calls=%async_computation.6 | async-start | bytes 6635520 | tf_op jit(solution)/shard_map/reduce_scatter | solution.py:696
  158.9 35.7 %collective-permute-start.19 = (bf16[128,2304]{1,0:T(8,128)(2,1)S(1)}, bf16[128,2304]{1,0:T(8,128)(2,1)S(1)}, u32[]{:S(2)}, u32[]{:S(2)}) collective-permute-start(bf16[128,2304]{1,0:T(8,128)(2,1)S(1)} %get-tuple-element.63), channel_id=1, source_target_pairs={{0,3},{1,0},{2,1},{3,2},{4,7},{5,4},{6,5},{7,6},{8,11},{9,8},{10,9... | collective-permute-start | bytes 1769480 | tf_op jit(solution)/shard_map/ppermute | solution.py:594
  160.9 73.6 %collective-permute-start.20 = (bf16[128,2304]{1,0:T(8,128)(2,1)S(1)}, bf16[128,2304]{1,0:T(8,128)(2,1)S(1)}, u32[]{:S(2)}, u32[]{:S(2)}) collective-permute-start(bf16[128,2304]{1,0:T(8,128)(2,1)S(1)} %get-tuple-element.63), channel_id=1, source_target_pairs={{0,2},{1,3},{2,0},{3,1},{4,6},{5,7},{6,4},{7,5},{8,10},{9,11},{10,... | collective-permute-start | bytes 1769480 | tf_op jit(solution)/shard_map/ppermute | solution.py:594
  183.7 50.7 %collective-permute-start.21 = (bf16[128,2304]{1,0:T(8,128)(2,1)S(1)}, bf16[128,2304]{1,0:T(8,128)(2,1)S(1)}, u32[]{:S(2)}, u32[]{:S(2)}) collective-permute-start(bf16[128,2304]{1,0:T(8,128)(2,1)S(1)} %get-tuple-element.63), channel_id=1, source_target_pairs={{0,1},{1,2},{2,3},{3,0},{4,5},{5,6},{6,7},{7,4},{8,9},{9,10},{10,1... | collective-permute-start | bytes 1769480 | tf_op jit(solution)/shard_map/ppermute | solution.py:594
  185.7 51.8 %collective-permute-start.22 = (bf16[128,2304]{1,0:T(8,128)(2,1)S(1)}, bf16[128,2304]{1,0:T(8,128)(2,1)S(1)}, u32[]{:S(2)}, u32[]{:S(2)}) collective-permute-start(bf16[128,2304]{1,0:T(8,128)(2,1)S(1)} %get-tuple-element.63), channel_id=1, source_target_pairs={{0,4},{4,0},{1,5},{5,1},{2,6},{6,2},{3,7},{7,3},{8,12},{12,8},{9,1... | collective-permute-start | bytes 1769480 | tf_op jit(solution)/shard_map/ppermute | solution.py:449
  194.6 43.8 %collective-permute-start.23 = (bf16[128,2304]{1,0:T(8,128)(2,1)S(1)}, bf16[128,2304]{1,0:T(8,128)(2,1)S(1)}, u32[]{:S(2)}, u32[]{:S(2)}) collective-permute-start(bf16[128,2304]{1,0:T(8,128)(2,1)S(1)} %collective-permute-done.19), channel_id=1, source_target_pairs={{0,4},{4,0},{1,5},{5,1},{2,6},{6,2},{3,7},{7,3},{8,12},{12,8},{9,1... | collective-permute-start | bytes 1769480 | tf_op jit(solution)/shard_map/ppermute | solution.py:449
  234.4 4.8 collective-permute-start.24
  234.4 5.7 collective-permute-start.25
  268.7 5.4 collective-permute-start.28
  269.6 12.2 %collective-permute-start.32 = (bf16[64,2304]{1,0:T(8,128)(2,1)}, bf16[64,2304]{1,0:T(8,128)(2,1)S(1)}, u32[]{:S(2)}, u32[]{:S(2)}) collective-permute-start(bf16[64,2304]{1,0:T(8,128)(2,1)} %get-tuple-element.123), channel_id=1, source_target_pairs={{0,8},{8,0},{1,9},{9,1},{2,10},{10,2},{3,11},{11,3},{4,12},{12,4},... | collective-permute-start | bytes 884744 | tf_op jit(solution)/shard_map/ppermute | solution.py:449
  277.3 30.9 %collective-permute-start.31 = (bf16[128,2304]{1,0:T(8,128)(2,1)}, bf16[128,2304]{1,0:T(8,128)(2,1)}, u32[]{:S(2)}, u32[]{:S(2)}) collective-permute-start(bf16[128,2304]{1,0:T(8,128)(2,1)} %get-tuple-element.89), channel_id=1, source_target_pairs={{0,2},{1,3},{2,0},{3,1},{4,6},{5,7},{6,4},{7,5},{8,10},{9,11},{10,... | collective-permute-start | bytes 1769480 | tf_op jit(solution)/shard_map/ppermute | solution.py:594
  277.3 30.9 %collective-permute-start.30 = (bf16[128,2304]{1,0:T(8,128)(2,1)}, bf16[128,2304]{1,0:T(8,128)(2,1)}, u32[]{:S(2)}, u32[]{:S(2)}) collective-permute-start(bf16[128,2304]{1,0:T(8,128)(2,1)} %get-tuple-element.90), channel_id=1, source_target_pairs={{0,1},{1,2},{2,3},{3,0},{4,5},{5,6},{6,7},{7,4},{8,9},{9,10},{10,1... | collective-permute-start | bytes 1769480 | tf_op jit(solution)/shard_map/ppermute | solution.py:594
  277.3 42.2 %collective-permute-start.29 = (bf16[128,2304]{1,0:T(8,128)(2,1)}, bf16[128,2304]{1,0:T(8,128)(2,1)}, u32[]{:S(2)}, u32[]{:S(2)}) collective-permute-start(bf16[128,2304]{1,0:T(8,128)(2,1)} %get-tuple-element.88), channel_id=1, source_target_pairs={{0,3},{1,0},{2,1},{3,2},{4,7},{5,4},{6,5},{7,6},{8,11},{9,8},{10,9... | collective-permute-start | bytes 1769480 | tf_op jit(solution)/shard_map/ppermute | solution.py:594
  323.3 15.4 %collective-permute-start.34 = (bf16[128,2304]{1,0:T(8,128)(2,1)S(1)}, bf16[128,2304]{1,0:T(8,128)(2,1)S(1)}, u32[]{:S(2)}, u32[]{:S(2)}) collective-permute-start(bf16[128,2304]{1,0:T(8,128)(2,1)S(1)} %get-tuple-element.106), channel_id=1, source_target_pairs={{0,3},{1,0},{2,1},{3,2},{4,7},{5,4},{6,5},{7,6},{8,11},{9,8},{10,9... | collective-permute-start | bytes 1769480 | tf_op jit(solution)/shard_map/ppermute | solution.py:594
  324.4 53.4 %collective-permute-start.35 = (bf16[128,2304]{1,0:T(8,128)(2,1)S(1)}, bf16[128,2304]{1,0:T(8,128)(2,1)S(1)}, u32[]{:S(2)}, u32[]{:S(2)}) collective-permute-start(bf16[128,2304]{1,0:T(8,128)(2,1)S(1)} %get-tuple-element.106), channel_id=1, source_target_pairs={{0,2},{1,3},{2,0},{3,1},{4,6},{5,7},{6,4},{7,5},{8,10},{9,11},{10,... | collective-permute-start | bytes 1769480 | tf_op jit(solution)/shard_map/ppermute | solution.py:594
  326.7 51.2 %collective-permute-start.36 = (bf16[128,2304]{1,0:T(8,128)(2,1)S(1)}, bf16[128,2304]{1,0:T(8,128)(2,1)S(1)}, u32[]{:S(2)}, u32[]{:S(2)}) collective-permute-start(bf16[128,2304]{1,0:T(8,128)(2,1)S(1)} %get-tuple-element.106), channel_id=1, source_target_pairs={{0,1},{1,2},{2,3},{3,0},{4,5},{5,6},{6,7},{7,4},{8,9},{9,10},{10,1... | collective-permute-start | bytes 1769480 | tf_op jit(solution)/shard_map/ppermute | solution.py:594
  326.7 51.9 %collective-permute-start.37 = (bf16[128,2304]{1,0:T(8,128)(2,1)S(1)}, bf16[128,2304]{1,0:T(8,128)(2,1)S(1)}, u32[]{:S(2)}, u32[]{:S(2)}) collective-permute-start(bf16[128,2304]{1,0:T(8,128)(2,1)S(1)} %get-tuple-element.106), channel_id=1, source_target_pairs={{0,4},{4,0},{1,5},{5,1},{2,6},{6,2},{3,7},{7,3},{8,12},{12,8},{9,1... | collective-permute-start | bytes 1769480 | tf_op jit(solution)/shard_map/ppermute | solution.py:449
  326.7 9.5 %collective-permute-start.33 = (bf16[64,2304]{1,0:T(8,128)(2,1)S(1)}, bf16[64,2304]{1,0:T(8,128)(2,1)S(1)}, u32[]{:S(2)}, u32[]{:S(2)}) collective-permute-start(bf16[64,2304]{1,0:T(8,128)(2,1)S(1)} %get-tuple-element.121), channel_id=1, source_target_pairs={{0,8},{8,0},{1,9},{9,1},{2,10},{10,2},{3,11},{11,3},{4,12},{12,4},... | collective-permute-start | bytes 884744 | tf_op jit(solution)/shard_map/ppermute | solution.py:449
  338.7 39.9 %collective-permute-start.38 = (bf16[128,2304]{1,0:T(8,128)(2,1)S(1)}, bf16[128,2304]{1,0:T(8,128)(2,1)S(1)}, u32[]{:S(2)}, u32[]{:S(2)}) collective-permute-start(bf16[128,2304]{1,0:T(8,128)(2,1)S(1)} %collective-permute-done.34), channel_id=1, source_target_pairs={{0,4},{4,0},{1,5},{5,1},{2,6},{6,2},{3,7},{7,3},{8,12},{12,8},{9,1... | collective-permute-start | bytes 1769480 | tf_op jit(solution)/shard_map/ppermute | solution.py:449
  421.4 235.9 %reduce-scatter.5.cloned.1.call-start = ((), (), s32[]{:S(2)}) async-start(), calls=%async_computation.7 | async-start | bytes 13271040 | tf_op jit(solution)/shard_map/reduce_scatter | solution.py:696
  424.3 39.0 %collective-permute-start.44 = (bf16[128,2304]{1,0:T(8,128)(2,1)}, bf16[128,2304]{1,0:T(8,128)(2,1)}, u32[]{:S(2)}, u32[]{:S(2)}) collective-permute-start(bf16[128,2304]{1,0:T(8,128)(2,1)} %get-tuple-element.86), channel_id=1, source_target_pairs={{0,2},{1,3},{2,0},{3,1},{4,6},{5,7},{6,4},{7,5},{8,10},{9,11},{10,... | collective-permute-start | bytes 1769480 | tf_op jit(solution)/shard_map/ppermute | solution.py:594
  424.3 39.0 %collective-permute-start.43 = (bf16[128,2304]{1,0:T(8,128)(2,1)}, bf16[128,2304]{1,0:T(8,128)(2,1)}, u32[]{:S(2)}, u32[]{:S(2)}) collective-permute-start(bf16[128,2304]{1,0:T(8,128)(2,1)} %get-tuple-element.87), channel_id=1, source_target_pairs={{0,1},{1,2},{2,3},{3,0},{4,5},{5,6},{6,7},{7,4},{8,9},{9,10},{10,1... | collective-permute-start | bytes 1769480 | tf_op jit(solution)/shard_map/ppermute | solution.py:594
  424.3 42.1 %collective-permute-start.42 = (bf16[128,2304]{1,0:T(8,128)(2,1)}, bf16[128,2304]{1,0:T(8,128)(2,1)}, u32[]{:S(2)}, u32[]{:S(2)}) collective-permute-start(bf16[128,2304]{1,0:T(8,128)(2,1)} %get-tuple-element.85), channel_id=1, source_target_pairs={{0,3},{1,0},{2,1},{3,2},{4,7},{5,4},{6,5},{7,6},{8,11},{9,8},{10,9... | collective-permute-start | bytes 1769480 | tf_op jit(solution)/shard_map/ppermute | solution.py:594
  471.9 23.6 %collective-permute-start.45 = (bf16[128,2304]{1,0:T(8,128)(2,1)S(1)}, bf16[128,2304]{1,0:T(8,128)(2,1)}, u32[]{:S(2)}, u32[]{:S(2)}) collective-permute-start(bf16[128,2304]{1,0:T(8,128)(2,1)S(1)} %get-tuple-element.58), channel_id=1, source_target_pairs={{0,3},{1,0},{2,1},{3,2},{4,7},{5,4},{6,5},{7,6},{8,11},{9,8},{10,9... | collective-permute-start | bytes 1769480 | tf_op jit(solution)/shard_map/ppermute | solution.py:594
  473.0 61.5 %collective-permute-start.46 = (bf16[128,2304]{1,0:T(8,128)(2,1)S(1)}, bf16[128,2304]{1,0:T(8,128)(2,1)S(1)}, u32[]{:S(2)}, u32[]{:S(2)}) collective-permute-start(bf16[128,2304]{1,0:T(8,128)(2,1)S(1)} %get-tuple-element.58), channel_id=1, source_target_pairs={{0,2},{1,3},{2,0},{3,1},{4,6},{5,7},{6,4},{7,5},{8,10},{9,11},{10,... | collective-permute-start | bytes 1769480 | tf_op jit(solution)/shard_map/ppermute | solution.py:594
  483.3 51.2 %collective-permute-start.47 = (bf16[128,2304]{1,0:T(8,128)(2,1)S(1)}, bf16[128,2304]{1,0:T(8,128)(2,1)S(1)}, u32[]{:S(2)}, u32[]{:S(2)}) collective-permute-start(bf16[128,2304]{1,0:T(8,128)(2,1)S(1)} %get-tuple-element.58), channel_id=1, source_target_pairs={{0,1},{1,2},{2,3},{3,0},{4,5},{5,6},{6,7},{7,4},{8,9},{9,10},{10,1... | collective-permute-start | bytes 1769480 | tf_op jit(solution)/shard_map/ppermute | solution.py:594
  483.4 53.4 %collective-permute-start.48 = (bf16[128,2304]{1,0:T(8,128)(2,1)S(1)}, bf16[128,2304]{1,0:T(8,128)(2,1)S(1)}, u32[]{:S(2)}, u32[]{:S(2)}) collective-permute-start(bf16[128,2304]{1,0:T(8,128)(2,1)S(1)} %get-tuple-element.58), channel_id=1, source_target_pairs={{0,4},{4,0},{1,5},{5,1},{2,6},{6,2},{3,7},{7,3},{8,12},{12,8},{9,1... | collective-permute-start | bytes 1769480 | tf_op jit(solution)/shard_map/ppermute | solution.py:449
  495.5 42.2 %collective-permute-start.49 = (bf16[128,2304]{1,0:T(8,128)(2,1)}, bf16[128,2304]{1,0:T(8,128)(2,1)S(1)}, u32[]{:S(2)}, u32[]{:S(2)}) collective-permute-start(bf16[128,2304]{1,0:T(8,128)(2,1)} %collective-permute-done.45), channel_id=1, source_target_pairs={{0,4},{4,0},{1,5},{5,1},{2,6},{6,2},{3,7},{7,3},{8,12},{12,8},{9,1... | collective-permute-start | bytes 1769480 | tf_op jit(solution)/shard_map/ppermute | solution.py:449
  534.5 4.9 collective-permute-start.51
  566.2 4.7 collective-permute-start.53
  574.7 32.6 %collective-permute-start.56 = (bf16[128,2304]{1,0:T(8,128)(2,1)}, bf16[128,2304]{1,0:T(8,128)(2,1)S(1)}, u32[]{:S(2)}, u32[]{:S(2)}) collective-permute-start(bf16[128,2304]{1,0:T(8,128)(2,1)} %get-tuple-element.83), channel_id=1, source_target_pairs={{0,2},{1,3},{2,0},{3,1},{4,6},{5,7},{6,4},{7,5},{8,10},{9,11},{10,... | collective-permute-start | bytes 1769480 | tf_op jit(solution)/shard_map/ppermute | solution.py:594
  574.7 32.6 %collective-permute-start.55 = (bf16[128,2304]{1,0:T(8,128)(2,1)}, bf16[128,2304]{1,0:T(8,128)(2,1)}, u32[]{:S(2)}, u32[]{:S(2)}) collective-permute-start(bf16[128,2304]{1,0:T(8,128)(2,1)} %get-tuple-element.84), channel_id=1, source_target_pairs={{0,1},{1,2},{2,3},{3,0},{4,5},{5,6},{6,7},{7,4},{8,9},{9,10},{10,1... | collective-permute-start | bytes 1769480 | tf_op jit(solution)/shard_map/ppermute | solution.py:594
  574.7 42.2 %collective-permute-start.54 = (bf16[128,2304]{1,0:T(8,128)(2,1)}, bf16[128,2304]{1,0:T(8,128)(2,1)}, u32[]{:S(2)}, u32[]{:S(2)}) collective-permute-start(bf16[128,2304]{1,0:T(8,128)(2,1)} %get-tuple-element.82), channel_id=1, source_target_pairs={{0,3},{1,0},{2,1},{3,2},{4,7},{5,4},{6,5},{7,6},{8,11},{9,8},{10,9... | collective-permute-start | bytes 1769480 | tf_op jit(solution)/shard_map/ppermute | solution.py:594
  595.7 22.9 %collective-permute-start.57 = (bf16[2,288,768]{2,1,0:T(8,128)(2,1)S(1)}, bf16[2,288,768]{2,1,0:T(8,128)(2,1)S(1)}, u32[]{:S(2)}, u32[]{:S(2)}) collective-permute-start(bf16[2,288,768]{2,1,0:T(8,128)(2,1)S(1)} %slice_bitcast_fusion.1), channel_id=1, source_target_pairs={{0,16},{16,0},{1,17},{17,1},{2,18},{18,2},{3,19},{19,3},{4,20},{20... | collective-permute-start | bytes 2654216 | tf_op jit(solution)/shard_map/ppermute | solution.py:449
  597.2 21.4 %collective-permute-start.58 = (bf16[2,288,768]{2,1,0:T(8,128)(2,1)S(1)}, bf16[2,288,768]{2,1,0:T(8,128)(2,1)S(1)}, u32[]{:S(2)}, u32[]{:S(2)}) collective-permute-start(bf16[2,288,768]{2,1,0:T(8,128)(2,1)S(1)} %slice_bitcast_fusion), channel_id=1, source_target_pairs={{0,8},{8,0},{1,9},{9,1},{2,10},{10,2},{3,11},{11,3},{4,12},{12,4},... | collective-permute-start | bytes 2654216 | tf_op jit(solution)/shard_map/ppermute | solution.py:449
  618.8 13.2 %collective-permute-start.60 = (bf16[288,768]{1,0:T(8,128)(2,1)S(1)}, bf16[288,768]{1,0:T(8,128)(2,1)S(1)}, u32[]{:S(2)}, u32[]{:S(2)}) collective-permute-start(bf16[288,768]{1,0:T(8,128)(2,1)S(1)} %get-tuple-element.77), channel_id=1, source_target_pairs={{0,8},{8,0},{1,9},{9,1},{2,10},{10,2},{3,11},{11,3},{4,12},{12,4},... | collective-permute-start | bytes 1327112 | tf_op jit(solution)/shard_map/ppermute | solution.py:449
  619.9 12.1 %collective-permute-start.61 = (bf16[288,768]{1,0:T(8,128)(2,1)S(1)}, bf16[288,768]{1,0:T(8,128)(2,1)S(1)}, u32[]{:S(2)}, u32[]{:S(2)}) collective-permute-start(bf16[288,768]{1,0:T(8,128)(2,1)S(1)} %get-tuple-element.76), channel_id=1, source_target_pairs={{0,16},{16,0},{1,17},{17,1},{2,18},{18,2},{3,19},{19,3},{4,20},{20... | collective-permute-start | bytes 1327112 | tf_op jit(solution)/shard_map/ppermute | solution.py:449
  621.9 16.5 %collective-permute-start.59 = (bf16[64,2304]{1,0:T(8,128)(2,1)S(1)}, bf16[64,2304]{1,0:T(8,128)(2,1)}, u32[]{:S(2)}, u32[]{:S(2)}) collective-permute-start(bf16[64,2304]{1,0:T(8,128)(2,1)S(1)} %get-tuple-element.119), channel_id=1, source_target_pairs={{0,8},{8,0},{1,9},{9,1},{2,10},{10,2},{3,11},{11,3},{4,12},{12,4},... | collective-permute-start | bytes 884744 | tf_op jit(solution)/shard_map/ppermute | solution.py:449
  632.4 14.1 %collective-permute-start.62 = (bf16[288,768]{1,0:T(8,128)(2,1)S(1)}, bf16[288,768]{1,0:T(8,128)(2,1)S(1)}, u32[]{:S(2)}, u32[]{:S(2)}) collective-permute-start(bf16[288,768]{1,0:T(8,128)(2,1)S(1)} %select_convert_fusion), channel_id=1, source_target_pairs={{0,4},{4,0},{1,5},{5,1},{2,6},{6,2},{3,7},{7,3},{8,12},{12,8},{9,1... | collective-permute-start | bytes 1327112 | tf_op jit(solution)/shard_map/ppermute | solution.py:449
  633.2 12.7 %all-to-all-start = ((f32[32,4,72]{2,1,0:T(4,128)}), f32[32,4,72]{2,1,0:T(4,128)S(1)}, u32[]{:S(2)}, u32[]{:S(2)}) async-start(f32[32,4,72]{2,1,0:T(4,128)} %copy.79), calls=%async_computation.2 | async-start | bytes 131072 | tf_op jit(solution)/shard_map/all_to_all | solution.py:865
  648.3 4.8 collective-permute-start.63
  649.2 7.9 %collective-permute-start.64 = (bf16[72,512]{1,0:T(8,128)(2,1)S(1)}, bf16[72,512]{1,0:T(8,128)(2,1)S(1)}, u32[]{:S(2)}, u32[]{:S(2)}) collective-permute-start(bf16[72,512]{1,0:T(8,128)(2,1)S(1)} %get-tuple-element.132), channel_id=1, source_target_pairs={{0,2},{1,3},{2,0},{3,1},{4,6},{5,7},{6,4},{7,5},{8,10},{9,11},{10,... | collective-permute-start | bytes 221192 | tf_op jit(solution)/shard_map/ppermute | solution.py:587
  650.1 7.1 %collective-permute-start.65 = (bf16[72,512]{1,0:T(8,128)(2,1)S(1)}, bf16[72,512]{1,0:T(8,128)(2,1)S(1)}, u32[]{:S(2)}, u32[]{:S(2)}) collective-permute-start(bf16[72,512]{1,0:T(8,128)(2,1)S(1)} %get-tuple-element.130), channel_id=1, source_target_pairs={{0,1},{1,2},{2,3},{3,0},{4,5},{5,6},{6,7},{7,4},{8,9},{9,10},{10,1... | collective-permute-start | bytes 221192 | tf_op jit(solution)/shard_map/ppermute | solution.py:587
  659.3 5.5 collective-permute-start.67
  661.7 4.9 collective-permute-start.66
  (110 other events, 1290.8 us)
Sparse Core Ops, SparseCore 0:
  26.0 49.8 all-gather.3
  78.4 104.9 all-gather.5
  185.2 61.9 all-gather.7
  421.5 59.4 reduce-scatter.2
  484.0 104.8 reduce-scatter.4
